TPU v7x, 32 devices: a whole 2x2x4 slice. The times are simulated.
32 devices in a mesh: dp: 8 (over z, x), fsdp: 4 (over y, core).
Axes of the slice: x: 2, y: 2, z: 4, core: 2. Of those that a mesh axis runs over, the one named last changes fastest.
Arguments:
- tokens: bfloat16 [8, 2048, 960], P('dp', 'fsdp'), may hold values from -6 to 6
- seq_cuts: int32 [8, 3], P('dp'), may hold values from 0 to 2048, as said below
- w_query: bfloat16 [960, 960], P('fsdp'), may hold values from -0.1875 to 0.1875
- w_key: bfloat16 [960, 320], P('fsdp'), may hold values from -0.1875 to 0.1875
- w_value: bfloat16 [960, 320], P('fsdp'), may hold values from -0.1875 to 0.1875
- w_output: bfloat16 [960, 960], P('fsdp'), may hold values from -1.5 to 1.5
- w_gate: bfloat16 [960, 2560], P('fsdp'), may hold values from -0.1875 to 0.1875
- w_up: bfloat16 [960, 2560], P('fsdp'), may hold values from -0.1875 to 0.1875
- w_down: bfloat16 [2560, 960], P('fsdp'), may hold values from -0.15625 to 0.15625
- gain_attn: float32 [960], replicated, may hold values from 0.5 to 1.5
- gain_ffn: float32 [960], replicated, may hold values from 0.5 to 1.5
- cotangent: bfloat16 [8, 2048, 960], P('dp', 'fsdp'), may hold values from -6 to 6
Outputs:
- output: bfloat16 [8, 2048, 960], P('dp', 'fsdp')
- grad_tokens: bfloat16 [8, 2048, 960], P('dp', 'fsdp')
- grad_query: float32 [960, 960], P('fsdp')
- grad_key: float32 [960, 320], P('fsdp')
- grad_value: float32 [960, 320], P('fsdp')
- grad_output: float32 [960, 960], P('fsdp')
- grad_gate: float32 [960, 2560], P('fsdp')
- grad_up: float32 [960, 2560], P('fsdp')
- grad_down: float32 [2560, 960], P('fsdp')
- grad_gain_attn: float32 [960], P('fsdp')
- grad_gain_ffn: float32 [960], P('fsdp')
Inputs may be any that keep to these rules, and one draw needn't show every extreme that they name: For every group g: seq_cuts[g, 0] < 512, 1536 < seq_cuts[g, 1] <= seq_cuts[g, 2] <= 2048. The group's sequences are the nonempty ranges between 0, the cuts and 2048. In every draw some group holds a single sequence.
All inputs are finite; a program needn't handle non-finite values.
Results may differ from a plain program's by a relative error of at most 0.025.
Values may be sent and summed in bfloat16 or wider, within the bound.
No kernel may reach another device: no remote copies, remote signals or barrier semaphores. Data moves between devices by JAX's collectives and lax.ppermute only.
A program may use at most 192 MiB of HBM per device.

v0:
```python
import jax
import jax.numpy as jnp
from jax import lax
from jax.sharding import PartitionSpec as P

HEADS = 15
KV_HEADS = 5
HEAD = 64


EPS = 1e-05
NEGATIVE = -1e30


def for_sending(array):
    return jax.tree.map(lambda a: a.astype(jnp.bfloat16) if a.dtype == jnp.float32 else a, array)


def rotate(values, cosine, sine_table):
    half_width = values.shape[-1] // 2
    lower_half = values[..., :half_width]
    upper_half = values[..., half_width:]
    return jnp.concatenate(
        [
            lower_half * cosine - upper_half * sine_table,
            upper_half * cosine + lower_half * sine_table,
        ],
        axis=-1,
    )


def unrotate(values, cosine, sine_table):
    half_width = values.shape[-1] // 2
    lower_half = values[..., :half_width]
    upper_half = values[..., half_width:]
    return jnp.concatenate(
        [
            lower_half * cosine + upper_half * sine_table,
            upper_half * cosine - lower_half * sine_table,
        ],
        axis=-1,
    )


def tables(positions):
    half_width = HEAD // 2
    frequency = jnp.power(10000.0, -2.0 * jnp.arange(half_width, dtype=jnp.float32) / HEAD)
    angle_table = positions.astype(jnp.float32)[:, None] * frequency[None, :]
    return (jnp.cos(angle_table)[:, None, :], jnp.sin(angle_table)[:, None, :])


def locate(token_index, bounds):
    passed = token_index[:, None] >= bounds[None, :]
    doc_ids = jnp.sum(passed.astype(jnp.int32), axis=1)
    starts = jnp.max(jnp.where(passed, bounds[None, :], 0), axis=1)
    return (token_index - starts, doc_ids)


def product(left, right):
    return jnp.dot(left, right, preferred_element_type=jnp.float32)


def outer_sum(left, right):
    return jnp.einsum("ti,tj->ij", left, right, preferred_element_type=jnp.float32)


def against(left, right):
    return jnp.einsum("tj,ij->ti", left, right, preferred_element_type=jnp.float32)


def norm_forward(hidden, gain):
    inverse = lax.rsqrt(jnp.mean(hidden * hidden, axis=-1, keepdims=True) + EPS)
    return (hidden * inverse * gain, inverse)


def norm_backward(upstream, hidden, inverse, gain):
    scaled = upstream * gain
    gain_grad = jnp.sum(upstream * hidden * inverse, axis=0)
    grad_hidden = inverse * scaled - inverse * inverse * inverse * hidden * jnp.mean(
        scaled * hidden, axis=-1, keepdims=True
    )
    return (grad_hidden, gain_grad)


def head_forward(operands, allowed, score_scale):
    query_block, key_block, value_block = operands
    raw_scores = jnp.einsum(
        "qgd,sd->gqs", query_block, key_block, preferred_element_type=jnp.float32
    )
    scores = jnp.where(allowed[None], raw_scores * score_scale, NEGATIVE)
    peak_score = jnp.max(scores, axis=-1, keepdims=True)
    weights = jnp.exp(scores - peak_score)
    denominator = jnp.sum(weights, axis=-1, keepdims=True)
    probabilities = (weights / denominator).astype(jnp.bfloat16)
    mixed_heads = jnp.einsum(
        "gqs,sd->qgd", probabilities, value_block, preferred_element_type=jnp.float32
    )
    return (mixed_heads, (peak_score + jnp.log(denominator))[..., 0])


def head_backward(operands, allowed, score_scale):
    query_block, key_block, value_block, grad_block, log_total, correction = operands
    raw_scores = jnp.einsum(
        "qgd,sd->gqs", query_block, key_block, preferred_element_type=jnp.float32
    )
    scores = jnp.where(allowed[None], raw_scores * score_scale, NEGATIVE)
    probabilities = jnp.exp(scores - log_total[..., None])
    grad_probs = jnp.einsum(
        "qgd,sd->gqs", grad_block, value_block, preferred_element_type=jnp.float32
    )
    grad_scores = (probabilities * (grad_probs - correction[..., None])).astype(jnp.bfloat16)
    grad_values = jnp.einsum(
        "gqs,qgd->sd",
        probabilities.astype(jnp.bfloat16),
        grad_block,
        preferred_element_type=jnp.float32,
    )
    grad_queries = (
        jnp.einsum("gqs,sd->qgd", grad_scores, key_block, preferred_element_type=jnp.float32)
        * score_scale
    )
    grad_keys = (
        jnp.einsum("gqs,qgd->sd", grad_scores, query_block, preferred_element_type=jnp.float32)
        * score_scale
    )
    return (grad_queries, grad_keys, grad_values)


def split_heads(queries, all_keys, all_values):
    row_count = queries.shape[0]
    key_count = all_keys.shape[0]
    group_size = HEADS // KV_HEADS
    query_heads = queries.reshape(row_count, KV_HEADS, group_size, HEAD).transpose(1, 0, 2, 3)
    key_heads = all_keys.reshape(key_count, KV_HEADS, HEAD).transpose(1, 0, 2)
    value_heads = all_values.reshape(key_count, KV_HEADS, HEAD).transpose(1, 0, 2)
    return (query_heads, key_heads, value_heads)


def run_forward(hidden, matrices, gain_pair, context):
    w_query, w_key, w_value, w_output, w_gate, w_up, w_down = matrices
    gain_attn, gain_ffn = gain_pair
    cosine, sine_table, allowed = context
    row_count = hidden.shape[0]
    normed, inverse_attn = norm_forward(hidden, gain_attn)
    normed = normed.astype(jnp.bfloat16)
    queries = rotate(
        product(normed, w_query).reshape(row_count, HEADS, HEAD), cosine, sine_table
    ).astype(jnp.bfloat16)
    key_rows = (
        rotate(product(normed, w_key).reshape(row_count, KV_HEADS, HEAD), cosine, sine_table)
        .astype(jnp.bfloat16)
        .reshape(row_count, KV_HEADS * HEAD)
    )
    value_rows = product(normed, w_value).astype(jnp.bfloat16)
    all_keys, all_values = (
        lax.all_gather(key_rows, "fsdp", axis=0, tiled=True),
        lax.all_gather(value_rows, "fsdp", axis=0, tiled=True),
    )
    query_heads, key_heads, value_heads = split_heads(queries, all_keys, all_values)
    score_scale = HEAD ** (-0.5)
    mixed_heads, log_total = lax.map(
        lambda operands: head_forward(operands, allowed, score_scale),
        (query_heads, key_heads, value_heads),
    )
    mixed_heads = mixed_heads.transpose(1, 0, 2, 3).reshape(row_count, HEADS * HEAD)
    attended = mixed_heads.astype(jnp.bfloat16)
    after_attn = hidden + product(attended, w_output)
    normed_ffn, inverse_ffn = norm_forward(after_attn, gain_ffn)
    normed_ffn = normed_ffn.astype(jnp.bfloat16)
    gate_act = product(normed_ffn, w_gate)
    up_act = product(normed_ffn, w_up)
    hidden_act = (gate_act * jax.nn.sigmoid(gate_act) * up_act).astype(jnp.bfloat16)
    result = after_attn + product(hidden_act, w_down)
    kept_pair = (all_keys, all_values)
    stored = {
        "hidden": hidden,
        "inverse_attn": inverse_attn,
        "normed": normed,
        "queries": queries,
        "kept_pair": kept_pair,
        "mixed_heads": mixed_heads,
        "log_total": log_total,
        "attended": attended,
        "after_attn": after_attn,
        "inverse_ffn": inverse_ffn,
        "normed_ffn": normed_ffn,
        "gate_act": gate_act,
        "up_act": up_act,
        "hidden_act": hidden_act,
    }
    return (result, stored)


def run_backward(upstream, stored, matrices, gain_pair, context):
    w_query, w_key, w_value, w_output, w_gate, w_up, w_down = matrices
    gain_attn, gain_ffn = gain_pair
    cosine, sine_table, allowed = context
    row_count = upstream.shape[0]
    group_size = HEADS // KV_HEADS
    grad_ffn = upstream.astype(jnp.bfloat16)
    grad_down_w = outer_sum(stored["hidden_act"], grad_ffn)
    grad_hidden = against(grad_ffn, w_down)
    gate_act = stored["gate_act"]
    logistic = jax.nn.sigmoid(gate_act)
    grad_gate_act = (
        grad_hidden * stored["up_act"] * (logistic * (1.0 + gate_act * (1.0 - logistic)))
    ).astype(jnp.bfloat16)
    grad_up_act = (grad_hidden * (gate_act * logistic)).astype(jnp.bfloat16)
    grad_gate_w = outer_sum(stored["normed_ffn"], grad_gate_act)
    grad_up_w = outer_sum(stored["normed_ffn"], grad_up_act)
    grad_normed_ffn = against(grad_gate_act, w_gate) + against(grad_up_act, w_up)
    grad_after, grad_gain_ffn = norm_backward(
        grad_normed_ffn, stored["after_attn"], stored["inverse_ffn"], gain_ffn
    )
    grad_after = grad_after + upstream
    grad_branch = grad_after.astype(jnp.bfloat16)
    grad_output_w = outer_sum(stored["attended"], grad_branch)
    grad_attended = against(grad_branch, w_output).astype(jnp.bfloat16)
    all_keys, all_values = stored["kept_pair"]
    query_heads, key_heads, value_heads = split_heads(stored["queries"], all_keys, all_values)
    grad_heads = grad_attended.reshape(row_count, KV_HEADS, group_size, HEAD).transpose(1, 0, 2, 3)
    correction = jnp.sum(
        (grad_attended.astype(jnp.float32) * stored["mixed_heads"]).reshape(
            row_count, KV_HEADS, group_size, HEAD
        ),
        axis=-1,
    ).transpose(1, 2, 0)
    score_scale = HEAD ** (-0.5)
    grad_queries, grad_keys, grad_values = lax.map(
        lambda operands: head_backward(operands, allowed, score_scale),
        (query_heads, key_heads, value_heads, grad_heads, stored["log_total"], correction),
    )
    key_count = all_keys.shape[0]
    grad_keys = grad_keys.transpose(1, 0, 2).reshape(key_count, KV_HEADS * HEAD)
    grad_values = grad_values.transpose(1, 0, 2).reshape(key_count, KV_HEADS * HEAD)
    grad_keys, grad_values = (
        lax.psum_scatter(
            grad_keys.astype(jnp.bfloat16), "fsdp", scatter_dimension=0, tiled=True
        ).astype(jnp.float32),
        lax.psum_scatter(
            grad_values.astype(jnp.bfloat16), "fsdp", scatter_dimension=0, tiled=True
        ).astype(jnp.float32),
    )
    grad_queries = grad_queries.transpose(1, 0, 2, 3).reshape(row_count, HEADS, HEAD)
    grad_q = (
        unrotate(grad_queries, cosine, sine_table)
        .reshape(row_count, HEADS * HEAD)
        .astype(jnp.bfloat16)
    )
    grad_k = (
        unrotate(grad_keys.reshape(row_count, KV_HEADS, HEAD), cosine, sine_table)
        .reshape(row_count, KV_HEADS * HEAD)
        .astype(jnp.bfloat16)
    )
    grad_v = grad_values.astype(jnp.bfloat16)
    normed = stored["normed"]
    grad_query_w = outer_sum(normed, grad_q)
    grad_key_w = outer_sum(normed, grad_k)
    grad_value_w = outer_sum(normed, grad_v)
    grad_normed = against(grad_q, w_query) + against(grad_k, w_key) + against(grad_v, w_value)
    grad_input, grad_gain_attn = norm_backward(
        grad_normed, stored["hidden"], stored["inverse_attn"], gain_attn
    )
    grad_input = grad_input + grad_after
    return (
        grad_input,
        (
            grad_query_w,
            grad_key_w,
            grad_value_w,
            grad_output_w,
            grad_gate_w,
            grad_up_w,
            grad_down_w,
            grad_gain_attn,
            grad_gain_ffn,
        ),
    )


def per_device(
    tokens,
    seq_cuts,
    w_query,
    w_key,
    w_value,
    w_output,
    w_gate,
    w_up,
    w_down,
    gain_attn,
    gain_ffn,
    cotangent,
):
    matrices = (
        lax.all_gather(w_query, "fsdp", axis=0, tiled=True),
        lax.all_gather(w_key, "fsdp", axis=0, tiled=True),
        lax.all_gather(w_value, "fsdp", axis=0, tiled=True),
        lax.all_gather(w_output, "fsdp", axis=0, tiled=True),
        lax.all_gather(w_gate, "fsdp", axis=0, tiled=True),
        lax.all_gather(w_up, "fsdp", axis=0, tiled=True),
        lax.all_gather(w_down, "fsdp", axis=0, tiled=True),
    )
    gain_pair = (gain_attn, gain_ffn)
    row_count = tokens.shape[1]
    key_count = row_count * lax.axis_size("fsdp")
    bounds = seq_cuts[0]
    local_index = lax.axis_index("fsdp") * row_count + jnp.arange(row_count, dtype=jnp.int32)
    all_index = jnp.arange(key_count, dtype=jnp.int32)
    local_positions, local_docs = locate(local_index, bounds)
    unused_positions, key_docs = locate(all_index, bounds)
    allowed = (local_docs[:, None] == key_docs[None, :]) & (
        all_index[None, :] <= local_index[:, None]
    )
    cosine, sine_table = tables(local_positions)
    context = (cosine, sine_table, allowed)
    first_out, first_stored = run_forward(
        tokens[0].astype(jnp.float32), matrices, gain_pair, context
    )
    second_out, second_stored = run_forward(first_out, matrices, gain_pair, context)
    grad_middle, second_grads = run_backward(
        cotangent[0].astype(jnp.float32), second_stored, matrices, gain_pair, context
    )
    grad_input, first_grads = run_backward(grad_middle, first_stored, matrices, gain_pair, context)
    summed = jax.tree.map(
        lambda lower_part, upper_part: lower_part + upper_part, first_grads, second_grads
    )
    summed_rows = jax.tree.map(
        lambda part: part.astype(jnp.float32),
        lax.psum_scatter(for_sending(summed), "fsdp", scatter_dimension=0, tiled=True),
    )
    totals = lax.psum(summed_rows, "dp")
    return (
        second_out.astype(jnp.bfloat16)[None],
        grad_input.astype(jnp.bfloat16)[None],
        totals[0],
        totals[1],
        totals[2],
        totals[3],
        totals[4],
        totals[5],
        totals[6],
        totals[7],
        totals[8],
    )


def solution(mesh):
    return jax.shard_map(
        per_device,
        mesh=mesh,
        in_specs=(
            P("dp", "fsdp", None),
            P("dp", None),
            P("fsdp", None),
            P("fsdp", None),
            P("fsdp", None),
            P("fsdp", None),
            P("fsdp", None),
            P("fsdp", None),
            P("fsdp", None),
            P(),
            P(),
            P("dp", "fsdp", None),
        ),
        out_specs=(
            P("dp", "fsdp", None),
            P("dp", "fsdp", None),
            P("fsdp", None),
            P("fsdp", None),
            P("fsdp", None),
            P("fsdp", None),
            P("fsdp", None),
            P("fsdp", None),
            P("fsdp", None),
            P("fsdp"),
            P("fsdp"),
        ),
        check_vma=False,
    )
```

profile of v0, /device:TPU:0, one launch (start us, length us, event | category | flops | bytes accessed | tf_op | source)
XLA Modules:
  0.0 1420.7 jit_solution(4811915320498483831)
XLA Ops:
  8.0 9.6 all-gather
  20.9 11.9 all-gather.1
  46.8 11.3 all-gather.12.cloned.1.call-done
  58.0 20.4 %all-gather.14.cloned.1.call-done = bf16[2048,320]{0,1:T(8,128)(2,1)} async-done(((bf16[512,320]{0,1:T(8,128)(2,1)}), bf16[2048,320]{0,1:T(8,128)(2,1)}) %all-gather.14.cloned.1.call-update) | async-done | bytes 1310736 | tf_op jit(solution)/shard_map/all_gather | solution.py:156
  79.9 72.1 %while.56 = (s32[]{:T(128)}, f32[5,512,3,64]{1,3,2,0:T(8,128)}, f32[5,3,512]{2,1,0:T(4,128)S(1)}, bf16[5,2048,64]{1,2,0:T(8,128)(2,1)}, bf16[5,2048,64]{1,2,0:T(...) while((s32[]{:T(128)}, f32[5,512,3,64]{1,3,2,0:T(8,128)}, ...), condition=%wide.region_7.8_spmd.clone, body=%wide.region_4.7_spmd.clone.sunk | while | flops 846199296 | bytes 47321228 | solution.py:161
  88.7 5.7 fusion.312
  103.1 5.7 fusion.312
  117.5 5.7 fusion.312
  131.9 5.7 fusion.312
  146.3 5.7 fusion.312
  158.8 7.4 fusion.179
  166.2 15.6 %all-gather.22.cloned.1.call-done = bf16[960,2560]{1,0:T(8,128)(2,1)} async-done(((bf16[240,2560]{1,0:T(8,128)(2,1)}), bf16[960,2560]{1,0:T(8,128)(2,1)}) %all-gather.22.cloned.1.call-update) | async-done | bytes 4915216 | tf_op jit(solution)/shard_map/all_gather | solution.py:301
  181.8 9.3 multiply_convert_fusion.5
  191.1 30.8 %all-gather.24.cloned.1.call-done = bf16[2560,960]{0,1:T(8,128)(2,1)} async-done(((bf16[640,960]{0,1:T(8,128)(2,1)}), bf16[2560,960]{0,1:T(8,128)(2,1)}) %all-gather.24.cloned.1.call-update) | async-done | bytes 4915216 | tf_op jit(solution)/shard_map/all_gather | solution.py:302
  236.1 12.6 all-gather.26.cloned.1.call-done
  248.6 20.4 %all-gather.28.cloned.1.call-done = bf16[2048,320]{0,1:T(8,128)(2,1)} async-done(((bf16[512,320]{0,1:T(8,128)(2,1)}), bf16[2048,320]{0,1:T(8,128)(2,1)}) %all-gather.28.cloned.1.call-update) | async-done | bytes 1310736 | tf_op jit(solution)/shard_map/all_gather | solution.py:156
  270.6 72.2 %while.57 = (s32[]{:T(128)}, f32[5,512,3,64]{1,3,2,0:T(8,128)}, f32[5,3,512]{2,1,0:T(4,128)S(1)}, bf16[5,2048,64]{1,2,0:T(8,128)(2,1)}, bf16[5,2048,64]{1,2,0:T(...) while((s32[]{:T(128)}, f32[5,512,3,64]{1,3,2,0:T(8,128)}, ...), condition=%wide.region_13.14_spmd.clone, body=%wide.region_10.13_spmd.clone.sunk | while | flops 846199296 | bytes 47321228 | solution.py:161
  279.3 5.7 fusion.317
  293.7 5.7 fusion.317
  322.5 5.7 fusion.317
  336.9 5.7 fusion.317
  354.8 9.4 multiply_convert_fusion.2
  381.3 111.1 %while.58 = (s32[]{:T(128)}, f32[5,512,3,64]{1,3,2,0:T(8,128)}, bf16[5,2048,64]{1,2,0:T(8,128)(2,1)}, bf16[5,2048,64]{1,2,0:T(8,128)(2,1)}, bf16[5,2048,64]{1,2,...) while((s32[]{:T(128)}, f32[5,512,3,64]{1,3,2,0:T(8,128)}, ...), condition=%wide.region_18.19_spmd.clone, body=%wide.region_17.18_spmd.clone.sunk | while | flops 2048098304 | bytes 67038380 | solution.py:229
  386.1 5.7 fusion.330
  408.3 5.7 fusion.330
  430.4 5.7 fusion.330
  452.6 5.7 fusion.330
  474.8 5.7 fusion.330
  498.3 20.8 %reduce-scatter.18.cloned.1.call-done = bf16[512,320]{0,1:T(8,128)(2,1)} async-done(((bf16[2048,320]{0,1:T(8,128)(2,1)}), bf16[512,320]{0,1:T(8,128)(2,1)}) %reduce-scatter.18.cloned.1.call-update) | async-done | bytes 327696 | tf_op jit(solution)/shard_map/reduce_scatter | solution.py:237
  522.4 25.9 %reduce-scatter.20.cloned.1.call-done = bf16[512,320]{0,1:T(8,128)(2,1)} async-done(((bf16[2048,320]{0,1:T(8,128)(2,1)}), bf16[512,320]{0,1:T(8,128)(2,1)}) %reduce-scatter.20.cloned.1.call-update) | async-done | bytes 327696 | tf_op jit(solution)/shard_map/reduce_scatter | solution.py:240
  553.5 9.9 multiply_convert_fusion
  578.8 114.3 %while.59 = (s32[]{:T(128)}, f32[5,512,3,64]{1,3,2,0:T(8,128)}, bf16[5,2048,64]{1,2,0:T(8,128)(2,1)}, bf16[5,2048,64]{1,2,0:T(8,128)(2,1)}, bf16[5,2048,64]{1,2,...) while((s32[]{:T(128)}, f32[5,512,3,64]{1,3,2,0:T(8,128)}, ...), condition=%wide.region_25.26_spmd.clone, body=%wide.region_24.25_spmd.clone.sunk | while | flops 2048098304 | bytes 67038380 | solution.py:229
  584.2 5.7 fusion.346
  607.1 5.7 fusion.346
  629.9 5.7 fusion.346
  652.7 5.7 fusion.346
  675.6 5.7 fusion.346
  706.5 13.3 reduce-scatter.22.cloned.1.call-done
  724.2 24.9 %reduce-scatter.24.cloned.1.call-done = bf16[512,320]{0,1:T(8,128)(2,1)} async-done(((bf16[2048,320]{0,1:T(8,128)(2,1)}), bf16[512,320]{0,1:T(8,128)(2,1)}) %reduce-scatter.24.cloned.1.call-update) | async-done | bytes 327696 | tf_op jit(solution)/shard_map/reduce_scatter | solution.py:240
  763.5 7.9 copy.77
  793.2 7.2 fusion.148
  805.8 6.2 all-reduce.3
  816.2 26.0 %reduce-scatter.34.cloned.1.call-done = bf16[240,320]{1,0:T(8,128)(2,1)} async-done(((bf16[960,320]{1,0:T(8,128)(2,1)}), bf16[240,320]{1,0:T(8,128)(2,1)}) %reduce-scatter.34.cloned.1.call-update) | async-done | bytes 153616
  843.2 24.5 %reduce-scatter.36.cloned.1.call-done = bf16[240,320]{1,0:T(8,128)(2,1)} async-done(((bf16[960,320]{1,0:T(8,128)(2,1)}), bf16[240,320]{1,0:T(8,128)(2,1)}) %reduce-scatter.36.cloned.1.call-update) | async-done | bytes 153616
  868.7 52.8 %reduce-scatter.38.cloned.1.call-done = bf16[640,960]{1,0:T(8,128)(2,1)} async-done(((bf16[2560,960]{1,0:T(8,128)(2,1)}), bf16[640,960]{1,0:T(8,128)(2,1)}) %reduce-scatter.38.cloned.1.call-update) | async-done | bytes 1228816
  923.6 49.9 %reduce-scatter.30.cloned.1.call-done = bf16[240,2560]{1,0:T(8,128)(2,1)} async-done(((bf16[960,2560]{1,0:T(8,128)(2,1)}), bf16[240,2560]{1,0:T(8,128)(2,1)}) %reduce-scatter.30.cloned.1.call-update) | async-done | bytes 1228816 | tf_op jit(solution)/shard_map/reduce_scatter | solution.py:330
  973.5 51.7 %reduce-scatter.32.cloned.1.call-done = bf16[240,2560]{1,0:T(8,128)(2,1)} async-done(((bf16[960,2560]{1,0:T(8,128)(2,1)}), bf16[240,2560]{1,0:T(8,128)(2,1)}) %reduce-scatter.32.cloned.1.call-update) | async-done | bytes 1228816 | tf_op jit(solution)/shard_map/reduce_scatter | solution.py:330
  1025.2 388.3 %all-reduce.5 = (f32[240,960]{1,0:T(8,128)}, f32[240,320]{0,1:T(8,128)}, f32[240,320]{0,1:T(8,128)}, f32[240,960]{1,0:T(8,128)}, f32[240,2560]{1,0:T(8,128)}, /*...) all-reduce(bf16[240,960]{1,0:T(8,128)(2,1)S(1)} %copy-done.65, ...), channel_id=1, replica_groups=mesh['dp'=8,'fsdp'=4] {'dp'}, use_global_device_ids=true, to_apply=%region_30.31 | all-reduce | flops 2458080 | bytes 14749440 | tf_op jit(solution)/shard_map/psum | solution.py:332
  (493 shorter events, 426.7 us)
Async XLA Ops:
  7.2 11.4 copy-start.25
  7.2 31.5 %all-gather.16.cloned.1.call-start = ((), (), s32[]{:S(2)}) async-start(), calls=%async_computation.13 | async-start | bytes 2457600 | tf_op jit(solution)/shard_map/all_gather | solution.py:296
  7.9 50.1 %all-gather.12.cloned.1.call-start = ((), (), s32[]{:S(2)}) async-start(), calls=%async_computation.11 | async-start | bytes 1638400 | tf_op jit(solution)/shard_map/all_gather | solution.py:157
  19.5 23.1 %copy-start.79 = (f32[512]{0:T(512)}, f32[512]{0:T(512)S(1)}, u32[]{:S(2)}) copy-start(f32[512]{0:T(512)S(1)} %get-tuple-element.464) | copy-start | bytes 6148
  20.8 13.1 copy-start.87
  20.8 57.6 %all-gather.14.cloned.1.call-start = ((), (), s32[]{:S(2)}) async-start(), calls=%async_computation.12 | async-start | bytes 1638400 | tf_op jit(solution)/shard_map/all_gather | solution.py:156
  34.3 11.1 copy-start.42
  34.3 11.1 copy-start.45
  35.8 118.3 %all-gather.18.cloned.1.call-start = ((), (), s32[]{:S(2)}) async-start(), calls=%async_computation.14 | async-start | bytes 2457600 | tf_op jit(solution)/shard_map/all_gather | solution.py:299
  36.4 122.4 %all-gather.20.cloned.1.call-start = ((), (), s32[]{:S(2)}) async-start(), calls=%async_computation.15 | async-start | bytes 6144000 | tf_op jit(solution)/shard_map/all_gather | solution.py:300
  37.0 144.8 %all-gather.22.cloned.1.call-start = ((), (), s32[]{:S(2)}) async-start(), calls=%async_computation.16 | async-start | bytes 6144000 | tf_op jit(solution)/shard_map/all_gather | solution.py:301
  37.6 184.3 %all-gather.24.cloned.1.call-start = ((), (), s32[]{:S(2)}) async-start(), calls=%async_computation.17 | async-start | bytes 6144000 | tf_op jit(solution)/shard_map/all_gather | solution.py:302
  38.3 210.3 %all-gather.26.cloned.1.call-start = ((), (), s32[]{:S(2)}) async-start(), calls=%async_computation.18 | async-start | bytes 1638400 | tf_op jit(solution)/shard_map/all_gather | solution.py:157
  157.9 8.3 copy-start.77
  158.8 23.0 %copy-start.48 = (bf16[512,960]{0,1:T(8,128)(2,1)}, bf16[512,960]{0,1:T(8,128)(2,1)S(1)}, u32[]{:S(2)}) copy-start(bf16[512,960]{0,1:T(8,128)(2,1)S(1)} %multiply_convert_fusion.8) | copy-start | bytes 2949124
  166.2 55.7 %copy-start.32 = (f32[512,960]{0,1:T(8,128)S(1)}, f32[512,960]{0,1:T(8,128)}, u32[]{:S(2)}) copy-start(f32[512,960]{0,1:T(8,128)} %copy-done.31) | copy-start | bytes 5898244
  230.3 38.7 %all-gather.28.cloned.1.call-start = ((), (), s32[]{:S(2)}) async-start(), calls=%async_computation.19 | async-start | bytes 1638400 | tf_op jit(solution)/shard_map/all_gather | solution.py:156
  231.8 287.2 %reduce-scatter.18.cloned.1.call-start = ((), (), s32[]{:S(2)}) async-start(), calls=%async_computation.20 | async-start | bytes 1638400 | tf_op jit(solution)/shard_map/reduce_scatter | solution.py:237
  270.6 77.9 %copy-start.74 = (f32[960]{0:T(1024)S(1)}, f32[960]{0:T(1024)}, u32[]{:S(2)}) copy-start(f32[960]{0:T(1024)} %param.30) | copy-start | bytes 11524
  348.4 24.9 %copy-start.34 = (f32[512,960]{0,1:T(8,128)}, f32[512,960]{0,1:T(8,128)S(1)}, u32[]{:S(2)}) copy-start(f32[512,960]{0,1:T(8,128)S(1)} %get-tuple-element.478) | copy-start | bytes 5898244
  492.4 55.9 %reduce-scatter.20.cloned.1.call-start = ((), (), s32[]{:S(2)}) async-start(), calls=%async_computation.21 | async-start | bytes 1638400 | tf_op jit(solution)/shard_map/reduce_scatter | solution.py:240
  493.1 226.7 %reduce-scatter.22.cloned.1.call-start = ((), (), s32[]{:S(2)}) async-start(), calls=%async_computation.22 | async-start | bytes 1638400 | tf_op jit(solution)/shard_map/reduce_scatter | solution.py:237
  498.3 22.0 %copy-start.21 = (bf16[960,320]{0,1:T(8,128)(2,1)S(1)}, bf16[960,320]{0,1:T(8,128)(2,1)}, u32[]{:S(2)}) copy-start(bf16[960,320]{0,1:T(8,128)(2,1)} %copy-done.19) | copy-start | bytes 1843204
  520.2 28.1 %copy-start.40 = (bf16[960,320]{0,1:T(8,128)(2,1)S(1)}, bf16[960,320]{0,1:T(8,128)(2,1)}, u32[]{:S(2)}) copy-start(bf16[960,320]{0,1:T(8,128)(2,1)} %copy-done.38) | copy-start | bytes 1843204
  520.2 28.1 %copy-start.72 = (f32[960]{0:T(1024)S(1)}, f32[960]{0:T(1024)}, u32[]{:S(2)}) copy-start(f32[960]{0:T(1024)} %param.29) | copy-start | bytes 11524
  520.2 28.1 %copy-start.76 = (f32[512]{0:T(512)S(1)}, f32[512]{0:T(512)}, u32[]{:S(2)}) copy-start(f32[512]{0:T(512)} %copy-done.75) | copy-start | bytes 6148
  520.3 32.7 %copy-start.54 = (bf16[512,5,64]{0,2,1:T(8,128)(2,1)}, bf16[512,5,64]{0,2,1:T(8,128)(2,1)S(1)}, u32[]{:S(2)}) copy-start(bf16[512,5,64]{0,2,1:T(8,128)(2,1)S(1)} %pad_maximum_fusion.3) | copy-start | bytes 983044
  522.4 30.6 %copy-start.3 = (f32[512,960]{0,1:T(8,128)S(1)}, f32[512,960]{0,1:T(8,128)}, u32[]{:S(2)}) copy-start(f32[512,960]{0,1:T(8,128)} %copy-done.2) | copy-start | bytes 5898244
  522.4 30.6 %copy-start.84 = (f32[512]{0:T(512)S(1)}, f32[512]{0:T(512)}, u32[]{:S(2)}) copy-start(f32[512]{0:T(512)} %get-tuple-element.467) | copy-start | bytes 6148
  553.0 10.5 slice-start.2
  553.1 13.3 slice-start.6
  553.5 16.7 %copy-start.15 = (f32[512,960]{0,1:T(8,128)}, f32[512,960]{0,1:T(8,128)S(1)}, u32[]{:S(2)}) copy-start(f32[512,960]{0,1:T(8,128)S(1)} %subtract_add_fusion.1) | copy-start | bytes 5898244
  553.5 10.0 slice-start.3
  553.5 12.8 slice-start.7
  693.2 56.0 %reduce-scatter.24.cloned.1.call-start = ((), (), s32[]{:S(2)}) async-start(), calls=%async_computation.23 | async-start | bytes 1638400 | tf_op jit(solution)/shard_map/reduce_scatter | solution.py:240
  693.9 121.1 %reduce-scatter.26.cloned.1.call-start = ((), (), s32[]{:S(2)}) async-start(), calls=%async_computation.24 | async-start | bytes 2457600 | tf_op jit(solution)/shard_map/reduce_scatter | solution.py:330
  700.1 116.1 %reduce-scatter.28.cloned.1.call-start = ((), (), s32[]{:S(2)}) async-start(), calls=%async_computation.25 | async-start | bytes 2457600 | tf_op jit(solution)/shard_map/reduce_scatter | solution.py:330
  706.5 15.3 %copy-start.28 = (bf16[1,512,960]{1,2,0:T(8,128)(2,1)S(1)}, bf16[1,512,960]{1,2,0:T(8,128)(2,1)}, u32[]{:S(2)}) copy-start(bf16[1,512,960]{1,2,0:T(8,128)(2,1)} %param.20) | copy-start | bytes 2949124
  706.5 135.7 %reduce-scatter.34.cloned.1.call-start = ((), (), s32[]{:S(2)}) async-start(), calls=%async_computation.28 | async-start | bytes 921600
  724.1 26.6 %copy-start.58 = (bf16[512,320]{0,1:T(8,128)(2,1)S(1)}, bf16[512,320]{0,1:T(8,128)(2,1)}, u32[]{:S(2)}) copy-start(bf16[512,320]{0,1:T(8,128)(2,1)} %reduce-scatter.20.cloned.1.call-done) | copy-start | bytes 983044
  724.1 143.5 %reduce-scatter.36.cloned.1.call-start = ((), (), s32[]{:S(2)}) async-start(), calls=%async_computation.29 | async-start | bytes 921600
  754.4 167.1 %reduce-scatter.38.cloned.1.call-start = ((), (), s32[]{:S(2)}) async-start(), calls=%async_computation.30 | async-start | bytes 6553600
  771.5 202.0 %reduce-scatter.30.cloned.1.call-start = ((), (), s32[]{:S(2)}) async-start(), calls=%async_computation.26 | async-start | bytes 6144000 | tf_op jit(solution)/shard_map/reduce_scatter | solution.py:330
  781.7 243.4 %reduce-scatter.32.cloned.1.call-start = ((), (), s32[]{:S(2)}) async-start(), calls=%async_computation.27 | async-start | bytes 6144000 | tf_op jit(solution)/shard_map/reduce_scatter | solution.py:330
  803.3 8.7 copy-start.6
  803.3 8.7 copy-start.82
  815.0 210.1 %copy-start.65 = (bf16[240,960]{1,0:T(8,128)(2,1)S(1)}, bf16[240,960]{1,0:T(8,128)(2,1)}, u32[]{:S(2)}) copy-start(bf16[240,960]{1,0:T(8,128)(2,1)} %reduce-scatter.26.cloned.1.call-done) | copy-start | bytes 1382404
  816.2 209.0 %copy-start.66 = (bf16[240,960]{1,0:T(8,128)(2,1)S(1)}, bf16[240,960]{1,0:T(8,128)(2,1)}, u32[]{:S(2)}) copy-start(bf16[240,960]{1,0:T(8,128)(2,1)} %reduce-scatter.28.cloned.1.call-done) | copy-start | bytes 1382404
  (91 other events, 279.6 us)
Sparse Core Ops, SparseCore 0:
  9.6 28.0 all-gather.15
  39.8 18.1 all-gather.11
  60.2 18.1 all-gather.13
  79.8 21.8 all-gather.17
  103.1 38.5 all-gather.19
  143.2 38.5 all-gather.21
  183.3 38.5 all-gather.23
  230.4 18.1 all-gather.25
  250.8 18.1 all-gather.27
  492.5 26.5 reduce-scatter.17
  521.8 26.5 reduce-scatter.19
  693.3 26.5 reduce-scatter.21
  722.5 26.5 reduce-scatter.23
  752.1 30.6 reduce-scatter.25
  785.4 30.7 reduce-scatter.27
  819.1 22.9 reduce-scatter.33
  844.7 22.9 reduce-scatter.35
  870.1 51.3 reduce-scatter.37
  924.3 49.1 reduce-scatter.29
  975.9 49.1 reduce-scatter.31
where the time goes:
time: 1430 us; the launch traced here: 1420 us
  matrix products  444 us (31%)
  blocking collectives  416 us (29%)
  waiting for transfers between devices  406 us (28%)
  other arithmetic  85.2 us (6%)
  local copies, waits for them, and re-layouts  49.1 us (3%)
  between operations  16.8 us (1%)
    psum x1, blocking collectives, per_device(): totals = lax.psum(summed_rows, 'dp')  388 us
    unnamed x23, waiting for transfers between devices  108 us
    reduce_scatter x4, waiting for transfers between devices, per_device(): lax.psum_scatter(for_sending(summed), 'fsdp', scatter_dimension=0, tiled=...  103 us
    dot_general x10, matrix products, head_backward(): jnp.einsum('qgd,sd->gqs', grad_block, value_block, preferred_element_type...  57.2 us
    dot_general x10, matrix products, head_forward(): jnp.einsum('gqs,sd->qgd', probabilities, value_block, preferred_element_t...  56.7 us
    dot_general x14, matrix products, against(): jnp.einsum('tj,ij->ti', left, right, preferred_element_type=jnp.float32)  52.7 us
    dot_general x10, matrix products, head_backward(): jnp.einsum('gqs,qgd->sd', probabilities.astype(jnp.bfloat16), grad_block,...  52.4 us
    dot_general x14, matrix products, product(): return jnp.dot(left, right, preferred_element_type=jnp.float32)  51 us
  transfers between devices with their start and end apart: 20, of which 16 were waited for; matrix products, arithmetic and copies ran while one was open for 14% of the time, Pallas kernels for 0%

commit v1 on v0

v1 whole, which is shorter than its diff:
```python
import functools
import jax
import jax.numpy as jnp
from jax import lax
from jax.experimental import pallas as pl
from jax.experimental.pallas import tpu as pltpu
from jax.sharding import PartitionSpec as P

HEADS = 15
KV_HEADS = 5
HEAD = 64
GROUP = HEADS // KV_HEADS
LANES = 128
NEGATIVE = -1e30
LOG2E = 1.4426950408889634
LN2 = 0.6931471805599453
MIB = 1 << 20
f32 = jnp.float32
bf16 = jnp.bfloat16


def nn(left, right):
    return lax.dot_general(left, right, (((1,), (0,)), ((), ())), preferred_element_type=f32)


def nt(left, right):
    return lax.dot_general(left, right, (((1,), (1,)), ((), ())), preferred_element_type=f32)


def lane_index(shape):
    return lax.broadcasted_iota(jnp.int32, shape, len(shape) - 1)


def block_of(device, half):
    return 2 * device if half == 0 else 7 - 2 * device


def swap_halves(tile):
    low = lane_index(tile.shape) % HEAD < HEAD // 2
    return jnp.where(low, pltpu.roll(tile, LANES - HEAD // 2, 1), pltpu.roll(tile, HEAD // 2, 1))


def three_terms(column, lane):
    high = column.astype(bf16).astype(f32)
    rest = column - high
    middle = rest.astype(bf16).astype(f32)
    low = rest - middle
    return jnp.where(lane == 8, high, jnp.where(lane == 9, middle, jnp.where(lane == 10, low, 0.0)))


def gather_keys(f, g, pieces, key_marks, kvf):
    block = kvf.shape[1]
    for m, piece in enumerate(pieces):
        device = f ^ m
        for half in (0, 1):
            kvf[block_of(device, half), :, :LANES] = piece[0, half * block : (half + 1) * block, :]

    @pl.when(g == 0)
    def _():
        for j in range(kvf.shape[0]):
            kvf[j, :, LANES:] = key_marks[j * block : (j + 1) * block, :]


def attend_kernel(f_ref, q, q_marks, key_marks, own, near, far, last, attended, marks_out, kvf, scores, peak, acc):
    g, b = pl.program_id(0), pl.program_id(1)
    f = f_ref[0]
    block = kvf.shape[1]
    rows = GROUP * block

    @pl.when(b == 0)
    def _():
        gather_keys(f, g, (own, near, far, last), key_marks, kvf)

    count = jnp.where(b == 0, 2 * f, 7 - 2 * f)
    marks = q_marks[...]
    qf = jnp.concatenate(
        [q[...].reshape(rows, LANES), jnp.concatenate([marks] * GROUP, axis=0)], axis=1
    )
    peak[...] = jnp.full(peak.shape, NEGATIVE, f32)

    def score(j, diagonal):
        s = nt(qf, kvf[j])
        if diagonal:
            row = lax.broadcasted_iota(jnp.int32, (block, block), 0)
            column = lax.broadcasted_iota(jnp.int32, (block, block), 1)
            shift = jnp.where(column <= row, 0.0, NEGATIVE)
            s = (s.reshape(GROUP, block, block) + shift[None]).reshape(rows, block)
        scores[j] = s
        best = s[:, :LANES]
        for t in range(1, block // LANES):
            best = jnp.maximum(best, s[:, t * LANES : (t + 1) * LANES])
        peak[...] = jnp.maximum(peak[...], best)

    lax.fori_loop(0, count, lambda j, c: (score(j, False), c)[1], 0)
    score(count, True)
    top = jnp.max(peak[...], axis=1, keepdims=True)
    acc[...] = jnp.zeros(acc.shape, f32)

    def mix(j, c):
        p = jnp.exp2(scores[j] - top).astype(bf16)
        acc[...] += nn(p, kvf[j])
        return c

    lax.fori_loop(0, count + 1, mix, 0)
    total = acc[:, LANES + 8 : LANES + 9]
    out = acc[:, :LANES] / total
    log_total = top + jnp.log2(total)
    lane = lane_index((rows, LANES))
    new_marks = jnp.concatenate([marks] * GROUP, axis=0).astype(f32) + three_terms(-log_total, lane)
    marks_out[...] = new_marks.astype(bf16).reshape(GROUP, block, LANES)
    row0 = pl.multiple_of(b * block, block)
    lane = lane_index((block, LANES))
    for i in range(GROUP):
        h = GROUP * g + i
        pair = pl.multiple_of((h // 2) * LANES, LANES)
        odd = h % 2 == 1
        tile = out[i * block : (i + 1) * block, :]
        turned = pltpu.roll(tile, HEAD, 1)
        old = attended[pl.ds(row0, block), pl.ds(pair, LANES)].astype(f32)
        new = jnp.where(
            odd, jnp.where(lane >= HEAD, tile, old), jnp.where(lane < HEAD, turned, 0.0)
        )
        attended[pl.ds(row0, block), pl.ds(pair, LANES)] = new.astype(bf16)


def attend(f, q, q_marks, key_marks, pieces):
    tokens = q.shape[1]
    block = tokens // 2
    blocks = key_marks.shape[0] // block
    piece = pl.BlockSpec((1, tokens, LANES), lambda g, b, f: (g, 0, 0))
    heads = pl.BlockSpec((GROUP, block, LANES), lambda g, b, f: (g, b, 0))
    width = (HEADS + 1) * HEAD
    return pl.pallas_call(
        attend_kernel,
        grid_spec=pltpu.PrefetchScalarGridSpec(
            num_scalar_prefetch=1,
            grid=(KV_HEADS, 2),
            in_specs=[
                heads,
                pl.BlockSpec((block, LANES), lambda g, b, f: (b, 0)),
                pl.BlockSpec(key_marks.shape, lambda g, b, f: (0, 0)),
                piece,
                piece,
                piece,
                piece,
            ],
            out_specs=[
                pl.BlockSpec((tokens, width), lambda g, b, f: (0, 0)),
                heads,
            ],
            scratch_shapes=[
                pltpu.VMEM((blocks, block, 2 * LANES), bf16),
                pltpu.VMEM((blocks, GROUP * block, block), f32),
                pltpu.VMEM((GROUP * block, LANES), f32),
                pltpu.VMEM((GROUP * block, 2 * LANES), f32),
            ],
        ),
        out_shape=[
            jax.ShapeDtypeStruct((tokens, width), bf16),
            jax.ShapeDtypeStruct((HEADS, tokens, LANES), bf16),
        ],
        compiler_params=pltpu.CompilerParams(vmem_limit_bytes=48 * MIB),
        cost_estimate=pl.CostEstimate(flops=12_000_000_000, bytes_accessed=8_000_000, transcendentals=9_000_000),
        name="attend",
    )(f, q, q_marks, key_marks, *pieces)


def attend_back_kernel(
    f_ref, q, marks, key_marks, own, near, far, last, grad, attended, cos_ref, sin_ref,
    grad_q, keep, send, kvf, kv_sum, both, turned, acc,
):
    g, b = pl.program_id(0), pl.program_id(1)
    f = f_ref[0]
    block = kvf.shape[1]
    rows = GROUP * block

    @pl.when(b == 0)
    def _():
        gather_keys(f, g, (own, near, far, last), key_marks, kvf)
        kv_sum[...] = jnp.zeros(kv_sum.shape, f32)

    count = jnp.where(b == 0, 2 * f, 7 - 2 * f)
    row0 = pl.multiple_of(b * block, block)
    lane = lane_index((block, LANES))
    both[:rows, :LANES] = q[...].reshape(rows, LANES)
    both[:rows, LANES:] = marks[...].reshape(rows, LANES)
    for i in range(GROUP):
        h = GROUP * g + i
        pair = pl.multiple_of((h // 2) * LANES, LANES)
        odd = h % 2 == 1
        d_tile = grad[pl.ds(row0, block), pl.ds(pair, LANES)].astype(f32)
        o_tile = attended[pl.ds(row0, block), pl.ds(pair, LANES)].astype(f32)
        mine = (lane >= HEAD) == odd
        inner = jnp.sum(jnp.where(mine, d_tile * o_tile, 0.0), axis=1, keepdims=True)
        moved = jnp.where(odd, d_tile, pltpu.roll(d_tile, HEAD, 1))
        moved = jnp.where(lane >= HEAD, moved, 0.0)
        first = rows + i * block
        both[first : first + block, :LANES] = moved.astype(bf16)
        both[first : first + block, LANES:] = three_terms(-inner, lane).astype(bf16)
        joined = moved + q[i].astype(f32)
        turned[:, i * block : (i + 1) * block] = joined.T.astype(bf16)
    acc[...] = jnp.zeros(acc.shape, f32)

    def step(j, diagonal):
        keys = kvf[j]
        s = nt(both[...], keys)
        p = jnp.exp2(s[:rows])
        if diagonal:
            row = lax.broadcasted_iota(jnp.int32, (block, block), 0)
            column = lax.broadcasted_iota(jnp.int32, (block, block), 1)
            p = jnp.where((column <= row)[None], p.reshape(GROUP, block, block), 0.0).reshape(rows, block)
        ds = (p * s[rows:]).astype(bf16)
        p = p.astype(bf16)
        acc[...] += nn(ds, keys[:, :LANES])
        kv_sum[j, :HEAD] += nn(turned[:HEAD], ds)
        kv_sum[j, HEAD:] += nn(turned[HEAD:], p)

    lax.fori_loop(0, count, lambda j, c: (step(j, False), c)[1], 0)
    step(count, True)
    scale = HEAD ** (-0.5)
    for i in range(GROUP):
        h = GROUP * g + i
        pair = pl.multiple_of((h // 2) * LANES, LANES)
        odd = h % 2 == 1
        tile = acc[i * block : (i + 1) * block, :] * scale
        tile = tile * cos_ref[...] - swap_halves(tile) * sin_ref[...]
        other = pltpu.roll(tile, HEAD, 1)
        old = grad_q[pl.ds(row0, block), pl.ds(pair, LANES)].astype(f32)
        new = jnp.where(odd, jnp.where(lane >= HEAD, other, old), jnp.where(lane < HEAD, tile, 0.0))
        grad_q[pl.ds(row0, block), pl.ds(pair, LANES)] = new.astype(bf16)

    @pl.when(b == 1)
    def _():
        factor = jnp.where(lane < HEAD, LN2, 1.0)
        for m in range(4):
            device = f ^ m
            for half in (0, 1):
                total = kv_sum[block_of(device, half)].T * factor
                ref = send if m % 2 else keep
                ref[m // 2, 0, half * block : (half + 1) * block, :] = total.astype(ref.dtype)


def attend_back(f, q, marks, key_marks, pieces, grad, attended, cos, sin):
    tokens = q.shape[1]
    block = tokens // 2
    blocks = key_marks.shape[0] // block
    piece = pl.BlockSpec((1, tokens, LANES), lambda g, b, f: (g, 0, 0))
    heads = pl.BlockSpec((GROUP, block, LANES), lambda g, b, f: (g, b, 0))
    width = (HEADS + 1) * HEAD
    whole = pl.BlockSpec((tokens, width), lambda g, b, f: (0, 0))
    table = pl.BlockSpec((block, LANES), lambda g, b, f: (b, 0))
    pair = pl.BlockSpec((2, 1, tokens, LANES), lambda g, b, f: (0, g, 0, 0))
    rows = GROUP * block
    return pl.pallas_call(
        attend_back_kernel,
        grid_spec=pltpu.PrefetchScalarGridSpec(
            num_scalar_prefetch=1,
            grid=(KV_HEADS, 2),
            in_specs=[
                heads,
                heads,
                pl.BlockSpec(key_marks.shape, lambda g, b, f: (0, 0)),
                piece,
                piece,
                piece,
                piece,
                whole,
                whole,
                table,
                table,
            ],
            out_specs=[whole, pair, pair],
            scratch_shapes=[
                pltpu.VMEM((blocks, block, 2 * LANES), bf16),
                pltpu.VMEM((blocks, LANES, block), f32),
                pltpu.VMEM((2 * rows, 2 * LANES), bf16),
                pltpu.VMEM((LANES, rows), bf16),
                pltpu.VMEM((rows, LANES), f32),
            ],
        ),
        out_shape=[
            jax.ShapeDtypeStruct((tokens, width), bf16),
            jax.ShapeDtypeStruct((2, KV_HEADS, tokens, LANES), bf16),
            jax.ShapeDtypeStruct((2, KV_HEADS, tokens, LANES), bf16),
        ],
        compiler_params=pltpu.CompilerParams(vmem_limit_bytes=48 * MIB),
        cost_estimate=pl.CostEstimate(flops=30_000_000_000, bytes_accessed=12_000_000, transcendentals=9_000_000),
        name="attend_back",
    )(f, q, marks, key_marks, *pieces, grad, attended, cos, sin)


EPS = 1e-05
ANY = pl.BlockSpec(memory_space=pl.ANY)


def params(mib):
    return pltpu.CompilerParams(vmem_limit_bytes=mib * MIB)


def cost(flops, moved):
    return pl.CostEstimate(flops=int(flops), bytes_accessed=int(moved), transcendentals=0)


def row_copies(f, pieces, target, sems):
    rows = pieces[0].shape[0]
    return [
        pltpu.make_async_copy(
            piece, target.at[pl.ds(pl.multiple_of((f ^ m) * rows, 16), rows), :], sems.at[m]
        )
        for m, piece in enumerate(pieces)
    ]


def tile_copies(f, t, pieces, target, sems):
    rows, width = pieces[0].shape[0], target.shape[2]
    return [
        pltpu.make_async_copy(
            piece.at[:, pl.ds(pl.multiple_of(t * width, width), width)],
            target.at[t, pl.ds(pl.multiple_of((f ^ m) * rows, 16), rows), :],
            sems.at[t, m],
        )
        for m, piece in enumerate(pieces)
    ]


def start(copies):
    for copy in copies:
        copy.start()


def wait(copies):
    for copy in copies:
        copy.wait()


def inverse_of(values):
    return lax.rsqrt(jnp.mean(values * values, axis=-1, keepdims=True) + EPS)


def norm_back(upstream, values, gain):
    inverse = inverse_of(values)
    scaled = upstream * gain
    gain_grad = jnp.sum(upstream * (values * inverse), axis=0, keepdims=True)
    middle = jnp.mean(scaled * values, axis=-1, keepdims=True)
    return inverse * scaled - (inverse * inverse * inverse * middle) * values, gain_grad


def project_kernel(f_ref, h, gain, cos_ref, sin_ref, own, near, far, last, normed_t, q_out, kv_out, w, sems):
    copies = row_copies(f_ref[0], (own, near, far, last), w, sems)
    start(copies)
    hidden = h[...].astype(f32)
    normed = (hidden * inverse_of(hidden) * gain[...]).astype(bf16)
    normed_t[...] = normed.T
    cos, sin = cos_ref[...], sin_ref[...]
    lane = lane_index(cos.shape)
    kv_cos, kv_sin = jnp.where(lane < HEAD, cos, 1.0), jnp.where(lane < HEAD, sin, 0.0)
    wait(copies)
    for g in range(KV_HEADS):
        tile = nn(normed, w[:, g * LANES : (g + 1) * LANES])
        kv_out[g] = (tile * kv_cos + swap_halves(tile) * kv_sin).astype(bf16)
    first = KV_HEADS * LANES
    for p in range((HEADS + 1) // 2):
        tile = nn(normed, w[:, first + p * LANES : first + (p + 1) * LANES])
        tile = (tile * cos + swap_halves(tile) * sin) * (HEAD ** (-0.5) * LOG2E)
        q_out[2 * p] = jnp.where(lane < HEAD, tile, 0.0).astype(bf16)
        if 2 * p + 1 < HEADS:
            q_out[2 * p + 1] = jnp.where(lane < HEAD, pltpu.roll(tile, HEAD, 1), 0.0).astype(bf16)


def project(f, hidden, gain, cos, sin, pieces):
    tokens, width = hidden.shape
    rows, columns = pieces[0].shape
    full = lambda *shape: pl.BlockSpec(shape, lambda i, f: (0,) * len(shape))
    return pl.pallas_call(
        project_kernel,
        grid_spec=pltpu.PrefetchScalarGridSpec(
            num_scalar_prefetch=1,
            grid=(1,),
            in_specs=[full(tokens, width), full(1, width), full(*cos.shape), full(*sin.shape)] + [ANY] * 4,
            out_specs=[
                full(width, tokens),
                full(HEADS, tokens, LANES),
                full(KV_HEADS, tokens, LANES),
            ],
            scratch_shapes=[pltpu.VMEM((4 * rows, columns), bf16), pltpu.SemaphoreType.DMA((4,))],
        ),
        out_shape=[
            jax.ShapeDtypeStruct((width, tokens), bf16),
            jax.ShapeDtypeStruct((HEADS, tokens, LANES), bf16),
            jax.ShapeDtypeStruct((KV_HEADS, tokens, LANES), bf16),
        ],
        compiler_params=params(40),
        cost_estimate=cost(4e9, 8e6),
        name="project",
    )(f, hidden, gain, cos, sin, *pieces)


def feed_kernel(
    f_ref, h, attended, gain, *refs,
):
    o, gate, up, down = (refs[4 * i : 4 * i + 4] for i in range(4))
    after, attended_t, normed_t, gate_out, up_out, hidden_t, result = refs[16:23]
    w_o, w_gate, w_up, w_down, n16, acc, o_sem, gate_sem, up_sem, down_sem = refs[23:]
    f, t = f_ref[0], pl.program_id(0)
    tiles = w_gate.shape[0]
    depth = 4 * o[0].shape[0]

    @pl.when(t == 0)
    def _():
        o_copies = row_copies(f, o, w_o, o_sem)
        start(o_copies)
        for tile in range(tiles):
            start(tile_copies(f, tile, gate, w_gate, gate_sem))
            start(tile_copies(f, tile, up, w_up, up_sem))
            if tile == 0:
                start(row_copies(f, down, w_down, down_sem))
        att = attended[...]
        attended_t[...] = att.T
        w_o[depth:, :] = jnp.zeros((w_o.shape[0] - depth, w_o.shape[1]), bf16)
        wait(o_copies)
        value = h[...].astype(f32) + nn(att, w_o[...])
        after[...] = value
        normed = (value * inverse_of(value) * gain[...]).astype(bf16)
        n16[...] = normed
        normed_t[...] = normed.T
        acc[...] = value
        wait(row_copies(f, down, w_down, down_sem))

    wait(tile_copies(f, t, gate, w_gate, gate_sem))
    wait(tile_copies(f, t, up, w_up, up_sem))
    gate_act = nn(n16[...], w_gate[t])
    up_act = nn(n16[...], w_up[t])
    hidden = (gate_act * jax.nn.sigmoid(gate_act) * up_act).astype(bf16)
    gate_out[0] = gate_act.astype(bf16)
    up_out[0] = up_act.astype(bf16)
    hidden_t[0] = hidden.T
    wide = hidden.shape[1]
    acc[...] += nn(hidden, w_down[pl.ds(pl.multiple_of(t * wide, wide), wide), :])

    @pl.when(t == tiles - 1)
    def _():
        result[...] = acc[...].astype(result.dtype)


TILE = 512


def weight_scratch(o, gate, down):
    rows, width = o.shape
    tiles = gate.shape[1] // TILE
    return [
        pltpu.VMEM((4 * rows + HEAD, width), bf16),
        pltpu.VMEM((tiles, 4 * rows, TILE), bf16),
        pltpu.VMEM((tiles, 4 * rows, TILE), bf16),
        pltpu.VMEM((4 * down.shape[0], width), bf16),
    ]


def weight_sems(gate):
    tiles = gate.shape[1] // TILE
    dma = pltpu.SemaphoreType.DMA
    return [dma((4,)), dma((tiles, 4)), dma((tiles, 4)), dma((4,))]


def feed(f, hidden, attended, gain, o, gate, up, down, result_type):
    tokens, width = hidden.shape
    tiles = gate[0].shape[1] // TILE
    full = lambda *shape: pl.BlockSpec(shape, lambda i, f: (0,) * len(shape))
    tile = lambda *shape: pl.BlockSpec((1,) + shape, lambda i, f: (i, 0, 0))
    like = jax.ShapeDtypeStruct
    return pl.pallas_call(
        feed_kernel,
        grid_spec=pltpu.PrefetchScalarGridSpec(
            num_scalar_prefetch=1,
            grid=(tiles,),
            in_specs=[full(tokens, width), full(*attended.shape), full(1, width)] + [ANY] * 16,
            out_specs=[
                full(tokens, width),
                full(attended.shape[1], tokens),
                full(width, tokens),
                tile(tokens, TILE),
                tile(tokens, TILE),
                tile(TILE, tokens),
                full(tokens, width),
            ],
            scratch_shapes=weight_scratch(o[0], gate[0], down[0])
            + [pltpu.VMEM((tokens, width), bf16), pltpu.VMEM((tokens, width), f32)]
            + weight_sems(gate[0]),
        ),
        out_shape=[
            like((tokens, width), f32),
            like((attended.shape[1], tokens), bf16),
            like((width, tokens), bf16),
            like((tiles, tokens, TILE), bf16),
            like((tiles, tokens, TILE), bf16),
            like((tiles, TILE, tokens), bf16),
            like((tokens, width), result_type),
        ],
        compiler_params=params(56),
        cost_estimate=cost(10e9, 30e6),
        name="feed",
    )(f, hidden, attended, gain, *o, *gate, *up, *down)


def feed_back_kernel(f_ref, g, after, gain, gate_act, up_act, *refs):
    o, gate, up, down = (refs[4 * i : 4 * i + 4] for i in range(4))
    grad_gate, grad_up, g_out, grad_after, branch_out, grad_attended, gain_grad = refs[16:23]
    w_o, w_gate, w_up, w_down, acc, o_sem, gate_sem, up_sem, down_sem = refs[23:]
    f, t = f_ref[0], pl.program_id(0)
    tiles = w_gate.shape[0]
    depth = 4 * o[0].shape[0]

    @pl.when(t == 0)
    def _():
        down_copies = row_copies(f, down, w_down, down_sem)
        start(down_copies)
        for tile in range(tiles):
            start(tile_copies(f, tile, gate, w_gate, gate_sem))
            start(tile_copies(f, tile, up, w_up, up_sem))
        start(row_copies(f, o, w_o, o_sem))
        g_out[...] = g[...].astype(bf16)
        acc[...] = jnp.zeros(acc.shape, f32)
        w_o[depth:, :] = jnp.zeros((w_o.shape[0] - depth, w_o.shape[1]), bf16)
        wait(down_copies)

    wait(tile_copies(f, t, gate, w_gate, gate_sem))
    wait(tile_copies(f, t, up, w_up, up_sem))
    wide = w_gate.shape[2]
    grad_hidden = nt(g_out[...], w_down[pl.ds(pl.multiple_of(t * wide, wide), wide), :])
    value = gate_act[0].astype(f32)
    logistic = jax.nn.sigmoid(value)
    d_gate = grad_hidden * up_act[0].astype(f32) * (logistic * (1.0 + value * (1.0 - logistic)))
    d_gate = d_gate.astype(bf16)
    d_up = (grad_hidden * (value * logistic)).astype(bf16)
    grad_gate[0] = d_gate
    grad_up[0] = d_up
    acc[...] += nt(d_gate, w_gate[t]) + nt(d_up, w_up[t])

    @pl.when(t == tiles - 1)
    def _():
        back, gain_part = norm_back(acc[...], after[...], gain[...])
        back = back + g[...].astype(f32)
        gain_grad[...] = gain_part
        grad_after[...] = back
        branch = back.astype(bf16)
        branch_out[...] = branch
        wait(row_copies(f, o, w_o, o_sem))
        grad_attended[...] = nt(branch, w_o[...]).astype(bf16)


def feed_back(f, g, after, gain, gate_act, up_act, o, gate, up, down):
    tokens, width = after.shape
    tiles = gate[0].shape[1] // TILE
    full = lambda *shape: pl.BlockSpec(shape, lambda i, f: (0,) * len(shape))
    tile = lambda *shape: pl.BlockSpec((1,) + shape, lambda i, f: (i, 0, 0))
    like = jax.ShapeDtypeStruct
    depth = 4 * o[0].shape[0] + HEAD
    return pl.pallas_call(
        feed_back_kernel,
        grid_spec=pltpu.PrefetchScalarGridSpec(
            num_scalar_prefetch=1,
            grid=(tiles,),
            in_specs=[full(tokens, width), full(tokens, width), full(1, width)]
            + [tile(tokens, TILE), tile(tokens, TILE)]
            + [ANY] * 16,
            out_specs=[
                tile(tokens, TILE),
                tile(tokens, TILE),
                full(tokens, width),
                full(tokens, width),
                full(tokens, width),
                full(tokens, depth),
                full(1, width),
            ],
            scratch_shapes=weight_scratch(o[0], gate[0], down[0])
            + [pltpu.VMEM((tokens, width), f32)]
            + weight_sems(gate[0]),
        ),
        out_shape=[
            like((tiles, tokens, TILE), bf16),
            like((tiles, tokens, TILE), bf16),
            like((tokens, width), bf16),
            like((tokens, width), f32),
            like((tokens, width), bf16),
            like((tokens, depth), bf16),
            like((1, width), f32),
        ],
        compiler_params=params(56),
        cost_estimate=cost(10e9, 30e6),
        name="feed_back",
    )(f, g, after, gain, gate_act, up_act, *o, *gate, *up, *down)


def project_back_kernel(
    f_ref, grad_q, kept, came, cos_ref, sin_ref, h, gain, grad_after, own, near, far, last,
    grads, grad_in, gain_grad, w, sems,
):
    copies = row_copies(f_ref[0], (own, near, far, last), w, sems)
    start(copies)
    cos, sin = cos_ref[...], sin_ref[...]
    lane = lane_index(cos.shape)
    cos, sin = jnp.where(lane < HEAD, cos, 1.0), jnp.where(lane < HEAD, sin, 0.0)
    for g in range(KV_HEADS):
        tile = kept[g].astype(f32) + came[g].astype(f32)
        tile = tile * cos - swap_halves(tile) * sin
        grads[:, g * LANES : (g + 1) * LANES] = tile.astype(bf16)
    grads[:, KV_HEADS * LANES :] = grad_q[...]
    wait(copies)
    grad_normed = nt(grads[...], w[...])
    back, gain_part = norm_back(grad_normed, h[...].astype(f32), gain[...])
    gain_grad[...] = gain_part
    grad_in[...] = (back + grad_after[...]).astype(grad_in.dtype)


def project_back(f, grad_q, kept, came, cos, sin, hidden, gain, grad_after, pieces, result_type):
    tokens, width = hidden.shape
    rows, columns = pieces[0].shape
    full = lambda *shape: pl.BlockSpec(shape, lambda i, f: (0,) * len(shape))
    like = jax.ShapeDtypeStruct
    return pl.pallas_call(
        project_back_kernel,
        grid_spec=pltpu.PrefetchScalarGridSpec(
            num_scalar_prefetch=1,
            grid=(1,),
            in_specs=[
                full(*grad_q.shape),
                full(*kept.shape),
                full(*came.shape),
                full(*cos.shape),
                full(*sin.shape),
                full(tokens, width),
                full(1, width),
                full(tokens, width),
            ]
            + [ANY] * 4,
            out_specs=[full(tokens, columns), full(tokens, width), full(1, width)],
            scratch_shapes=[pltpu.VMEM((4 * rows, columns), bf16), pltpu.SemaphoreType.DMA((4,))],
        ),
        out_shape=[
            like((tokens, columns), bf16),
            like((tokens, width), result_type),
            like((1, width), f32),
        ],
        compiler_params=params(40),
        cost_estimate=cost(4e9, 12e6),
        name="project_back",
    )(f, grad_q, kept, came, cos, sin, hidden, gain, grad_after, *pieces)


def outer_kernel(f_ref, *refs, pairs, rows):
    lefts, rights = refs[:2], refs[2 : 2 + 2 * pairs]
    outs = refs[2 + 2 * pairs : 2 + 4 * pairs]
    acc = refs[-1]
    f = f_ref[0]
    for k in range(pairs):
        first, second = rights[2 * k], rights[2 * k + 1]
        value = lambda ref: ref[0] if len(ref.shape) == 3 else ref[...]
        acc[...] = nn(lefts[0][...], value(first)) + nn(lefts[1][...], value(second))
        for m in range(4):
            out = outs[2 * k + m % 2]
            out[m // 2] = acc[pl.ds(pl.multiple_of((f ^ m) * rows, 16), rows), :].astype(bf16)


def outer(f, lefts, rights, rows, name):
    width, tokens = lefts[0].shape
    tiled = rights[0][0].ndim == 3
    tiles = rights[0][0].shape[0] if tiled else 1
    columns = rights[0][0].shape[-1]
    pairs = len(rights)
    right_spec = (
        pl.BlockSpec((1, tokens, columns), lambda i, f: (i, 0, 0))
        if tiled
        else pl.BlockSpec((tokens, columns), lambda i, f: (0, 0))
    )
    left_spec = pl.BlockSpec((width, tokens), lambda i, f: (0, 0))
    out_spec = pl.BlockSpec((2, rows, columns), lambda i, f: (0, 0, i))
    shape = jax.ShapeDtypeStruct((2, rows, tiles * columns), bf16)
    return pl.pallas_call(
        functools.partial(outer_kernel, pairs=pairs, rows=rows),
        grid_spec=pltpu.PrefetchScalarGridSpec(
            num_scalar_prefetch=1,
            grid=(tiles,),
            in_specs=[left_spec] * 2 + [right_spec] * (2 * pairs),
            out_specs=[out_spec] * (2 * pairs),
            scratch_shapes=[pltpu.VMEM((width, columns), f32)],
        ),
        out_shape=[shape] * (2 * pairs),
        compiler_params=params(48),
        cost_estimate=cost(4 * width * tokens * tiles * columns * pairs, 20e6),
        name=name,
    )(f, *lefts, *[r for pair in rights for r in pair])


def outer_rows_kernel(f_ref, left_first, left_second, right_first, right_second, keep, send):
    value = nn(left_first[...], right_first[...]) + nn(left_second[...], right_second[...])
    s = pl.program_id(0)

    @pl.when(s < 2)
    def _():
        send[0] = value.astype(bf16)

    @pl.when(s >= 2)
    def _():
        keep[0] = value.astype(bf16)


def outer_rows(f, lefts, rights, name):
    width, tokens = lefts[0].shape
    rows, columns = width // 4, rights[0].shape[1]

    def quarter(s, f):
        slot = jnp.where(s < 2, 2 * s + 1, 2 * s - 4)
        return (f[0] ^ slot, 0)

    left_spec = pl.BlockSpec((rows, tokens), quarter)
    right_spec = pl.BlockSpec((tokens, columns), lambda s, f: (0, 0))
    shape = jax.ShapeDtypeStruct((2, rows, columns), bf16)
    return pl.pallas_call(
        outer_rows_kernel,
        grid_spec=pltpu.PrefetchScalarGridSpec(
            num_scalar_prefetch=1,
            grid=(4,),
            in_specs=[left_spec, left_spec, right_spec, right_spec],
            out_specs=[
                pl.BlockSpec((1, rows, columns), lambda s, f: (jnp.maximum(s - 2, 0), 0, 0)),
                pl.BlockSpec((1, rows, columns), lambda s, f: (jnp.minimum(s, 1), 0, 0)),
            ],
        ),
        out_shape=[shape] * 2,
        compiler_params=params(48),
        cost_estimate=cost(4 * width * tokens * columns, 12e6),
        name=name,
    )(f, *lefts, *rights)


def flip(array, axis, bit):
    size = lax.axis_size(axis)
    return lax.ppermute(array, axis, [(i, i ^ bit) for i in range(size)])


def pieces_of(shard):
    far = flip(shard, "fsdp", 2)
    return (shard, flip(shard, "fsdp", 1), far, flip(far, "fsdp", 1))


def exchange_halves(array):
    half = array.shape[0] // 2
    return jnp.concatenate([array[:half], flip(array[half:], "fsdp", 3)], axis=0)


def scatter_kept(keep, send):
    came = flip(send, "fsdp", 1)
    half = keep.astype(f32) + came.astype(f32)
    return half[0], flip(half[1].astype(bf16), "fsdp", 2)


def total_over_dp(array):
    size = lax.axis_size("dp")
    index = lax.axis_index("dp")
    bits = [1 << b for b in range(size.bit_length() - 1)]
    part = array
    dims = []
    for bit in bits:
        dim = next((d for d, t in ((1, 128), (0, 8)) if part.shape[d] % (2 * t) == 0), 1)
        dims.append(dim)
        width = part.shape[dim] // 2
        mine = (index // bit) % 2
        send = lax.dynamic_slice_in_dim(part, (1 - mine) * width, width, dim).astype(bf16)
        keep = lax.dynamic_slice_in_dim(part, mine * width, width, dim).astype(f32)
        part = keep + flip(send, "dp", bit).astype(f32)
    part = part.astype(bf16)
    for bit, dim in zip(reversed(bits), reversed(dims)):
        other = flip(part, "dp", bit)
        mine = (index // bit) % 2
        part = jnp.where(
            mine == 0, jnp.concatenate([part, other], dim), jnp.concatenate([other, part], dim)
        )
    return part.astype(f32)


def total_small(array):
    for bit in (1, 2):
        array = array + flip(array, "fsdp", bit)
    for b in range(lax.axis_size("dp").bit_length() - 1):
        array = array + flip(array, "dp", 1 << b)
    return array


def reduce_unit(keep, send):
    kept, came = scatter_kept(keep, send)
    return total_over_dp(kept + came.astype(f32))


def per_device(
    tokens, seq_cuts, w_query, w_key, w_value, w_output, w_gate, w_up, w_down, gain_attn, gain_ffn, cotangent
):
    rows, width = tokens.shape[1], tokens.shape[2]
    half = rows // 2
    index = lax.axis_index("fsdp")
    f = index.astype(jnp.int32).reshape(1)
    count = rows * lax.axis_size("fsdp")
    shard_rows = w_key.shape[0]

    key_value = jnp.stack(
        [w_key.reshape(shard_rows, KV_HEADS, HEAD), w_value.reshape(shard_rows, KV_HEADS, HEAD)], axis=2
    ).reshape(shard_rows, 2 * KV_HEADS * HEAD)
    w_in = pieces_of(jnp.concatenate([key_value, w_query, jnp.zeros((shard_rows, HEAD), bf16)], axis=1))
    h0 = exchange_halves(tokens[0])
    o, gate, up, down = pieces_of(w_output), pieces_of(w_gate), pieces_of(w_up), pieces_of(w_down)

    bounds = seq_cuts[0]
    within = jnp.arange(half, dtype=jnp.int32)
    local = jnp.concatenate([2 * index * half + within, (7 - 2 * index) * half + within]).astype(jnp.int32)
    every = jnp.arange(count, dtype=jnp.int32)
    passed = local[:, None] >= bounds[None, :]
    docs = jnp.sum(passed.astype(jnp.int32), axis=1)
    positions = local - jnp.max(jnp.where(passed, bounds[None, :], 0), axis=1)
    key_docs = jnp.sum((every[:, None] >= bounds[None, :]).astype(jnp.int32), axis=1)
    lane = jnp.arange(LANES, dtype=jnp.int32)[None, :]
    one = ((lane == key_docs[:, None]) & (lane < 4)) | ((lane >= 8) & (lane < 11))
    key_marks = one.astype(bf16)
    q_marks = jnp.where((lane < 4) & (lane != docs[:, None]), NEGATIVE, 0.0).astype(bf16)
    frequency = jnp.power(10000.0, -2.0 * jnp.arange(HEAD // 2, dtype=f32) / HEAD)
    angle = positions.astype(f32)[:, None] * frequency[None, :]
    cosine, sine = jnp.cos(angle), jnp.sin(angle)
    cos = jnp.concatenate([cosine] * 4, axis=1)
    sin = jnp.concatenate([-sine, sine] * 2, axis=1)
    gain_a, gain_f = gain_attn[None, :], gain_ffn[None, :]

    def forward(hidden, result_type):
        normed_t, q, kv = project(f, hidden, gain_a, cos, sin, w_in)
        far = flip(kv, "fsdp", 2)
        pieces = (kv, flip(kv, "fsdp", 1), far, flip(far, "fsdp", 1))
        attended, marks = attend(f, q, q_marks, key_marks, pieces)
        after, attended_t, normed_ffn_t, gate_act, up_act, hidden_t, result = feed(
            f, hidden, attended, gain_f, o, gate, up, down, result_type
        )
        return result, (
            hidden, normed_t, q, pieces, attended, marks, after, attended_t, normed_ffn_t, gate_act, up_act,
            hidden_t,
        )

    def backward(g, stored, result_type):
        hidden, _, q, pieces, attended, marks, after, _, _, gate_act, up_act, _ = stored
        grad_gate, grad_up, g16, grad_after, branch, grad_attended, gain_f_part = feed_back(
            f, g, after, gain_f, gate_act, up_act, o, gate, up, down
        )
        grad_q, keep, send = attend_back(f, q, marks, key_marks, pieces, grad_attended, attended, cos, sin)
        kept, came = scatter_kept(keep, send)
        grads, grad_in, gain_a_part = project_back(
            f, grad_q, kept, came, cos, sin, hidden, gain_a, grad_after, w_in, result_type
        )
        return grad_in, (grad_gate, grad_up, g16, branch, grads, gain_a_part, gain_f_part)

    h1, first = forward(h0, f32)
    h2, second = forward(h1, bf16)
    output = exchange_halves(h2)
    middle, back2 = backward(exchange_halves(cotangent[0]), second, f32)
    grad_tokens, back1 = backward(middle, first, bf16)
    grad_tokens = exchange_halves(grad_tokens)

    flat = lambda a: a.reshape(-1, a.shape[-1])
    down_k, down_s = outer_rows(f, (flat(first[11]), flat(second[11])), (back1[2], back2[2]), "outer_down")
    gate_k, gate_s, up_k, up_s = outer(
        f, (first[8], second[8]), [(back1[0], back2[0]), (back1[1], back2[1])], shard_rows, "outer_ffn"
    )
    o_k, o_s = outer(f, (first[7], second[7]), [(back1[3], back2[3])], shard_rows, "outer_o")
    in_k, in_s = outer(f, (first[1], second[1]), [(back1[4], back2[4])], shard_rows, "outer_in")
    grad_down = reduce_unit(down_k, down_s)
    grad_gate = reduce_unit(gate_k, gate_s)
    grad_up = reduce_unit(up_k, up_s)
    grad_o = reduce_unit(o_k, o_s)
    grad_in = reduce_unit(in_k, in_s)
    kv_width = 2 * KV_HEADS * HEAD
    pairs = grad_in[:, :kv_width].reshape(shard_rows, KV_HEADS, 2, HEAD)
    grad_key = pairs[:, :, 0].reshape(shard_rows, KV_HEADS * HEAD)
    grad_value = pairs[:, :, 1].reshape(shard_rows, KV_HEADS * HEAD)
    grad_query = grad_in[:, kv_width : kv_width + HEADS * HEAD]
    gains = total_small(jnp.concatenate([back1[5] + back2[5], back1[6] + back2[6]], axis=0))
    share = width // 4
    gains = lax.dynamic_slice_in_dim(gains, index * share, share, 1)
    return (
        output[None], grad_tokens[None], grad_query, grad_key, grad_value, grad_o, grad_gate, grad_up,
        grad_down, gains[0], gains[1],
    )


def solution(mesh):
    split, whole = P("fsdp", None), P("dp", "fsdp", None)
    return jax.shard_map(
        per_device,
        mesh=mesh,
        in_specs=(whole, P("dp", None)) + (split,) * 7 + (P(), P(), whole),
        out_specs=(whole, whole) + (split,) * 7 + (P("fsdp"), P("fsdp")),
        check_vma=False,
    )
```

time: 1430 us -> 852 us (0.60)
  matrix products: 444 us -> 0 us
  blocking collectives: 416 us -> 0 us
  Pallas kernels: 0 us -> 324 us
  waiting for transfers between devices: 406 us -> 316 us
  starting transfers between devices: 1.89 us -> 68.3 us
  other arithmetic: 85.2 us -> 49.9 us
  local copies, waits for them, and re-layouts: 49.1 us -> 82 us
  between operations: 16.8 us -> 2.35 us
    dot_general x112 -> x0, matrix products: 444 us -> none  [the longest x10 57.2 us: head_backward(): jnp.einsum('qgd,sd->gqs', grad_block, value_block, preferred_element_type...]
    psum x1 -> x0, blocking collectives: 388 us -> none  [per_device(): totals = lax.psum(summed_rows, 'dp')]
    pallas_call x0 -> x16, Pallas kernels: none -> 324 us  [the longest x2 103 us: attend_back(): pl.pallas_call(attend_back_kernel, grid_spec=pltpu.PrefetchScalarGridSpec...]
    ppermute x0 -> x74, waiting for transfers between devices: none -> 316 us  [flip(): return lax.ppermute(array, axis, [(i, i ^ bit) for i in range(size)])]
    reduce_scatter x8 -> x0, waiting for transfers between devices: 188 us -> none  [the longest x4 103 us: per_device(): lax.psum_scatter(for_sending(summed), 'fsdp', scatter_dimension=0, tiled=...]
    all_gather x9 -> x0, waiting for transfers between devices: 111 us -> none  [the longest x2 40.7 us: run_forward(): lax.all_gather(key_rows, 'fsdp', axis=0, tiled=True)]
    unnamed x23 -> x0, waiting for transfers between devices: 108 us -> none
    ppermute x0 -> x74, starting transfers between devices: none -> 68.3 us  [flip(): return lax.ppermute(array, axis, [(i, i ^ bit) for i in range(size)])]
  transfers between devices with their start and end apart: 20 -> 74, of which waited for: 16 -> 31; matrix products, arithmetic and copies ran while one was open for 14% -> 12% of each run, Pallas kernels for 0% -> 9%
where the time goes in v1:
time: 852 us; the launch traced here: 842 us
  Pallas kernels  324 us (38%)
  waiting for transfers between devices  316 us (37%)
  local copies, waits for them, and re-layouts  82 us (10%)
  starting transfers between devices  68.3 us (8%)
  other arithmetic  49.9 us (6%)
    ppermute x74, waiting for transfers between devices, flip(): return lax.ppermute(array, axis, [(i, i ^ bit) for i in range(size)])  316 us
    pallas_call x2, Pallas kernels, attend_back(): pl.pallas_call(attend_back_kernel, grid_spec=pltpu.PrefetchScalarGridSpec...  103 us
    pallas_call x2, Pallas kernels, attend(): pl.pallas_call(attend_kernel, grid_spec=pltpu.PrefetchScalarGridSpec(num_...  71.2 us
    ppermute x74, starting transfers between devices, flip(): return lax.ppermute(array, axis, [(i, i ^ bit) for i in range(size)])  68.3 us
    pallas_call x2, Pallas kernels, feed_back(): pl.pallas_call(feed_back_kernel, grid_spec=pltpu.PrefetchScalarGridSpec(n...  49.2 us
    pallas_call x2, Pallas kernels, feed(): pl.pallas_call(feed_kernel, grid_spec=pltpu.PrefetchScalarGridSpec(num_sc...  43.3 us
    unnamed x150, local copies, waits for them, and re-layouts  40.4 us
    pallas_call x3, Pallas kernels, outer(): pl.pallas_call(functools.partial(outer_kernel, pairs=pairs, rows=rows), g...  24.9 us
  transfers between devices with their start and end apart: 74, of which 31 were waited for; matrix products, arithmetic and copies ran while one was open for 12% of the time, Pallas kernels for 9%

profile of v1, /device:TPU:0, one launch (start us, length us, event | category | flops | bytes accessed | tf_op | source)
XLA Modules:
  0.0 842.4 jit_solution(4388959263039244575)
XLA Ops:
  3.2 3.0 collective-permute-start.2
  10.7 14.1 %collective-permute-done.2.far = bf16[240,1664]{1,0:T(8,128)(2,1)S(1)} collective-permute-done((bf16[240,1664]{1,0:T(8,128)(2,1)S(1)}, bf16[240,1664]{1,0:T(8,128)(2,1)S(1)}, u32[]{:S(2)}, u32[]{:S(2)}) %collective-permute-start.2) | collective-permute-done | bytes 798752 | tf_op jit(solution)/shard_map/ppermute | solution.py:738
  30.4 5.4 collective-permute-done
  39.2 23.3 %collective-permute-done.17 = bf16[640,960]{0,1:T(8,128)(2,1)} collective-permute-done((bf16[640,960]{0,1:T(8,128)(2,1)}, bf16[640,960]{0,1:T(8,128)(2,1)}, u32[]{:S(2)}, u32[]{:S(2)}) %collective-permute-start.17) | collective-permute-done | bytes 1228832 | tf_op jit(solution)/shard_map/ppermute | solution.py:738
  64.6 5.6 project.2
  72.4 26.8 %collective-permute-done.8.refs_2_ = bf16[240,960]{1,0:T(8,128)(2,1)S(1)} collective-permute-done((bf16[240,960]{1,0:T(8,128)(2,1)}, bf16[240,960]{1,0:T(8,128)(2,1)S(1)}, u32[]{:S(2)}, u32[]{:S(2)}) %collective-permute-start.8) | collective-permute-done | bytes 460832 | tf_op jit(solution)/shard_map/ppermute | solution.py:738
  102.3 36.7 %collective-permute-done.5.far = bf16[5,512,128]{2,1,0:T(8,128)(2,1)} collective-permute-done((bf16[5,512,128]{2,1,0:T(8,128)(2,1)S(1)}, bf16[5,512,128]{2,1,0:T(8,128)(2,1)}, u32[]{:S(2)}, u32[]{:S(2)}) %collective-permute-start.5) | collective-permute-done | bytes 655392 | tf_op jit(solution)/shard_map/ppermute | solution.py:738
  155.0 35.5 %attend.2 = (bf16[512,1024]{1,0:T(8,128)(2,1)S(1)}, bf16[15,512,128]{2,1,0:T(8,128)(2,1)}) custom-call(s32[1]{0:T(128)} %bitcast.f_ref, bf16[15,512,128]{2,1,0:T(8,128)(2,1)} %copy-done.37, bf16[512,128]{1,0:T(8,128)(2,1)S(1)} %select_convert_fusion.q_marks, bf16[2048,128]{1,0:T(8,128)(2,1)S(1)} %fusion.12.key_marks, bf16[5,512,128]{2,1,0:T(8,128)(2,1)S(1)} %copy-done.12, ...), custom_call_target="tpu_custom_call" | custom-call | flops 12000000000 | bytes 8000000 | tf_op jit(solution)/shard_map/attend/pallas_call | solution.py:133
  192.3 21.6 %feed.2 = (f32[512,960]{1,0:T(8,128)}, bf16[1024,512]{1,0:T(8,128)(2,1)}, bf16[960,512]{1,0:T(8,128)(2,1)}, bf16[5,512,512]{2,1,0:T(8,128)(2,1)}, bf16[5,512,512...) custom-call(s32[1]{0:T(128)} %bitcast.f_ref, bf16[512,960]{1,0:T(8,128)(2,1)} %copy-done.3, ...), custom_call_target="tpu_custom_call" | custom-call | flops 10000000000 | bytes 30000000 | tf_op jit(solution)/shard_map/feed/pallas_call | solution.py:471
  215.5 6.3 project.3
  225.8 15.4 %collective-permute-done.20.far = bf16[5,512,128]{2,1,0:T(8,128)(2,1)} collective-permute-done((bf16[5,512,128]{2,1,0:T(8,128)(2,1)}, bf16[5,512,128]{2,1,0:T(8,128)(2,1)}, u32[]{:S(2)}, u32[]{:S(2)}) %collective-permute-start.20) | collective-permute-done | bytes 655392 | tf_op jit(solution)/shard_map/ppermute | solution.py:738
  248.1 10.2 %collective-permute-done.23 = bf16[256,960]{1,0:T(8,128)(2,1)} collective-permute-done((bf16[256,960]{1,0:T(8,128)(2,1)}, bf16[256,960]{1,0:T(8,128)(2,1)}, u32[]{:S(2)}, u32[]{:S(2)}) %collective-permute-start.23) | collective-permute-done | bytes 491552 | tf_op jit(solution)/shard_map/ppermute | solution.py:738
  260.5 35.7 %attend.3 = (bf16[512,1024]{1,0:T(8,128)(2,1)S(1)}, bf16[15,512,128]{2,1,0:T(8,128)(2,1)}) custom-call(s32[1]{0:T(128)} %bitcast.f_ref, bf16[15,512,128]{2,1,0:T(8,128)(2,1)} %copy-done.32, bf16[512,128]{1,0:T(8,128)(2,1)S(1)} %select_convert_fusion.q_marks, bf16[2048,128]{1,0:T(8,128)(2,1)S(1)} %fusion.12.key_marks, ...), custom_call_target="tpu_custom_call" | custom-call | flops 12000000000 | bytes 8000000 | tf_op jit(solution)/shard_map/attend/pallas_call | solution.py:133
  297.2 21.7 %feed.3 = (f32[512,960]{1,0:T(8,128)}, bf16[1024,512]{1,0:T(8,128)(2,1)}, bf16[960,512]{1,0:T(8,128)(2,1)}, bf16[5,512,512]{2,1,0:T(8,128)(2,1)}, bf16[5,512,512...) custom-call(s32[1]{0:T(128)} %bitcast.f_ref, f32[512,960]{1,0:T(8,128)} %get-tuple-element.74.h, ...), custom_call_target="tpu_custom_call" | custom-call | flops 10000000000 | bytes 30000000 | tf_op jit(solution)/shard_map/feed/pallas_call | solution.py:471
  319.0 24.4 %feed_back.2 = (bf16[5,512,512]{2,1,0:T(8,128)(2,1)}, bf16[5,512,512]{2,1,0:T(8,128)(2,1)}, bf16[512,960]{1,0:T(8,128)(2,1)}, f32[512,960]{1,0:T(8,128)}, bf16[5...) custom-call(s32[1]{0:T(128)} %bitcast.f_ref, bf16[512,960]{1,0:T(8,128)(2,1)} %pad_maximum_fusion.1.g, ...), custom_call_target="tpu_custom_call" | custom-call | flops 10000000000 | bytes 30000000 | tf_op jit(solution)/shard_map/feed_back/pallas_call | solution.py:558
  344.6 51.5 %attend_back.2 = (bf16[512,1024]{1,0:T(8,128)(2,1)S(1)}, bf16[2,5,512,128]{3,2,1,0:T(8,128)(2,1)}, bf16[2,5,512,128]{3,2,1,0:T(8,128)(2,1)}) custom-call(s32[1]{0:T(128)} %bitcast.f_ref, bf16[15,512,128]{2,1,0:T(8,128)(2,1)} %copy-done.32, bf16[15,512,128]{2,1,0:T(8,128)(2,1)} %get-tuple-element.80.marks, bf16[2048,128]{1,0:T(8,128)(2,1)S(1)} %fusion.12.key_marks, ...), custom_call_target="tpu_custom_call" | custom-call | flops 30000001024 | bytes 12000000 | tf_op jit(solution)/shard_map/attend_back/pallas_call | solution.py:254
  403.1 8.5 %collective-permute-done.22 = bf16[256,960]{1,0:T(8,128)(2,1)} collective-permute-done((bf16[256,960]{1,0:T(8,128)(2,1)}, bf16[256,960]{1,0:T(8,128)(2,1)}, u32[]{:S(2)}, u32[]{:S(2)}) %collective-permute-start.22) | collective-permute-done | bytes 491552 | tf_op jit(solution)/shard_map/ppermute | solution.py:738
  417.6 8.4 %collective-permute-done.25.came = bf16[5,512,128]{2,1,0:T(8,128)(2,1)} collective-permute-done((bf16[5,512,128]{2,1,0:T(8,128)(2,1)}, bf16[5,512,128]{2,1,0:T(8,128)(2,1)}, u32[]{:S(2)}, u32[]{:S(2)}) %collective-permute-start.25) | collective-permute-done | bytes 655392 | tf_op jit(solution)/shard_map/ppermute | solution.py:738
  427.3 6.7 project_back.2
  436.5 24.8 %feed_back.3 = (bf16[5,512,512]{2,1,0:T(8,128)(2,1)}, bf16[5,512,512]{2,1,0:T(8,128)(2,1)}, bf16[512,960]{1,0:T(8,128)(2,1)}, f32[512,960]{1,0:T(8,128)}, bf16[5...) custom-call(s32[1]{0:T(128)} %bitcast.f_ref, f32[512,960]{1,0:T(8,128)} %copy-done.20, ...), custom_call_target="tpu_custom_call" | custom-call | flops 10000000000 | bytes 30000000 | tf_op jit(solution)/shard_map/feed_back/pallas_call | solution.py:558
  462.5 51.5 %attend_back.3 = (bf16[512,1024]{1,0:T(8,128)(2,1)S(1)}, bf16[2,5,512,128]{3,2,1,0:T(8,128)(2,1)}, bf16[2,5,512,128]{3,2,1,0:T(8,128)(2,1)}) custom-call(s32[1]{0:T(128)} %bitcast.f_ref, bf16[15,512,128]{2,1,0:T(8,128)(2,1)} %copy-done.37, bf16[15,512,128]{2,1,0:T(8,128)(2,1)} %get-tuple-element.79.marks, bf16[2048,128]{1,0:T(8,128)(2,1)S(1)} %fusion.12.key_marks, ...), custom_call_target="tpu_custom_call" | custom-call | flops 30000001024 | bytes 12000000 | tf_op jit(solution)/shard_map/attend_back/pallas_call | solution.py:254
  517.2 15.2 %outer_ffn.1 = (bf16[2,240,2560]{2,1,0:T(8,128)(2,1)S(1)}, bf16[2,240,2560]{2,1,0:T(8,128)(2,1)}, bf16[2,240,2560]{2,1,0:T(8,128)(2,1)}, bf16[2,240,2560]{2,1,0:T(8,128)(2,1)}) custom-call(s32[1]{0:T(128)} %bitcast.f_ref, bf16[960,512]{1,0:T(8,128)(2,1)S(1)} %copy-done.45, bf16[960,512]{1,0:T(8,128)(2,1)S(1)} %copy-done.43, ...), custom_call_target="tpu_custom_call" | custom-call | flops 10066329600 | bytes 20000000 | tf_op jit(solution)/shard_map/outer_ffn/pallas_call | solution.py:678
  536.3 9.1 %outer_down.1 = (bf16[2,640,960]{2,1,0:T(8,128)(2,1)S(1)}, bf16[2,640,960]{2,1,0:T(8,128)(2,1)}) custom-call(s32[1]{0:T(128)} %bitcast.f_ref, bf16[2560,512]{1,0:T(8,128)(2,1)} %bitcast.87, bf16[2560,512]{1,0:T(8,128)(2,1)} %bitcast.88, bf16[512,960]{1,0:T(8,128)(2,1)S(1)} %copy-done.38, bf16[512,960]{1,0:T(8,128)(2,1)S(1)} %copy-done.40), custom_call_target="tpu_custom_call" | custom-call | flops 5033164800 | bytes 12000000 | tf_op jit(solution)/shard_map/outer_down/pallas_call | solution.py:718
  545.5 4.4 copy.144
  555.6 6.2 collective-permute-done.39
  563.8 3.3 collective-permute-done.40
  572.0 4.8 project_back.3
  580.3 3.4 collective-permute-done.42
  585.2 3.6 collective-permute-done.43
  595.5 7.2 outer_in.1
  605.0 5.3 collective-permute-done.44
  614.8 3.1 convert_add_fusion.2
  627.9 4.5 copy.145
  632.4 5.2 convert_add_fusion
  646.2 3.1 collective-permute-done.46
  653.1 22.5 %collective-permute-done.54 = bf16[240,2560]{1,0:T(8,128)(2,1)} collective-permute-done((bf16[240,2560]{1,0:T(8,128)(2,1)}, bf16[240,2560]{1,0:T(8,128)(2,1)}, u32[]{:S(2)}, u32[]{:S(2)}) %collective-permute-start.54) | collective-permute-done | bytes 1228832 | tf_op jit(solution)/shard_map/ppermute | solution.py:738
  678.6 23.3 %collective-permute-done.62 = bf16[640,960]{0,1:T(8,128)(2,1)} collective-permute-done((bf16[640,960]{0,1:T(8,128)(2,1)}, bf16[640,960]{0,1:T(8,128)(2,1)}, u32[]{:S(2)}, u32[]{:S(2)}) %collective-permute-start.62) | collective-permute-done | bytes 1228832 | tf_op jit(solution)/shard_map/ppermute | solution.py:738
  712.4 10.8 %collective-permute-done.63 = bf16[320,960]{1,0:T(8,128)(2,1)S(1)} collective-permute-done((bf16[320,960]{1,0:T(8,128)(2,1)S(1)}, bf16[320,960]{1,0:T(8,128)(2,1)S(1)}, u32[]{:S(2)}, u32[]{:S(2)}) %collective-permute-start.63) | collective-permute-done | bytes 614432 | tf_op jit(solution)/shard_map/ppermute | solution.py:738
  729.1 6.5 collective-permute-done.64
  741.7 17.3 %collective-permute-done.57 = bf16[120,640]{1,0:T(8,128)(2,1)S(1)} collective-permute-done((bf16[120,640]{1,0:T(8,128)(2,1)S(1)}, bf16[120,640]{1,0:T(8,128)(2,1)S(1)}, u32[]{:S(2)}, u32[]{:S(2)}) %collective-permute-start.57) | collective-permute-done | bytes 153632 | tf_op jit(solution)/shard_map/ppermute | solution.py:738
  759.5 3.0 collective-permute-start.33
  762.7 10.7 %collective-permute-done.33 = bf16[120,416]{1,0:T(8,128)(2,1)S(1)} collective-permute-done((bf16[120,416]{1,0:T(8,128)(2,1)S(1)}, bf16[120,416]{1,0:T(8,128)(2,1)S(1)}, u32[]{:S(2)}, u32[]{:S(2)}) %collective-permute-start.33) | collective-permute-done | bytes 99872 | tf_op jit(solution)/shard_map/ppermute | solution.py:738
  773.7 5.7 collective-permute-done.34
  782.0 7.9 collective-permute-done.35
  793.2 8.5 %collective-permute-done.67 = bf16[160,960]{1,0:T(8,128)(2,1)S(1)} collective-permute-done((bf16[160,960]{1,0:T(8,128)(2,1)S(1)}, bf16[160,960]{1,0:T(8,128)(2,1)S(1)}, u32[]{:S(2)}, u32[]{:S(2)}) %collective-permute-start.67) | collective-permute-done | bytes 307232 | tf_op jit(solution)/shard_map/ppermute | solution.py:738
  809.3 20.4 %collective-permute-done.68 = bf16[320,960]{1,0:T(8,128)(2,1)} collective-permute-done((bf16[320,960]{1,0:T(8,128)(2,1)S(1)}, bf16[320,960]{1,0:T(8,128)(2,1)}, u32[]{:S(2)}, u32[]{:S(2)}) %collective-permute-start.68) | collective-permute-done | bytes 614432 | tf_op jit(solution)/shard_map/ppermute | solution.py:738
  833.4 3.4 fusion.8
  838.5 3.5 fusion.9
  (377 shorter events, 181.2 us)
Async XLA Ops:
  3.2 21.7 %collective-permute-start.2 = (bf16[240,1664]{1,0:T(8,128)(2,1)S(1)}, bf16[240,1664]{1,0:T(8,128)(2,1)S(1)}, u32[]{:S(2)}, u32[]{:S(2)}) collective-permute-start(bf16[240,1664]{1,0:T(8,128)(2,1)S(1)} %concatenate.125.own), channel_id=1, source_target_pairs={{0,2},{1,3},{2,0},{3,1},{4,6},{5,7},{6,4},{7,5},{8,10},{9,11},{10,... | collective-permute-start | bytes 2396168 | tf_op jit(solution)/shard_map/ppermute | solution.py:738
  6.2 31.1 %collective-permute-start.1 = (bf16[240,1664]{1,0:T(8,128)(2,1)S(1)}, bf16[240,1664]{1,0:T(8,128)(2,1)}, u32[]{:S(2)}, u32[]{:S(2)}) collective-permute-start(bf16[240,1664]{1,0:T(8,128)(2,1)S(1)} %concatenate.125.own), channel_id=1, source_target_pairs={{0,1},{1,0},{2,3},{3,2},{4,5},{5,4},{6,7},{7,6},{8,9},{9,8},{10,11... | collective-permute-start | bytes 2396168 | tf_op jit(solution)/shard_map/ppermute | solution.py:738
  8.5 27.3 %collective-permute-start = (bf16[256,960]{1,0:T(8,128)(2,1)}, bf16[256,960]{1,0:T(8,128)(2,1)}, u32[]{:S(2)}, u32[]{:S(2)}) collective-permute-start(bf16[256,960]{1,0:T(8,128)(2,1)} %bitcast.2), channel_id=1, source_target_pairs={{0,3},{1,2},{2,1},{3,0},{4,7},{5,6},{6,5},{7,4},{8,11},{9,10},{10,... | collective-permute-start | bytes 1474568 | tf_op jit(solution)/shard_map/ppermute | solution.py:738
  9.0 53.5 %collective-permute-start.17 = (bf16[640,960]{0,1:T(8,128)(2,1)}, bf16[640,960]{0,1:T(8,128)(2,1)}, u32[]{:S(2)}, u32[]{:S(2)}) collective-permute-start(bf16[640,960]{0,1:T(8,128)(2,1)} %param.20), channel_id=1, source_target_pairs={{0,2},{1,3},{2,0},{3,1},{4,6},{5,7},{6,4},{7,5},{8,10},{9,11},{10,... | collective-permute-start | bytes 3686408 | tf_op jit(solution)/shard_map/ppermute | solution.py:738
  24.9 39.7 %collective-permute-start.3 = (bf16[240,1664]{1,0:T(8,128)(2,1)S(1)}, bf16[240,1664]{1,0:T(8,128)(2,1)}, u32[]{:S(2)}, u32[]{:S(2)}) collective-permute-start(bf16[240,1664]{1,0:T(8,128)(2,1)S(1)} %collective-permute-done.2.far), channel_id=1, source_target_pairs={{0,1},{1,0},{2,3},{3,2},{4,5},{5,4},{6,7},{7,6},{8,9},{9,8},{10,11... | collective-permute-start | bytes 2396168 | tf_op jit(solution)/shard_map/ppermute | solution.py:738
  25.7 75.6 %collective-permute-start.11 = (bf16[240,2560]{1,0:T(8,128)(2,1)}, bf16[240,2560]{1,0:T(8,128)(2,1)}, u32[]{:S(2)}, u32[]{:S(2)}) collective-permute-start(bf16[240,2560]{1,0:T(8,128)(2,1)} %refs_4_.7), channel_id=1, source_target_pairs={{0,2},{1,3},{2,0},{3,1},{4,6},{5,7},{6,4},{7,5},{8,10},{9,11},{10,... | collective-permute-start | bytes 3686408 | tf_op jit(solution)/shard_map/ppermute | solution.py:738
  35.8 63.5 %collective-permute-start.8 = (bf16[240,960]{1,0:T(8,128)(2,1)}, bf16[240,960]{1,0:T(8,128)(2,1)S(1)}, u32[]{:S(2)}, u32[]{:S(2)}) collective-permute-start(bf16[240,960]{1,0:T(8,128)(2,1)} %refs_0_.7), channel_id=1, source_target_pairs={{0,2},{1,3},{2,0},{3,1},{4,6},{5,7},{6,4},{7,5},{8,10},{9,11},{10,... | collective-permute-start | bytes 1382408 | tf_op jit(solution)/shard_map/ppermute | solution.py:738
  37.3 102.6 %collective-permute-start.16 = (bf16[640,960]{0,1:T(8,128)(2,1)S(1)}, bf16[640,960]{0,1:T(8,128)(2,1)S(1)}, u32[]{:S(2)}, u32[]{:S(2)}) collective-permute-start(bf16[640,960]{0,1:T(8,128)(2,1)S(1)} %copy-done.57), channel_id=1, source_target_pairs={{0,1},{1,0},{2,3},{3,2},{4,5},{5,4},{6,7},{7,6},{8,9},{9,8},{10,11... | collective-permute-start | bytes 3686408 | tf_op jit(solution)/shard_map/ppermute | solution.py:738
  62.5 76.8 %collective-permute-start.14 = (bf16[240,2560]{1,0:T(8,128)(2,1)}, bf16[240,2560]{1,0:T(8,128)(2,1)}, u32[]{:S(2)}, u32[]{:S(2)}) collective-permute-start(bf16[240,2560]{1,0:T(8,128)(2,1)} %refs_8_.7), channel_id=1, source_target_pairs={{0,2},{1,3},{2,0},{3,1},{4,6},{5,7},{6,4},{7,5},{8,10},{9,11},{10,... | collective-permute-start | bytes 3686408 | tf_op jit(solution)/shard_map/ppermute | solution.py:738
  64.6 76.7 %collective-permute-start.18 = (bf16[640,960]{0,1:T(8,128)(2,1)}, bf16[640,960]{0,1:T(8,128)(2,1)S(1)}, u32[]{:S(2)}, u32[]{:S(2)}) collective-permute-start(bf16[640,960]{0,1:T(8,128)(2,1)} %collective-permute-done.17), channel_id=1, source_target_pairs={{0,1},{1,0},{2,3},{3,2},{4,5},{5,4},{6,7},{7,6},{8,9},{9,8},{10,11... | collective-permute-start | bytes 3686408 | tf_op jit(solution)/shard_map/ppermute | solution.py:738
  99.3 39.7 %collective-permute-start.5 = (bf16[5,512,128]{2,1,0:T(8,128)(2,1)S(1)}, bf16[5,512,128]{2,1,0:T(8,128)(2,1)}, u32[]{:S(2)}, u32[]{:S(2)}) collective-permute-start(bf16[5,512,128]{2,1,0:T(8,128)(2,1)S(1)} %get-tuple-element.72.own), channel_id=1, source_target_pairs={{0,2},{1,3},{2,0},{3,1},{4,6},{5,7},{6,4},{7,5},{8,10},{9,11},{10,... | collective-permute-start | bytes 1966088 | tf_op jit(solution)/shard_map/ppermute | solution.py:738
  101.4 38.6 %collective-permute-start.4 = (bf16[5,512,128]{2,1,0:T(8,128)(2,1)S(1)}, bf16[5,512,128]{2,1,0:T(8,128)(2,1)S(1)}, u32[]{:S(2)}, u32[]{:S(2)}) collective-permute-start(bf16[5,512,128]{2,1,0:T(8,128)(2,1)S(1)} %get-tuple-element.72.own), channel_id=1, source_target_pairs={{0,1},{1,0},{2,3},{3,2},{4,5},{5,4},{6,7},{7,6},{8,9},{9,8},{10,11... | collective-permute-start | bytes 1966088 | tf_op jit(solution)/shard_map/ppermute | solution.py:738
  139.3 52.2 %collective-permute-start.10 = (bf16[240,2560]{1,0:T(8,128)(2,1)}, bf16[240,2560]{1,0:T(8,128)(2,1)}, u32[]{:S(2)}, u32[]{:S(2)}) collective-permute-start(bf16[240,2560]{1,0:T(8,128)(2,1)} %refs_4_.7), channel_id=1, source_target_pairs={{0,1},{1,0},{2,3},{3,2},{4,5},{5,4},{6,7},{7,6},{8,9},{9,8},{10,11... | collective-permute-start | bytes 3686408 | tf_op jit(solution)/shard_map/ppermute | solution.py:738
  139.9 51.6 %collective-permute-start.13 = (bf16[240,2560]{1,0:T(8,128)(2,1)}, bf16[240,2560]{1,0:T(8,128)(2,1)}, u32[]{:S(2)}, u32[]{:S(2)}) collective-permute-start(bf16[240,2560]{1,0:T(8,128)(2,1)} %refs_8_.7), channel_id=1, source_target_pairs={{0,1},{1,0},{2,3},{3,2},{4,5},{5,4},{6,7},{7,6},{8,9},{9,8},{10,11... | collective-permute-start | bytes 3686408 | tf_op jit(solution)/shard_map/ppermute | solution.py:738
  141.1 50.4 %collective-permute-start.12 = (bf16[240,2560]{1,0:T(8,128)(2,1)}, bf16[240,2560]{1,0:T(8,128)(2,1)}, u32[]{:S(2)}, u32[]{:S(2)}) collective-permute-start(bf16[240,2560]{1,0:T(8,128)(2,1)} %collective-permute-done.11.refs_6_), channel_id=1, source_target_pairs={{0,1},{1,0},{2,3},{3,2},{4,5},{5,4},{6,7},{7,6},{8,9},{9,8},{10,11... | collective-permute-start | bytes 3686408 | tf_op jit(solution)/shard_map/ppermute | solution.py:738
  141.3 50.3 %collective-permute-start.15 = (bf16[240,2560]{1,0:T(8,128)(2,1)}, bf16[240,2560]{1,0:T(8,128)(2,1)}, u32[]{:S(2)}, u32[]{:S(2)}) collective-permute-start(bf16[240,2560]{1,0:T(8,128)(2,1)} %collective-permute-done.14.refs_10_), channel_id=1, source_target_pairs={{0,1},{1,0},{2,3},{3,2},{4,5},{5,4},{6,7},{7,6},{8,9},{9,8},{10,11... | collective-permute-start | bytes 3686408 | tf_op jit(solution)/shard_map/ppermute | solution.py:738
  152.4 39.1 %collective-permute-start.9 = (bf16[240,960]{1,0:T(8,128)(2,1)}, bf16[240,960]{1,0:T(8,128)(2,1)S(1)}, u32[]{:S(2)}, u32[]{:S(2)}) collective-permute-start(bf16[240,960]{1,0:T(8,128)(2,1)} %copy-done.67), channel_id=1, source_target_pairs={{0,1},{1,0},{2,3},{3,2},{4,5},{5,4},{6,7},{7,6},{8,9},{9,8},{10,11... | collective-permute-start | bytes 1382408 | tf_op jit(solution)/shard_map/ppermute | solution.py:738
  224.1 17.1 %collective-permute-start.20 = (bf16[5,512,128]{2,1,0:T(8,128)(2,1)}, bf16[5,512,128]{2,1,0:T(8,128)(2,1)}, u32[]{:S(2)}, u32[]{:S(2)}) collective-permute-start(bf16[5,512,128]{2,1,0:T(8,128)(2,1)} %get-tuple-element.76.own), channel_id=1, source_target_pairs={{0,2},{1,3},{2,0},{3,1},{4,6},{5,7},{6,4},{7,5},{8,10},{9,11},{10,... | collective-permute-start | bytes 1966088 | tf_op jit(solution)/shard_map/ppermute | solution.py:738
  225.8 34.7 %collective-permute-start.19 = (bf16[5,512,128]{2,1,0:T(8,128)(2,1)}, bf16[5,512,128]{2,1,0:T(8,128)(2,1)}, u32[]{:S(2)}, u32[]{:S(2)}) collective-permute-start(bf16[5,512,128]{2,1,0:T(8,128)(2,1)} %get-tuple-element.76.own), channel_id=1, source_target_pairs={{0,1},{1,0},{2,3},{3,2},{4,5},{5,4},{6,7},{7,6},{8,9},{9,8},{10,11... | collective-permute-start | bytes 1966088 | tf_op jit(solution)/shard_map/ppermute | solution.py:738
  241.2 19.4 %collective-permute-start.21 = (bf16[5,512,128]{2,1,0:T(8,128)(2,1)}, bf16[5,512,128]{2,1,0:T(8,128)(2,1)}, u32[]{:S(2)}, u32[]{:S(2)}) collective-permute-start(bf16[5,512,128]{2,1,0:T(8,128)(2,1)} %collective-permute-done.20.far), channel_id=1, source_target_pairs={{0,1},{1,0},{2,3},{3,2},{4,5},{5,4},{6,7},{7,6},{8,9},{9,8},{10,11... | collective-permute-start | bytes 1966088 | tf_op jit(solution)/shard_map/ppermute | solution.py:738
  401.5 24.6 %collective-permute-start.25 = (bf16[5,512,128]{2,1,0:T(8,128)(2,1)}, bf16[5,512,128]{2,1,0:T(8,128)(2,1)}, u32[]{:S(2)}, u32[]{:S(2)}) collective-permute-start(bf16[5,512,128]{2,1,0:T(8,128)(2,1)} %fusion.16), channel_id=1, source_target_pairs={{0,2},{1,3},{2,0},{3,1},{4,6},{5,7},{6,4},{7,5},{8,10},{9,11},{10,... | collective-permute-start | bytes 1966088 | tf_op jit(solution)/shard_map/ppermute | solution.py:738
  514.0 35.9 %collective-permute-start.26 = (bf16[2,5,512,128]{3,2,1,0:T(8,128)(2,1)}, bf16[2,5,512,128]{3,2,1,0:T(8,128)(2,1)}, u32[]{:S(2)}, u32[]{:S(2)}) collective-permute-start(bf16[2,5,512,128]{3,2,1,0:T(8,128)(2,1)} %get-tuple-element.96), channel_id=1, source_target_pairs={{0,1},{1,0},{2,3},{3,2},{4,5},{5,4},{6,7},{7,6},{8,9},{9,8},{10,11... | collective-permute-start | bytes 3932168 | tf_op jit(solution)/shard_map/ppermute | solution.py:738
  532.4 82.4 %collective-permute-start.45 = (bf16[2,240,2560]{2,1,0:T(8,128)(2,1)}, bf16[2,240,2560]{2,1,0:T(8,128)(2,1)}, u32[]{:S(2)}, u32[]{:S(2)}) collective-permute-start(bf16[2,240,2560]{2,1,0:T(8,128)(2,1)} %get-tuple-element.118), channel_id=1, source_target_pairs={{0,1},{1,0},{2,3},{3,2},{4,5},{5,4},{6,7},{7,6},{8,9},{9,8},{10,11... | collective-permute-start | bytes 7372808 | tf_op jit(solution)/shard_map/ppermute | solution.py:738
  532.4 88.2 %collective-permute-start.53 = (bf16[2,240,2560]{2,1,0:T(8,128)(2,1)}, bf16[2,240,2560]{2,1,0:T(8,128)(2,1)}, u32[]{:S(2)}, u32[]{:S(2)}) collective-permute-start(bf16[2,240,2560]{2,1,0:T(8,128)(2,1)} %get-tuple-element.120), channel_id=1, source_target_pairs={{0,1},{1,0},{2,3},{3,2},{4,5},{5,4},{6,7},{7,6},{8,9},{9,8},{10,11... | collective-permute-start | bytes 7372808 | tf_op jit(solution)/shard_map/ppermute | solution.py:738
  534.7 17.4 %collective-permute-start.38 = (bf16[240,960]{1,0:T(8,128)(2,1)}, bf16[240,960]{1,0:T(8,128)(2,1)}, u32[]{:S(2)}, u32[]{:S(2)}) collective-permute-start(bf16[240,960]{1,0:T(8,128)(2,1)} %fusion.18), channel_id=1, source_target_pairs={{0,2},{1,3},{2,0},{3,1},{4,6},{5,7},{6,4},{7,5},{8,10},{9,11},{10,... | collective-permute-start | bytes 1382408 | tf_op jit(solution)/shard_map/ppermute | solution.py:738
  549.8 78.1 %collective-permute-start.61 = (bf16[2,640,960]{1,2,0:T(8,128)(2,1)}, bf16[2,640,960]{1,2,0:T(8,128)(2,1)}, u32[]{:S(2)}, u32[]{:S(2)}) collective-permute-start(bf16[2,640,960]{1,2,0:T(8,128)(2,1)} %copy.144), channel_id=1, source_target_pairs={{0,1},{1,0},{2,3},{3,2},{4,5},{5,4},{6,7},{7,6},{8,9},{9,8},{10,11... | collective-permute-start | bytes 7372808 | tf_op jit(solution)/shard_map/ppermute | solution.py:738
  555.1 16.9 %collective-permute-start.27 = (bf16[5,512,128]{2,1,0:T(8,128)(2,1)S(1)}, bf16[5,512,128]{2,1,0:T(8,128)(2,1)S(1)}, u32[]{:S(2)}, u32[]{:S(2)}) collective-permute-start(bf16[5,512,128]{2,1,0:T(8,128)(2,1)S(1)} %fusion.17), channel_id=1, source_target_pairs={{0,2},{1,3},{2,0},{3,1},{4,6},{5,7},{6,4},{7,5},{8,10},{9,11},{10,... | collective-permute-start | bytes 1966088 | tf_op jit(solution)/shard_map/ppermute | solution.py:738
  590.2 21.2 %collective-permute-start.28 = (bf16[256,960]{1,0:T(8,128)(2,1)S(1)}, bf16[256,960]{1,0:T(8,128)(2,1)S(1)}, u32[]{:S(2)}, u32[]{:S(2)}) collective-permute-start(bf16[256,960]{1,0:T(8,128)(2,1)S(1)} %get-tuple-element.189), channel_id=1, source_target_pairs={{0,3},{1,2},{2,1},{3,0},{4,7},{5,6},{6,5},{7,4},{8,11},{9,10},{10,... | collective-permute-start | bytes 1474568 | tf_op jit(solution)/shard_map/ppermute | solution.py:738
  610.3 31.5 %collective-permute-start.29 = (bf16[2,240,1664]{2,1,0:T(8,128)(2,1)}, bf16[2,240,1664]{2,1,0:T(8,128)(2,1)}, u32[]{:S(2)}, u32[]{:S(2)}) collective-permute-start(bf16[2,240,1664]{2,1,0:T(8,128)(2,1)} %get-tuple-element.104), channel_id=1, source_target_pairs={{0,1},{1,0},{2,3},{3,2},{4,5},{5,4},{6,7},{7,6},{8,9},{9,8},{10,11... | collective-permute-start | bytes 4792328 | tf_op jit(solution)/shard_map/ppermute | solution.py:738
  619.1 30.1 %collective-permute-start.46 = (bf16[240,2560]{1,0:T(8,128)(2,1)}, bf16[240,2560]{1,0:T(8,128)(2,1)}, u32[]{:S(2)}, u32[]{:S(2)}) collective-permute-start(bf16[240,2560]{1,0:T(8,128)(2,1)} %fusion.6), channel_id=1, source_target_pairs={{0,2},{1,3},{2,0},{3,1},{4,6},{5,7},{6,4},{7,5},{8,10},{9,11},{10,... | collective-permute-start | bytes 3686408 | tf_op jit(solution)/shard_map/ppermute | solution.py:738
  626.4 49.2 %collective-permute-start.54 = (bf16[240,2560]{1,0:T(8,128)(2,1)}, bf16[240,2560]{1,0:T(8,128)(2,1)}, u32[]{:S(2)}, u32[]{:S(2)}) collective-permute-start(bf16[240,2560]{1,0:T(8,128)(2,1)} %fusion.7), channel_id=1, source_target_pairs={{0,2},{1,3},{2,0},{3,1},{4,6},{5,7},{6,4},{7,5},{8,10},{9,11},{10,... | collective-permute-start | bytes 3686408 | tf_op jit(solution)/shard_map/ppermute | solution.py:738
  641.3 60.6 %collective-permute-start.62 = (bf16[640,960]{0,1:T(8,128)(2,1)}, bf16[640,960]{0,1:T(8,128)(2,1)}, u32[]{:S(2)}, u32[]{:S(2)}) collective-permute-start(bf16[640,960]{0,1:T(8,128)(2,1)} %copy.146), channel_id=1, source_target_pairs={{0,2},{1,3},{2,0},{3,1},{4,6},{5,7},{6,4},{7,5},{8,10},{9,11},{10,... | collective-permute-start | bytes 3686408 | tf_op jit(solution)/shard_map/ppermute | solution.py:738
  644.6 80.3 %collective-permute-start.30 = (bf16[240,1664]{1,0:T(8,128)(2,1)}, bf16[240,1664]{1,0:T(8,128)(2,1)S(1)}, u32[]{:S(2)}, u32[]{:S(2)}) collective-permute-start(bf16[240,1664]{1,0:T(8,128)(2,1)} %fusion.14), channel_id=1, source_target_pairs={{0,2},{1,3},{2,0},{3,1},{4,6},{5,7},{6,4},{7,5},{8,10},{9,11},{10,... | collective-permute-start | bytes 2396168 | tf_op jit(solution)/shard_map/ppermute | solution.py:738
  652.5 55.2 %collective-permute-start.47 = (bf16[240,1280]{1,0:T(8,128)(2,1)}, bf16[240,1280]{1,0:T(8,128)(2,1)}, u32[]{:S(2)}, u32[]{:S(2)}) collective-permute-start(bf16[240,1280]{1,0:T(8,128)(2,1)} %dynamic-slice_convert_fusion.2), channel_id=1, source_target_pairs={{0,4},{4,0},{8,12},{12,8},{16,20},{20,16},{24,28},{28,24},{1,5},{5... | collective-permute-start | bytes 1843208 | tf_op jit(solution)/shard_map/ppermute | solution.py:738
  678.1 32.4 %collective-permute-start.55 = (bf16[240,1280]{1,0:T(8,128)(2,1)}, bf16[240,1280]{1,0:T(8,128)(2,1)}, u32[]{:S(2)}, u32[]{:S(2)}) collective-permute-start(bf16[240,1280]{1,0:T(8,128)(2,1)} %dynamic-slice_convert_fusion.1), channel_id=1, source_target_pairs={{0,4},{4,0},{8,12},{12,8},{16,20},{20,16},{24,28},{28,24},{1,5},{5... | collective-permute-start | bytes 1843208 | tf_op jit(solution)/shard_map/ppermute | solution.py:738
  709.0 16.8 %collective-permute-start.48 = (bf16[240,640]{1,0:T(8,128)(2,1)S(1)}, bf16[240,640]{1,0:T(8,128)(2,1)S(1)}, u32[]{:S(2)}, u32[]{:S(2)}) collective-permute-start(bf16[240,640]{1,0:T(8,128)(2,1)S(1)} %dynamic-slice_convert_fusion.6), channel_id=1, source_target_pairs={{0,8},{4,12},{8,0},{12,4},{16,24},{20,28},{24,16},{28,20},{1,9},{5... | collective-permute-start | bytes 921608 | tf_op jit(solution)/shard_map/ppermute | solution.py:738
  726.1 32.9 %collective-permute-start.57 = (bf16[120,640]{1,0:T(8,128)(2,1)S(1)}, bf16[120,640]{1,0:T(8,128)(2,1)S(1)}, u32[]{:S(2)}, u32[]{:S(2)}) collective-permute-start(bf16[120,640]{1,0:T(8,128)(2,1)S(1)} %dynamic-slice_convert_fusion.10), channel_id=1, source_target_pairs={{0,16},{4,20},{8,24},{12,28},{16,0},{20,4},{24,8},{28,12},{1,17},{... | collective-permute-start | bytes 460808 | tf_op jit(solution)/shard_map/ppermute | solution.py:738
  735.7 26.8 %collective-permute-start.65 = (bf16[80,960]{1,0:T(8,128)(2,1)S(1)}, bf16[80,960]{1,0:T(8,128)(2,1)S(1)}, u32[]{:S(2)}, u32[]{:S(2)}) collective-permute-start(bf16[80,960]{1,0:T(8,128)(2,1)S(1)} %dynamic-slice_convert_fusion.9), channel_id=1, source_target_pairs={{0,16},{4,20},{8,24},{12,28},{16,0},{20,4},{24,8},{28,12},{1,17},{... | collective-permute-start | bytes 460808 | tf_op jit(solution)/shard_map/ppermute | solution.py:738
  737.6 21.6 %collective-permute-start.32 = (bf16[120,832]{1,0:T(8,128)(2,1)S(1)}, bf16[120,832]{1,0:T(8,128)(2,1)S(1)}, u32[]{:S(2)}, u32[]{:S(2)}) collective-permute-start(bf16[120,832]{1,0:T(8,128)(2,1)S(1)} %dynamic-slice_convert_fusion.8), channel_id=1, source_target_pairs={{0,8},{4,12},{8,0},{12,4},{16,24},{20,28},{24,16},{28,20},{1,9},{5... | collective-permute-start | bytes 599048 | tf_op jit(solution)/shard_map/ppermute | solution.py:738
  741.6 32.0 %collective-permute-start.50 = (bf16[120,640]{1,0:T(8,128)(2,1)S(1)}, bf16[120,640]{1,0:T(8,128)(2,1)S(1)}, u32[]{:S(2)}, u32[]{:S(2)}) collective-permute-start(bf16[120,640]{1,0:T(8,128)(2,1)S(1)} %add_convert_fusion.2), channel_id=1, source_target_pairs={{0,16},{4,20},{8,24},{12,28},{16,0},{20,4},{24,8},{28,12},{1,17},{... | collective-permute-start | bytes 460808 | tf_op jit(solution)/shard_map/ppermute | solution.py:738
  759.1 20.6 %collective-permute-start.58 = (bf16[120,640]{1,0:T(8,128)(2,1)S(1)}, bf16[120,640]{1,0:T(8,128)(2,1)S(1)}, u32[]{:S(2)}, u32[]{:S(2)}) collective-permute-start(bf16[120,640]{1,0:T(8,128)(2,1)S(1)} %add_convert_fusion.1), channel_id=1, source_target_pairs={{0,16},{4,20},{8,24},{12,28},{16,0},{20,4},{24,8},{28,12},{1,17},{... | collective-permute-start | bytes 460808 | tf_op jit(solution)/shard_map/ppermute | solution.py:738
  762.6 19.3 %collective-permute-start.66 = (bf16[80,960]{1,0:T(8,128)(2,1)S(1)}, bf16[80,960]{1,0:T(8,128)(2,1)S(1)}, u32[]{:S(2)}, u32[]{:S(2)}) collective-permute-start(bf16[80,960]{1,0:T(8,128)(2,1)S(1)} %add_convert_fusion), channel_id=1, source_target_pairs={{0,16},{4,20},{8,24},{12,28},{16,0},{20,4},{24,8},{28,12},{1,17},{... | collective-permute-start | bytes 460808 | tf_op jit(solution)/shard_map/ppermute | solution.py:738
  773.7 17.7 %collective-permute-start.51 = (bf16[240,640]{1,0:T(8,128)(2,1)S(1)}, bf16[240,640]{1,0:T(8,128)(2,1)S(1)}, u32[]{:S(2)}, u32[]{:S(2)}) collective-permute-start(bf16[240,640]{1,0:T(8,128)(2,1)S(1)} %maximum_select_fusion.10), channel_id=1, source_target_pairs={{0,8},{4,12},{8,0},{12,4},{16,24},{20,28},{24,16},{28,20},{1,9},{5... | collective-permute-start | bytes 921608 | tf_op jit(solution)/shard_map/ppermute | solution.py:738
  779.8 22.8 %collective-permute-start.59 = (bf16[240,640]{1,0:T(8,128)(2,1)S(1)}, bf16[240,640]{1,0:T(8,128)(2,1)S(1)}, u32[]{:S(2)}, u32[]{:S(2)}) collective-permute-start(bf16[240,640]{1,0:T(8,128)(2,1)S(1)} %maximum_select_fusion.11), channel_id=1, source_target_pairs={{0,8},{4,12},{8,0},{12,4},{16,24},{20,28},{24,16},{28,20},{1,9},{5... | collective-permute-start | bytes 921608 | tf_op jit(solution)/shard_map/ppermute | solution.py:738
  781.9 19.8 %collective-permute-start.67 = (bf16[160,960]{1,0:T(8,128)(2,1)S(1)}, bf16[160,960]{1,0:T(8,128)(2,1)S(1)}, u32[]{:S(2)}, u32[]{:S(2)}) collective-permute-start(bf16[160,960]{1,0:T(8,128)(2,1)S(1)} %maximum_select_fusion.9), channel_id=1, source_target_pairs={{0,8},{4,12},{8,0},{12,4},{16,24},{20,28},{24,16},{28,20},{1,9},{5... | collective-permute-start | bytes 921608 | tf_op jit(solution)/shard_map/ppermute | solution.py:738
  792.4 41.0 %collective-permute-start.52 = (bf16[240,1280]{1,0:T(8,128)(2,1)}, bf16[240,1280]{1,0:T(8,128)(2,1)}, u32[]{:S(2)}, u32[]{:S(2)}) collective-permute-start(bf16[240,1280]{1,0:T(8,128)(2,1)} %maximum_select_fusion.5), channel_id=1, source_target_pairs={{0,4},{4,0},{8,12},{12,8},{16,20},{20,16},{24,28},{28,24},{1,5},{5... | collective-permute-start | bytes 1843208 | tf_op jit(solution)/shard_map/ppermute | solution.py:738
  802.0 27.7 %collective-permute-start.68 = (bf16[320,960]{1,0:T(8,128)(2,1)S(1)}, bf16[320,960]{1,0:T(8,128)(2,1)}, u32[]{:S(2)}, u32[]{:S(2)}) collective-permute-start(bf16[320,960]{1,0:T(8,128)(2,1)S(1)} %maximum_select_fusion.4), channel_id=1, source_target_pairs={{0,4},{4,0},{8,12},{12,8},{16,20},{20,16},{24,28},{28,24},{1,5},{5... | collective-permute-start | bytes 1843208 | tf_op jit(solution)/shard_map/ppermute | solution.py:738
  803.5 35.0 %collective-permute-start.60 = (bf16[240,1280]{1,0:T(8,128)(2,1)}, bf16[240,1280]{1,0:T(8,128)(2,1)}, u32[]{:S(2)}, u32[]{:S(2)}) collective-permute-start(bf16[240,1280]{1,0:T(8,128)(2,1)} %maximum_select_fusion.6), channel_id=1, source_target_pairs={{0,4},{4,0},{8,12},{12,8},{16,20},{20,16},{24,28},{28,24},{1,5},{5... | collective-permute-start | bytes 1843208 | tf_op jit(solution)/shard_map/ppermute | solution.py:738
  (97 other events, 2329.8 us)

commit v2 on v1

v2 whole, which is shorter than its diff:
```python
import functools
import jax
import jax.numpy as jnp
from jax import lax
from jax.experimental import pallas as pl
from jax.experimental.pallas import tpu as pltpu
from jax.sharding import PartitionSpec as P

HEADS = 15
KV_HEADS = 5
HEAD = 64
GROUP = HEADS // KV_HEADS
LANES = 128
NEGATIVE = -1e30
LOG2E = 1.4426950408889634
LN2 = 0.6931471805599453
MIB = 1 << 20
f32 = jnp.float32
bf16 = jnp.bfloat16


def nn(left, right):
    return lax.dot_general(left, right, (((1,), (0,)), ((), ())), preferred_element_type=f32)


def nt(left, right):
    return lax.dot_general(left, right, (((1,), (1,)), ((), ())), preferred_element_type=f32)


def lane_index(shape):
    return lax.broadcasted_iota(jnp.int32, shape, len(shape) - 1)


def swap_halves(tile):
    low = lane_index(tile.shape) % HEAD < HEAD // 2
    return jnp.where(low, pltpu.roll(tile, LANES - HEAD // 2, 1), pltpu.roll(tile, HEAD // 2, 1))


def three_terms(column, lane):
    high = column.astype(bf16).astype(f32)
    rest = column - high
    middle = rest.astype(bf16).astype(f32)
    low = rest - middle
    return jnp.where(lane == 8, high, jnp.where(lane == 9, middle, jnp.where(lane == 10, low, 0.0)))


def gather_keys(f, fresh, pieces, key_marks, kvf):
    block = kvf.shape[1]
    half = block // 2
    for m, piece in enumerate(pieces):
        device = f ^ m
        kvf[device, :half, :LANES] = piece[0, :half, :]
        kvf[3 - device, half:, :LANES] = piece[0, half:, :]

    @pl.when(fresh)
    def _():
        for j in range(kvf.shape[0]):
            kvf[j, :, LANES:] = key_marks[j * block : (j + 1) * block, :]


def causal(shape):
    row = lax.broadcasted_iota(jnp.int32, shape, 0)
    return lane_index(shape) <= row + (shape[1] - shape[0])


def score_parts(f):
    parts = [(0, f, 1, True), (1, 3 - f, 2, True)]
    for i in range(3):
        second = i >= f
        parts.append((second.astype(jnp.int32), jnp.where(second, i - f, i), 2, False))
    return parts


def attend_kernel(f_ref, q, q_marks, key_marks, own, near, far, last, attended, marks_out, kvf, qf, scores, best, top, acc):
    g = pl.program_id(0)
    f = f_ref[0]
    half = kvf.shape[1] // 2
    gather_keys(f, g == 0, (own, near, far, last), key_marks, kvf)
    parts = score_parts(f)

    @pl.when(g == 0)
    def _():
        for b in (0, 1):
            for i in range(GROUP):
                qf[b, i * half : (i + 1) * half, LANES:] = q_marks[b * half : (b + 1) * half, :]

    for b in (0, 1):
        for i in range(GROUP):
            qf[b, i * half : (i + 1) * half, :LANES] = q[i, b * half : (b + 1) * half, :]

    for n, (b, k, size, diagonal) in enumerate(parts):
        keys = kvf[k, : size * half, :]
        for i in range(GROUP):
            rows = slice(i * half, (i + 1) * half)
            s = nt(qf[b, rows, :], keys)
            if diagonal:
                s = jnp.where(causal(s.shape), s, NEGATIVE)
            scores[n, rows, : size * half] = s
            peak = s[:, :LANES]
            for t in range(1, size * half // LANES):
                peak = jnp.maximum(peak, s[:, t * LANES : (t + 1) * LANES])
            best[n, rows, :] = peak

    for b in (0, 1):
        for i in range(GROUP):
            rows = slice(i * half, (i + 1) * half)
            peak = best[b, rows, :]
            for n in (2, 3, 4):
                peak = jnp.maximum(peak, jnp.where(parts[n][0] == b, best[n, rows, :], NEGATIVE))
            top[b, rows, :] = jnp.broadcast_to(jnp.max(peak, axis=1, keepdims=True), peak.shape)

    for n, (b, k, size, _) in enumerate(parts):
        keys = kvf[k, : size * half, :]
        for i in range(GROUP):
            rows = slice(i * half, (i + 1) * half)
            high = jnp.concatenate([top[b, rows, :]] * (size * half // LANES), axis=1)
            p = jnp.exp2(scores[n, rows, : size * half] - high).astype(bf16)
            mixed = nn(p, keys)
            if n < 2:
                acc[b, rows, :] = mixed
            else:
                acc[b, rows, :] += mixed

    lane = lane_index((half, LANES))
    for b in (0, 1):
        outer = slice(b * half, (b + 1) * half)
        for i in range(GROUP):
            rows = slice(i * half, (i + 1) * half)
            total = acc[b, rows, LANES + 8 : LANES + 9]
            out = acc[b, rows, :LANES] * (1.0 / total)
            log_total = top[b, rows, :] + jnp.log2(total)
            new_marks = q_marks[outer, :].astype(f32) + three_terms(-log_total, lane)
            marks_out[i, outer, :] = new_marks.astype(bf16)
            h = GROUP * g + i
            pair = pl.multiple_of((h // 2) * LANES, LANES)
            odd = h % 2 == 1
            turned = pltpu.roll(out, HEAD, 1)
            old = attended[outer, pl.ds(pair, LANES)].astype(f32)
            new = jnp.where(odd, jnp.where(lane >= HEAD, out, old), jnp.where(lane < HEAD, turned, 0.0))
            attended[outer, pl.ds(pair, LANES)] = new.astype(bf16)


def pair_lanes(heads_here):
    return -(-GROUP * heads_here // 2) * LANES


def attend(f, q, q_marks, key_marks, pieces, group):
    first, heads_here = group
    tokens = q.shape[1]
    blocks = key_marks.shape[0] // tokens
    rows = GROUP * tokens // 2
    piece = pl.BlockSpec((1, tokens, LANES), lambda g, f: (g, 0, 0))
    width = pair_lanes(heads_here)
    return pl.pallas_call(
        attend_kernel,
        grid_spec=pltpu.PrefetchScalarGridSpec(
            num_scalar_prefetch=1,
            grid=(heads_here,),
            in_specs=[
                pl.BlockSpec((GROUP, tokens, LANES), lambda g, f: (first + g, 0, 0)),
                pl.BlockSpec((tokens, LANES), lambda g, f: (0, 0)),
                pl.BlockSpec(key_marks.shape, lambda g, f: (0, 0)),
                piece,
                piece,
                piece,
                piece,
            ],
            out_specs=[
                pl.BlockSpec((tokens, width), lambda g, f: (0, 0)),
                pl.BlockSpec((GROUP, tokens, LANES), lambda g, f: (g, 0, 0)),
            ],
            scratch_shapes=[
                pltpu.VMEM((blocks, tokens, 2 * LANES), bf16),
                pltpu.VMEM((2, rows, 2 * LANES), bf16),
                pltpu.VMEM((5, rows, tokens), f32),
                pltpu.VMEM((5, rows, LANES), f32),
                pltpu.VMEM((2, rows, LANES), f32),
                pltpu.VMEM((2, rows, 2 * LANES), f32),
            ],
        ),
        out_shape=[
            jax.ShapeDtypeStruct((tokens, width), bf16),
            jax.ShapeDtypeStruct((GROUP * heads_here, tokens, LANES), bf16),
        ],
        compiler_params=params(48),
        cost_estimate=cost(4e10, 1e6),
        name="attend",
    )(f, q, q_marks, key_marks, *pieces)


def attend_back_kernel(
    f_ref, q, marks, key_marks, own, near, far, last, grad, attended, cos_ref, sin_ref,
    grad_q, keep, send, kvf, kv_sum, qf, df, turned, acc, ds_all, p_all,
):
    g = pl.program_id(0)
    f = f_ref[0]
    half = kvf.shape[1] // 2
    gather_keys(f, g == 0, (own, near, far, last), key_marks, kvf)
    kv_sum[...] = jnp.zeros(kv_sum.shape, f32)
    lane = lane_index((half, LANES))
    for b in (0, 1):
        outer = slice(b * half, (b + 1) * half)
        for i in range(GROUP):
            rows = slice(i * half, (i + 1) * half)
            qf[b, rows, :LANES] = q[i, outer, :]
            qf[b, rows, LANES:] = marks[i, outer, :]
            h = GROUP * g + i
            pair = pl.multiple_of((h // 2) * LANES, LANES)
            odd = h % 2 == 1
            d_tile = grad[outer, pl.ds(pair, LANES)].astype(f32)
            o_tile = attended[outer, pl.ds(pair, LANES)].astype(f32)
            mine = (lane >= HEAD) == odd
            inner = jnp.sum(jnp.where(mine, d_tile * o_tile, 0.0), axis=1, keepdims=True)
            moved = jnp.where(odd, d_tile, pltpu.roll(d_tile, HEAD, 1))
            moved = jnp.where(lane >= HEAD, moved, 0.0)
            df[b, rows, :LANES] = moved.astype(bf16)
            df[b, rows, LANES:] = three_terms(-inner, lane).astype(bf16)
            joined = moved + q[i, outer, :].astype(f32)
            turned[b, :, rows] = joined.T.astype(bf16)

    for n, (b, k, size, diagonal) in enumerate(score_parts(f)):
        wide = size * half
        keys = kvf[k, :wide, :]
        for i in range(GROUP):
            rows = slice(i * half, (i + 1) * half)
            p = jnp.exp2(nt(qf[b, rows, :], keys))
            if diagonal:
                p = jnp.where(causal(p.shape), p, 0.0)
            ds_all[rows, :wide] = (p * nt(df[b, rows, :], keys)).astype(bf16)
            p_all[rows, :wide] = p.astype(bf16)
        part = nn(ds_all[:, :wide], keys[:, :LANES])
        if n < 2:
            acc[b] = part
        else:
            acc[b] += part
        kv_sum[k, :HEAD, :wide] += nn(turned[b, :HEAD, :], ds_all[:, :wide])
        kv_sum[k, HEAD:, :wide] += nn(turned[b, HEAD:, :], p_all[:, :wide])

    scale = HEAD ** (-0.5)
    for b in (0, 1):
        outer = slice(b * half, (b + 1) * half)
        for i in range(GROUP):
            rows = slice(i * half, (i + 1) * half)
            h = GROUP * g + i
            pair = pl.multiple_of((h // 2) * LANES, LANES)
            odd = h % 2 == 1
            tile = acc[b, rows, :] * scale
            tile = tile * cos_ref[outer, :] - swap_halves(tile) * sin_ref[outer, :]
            other = pltpu.roll(tile, HEAD, 1)
            old = grad_q[outer, pl.ds(pair, LANES)].astype(f32)
            new = jnp.where(odd, jnp.where(lane >= HEAD, other, old), jnp.where(lane < HEAD, tile, 0.0))
            grad_q[outer, pl.ds(pair, LANES)] = new.astype(bf16)

    factor = jnp.where(lane < HEAD, LN2, 1.0)
    for m in range(4):
        device = f ^ m
        ref = send if m % 2 else keep
        ref[m // 2, 0, :half, :] = (kv_sum[device, :, :half].T * factor).astype(bf16)
        ref[m // 2, 0, half:, :] = (kv_sum[3 - device, :, half:].T * factor).astype(bf16)


def attend_back(f, q, marks, key_marks, pieces, grad, attended, cos, sin, group):
    first, heads_here = group
    tokens = q.shape[1]
    blocks = key_marks.shape[0] // tokens
    rows = GROUP * tokens // 2
    piece = pl.BlockSpec((1, tokens, LANES), lambda g, f: (g, 0, 0))
    width = pair_lanes(heads_here)
    whole = pl.BlockSpec((tokens, width), lambda g, f: (0, 0))
    table = pl.BlockSpec((tokens, LANES), lambda g, f: (0, 0))
    pair = pl.BlockSpec((2, 1, tokens, LANES), lambda g, f: (0, g, 0, 0))
    return pl.pallas_call(
        attend_back_kernel,
        grid_spec=pltpu.PrefetchScalarGridSpec(
            num_scalar_prefetch=1,
            grid=(heads_here,),
            in_specs=[
                pl.BlockSpec((GROUP, tokens, LANES), lambda g, f: (first + g, 0, 0)),
                pl.BlockSpec((GROUP, tokens, LANES), lambda g, f: (g, 0, 0)),
                pl.BlockSpec(key_marks.shape, lambda g, f: (0, 0)),
                piece,
                piece,
                piece,
                piece,
                whole,
                whole,
                table,
                table,
            ],
            out_specs=[whole, pair, pair],
            scratch_shapes=[
                pltpu.VMEM((blocks, tokens, 2 * LANES), bf16),
                pltpu.VMEM((blocks, LANES, tokens), f32),
                pltpu.VMEM((2, rows, 2 * LANES), bf16),
                pltpu.VMEM((2, rows, 2 * LANES), bf16),
                pltpu.VMEM((2, LANES, rows), bf16),
                pltpu.VMEM((2, rows, LANES), f32),
                pltpu.VMEM((rows, tokens), bf16),
                pltpu.VMEM((rows, tokens), bf16),
            ],
        ),
        out_shape=[
            jax.ShapeDtypeStruct((tokens, width), bf16),
            jax.ShapeDtypeStruct((2, heads_here, tokens, LANES), bf16),
            jax.ShapeDtypeStruct((2, heads_here, tokens, LANES), bf16),
        ],
        compiler_params=params(48),
        cost_estimate=cost(4e10, 1e6),
        name="attend_back",
    )(f, q, marks, key_marks, *pieces, grad, attended, cos, sin)


EPS = 1e-05
ANY = pl.BlockSpec(memory_space=pl.ANY)


def params(mib):
    return pltpu.CompilerParams(vmem_limit_bytes=mib * MIB)


def cost(flops, moved):
    return pl.CostEstimate(flops=int(flops), bytes_accessed=int(moved), transcendentals=0)


def row_copies(f, pieces, target, sems):
    rows = pieces[0].shape[0]
    return [
        pltpu.make_async_copy(
            piece, target.at[pl.ds(pl.multiple_of((f ^ m) * rows, 16), rows), :], sems.at[m]
        )
        for m, piece in enumerate(pieces)
    ]


def tile_copies(info, bit, t, pieces, target, sems):
    own, near, far_mine, far_other, last_mine, last_other = pieces
    f = info[0]
    rows, width = own.shape[0], target.shape[2]
    chip = (f >> 1) ^ t

    def copy(source, m):
        at = pl.ds(pl.multiple_of((f ^ m) * rows, 16), rows)
        return lambda: pltpu.make_async_copy(source, target.at[t, at, :], sems.at[t, m])

    columns = pl.ds(pl.multiple_of(chip * width, width), width)
    mine = chip == info[bit]
    return [
        (None, copy(own.at[:, columns], 0)),
        (None, copy(near.at[:, columns], 1)),
        (mine, copy(far_mine, 2)),
        (~mine, copy(far_other, 2)),
        (mine, copy(last_mine, 3)),
        (~mine, copy(last_other, 3)),
    ]


def start_tile(copies):
    for condition, copy in copies:
        if condition is None:
            copy().start()
        else:
            pl.when(condition)(lambda copy=copy: copy().start())


def wait_tile(copies):
    for k in (0, 1, 2, 4):
        copies[k][1]().wait()


def down_copies(info, bit, t, pieces, target, sems):
    f = info[0]
    width = pieces[0].shape[1]
    copies = []
    for m in (2 * t, 2 * t + 1):
        columns = pl.ds(pl.multiple_of(((f ^ m) & 1) * width, width), width)
        if t == 0:
            copies.append(pltpu.make_async_copy(pieces[m], target.at[t, :, columns], sems.at[m, 0]))
            continue
        for k in (0, 1):
            source = pieces[2 + 2 * (m - 2) + k]
            rows = source.shape[0]
            at = pl.ds(pl.multiple_of((info[bit] ^ k) * rows, 16), rows)
            copies.append(pltpu.make_async_copy(source, target.at[t, at, columns], sems.at[m, k]))
    return copies


def start(copies):
    for copy in copies:
        copy.start()


def wait(copies):
    for copy in copies:
        copy.wait()


def inverse_of(values):
    return lax.rsqrt(jnp.mean(values * values, axis=-1, keepdims=True) + EPS)


def norm_back(upstream, values, gain):
    inverse = inverse_of(values)
    scaled = upstream * gain
    gain_grad = jnp.sum(upstream * (values * inverse), axis=0, keepdims=True)
    middle = jnp.mean(scaled * values, axis=-1, keepdims=True)
    return inverse * scaled - (inverse * inverse * inverse * middle) * values, gain_grad


def join_kernel(first, second, out, turned):
    half = out.shape[0] // 2
    turned[:, :half] = first[...]
    turned[:, half:] = second[...]
    out[:half, :] = first[...].T
    out[half:, :] = second[...].T


def join(turned, came):
    width, half = came.shape
    spec = pl.BlockSpec((width, half), lambda i: (0, 0))
    return pl.pallas_call(
        join_kernel,
        grid=(1,),
        in_specs=[spec, spec],
        out_specs=[
            pl.BlockSpec((2 * half, width), lambda i: (0, 0)),
            pl.BlockSpec((width, 2 * half), lambda i: (0, 0)),
        ],
        out_shape=[
            jax.ShapeDtypeStruct((2 * half, width), bf16),
            jax.ShapeDtypeStruct((width, 2 * half), bf16),
        ],
        compiler_params=params(16),
        cost_estimate=cost(4e10, 1e6),
        name="join",
    )(turned, came)


def part_kernel(rows, first, second):
    half = rows.shape[0] // 2
    first[...] = rows[:half, :].T
    second[...] = rows[half:, :].T


def part(rows):
    tokens, width = rows.shape
    half = tokens // 2
    spec = pl.BlockSpec((width, half), lambda i: (0, 0))
    return pl.pallas_call(
        part_kernel,
        grid=(1,),
        in_specs=[pl.BlockSpec((tokens, width), lambda i: (0, 0))],
        out_specs=[spec, spec],
        out_shape=[jax.ShapeDtypeStruct((width, half), bf16)] * 2,
        compiler_params=params(16),
        cost_estimate=cost(4e10, 1e6),
        name="part",
    )(rows)


def pack_kernel(key_t, value_t, query, out):
    rows = []
    for g in range(KV_HEADS):
        rows += [key_t[g * HEAD : (g + 1) * HEAD, :], value_t[g * HEAD : (g + 1) * HEAD, :]]
    width = 2 * KV_HEADS * HEAD
    out[:, :width] = jnp.concatenate(rows, axis=0).T
    out[:, width : width + HEADS * HEAD] = query[...]
    out[:, width + HEADS * HEAD :] = jnp.zeros((out.shape[0], HEAD), bf16)


def pack(key, value, query):
    rows = key.shape[0]
    width = (2 * KV_HEADS + HEADS + 1) * HEAD
    full = lambda *shape: pl.BlockSpec(shape, lambda i: (0, 0))
    return pl.pallas_call(
        pack_kernel,
        grid=(1,),
        in_specs=[full(KV_HEADS * HEAD, rows)] * 2 + [full(*query.shape)],
        out_specs=full(rows, width),
        out_shape=jax.ShapeDtypeStruct((rows, width), bf16),
        compiler_params=params(16),
        cost_estimate=cost(4e10, 1e6),
        name="pack",
    )(key.T, value.T, query)


GROUPS = ((4, 1), (0, 2), (2, 2))
ORDER = (1, 2, 0)


def project_kernel(f_ref, h, gain, cos_ref, sin_ref, own, near, far, last, normed_t, q_out, *refs):
    kv_out, (w, sems) = refs[: len(GROUPS)], refs[len(GROUPS) :]
    copies = row_copies(f_ref[0], (own, near, far, last), w, sems)
    start(copies)
    hidden = h[...].astype(f32)
    normed = (hidden * inverse_of(hidden) * gain[...]).astype(bf16)
    normed_t[...] = normed.T
    cos, sin = cos_ref[...], sin_ref[...]
    lane = lane_index(cos.shape)
    kv_cos, kv_sin = jnp.where(lane < HEAD, cos, 1.0), jnp.where(lane < HEAD, sin, 0.0)
    wait(copies)
    first = KV_HEADS * LANES
    both = nn(normed, w[:, :first])
    for (start_head, heads_here), out in zip(GROUPS, kv_out):
        for i in range(heads_here):
            g = start_head + i
            tile = both[:, g * LANES : (g + 1) * LANES]
            out[i] = (tile * kv_cos + swap_halves(tile) * kv_sin).astype(bf16)
    query = nn(normed, w[:, first:])
    for p in range((HEADS + 1) // 2):
        tile = query[:, p * LANES : (p + 1) * LANES]
        tile = (tile * cos + swap_halves(tile) * sin) * (HEAD ** (-0.5) * LOG2E)
        q_out[2 * p] = jnp.where(lane < HEAD, tile, 0.0).astype(bf16)
        if 2 * p + 1 < HEADS:
            q_out[2 * p + 1] = jnp.where(lane < HEAD, pltpu.roll(tile, HEAD, 1), 0.0).astype(bf16)


def project(f, hidden, gain, cos, sin, pieces):
    tokens, width = hidden.shape
    rows, columns = pieces[0].shape
    full = lambda *shape: pl.BlockSpec(shape, lambda i, f: (0,) * len(shape))
    like = jax.ShapeDtypeStruct
    return pl.pallas_call(
        project_kernel,
        grid_spec=pltpu.PrefetchScalarGridSpec(
            num_scalar_prefetch=1,
            grid=(1,),
            in_specs=[full(tokens, width), full(1, width), full(*cos.shape), full(*sin.shape)] + [ANY] * 4,
            out_specs=[full(width, tokens), full(HEADS, tokens, LANES)]
            + [full(heads_here, tokens, LANES) for _, heads_here in GROUPS],
            scratch_shapes=[pltpu.VMEM((4 * rows, columns), bf16), pltpu.SemaphoreType.DMA((4,))],
        ),
        out_shape=[like((width, tokens), bf16), like((HEADS, tokens, LANES), bf16)]
        + [like((heads_here, tokens, LANES), bf16) for _, heads_here in GROUPS],
        compiler_params=params(40),
        cost_estimate=cost(4e10, 1e6),
        name="project",
    )(f, hidden, gain, cos, sin, *pieces)


PARTS = len(GROUPS)


def split_pieces(refs):
    return refs[:4], refs[4:10], refs[10:16], refs[16:22], refs[22:]


CHUNK = 256


def feed_kernel(f_ref, h, *refs):
    attended, gain = refs[:PARTS], refs[PARTS]
    o, gate, up, down, refs = split_pieces(refs[PARTS + 1 :])
    outs, result = refs[:6], refs[6]
    w_o, w_gate, w_up, w_down, n16, acc, *refs = refs[7:]
    after, attended_t, normed_t, gate_out, up_out, hidden_out = refs[:6]
    o_sem, gate_sem, up_sem, down_sem, out_sem = refs[6:]
    f = f_ref[0]
    tiles, depth, wide = w_gate.shape[0], 4 * o[0].shape[0], w_gate.shape[2]

    def leave(k, tile=0):
        source, target = refs[k], outs[k]
        if len(source.shape) == 3:
            source, target = source.at[tile], target.at[tile]
        return pltpu.make_async_copy(source, target, out_sem.at[k, tile])

    bring = [
        lambda: start_tile(tile_copies(f_ref, 2, 0, up, w_up, up_sem)),
        lambda: start(down_copies(f_ref, 1, 0, down, w_down, down_sem)),
        lambda: start_tile(tile_copies(f_ref, 1, 1, gate, w_gate, gate_sem)),
        lambda: start_tile(tile_copies(f_ref, 2, 1, up, w_up, up_sem)),
        lambda: start(down_copies(f_ref, 1, 1, down, w_down, down_sem)),
    ]
    start(row_copies(f, o, w_o, o_sem))
    start_tile(tile_copies(f_ref, 1, 0, gate, w_gate, gate_sem))
    att = jnp.concatenate([attended[i][...] for i in ORDER], axis=1)
    attended_t[...] = att.T
    leave(1).start()
    w_o[depth:, :] = jnp.zeros((w_o.shape[0] - depth, w_o.shape[1]), bf16)
    wait(row_copies(f, o, w_o, o_sem))
    bring.pop(0)()
    value = h[...].astype(f32) + nn(att, w_o[...])
    after[...] = value
    normed = (value * inverse_of(value) * gain[...]).astype(bf16)
    n16[...] = normed
    normed_t[...] = normed.T
    for t in range(tiles):
        wait_tile(tile_copies(f_ref, 1, t, gate, w_gate, gate_sem))
        if t == 0:
            bring.pop(0)()
        wait_tile(tile_copies(f_ref, 2, t, up, w_up, up_sem))
        for at in range(0, wide, CHUNK):
            columns = slice(at, at + CHUNK)
            gate_act = nn(n16[...], w_gate[t, :, columns])
            up_act = nn(n16[...], w_up[t, :, columns])
            hidden = gate_act * jax.nn.sigmoid(gate_act) * up_act
            gate_out[t, :, columns] = gate_act.astype(bf16)
            up_out[t, :, columns] = up_act.astype(bf16)
            hidden_out[t, :, columns] = hidden.astype(bf16)
            if bring and at < 2 * CHUNK:
                bring.pop(0)()
        if t == 0:
            leave(0).start()
            leave(2).start()
        for k in (3, 4, 5):
            leave(k, t).start()
        wait(down_copies(f_ref, 1, t, down, w_down, down_sem))
        if bring:
            bring.pop(0)()
        part = nt(hidden_out[t], w_down[t])
        acc[...] = part if t == 0 else acc[...] + part
    result[...] = (after[...] + acc[...]).astype(result.dtype)
    for k in (0, 1, 2):
        leave(k).wait()
    for t in range(tiles):
        for k in (3, 4, 5):
            leave(k, t).wait()


def weight_scratch(o, gate):
    rows, width = o.shape
    columns = gate.shape[1]
    return [
        pltpu.VMEM((4 * rows + HEAD, width), bf16),
        pltpu.VMEM((2, 4 * rows, columns // 2), bf16),
        pltpu.VMEM((2, 4 * rows, columns // 2), bf16),
        pltpu.VMEM((2, width, columns // 2), bf16),
    ]


def weight_sems():
    dma = pltpu.SemaphoreType.DMA
    return [dma((4,)), dma((2, 4)), dma((2, 4)), dma((4, 2))]


def feed(f, hidden, attended, gain, o, gate, up, down, result_type):
    tokens, width = hidden.shape
    wide = gate[0].shape[1] // 2
    lanes = (HEADS + 1) * HEAD
    full = lambda *shape: pl.BlockSpec(shape, lambda i, f: (0,) * len(shape))
    like = jax.ShapeDtypeStruct
    kept = [((tokens, width), f32), ((lanes, tokens), bf16), ((width, tokens), bf16)] + [((2, tokens, wide), bf16)] * 3
    return pl.pallas_call(
        feed_kernel,
        grid_spec=pltpu.PrefetchScalarGridSpec(
            num_scalar_prefetch=1,
            grid=(1,),
            in_specs=[full(tokens, width)] + [full(*a.shape) for a in attended] + [full(1, width)] + [ANY] * 22,
            out_specs=[ANY] * 6 + [full(tokens, width)],
            scratch_shapes=weight_scratch(o[0], gate[0])
            + [pltpu.VMEM((tokens, width), bf16), pltpu.VMEM((tokens, width), f32)]
            + [pltpu.VMEM(*k) for k in kept]
            + weight_sems()
            + [pltpu.SemaphoreType.DMA((6, 2))],
        ),
        out_shape=[like(*k) for k in kept] + [like((tokens, width), result_type)],
        compiler_params=params(56),
        cost_estimate=cost(4e10, 1e6),
        name="feed",
    )(f, hidden, *attended, gain, *o, *gate, *up, *down)


def feed_back_kernel(f_ref, g, gain, *refs):
    held = refs[:3]
    o, gate, up, down, refs = split_pieces(refs[3:])
    outs, grad_after, branch_out = refs[:2], refs[2], refs[3]
    grad_attended, gain_grad = refs[4 : 4 + PARTS], refs[4 + PARTS]
    w_o, w_gate, w_up, w_down, g16, acc, *refs = refs[5 + PARTS :]
    after, gate_act, up_act, grad_gate, grad_up, o_sem, gate_sem, up_sem, down_sem, in_sem, out_sem = refs
    f = f_ref[0]
    tiles, depth, wide = w_gate.shape[0], 4 * o[0].shape[0], w_gate.shape[2]

    def arrive(k, tile=0):
        source, target = held[k], refs[k]
        if k:
            source, target = source.at[tile], target.at[tile]
        return pltpu.make_async_copy(source, target, in_sem.at[k, tile])

    def leave(k, tile):
        return pltpu.make_async_copy(refs[3 + k].at[tile], outs[k].at[tile], out_sem.at[k, tile])

    def bring_first(t):
        start(down_copies(f_ref, 1, t, down, w_down, down_sem))
        arrive(1, t).start()
        arrive(2, t).start()

    bring_first(0)
    g16[...] = g[...].astype(bf16)
    w_o[depth:, :] = jnp.zeros((w_o.shape[0] - depth, w_o.shape[1]), bf16)
    for t in range(tiles):
        wait(down_copies(f_ref, 1, t, down, w_down, down_sem))
        arrive(1, t).wait()
        arrive(2, t).wait()
        start_tile(tile_copies(f_ref, 1, t, gate, w_gate, gate_sem))
        for at in range(0, wide, CHUNK):
            columns = slice(at, at + CHUNK)
            grad_hidden = nn(g16[...], w_down[t, :, columns])
            value = gate_act[t, :, columns].astype(f32)
            logistic = jax.nn.sigmoid(value)
            steep = logistic * (1.0 + value * (1.0 - logistic))
            grad_gate[t, :, columns] = (grad_hidden * up_act[t, :, columns].astype(f32) * steep).astype(bf16)
            grad_up[t, :, columns] = (grad_hidden * (value * logistic)).astype(bf16)
            if at == CHUNK:
                start_tile(tile_copies(f_ref, 2, t, up, w_up, up_sem))
        leave(0, t).start()
        leave(1, t).start()
        wait_tile(tile_copies(f_ref, 1, t, gate, w_gate, gate_sem))
        part = nt(grad_gate[t], w_gate[t])
        acc[...] = part if t == 0 else acc[...] + part
        wait_tile(tile_copies(f_ref, 2, t, up, w_up, up_sem))
        if t + 1 < tiles:
            bring_first(t + 1)
        else:
            arrive(0).start()
            start(row_copies(f, o, w_o, o_sem))
        part = nt(grad_up[t], w_up[t])
        acc[...] += part
    arrive(0).wait()
    wait(row_copies(f, o, w_o, o_sem))
    back, gain_part = norm_back(acc[...], after[...], gain[...])
    back = back + g[...].astype(f32)
    gain_grad[...] = gain_part
    grad_after[...] = back
    branch = back.astype(bf16)
    branch_out[...] = branch
    whole = nt(branch, w_o[...]).astype(bf16)
    at = 0
    for i in ORDER:
        lanes = grad_attended[i].shape[1]
        grad_attended[i][...] = whole[:, at : at + lanes]
        at += lanes
    for t in range(tiles):
        leave(0, t).wait()
        leave(1, t).wait()


def feed_back(f, g, after, gain, gate_act, up_act, o, gate, up, down):
    tokens, width = after.shape
    wide = gate[0].shape[1] // 2
    full = lambda *shape: pl.BlockSpec(shape, lambda i, f: (0,) * len(shape))
    like = jax.ShapeDtypeStruct
    lanes = [pair_lanes(heads_here) for _, heads_here in GROUPS]
    tile = (2, tokens, wide)
    dma = pltpu.SemaphoreType.DMA
    return pl.pallas_call(
        feed_back_kernel,
        grid_spec=pltpu.PrefetchScalarGridSpec(
            num_scalar_prefetch=1,
            grid=(1,),
            in_specs=[full(tokens, width), full(1, width)] + [ANY] * 25,
            out_specs=[ANY, ANY, full(tokens, width), full(tokens, width)]
            + [full(tokens, n) for n in lanes]
            + [full(1, width)],
            scratch_shapes=weight_scratch(o[0], gate[0])
            + [pltpu.VMEM((tokens, width), bf16), pltpu.VMEM((tokens, width), f32)]
            + [pltpu.VMEM((tokens, width), f32)]
            + [pltpu.VMEM(tile, bf16)] * 4
            + weight_sems()
            + [dma((3, 2)), dma((2, 2))],
        ),
        out_shape=[like(tile, bf16), like(tile, bf16), like((tokens, width), f32), like((tokens, width), bf16)]
        + [like((tokens, n), bf16) for n in lanes]
        + [like((1, width), f32)],
        compiler_params=params(56),
        cost_estimate=cost(4e10, 1e6),
        name="feed_back",
    )(f, g, gain, after, gate_act, up_act, *o, *gate, *up, *down)


def project_back_kernel(f_ref, *refs):
    grad_q, kept, came = refs[:PARTS], refs[PARTS : 2 * PARTS], refs[2 * PARTS : 3 * PARTS]
    cos_ref, sin_ref, h, gain, grad_after, own, near, far, last = refs[3 * PARTS : 3 * PARTS + 9]
    grads, grad_in, turned, gain_grad, w, sems = refs[3 * PARTS + 9 :]
    copies = row_copies(f_ref[0], (own, near, far, last), w, sems)
    start(copies)
    cos, sin = cos_ref[...], sin_ref[...]
    lane = lane_index(cos.shape)
    cos, sin = jnp.where(lane < HEAD, cos, 1.0), jnp.where(lane < HEAD, sin, 0.0)
    at = KV_HEADS * LANES
    for k in ORDER:
        first, heads_here = GROUPS[k]
        for i in range(heads_here):
            g = first + i
            tile = kept[k][i].astype(f32) + came[k][i].astype(f32)
            tile = tile * cos - swap_halves(tile) * sin
            grads[:, g * LANES : (g + 1) * LANES] = tile.astype(bf16)
        lanes = grad_q[k].shape[1]
        grads[:, at : at + lanes] = grad_q[k][...]
        at += lanes
    wait(copies)
    grad_normed = nt(grads[...], w[...])
    back, gain_part = norm_back(grad_normed, h[...].astype(f32), gain[...])
    gain_grad[...] = gain_part
    back = back + grad_after[...]
    grad_in[...] = back.astype(grad_in.dtype)
    turned[...] = back.astype(bf16).T


def project_back(f, grad_q, kept, came, cos, sin, hidden, gain, grad_after, pieces, result_type):
    tokens, width = hidden.shape
    rows, columns = pieces[0].shape
    full = lambda *shape: pl.BlockSpec(shape, lambda i, f: (0,) * len(shape))
    like = jax.ShapeDtypeStruct
    arrays = (*grad_q, *kept, *came, cos, sin, hidden, gain, grad_after)
    return pl.pallas_call(
        project_back_kernel,
        grid_spec=pltpu.PrefetchScalarGridSpec(
            num_scalar_prefetch=1,
            grid=(1,),
            in_specs=[full(*a.shape) for a in arrays] + [ANY] * 4,
            out_specs=[full(tokens, columns), full(tokens, width), full(width, tokens), full(1, width)],
            scratch_shapes=[pltpu.VMEM((4 * rows, columns), bf16), pltpu.SemaphoreType.DMA((4,))],
        ),
        out_shape=[
            like((tokens, columns), bf16),
            like((tokens, width), result_type),
            like((width, tokens), bf16),
            like((1, width), f32),
        ],
        compiler_params=params(40),
        cost_estimate=cost(4e10, 1e6),
        name="project_back",
    )(f, *arrays, *pieces)


def outer_tiles_kernel(f_ref, *refs, rows):
    left_first, left_second, right_first, right_second, keep, send, acc = refs
    left = jnp.concatenate([left_first[...], left_second[...]], axis=1)
    acc[...] = nn(left, jnp.concatenate([right_first[0], right_second[0]], axis=0))
    half = acc.shape[1] // 2
    for m in range(4):
        out = send if m % 2 else keep
        from_row = pl.multiple_of((f_ref[0] ^ m) * rows, 16)
        for c in (0, 1):
            out[m // 2, c] = acc[pl.ds(from_row, rows), c * half : (c + 1) * half].astype(bf16)


def outer_tiles(f, lefts, rights, rows, name):
    width, tokens = lefts[0].shape
    wide = rights[0].shape[2]
    left = pl.BlockSpec((width, tokens), lambda i, f: (0, 0))
    right = pl.BlockSpec((1, tokens, wide), lambda i, f: (i, 0, 0))
    out = pl.BlockSpec((2, 2, rows, wide // 2), lambda i, f: (0, (f[0] >> 1) ^ i, 0, 0))
    return pl.pallas_call(
        functools.partial(outer_tiles_kernel, rows=rows),
        grid_spec=pltpu.PrefetchScalarGridSpec(
            num_scalar_prefetch=1,
            grid=(2,),
            in_specs=[left, left, right, right],
            out_specs=[out, out],
            scratch_shapes=[pltpu.VMEM((width, wide), f32)],
        ),
        out_shape=[jax.ShapeDtypeStruct((2, 4, rows, wide // 2), bf16)] * 2,
        compiler_params=params(48),
        cost_estimate=cost(4e10, 1e6),
        name=name,
    )(f, *lefts, *rights)


def outer_down_kernel(f_ref, left_first, left_second, right_first, right_second, keep, send):
    left = jnp.concatenate([left_first[...], left_second[...]], axis=1)
    value = nn(left, jnp.concatenate([right_first[0], right_second[0]], axis=0))
    half = value.shape[1] // 2
    own = (f_ref[0] & 1) == 0
    lower, upper = value[:, :half], value[:, half:]
    keep[0, 0] = jnp.where(own, lower, upper).astype(bf16)
    send[0, 0] = jnp.where(own, upper, lower).astype(bf16)


def outer_down(f, lefts, rights, name):
    width, tokens = lefts[0].shape
    wide = rights[0].shape[2]
    left = pl.BlockSpec((width, tokens), lambda i, f: (0, 0))
    right = pl.BlockSpec((1, tokens, wide), lambda i, f: (i, 0, 0))
    out = pl.BlockSpec((1, 1, width, wide // 2), lambda i, f: (i, 0, 0, 0))
    return pl.pallas_call(
        outer_down_kernel,
        grid_spec=pltpu.PrefetchScalarGridSpec(
            num_scalar_prefetch=1,
            grid=(2,),
            in_specs=[left, left, right, right],
            out_specs=[out, out],
        ),
        out_shape=[jax.ShapeDtypeStruct((2, 1, width, wide // 2), bf16)] * 2,
        compiler_params=params(48),
        cost_estimate=cost(4e10, 1e6),
        name=name,
    )(f, *lefts, *rights)


def outer_kernel(f_ref, left_first, left_second, right_first, right_second, extra, keep, send, acc, *, rows):
    left = jnp.concatenate([left_first[...], left_second[...]], axis=1)
    acc[...] = nn(left, jnp.concatenate([right_first[...], right_second[...]], axis=0))
    spare = keep.shape[2] - rows
    for m in range(4):
        out = send if m % 2 else keep
        device = f_ref[0] ^ m
        out[m // 2, 0, :rows] = acc[pl.ds(pl.multiple_of(device * rows, 16), rows), :].astype(bf16)
        out[m // 2, 0, rows:] = jnp.zeros((spare, acc.shape[1]), bf16)
        out[m // 2, 0, rows:, : extra.shape[2]] = extra[device]


def outer(f, lefts, rights, extra, rows, name):
    width, tokens = lefts[0].shape
    columns = rights[0].shape[1]
    padded = rows + extra.shape[1]
    full = lambda *shape: pl.BlockSpec(shape, lambda i, f: (0,) * len(shape))
    height = width if width % (4 * rows) == 0 else width
    return pl.pallas_call(
        functools.partial(outer_kernel, rows=rows),
        grid_spec=pltpu.PrefetchScalarGridSpec(
            num_scalar_prefetch=1,
            grid=(1,),
            in_specs=[full(width, tokens)] * 2 + [full(tokens, columns)] * 2 + [full(*extra.shape)],
            out_specs=[full(2, 1, padded, columns)] * 2,
            scratch_shapes=[pltpu.VMEM((height, columns), f32)],
        ),
        out_shape=[jax.ShapeDtypeStruct((2, 1, padded, columns), bf16)] * 2,
        compiler_params=params(48),
        cost_estimate=cost(4e10, 1e6),
        name=name,
    )(f, *lefts, *rights, extra)


def unpack_kernel(total, key_t, value_t, query):
    rows = query.shape[0]
    width = 2 * KV_HEADS * HEAD
    turned = total[:rows, :width].astype(f32).T
    for g in range(KV_HEADS):
        key_t[g * HEAD : (g + 1) * HEAD, :] = turned[2 * g * HEAD : (2 * g + 1) * HEAD, :]
        value_t[g * HEAD : (g + 1) * HEAD, :] = turned[(2 * g + 1) * HEAD : (2 * g + 2) * HEAD, :]
    query[...] = total[:rows, width : width + HEADS * HEAD].astype(f32)


def unpack(total, rows):
    full = lambda *shape: pl.BlockSpec(shape, lambda i: (0, 0))
    like = jax.ShapeDtypeStruct
    side = (KV_HEADS * HEAD, rows)
    key_t, value_t, query = pl.pallas_call(
        unpack_kernel,
        grid=(1,),
        in_specs=[full(*total.shape)],
        out_specs=[full(*side), full(*side), full(rows, HEADS * HEAD)],
        out_shape=[like(side, f32), like(side, f32), like((rows, HEADS * HEAD), f32)],
        compiler_params=params(16),
        cost_estimate=cost(4e10, 1e6),
        name="unpack",
    )(total)
    return key_t.T, value_t.T, query


def flip(array, axis, bit):
    size = lax.axis_size(axis)
    return lax.ppermute(array, axis, [(i, i ^ bit) for i in range(size)])


def add(left, right):
    return left.astype(f32) + right.astype(f32)


def levels_of(size):
    bits = size.bit_length() - 1
    levels = [(0, 2)] if bits else []
    at = 1
    while at < bits:
        step = min(2, bits - at)
        levels.append((at, 1 << step))
        at += step
    return levels


def cut(array, count):
    blocks, rows, columns = array.shape
    outer = next(n for n in (4, 2, 1) if n <= count and blocks % n == 0)
    inner = count // outer
    array = array.reshape(outer, blocks // outer, inner, rows // inner, columns)
    return [array[i // inner, :, i % inner] for i in range(count)]


def glue(parts, shape):
    count = len(parts)
    outer = next(n for n in (4, 2, 1) if n <= count and shape[0] % n == 0)
    inner = count // outer
    rows = [jnp.concatenate(parts[i * inner : (i + 1) * inner], axis=1) for i in range(outer)]
    return jnp.concatenate(rows, axis=0).reshape(shape)


def pick(parts, index):
    while len(parts) > 1:
        odd = index % 2 == 1
        parts = [jnp.where(odd, parts[i + 1], parts[i]) for i in range(0, len(parts), 2)]
        index = index // 2
    return parts[0]


def reduction(keep, send, halves):
    shape = keep.shape[1:]
    (near,) = yield [(send, "fsdp", 1)]
    far = [add(k, n).astype(bf16) for k, n in zip(cut(keep[1], halves), cut(near[1], halves))]
    came = []
    for piece in far:
        came += yield [(piece, "fsdp", 2)]
    came = glue(came, shape) if halves > 1 else came[0]
    part = add(keep[0], near[0]) + came.astype(f32)
    index = lax.axis_index("dp")
    shapes = []
    for bit, count in levels_of(lax.axis_size("dp")):
        shapes.append(part.shape)
        parts = cut(part, count)
        mine = (index >> bit) % count
        came = yield [(pick(parts, mine ^ j).astype(bf16), "dp", j << bit) for j in range(1, count)]
        part = pick(parts, mine).astype(f32)
        for other in came:
            part = part + other.astype(f32)
    part = part.astype(bf16)
    for (bit, count), wide in zip(reversed(levels_of(lax.axis_size("dp"))), reversed(shapes)):
        came = yield [(part, "dp", j << bit) for j in range(1, count)]
        mine = (index >> bit) % count
        held = [part] + came
        part = glue([pick(held, mine ^ p) for p in range(count)], wide)
    return part


class Unit:
    def __init__(self, keep, send, halves=1):
        self.steps = reduction(keep, send, halves)
        self.asks = next(self.steps)
        self.total = None

    def take(self, came):
        try:
            self.asks = self.steps.send(came)
        except StopIteration as end:
            self.asks, self.total = [], end.value


class Clock:
    def __init__(self, f):
        self.f = f
        self.before = []

    def phase(self, moves=(), work=None, units=(), extra=()):
        asks = list(moves)
        for unit in units:
            asks += unit.asks
        gated = lax.optimization_barrier((self.f, *(a[0] for a in asks), *extra, *self.before))
        came = [flip(g, axis, bit) for g, (_, axis, bit) in zip(gated[1:], asks)]
        done = None if work is None else work(gated[0])
        self.before = list(came) + ([] if done is None else [jax.tree.leaves(done)[0]])
        at = len(moves)
        for unit in units:
            count = len(unit.asks)
            unit.take(came[at : at + count])
            at += count
        return came[: len(moves)], done


def half_for(shard, low_first, dim):
    width = shard.shape[dim] // 2
    low = lax.slice_in_dim(shard, 0, width, axis=dim)
    high = lax.slice_in_dim(shard, width, 2 * width, axis=dim)
    return jnp.where(low_first, low, high)


def per_device(
    tokens, seq_cuts, w_query, w_key, w_value, w_output, w_gate, w_up, w_down, gain_attn, gain_ffn, cotangent
):
    rows, width = tokens.shape[1], tokens.shape[2]
    half = rows // 2
    index = lax.axis_index("fsdp")
    replica = lax.axis_index("dp")
    f = jnp.stack([index, replica % 2, replica // 2 % 2]).astype(jnp.int32)
    count = rows * lax.axis_size("fsdp")
    shard_rows = w_key.shape[0]
    core, y = ("fsdp", 1), ("fsdp", 2)
    side = (("dp", 1), ("dp", 2))

    bounds = seq_cuts[0]
    within = jnp.arange(half, dtype=jnp.int32)
    local = jnp.concatenate([2 * index * half + within, (7 - 2 * index) * half + within]).astype(jnp.int32)
    every = jnp.arange(count, dtype=jnp.int32)
    passed = local[:, None] >= bounds[None, :]
    docs = jnp.sum(passed.astype(jnp.int32), axis=1)
    positions = local - jnp.max(jnp.where(passed, bounds[None, :], 0), axis=1)
    key_docs = jnp.sum((every[:, None] >= bounds[None, :]).astype(jnp.int32), axis=1)
    lane = jnp.arange(LANES, dtype=jnp.int32)[None, :]
    one = ((lane == key_docs[:, None]) & (lane < 4)) | ((lane >= 8) & (lane < 11))
    key_marks = one.astype(bf16)
    q_marks = jnp.where((lane < 4) & (lane != docs[:, None]), NEGATIVE, 0.0).astype(bf16)
    frequency = jnp.power(10000.0, -2.0 * jnp.arange(HEAD // 2, dtype=f32) / HEAD)
    angle = positions.astype(f32)[:, None] * frequency[None, :]
    cosine, sine = jnp.cos(angle), jnp.sin(angle)
    cos = jnp.concatenate([cosine] * 4, axis=1)
    sin = jnp.concatenate([-sine, sine] * 2, axis=1)
    gain_a, gain_f = gain_attn[None, :], gain_ffn[None, :]

    clock = Clock(f)
    tokens_t, cotangent_t, down_t = tokens[0].T, cotangent[0].T, w_down.T
    shards = {"gate": w_gate, "up": w_up, "down": down_t}
    bit_of, dim_of = {"gate": 0, "up": 1, "down": 0}, {"gate": 1, "up": 1, "down": 0}
    across = lambda name: (half_for(shards[name], f[1 + bit_of[name]] == 0, dim_of[name]), *y)

    w_own = pack(w_key, w_value, w_query)
    (w_far, w_near, other_tokens), _ = clock.phase([(w_own, *y), (w_own, *core), (tokens_t[:, half:], "fsdp", 3)])
    (w_last, w_o_far), (h0, _) = clock.phase(
        [(w_far, *core), (w_output, *y)], lambda turn: join(tokens_t, other_tokens), extra=(key_marks, q_marks, cos, sin)
    )
    w_in = (w_own, w_near, w_far, w_last)

    def attend_phases(hidden, first, moves):
        came = []
        got, (normed_t, q, *parts) = clock.phase(first, lambda turn: project(turn, hidden, gain_a, cos, sin, w_in))
        came.append(got)
        a, b, c = parts
        got, _ = clock.phase([(a, *y), (a, *core), (b, *core)] + moves[0](came))
        a_far, a_near, b_near = got[:3]
        came.append(got[3:])
        got, _ = clock.phase([(a_far, *core), (b, *y), (c, *core)] + moves[1](came))
        a_last, b_far, c_near = got[:3]
        came.append(got[3:])
        gathered = [(a, a_near, a_far, a_last)]
        attended, marks = [], []

        def call(k):
            return lambda turn: attend(turn, q, q_marks, key_marks, gathered[k], GROUPS[k])

        got, (x, m) = clock.phase([(b_far, *core), (c, *y)] + moves[2](came), call(0))
        attended.append(x), marks.append(m)
        b_last, c_far = got[:2]
        came.append(got[2:])
        gathered.append((b, b_near, b_far, b_last))
        got, (x, m) = clock.phase([(c_far, *core)] + moves[3](came), call(1))
        attended.append(x), marks.append(m)
        came.append(got[1:])
        gathered.append((c, c_near, c_far, got[0]))
        got, (x, m) = clock.phase(moves[4](came), call(2))
        attended.append(x), marks.append(m)
        came.append(got)
        return (normed_t, q, gathered, attended, marks), came

    def feed_phase(hidden, weights, run, result_type):
        normed_t, q, gathered, attended, marks = run
        _, (after, attended_t, normed_ffn_t, gate_act, up_act, hidden_act, result) = clock.phase(
            (), lambda turn: feed(turn, hidden, attended, gain_f, *weights, result_type)
        )
        return result, (
            hidden, normed_t, q, gathered, attended, marks, after, attended_t, normed_ffn_t, gate_act, up_act, hidden_act,
        )

    none = lambda came: []
    run, came = attend_phases(
        h0,
        [across("gate")],
        (
            lambda came: [(w_o_far, *core)],
            lambda came: [(came[0][0], *side[0])],
            lambda came: [across("up")],
            lambda came: [across("down"), (came[3][0], *side[1])],
            lambda came: [(came[4][0], *side[0])] + [(shards[n], *core) for n in shards] + [(w_output, *core)],
        ),
    )
    fars = {"gate": (came[0][0], came[2][0]), "up": (came[3][0], came[4][1]), "down": (came[4][0], came[5][0])}
    nears = dict(zip(shards, came[5][1:4]))
    lasts, _ = clock.phase([(x, *core) for n in shards for x in fars[n]])
    lasts = {n: tuple(lasts[2 * i : 2 * i + 2]) for i, n in enumerate(shards)}
    o = (w_output, came[5][4], w_o_far, came[1][0])
    weights = (o,) + tuple((shards[n], nears[n], *fars[n], *lasts[n]) for n in ("gate", "up", "down"))
    h1, first = feed_phase(h0, weights, run, f32)

    run, came = attend_phases(h1, [], (none, none, none, lambda came: [(cotangent_t[:, half:], "fsdp", 3)], none))
    other_cotangent = came[4][0]
    h2, second = feed_phase(h1, weights, run, bf16)
    _, (cot, cot_turned) = clock.phase((), lambda turn: join(cotangent_t, other_cotangent))

    def feed_back_work(g, stored):
        return lambda turn: feed_back(turn, g, stored[6], gain_f, stored[9], stored[10], *weights)

    BACK = (1, 2, 0)

    def back_phases(grad_attended, stored, beside):
        q, gathered, attended, marks = stored[2], stored[3], stored[4], stored[5]
        grad_q, kept, far = [None] * PARTS, [None] * PARTS, [None] * PARTS
        extra = []

        def call(k):
            return lambda turn: attend_back(
                turn, q, marks[k], key_marks, gathered[k], grad_attended[k], attended[k], cos, sin, GROUPS[k]
            )

        def sums(k, keep, near):
            kept[k] = add(keep[0], near[0]).astype(bf16)
            return add(keep[1], near[1]).astype(bf16)

        b, c, a = BACK
        moves, units = beside(0)
        got, (grad_q[b], b_keep, b_send) = clock.phase(moves, call(b), units)
        extra += got
        moves, units = beside(1)
        got, (grad_q[c], c_keep, c_send) = clock.phase([(b_send, *core)] + moves, call(c), units)
        extra += got[1:]
        b_sum = sums(b, b_keep, got[0])
        moves, units = beside(2)
        got, (grad_q[a], a_keep, a_send) = clock.phase([(b_sum, *y), (c_send, *core)] + moves, call(a), units)
        far[b] = got[0]
        extra += got[2:]
        c_sum = sums(c, c_keep, got[1])
        moves, units = beside(3)
        got, _ = clock.phase([(c_sum, *y), (a_send, *core)] + moves, None, units)
        far[c] = got[0]
        extra += got[2:]
        a_sum = sums(a, a_keep, got[1])
        moves, units = beside(4)
        got, _ = clock.phase([(a_sum, *y)] + moves, None, units)
        far[a] = got[0]
        extra += got[1:]
        return (grad_q, kept, far), extra

    def project_back_work(parts, stored, grad_after, result_type):
        return lambda turn: project_back(
            turn, *parts, cos, sin, stored[0], gain_a, grad_after, w_in, result_type
        )

    _, fed2 = clock.phase((), feed_back_work(cot, second))
    out_first, out_second = part(h2)
    parts, extra = back_phases(
        fed2[4 : 4 + PARTS], second, lambda k: ([(out_second, "fsdp", 3)] if k == 0 else [], ())
    )
    output = jnp.concatenate([out_first, extra[0]], axis=1).T
    _, (grads2, middle, middle_turned, gain_a2) = clock.phase((), project_back_work(parts, second, fed2[2], f32))

    _, down_pair = clock.phase(
        (), lambda turn: outer_down(turn, (middle_turned, cot_turned), (first[11], second[11]), "outer_down")
    )
    down = Unit(*down_pair, 2)
    _, fed1 = clock.phase((), feed_back_work(middle, first), (down,))

    def outer_work(i, name):
        return lambda turn: outer_tiles(turn, (first[8], second[8]), (fed1[i], fed2[i]), shard_rows, name)

    nothing = jnp.zeros((4, 16, LANES), bf16)
    _, gate_pair = clock.phase((), outer_work(0, "outer_gate"), (down,))
    gate = Unit(*gate_pair, 2)
    _, up_pair = clock.phase((), outer_work(1, "outer_up"), (down, gate))
    up = Unit(*up_pair, 2)
    _, o_pair = clock.phase(
        (),
        lambda turn: outer(turn, (first[7], second[7]), (fed1[3], fed2[3]), nothing, shard_rows, "outer_o"),
        (down, up),
    )
    out = Unit(*o_pair)
    plan = ((gate, down, out), (gate, down), (down,), (), (gate,))
    parts, _ = back_phases(fed1[4 : 4 + PARTS], first, lambda k: ([], plan[k]))
    _, (grads1, grad_tokens, _, gain_a1) = clock.phase(
        (), project_back_work(parts, first, fed1[2], bf16), (up, gate)
    )
    gains = jnp.concatenate([gain_a1 + gain_a2, fed1[4 + PARTS] + fed2[4 + PARTS]], axis=0)
    gains = gains.reshape(2, 4, width // 4).transpose(1, 0, 2).astype(bf16)
    gains = jnp.pad(gains, ((0, 0), (0, 14), (0, 256 - width // 4)))
    _, in_pair = clock.phase(
        (),
        lambda turn: outer(turn, (first[1], second[1]), (grads1, grads2), gains, shard_rows, "outer_in"),
        (up, gate),
    )
    into = Unit(*in_pair)
    back_half, back_send = part(grad_tokens)
    clock.phase((), None, (into, gate, up))
    clock.phase((), None, (into, up))
    clock.phase((), None, (out, into, up))
    clock.phase((), None, (out, into, up))
    (other_tokens,), _ = clock.phase([(back_send, "fsdp", 3)], None, (out, into))
    grad_tokens = jnp.concatenate([back_half, other_tokens], axis=1).T
    units = (down, gate, up, out, into)
    while any(unit.asks for unit in units):
        clock.phase((), None, [unit for unit in units if unit.asks])

    grad_down = down.total[0].T.astype(f32)
    wide = lambda unit: jnp.concatenate([unit.total[i] for i in range(4)], axis=1).astype(f32)
    grad_gate, grad_up = wide(gate), wide(up)
    grad_o = out.total[0, :shard_rows].astype(f32)
    total = into.total[0]
    grad_key, grad_value, grad_query = unpack(total, shard_rows)
    gains = total[shard_rows : shard_rows + 2, : width // 4].astype(f32)
    return (
        output[None], grad_tokens[None], grad_query, grad_key, grad_value, grad_o, grad_gate, grad_up,
        grad_down, gains[0], gains[1],
    )


def solution(mesh):
    split, whole = P("fsdp", None), P("dp", "fsdp", None)
    return jax.shard_map(
        per_device,
        mesh=mesh,
        in_specs=(whole, P("dp", None)) + (split,) * 7 + (P(), P(), whole),
        out_specs=(whole, whole) + (split,) * 7 + (P("fsdp"), P("fsdp")),
        check_vma=False,
    )
```

time: 852 us -> 680 us (0.80)
  waiting for transfers between devices: 316 us -> 227 us
  Pallas kernels: 324 us -> 251 us
  starting transfers between devices: 68.3 us -> 96.1 us
  local copies, waits for them, and re-layouts: 82 us -> 56 us
    ppermute x74 -> x108, waiting for transfers between devices: 316 us -> 227 us  [flip(): return lax.ppermute(array, axis, [(i, i ^ bit) for i in range(size)])]
    pallas_call x2 -> x6, Pallas kernels: 103 us -> 67.1 us  [attend_back(): pl.pallas_call(attend_back_kernel, grid_spec=pltpu.PrefetchScalarGridSpec...]
    pallas_call x2 -> x6, Pallas kernels: 71.2 us -> 39.3 us  [attend(): pl.pallas_call(attend_kernel, grid_spec=pltpu.PrefetchScalarGridSpec(num_...]
    ppermute x74 -> x108, starting transfers between devices: 68.3 us -> 96.1 us  [flip(): return lax.ppermute(array, axis, [(i, i ^ bit) for i in range(size)])]
    add x29 -> x11, other arithmetic: 26.6 us -> 10.2 us  [the longest x5 5.68 us: reduction(): part = add(keep[0], near[0]) + came.astype(f32)]
    ppermute x5 -> x0, local copies, waits for them, and re-layouts: 14.4 us -> none  [flip(): return lax.ppermute(array, axis, [(i, i ^ bit) for i in range(size)])]
    convert_element_type x10 -> x31, other arithmetic: 10.1 us -> 22.4 us  [the longest x5 7.58 us: reduction(): add(k, n).astype(bf16)]
    convert_element_type x23 -> x2, local copies, waits for them, and re-layouts: 11.9 us -> 0.1 us  [per_device(): gains = gains.reshape(2, 4, width // 4).transpose(1, 0, 2).astype(bf16)]
  transfers between devices with their start and end apart: 74 -> 108, of which waited for: 31 -> 55; matrix products, arithmetic and copies ran while one was open for 12% -> 6% of each run, Pallas kernels for 9% -> 24%
where the time goes in v2:
time: 680 us; the launch traced here: 675 us
  Pallas kernels  251 us (37%)
  waiting for transfers between devices  227 us (33%)
  starting transfers between devices  96.1 us (14%)
  local copies, waits for them, and re-layouts  56 us (8%)
  other arithmetic  41.4 us (6%)
    ppermute x108, waiting for transfers between devices, flip(): return lax.ppermute(array, axis, [(i, i ^ bit) for i in range(size)])  227 us
    ppermute x108, starting transfers between devices, flip(): return lax.ppermute(array, axis, [(i, i ^ bit) for i in range(size)])  96.1 us
    pallas_call x6, Pallas kernels, attend_back(): pl.pallas_call(attend_back_kernel, grid_spec=pltpu.PrefetchScalarGridSpec...  67.1 us
    unnamed x394, local copies, waits for them, and re-layouts  49.4 us
    pallas_call x2, Pallas kernels, feed_back(): pl.pallas_call(feed_back_kernel, grid_spec=pltpu.PrefetchScalarGridSpec(n...  42 us
    pallas_call x6, Pallas kernels, attend(): pl.pallas_call(attend_kernel, grid_spec=pltpu.PrefetchScalarGridSpec(num_...  39.3 us
    pallas_call x2, Pallas kernels, feed(): pl.pallas_call(feed_kernel, grid_spec=pltpu.PrefetchScalarGridSpec(num_sc...  36.6 us
    pallas_call x2, Pallas kernels, outer_tiles(): pl.pallas_call(functools.partial(outer_tiles_kernel, rows=rows), grid_spe...  19.1 us
  transfers between devices with their start and end apart: 108, of which 55 were waited for; matrix products, arithmetic and copies ran while one was open for 6% of the time, Pallas kernels for 24%

profile of v2, /device:TPU:0, one launch (start us, length us, event | category | flops | bytes accessed | tf_op | source)
XLA Modules:
  0.0 675.0 jit_solution(1435610503411585164)
XLA Ops:
  11.3 25.0 %collective-permute-done.2.second = bf16[960,256]{1,0:T(8,128)(2,1)} collective-permute-done((bf16[960,256]{1,0:T(8,128)(2,1)}, bf16[960,256]{1,0:T(8,128)(2,1)}, u32[]{:S(2)}, u32[]{:S(2)}) %collective-permute-start.2) | collective-permute-done | bytes 491552 | tf_op jit(solution)/shard_map/ppermute | solution.py:953
  41.1 9.2 %collective-permute-done.4.refs_6_.refs_5_ = bf16[240,960]{1,0:T(8,128)(2,1)} collective-permute-done((bf16[240,960]{1,0:T(8,128)(2,1)S(1)}, bf16[240,960]{1,0:T(8,128)(2,1)}, u32[]{:S(2)}, u32[]{:S(2)}) %collective-permute-start.4) | collective-permute-done | bytes 460832 | tf_op jit(solution)/shard_map/ppermute | solution.py:953
  52.1 5.0 project.2
  59.4 5.9 collective-permute-done.5.refs_10_.refs_9_
  80.1 6.1 collective-permute-done.10.refs_11_.refs_10_
  88.3 5.1 attend.6
  94.8 10.6 %collective-permute-done.15.far = bf16[2,512,128]{2,1,0:T(8,128)(2,1)S(1)} collective-permute-done((bf16[2,512,128]{2,1,0:T(8,128)(2,1)S(1)}, bf16[2,512,128]{2,1,0:T(8,128)(2,1)S(1)}, u32[]{:S(2)}, u32[]{:S(2)}) %collective-permute-start.15) | collective-permute-done | bytes 262176 | tf_op jit(solution)/shard_map/ppermute | solution.py:953
  109.0 8.5 %attend.7 = (bf16[512,384]{1,0:T(8,128)(2,1)S(1)}, bf16[6,512,128]{2,1,0:T(8,128)(2,1)S(1)}) custom-call(s32[3]{0:T(128)S(1)} %pad_add_fusion.1.f_ref, bf16[15,512,128]{2,1,0:T(8,128)(2,1)S(1)} %copy-done.85, bf16[512,128]{1,0:T(8,128)(2,1)S(1)} %select_convert_fusion.14.q_marks, bf16[2048,128]{1,0:T(8,128)(2,1)S(1)} %fusion.2.key_marks, ...), custom_call_target="tpu_custom_call" | custom-call | flops 40000000000 | bytes 1000000 | tf_op jit(solution)/shard_map/attend/pallas_call | solution.py:154
  122.4 7.1 %attend.8 = (bf16[512,384]{1,0:T(8,128)(2,1)S(1)}, bf16[6,512,128]{2,1,0:T(8,128)(2,1)S(1)}) custom-call(s32[3]{0:T(128)S(1)} %pad_add_fusion.1.f_ref, bf16[15,512,128]{2,1,0:T(8,128)(2,1)S(1)} %copy-done.85, bf16[512,128]{1,0:T(8,128)(2,1)S(1)} %select_convert_fusion.14.q_marks, bf16[2048,128]{1,0:T(8,128)(2,1)S(1)} %fusion.2.key_marks, ...), custom_call_target="tpu_custom_call" | custom-call | flops 40000000000 | bytes 1000000 | tf_op jit(solution)/shard_map/attend/pallas_call | solution.py:154
  131.2 4.8 collective-permute-done.20.refs_23_.refs_22_
  143.7 18.4 %feed.2 = (f32[512,960]{1,0:T(8,128)}, bf16[1024,512]{1,0:T(8,128)(2,1)}, bf16[960,512]{1,0:T(8,128)(2,1)}, bf16[2,512,1280]{2,1,0:T(8,128)(2,1)}, bf16[2,512,12...) custom-call(s32[3]{0:T(128)} %copy-done.22, bf16[512,960]{1,0:T(8,128)(2,1)} %copy-done.93, ...), custom_call_target="tpu_custom_call" | custom-call | flops 40000000000 | bytes 1000000 | tf_op jit(solution)/shard_map/feed/pallas_call | solution.py:642
  163.7 4.4 project.3
  169.9 5.1 collective-permute-done.31.far
  177.4 5.5 collective-permute-done.34.far
  190.8 7.1 %attend.10 = (bf16[512,384]{1,0:T(8,128)(2,1)S(1)}, bf16[6,512,128]{2,1,0:T(8,128)(2,1)S(1)}) custom-call(s32[3]{0:T(128)S(1)} %copy-done.23, bf16[15,512,128]{2,1,0:T(8,128)(2,1)S(1)} %get-tuple-element.302.q, bf16[512,128]{1,0:T(8,128)(2,1)S(1)} %select_convert_fusion.14.q_marks, bf16[2048,128]{1,0:T(8,128)(2,1)S(1)} %fusion.2.key_marks, ...), custom_call_target="tpu_custom_call" | custom-call | flops 40000000000 | bytes 1000000 | tf_op jit(solution)/shard_map/attend/pallas_call | solution.py:154
  202.8 7.5 %attend.11 = (bf16[512,384]{1,0:T(8,128)(2,1)S(1)}, bf16[6,512,128]{2,1,0:T(8,128)(2,1)S(1)}) custom-call(s32[3]{0:T(128)S(1)} %copy-done.23, bf16[15,512,128]{2,1,0:T(8,128)(2,1)S(1)} %get-tuple-element.302.q, bf16[512,128]{1,0:T(8,128)(2,1)S(1)} %select_convert_fusion.14.q_marks, bf16[2048,128]{1,0:T(8,128)(2,1)S(1)} %fusion.2.key_marks, ...), custom_call_target="tpu_custom_call" | custom-call | flops 40000000000 | bytes 1000000 | tf_op jit(solution)/shard_map/attend/pallas_call | solution.py:154
  211.1 18.2 %feed.3 = (f32[512,960]{1,0:T(8,128)}, bf16[1024,512]{1,0:T(8,128)(2,1)}, bf16[960,512]{1,0:T(8,128)(2,1)}, bf16[2,512,1280]{2,1,0:T(8,128)(2,1)}, bf16[2,512,12...) custom-call(s32[3]{0:T(128)} %copy-done.22, f32[512,960]{1,0:T(8,128)} %get-tuple-element.288.h.refs_11_, ...), custom_call_target="tpu_custom_call" | custom-call | flops 40000000000 | bytes 1000000 | tf_op jit(solution)/shard_map/feed/pallas_call | solution.py:642
  233.1 20.9 %feed_back.2 = (bf16[2,512,1280]{2,1,0:T(8,128)(2,1)}, bf16[2,512,1280]{2,1,0:T(8,128)(2,1)}, f32[512,960]{1,0:T(8,128)}, bf16[512,960]{1,0:T(8,128)(2,1)}, bf16...) custom-call(s32[3]{0:T(128)} %copy-done.22, ...), custom_call_target="tpu_custom_call" | custom-call | flops 40000000000 | bytes 1000000 | tf_op jit(solution)/shard_map/feed_back/pallas_call | solution.py:744
  256.3 13.2 %attend_back.6 = (bf16[512,384]{1,0:T(8,128)(2,1)S(1)}, bf16[2,2,512,128]{3,2,1,0:T(8,128)(2,1)S(1)}, bf16[2,2,512,128]{3,2,1,0:T(8,128)(2,1)S(1)}) custom-call(s32[3]{0:T(128)S(1)} %copy-done.24, bf16[15,512,128]{2,1,0:T(8,128)(2,1)} %copy-done.82, bf16[6,512,128]{2,1,0:T(8,128)(2,1)S(1)} %copy-done.113, bf16[2048,128]{1,0:T(8,128)(2,1)S(1)} %fusion.2.key_marks, ...), custom_call_target="tpu_custom_call" | custom-call | flops 40000000000 | bytes 1000000 | tf_op jit(solution)/shard_map/attend_back/pallas_call | solution.py:272
  270.7 13.6 %attend_back.7 = (bf16[512,384]{1,0:T(8,128)(2,1)S(1)}, bf16[2,2,512,128]{3,2,1,0:T(8,128)(2,1)S(1)}, bf16[2,2,512,128]{3,2,1,0:T(8,128)(2,1)S(1)}) custom-call(s32[3]{0:T(128)S(1)} %copy-done.24, bf16[15,512,128]{2,1,0:T(8,128)(2,1)} %copy-done.82, bf16[6,512,128]{2,1,0:T(8,128)(2,1)S(1)} %copy-done.111, bf16[2048,128]{1,0:T(8,128)(2,1)S(1)} %fusion.2.key_marks, ...), custom_call_target="tpu_custom_call" | custom-call | flops 40000000000 | bytes 1000000 | tf_op jit(solution)/shard_map/attend_back/pallas_call | solution.py:272
  285.9 6.0 attend_back.8
  295.6 6.5 collective-permute-done.46.refs_8_
  302.6 4.8 collective-permute-done.47.refs_6_
  314.2 6.2 project_back.2
  323.0 8.9 %outer_down.1 = (bf16[2,1,960,640]{3,2,1,0:T(8,128)(2,1)S(1)}, bf16[2,1,960,640]{3,2,1,0:T(8,128)(2,1)}) custom-call(s32[3]{0:T(128)S(1)} %copy-done.24, bf16[960,512]{1,0:T(8,128)(2,1)S(1)} %get-tuple-element.349.left_first, bf16[960,512]{1,0:T(8,128)(2,1)S(1)} %copy-done.101, bf16[2,512,1280]{2,1,0:T(8,128)(2,1)} %get-tuple-element.351.right_first, ...), custom_call_target="tpu_custom_call" | custom-call | flops 40000000000 | bytes 1000000 | tf_op jit(solution)/shard_map/outer_down/pallas_call | solution.py:875
  333.6 21.1 %feed_back.3 = (bf16[2,512,1280]{2,1,0:T(8,128)(2,1)}, bf16[2,512,1280]{2,1,0:T(8,128)(2,1)}, f32[512,960]{1,0:T(8,128)}, bf16[512,960]{1,0:T(8,128)(2,1)}, bf16...) custom-call(s32[3]{0:T(128)} %copy-done.22, ...), custom_call_target="tpu_custom_call" | custom-call | flops 40000000000 | bytes 1000000 | tf_op jit(solution)/shard_map/feed_back/pallas_call | solution.py:744
  357.6 9.7 %outer_gate.1 = (bf16[2,4,240,640]{3,2,1,0:T(8,128)(2,1)S(1)}, bf16[2,4,240,640]{3,2,1,0:T(8,128)(2,1)}) custom-call(s32[3]{0:T(128)S(1)} %copy-done.25, bf16[960,512]{1,0:T(8,128)(2,1)S(1)} %copy-done.97, bf16[960,512]{1,0:T(8,128)(2,1)S(1)} %copy-done.96, bf16[2,512,1280]{2,1,0:T(8,128)(2,1)} %get-tuple-element.360.refs_2_, ...), custom_call_target="tpu_custom_call" | custom-call | flops 40000000000 | bytes 1000000 | tf_op jit(solution)/shard_map/outer_gate/pallas_call | solution.py:843
  373.3 9.5 %outer_up.1 = (bf16[2,4,240,640]{3,2,1,0:T(8,128)(2,1)S(1)}, bf16[2,4,240,640]{3,2,1,0:T(8,128)(2,1)}) custom-call(s32[3]{0:T(128)S(1)} %copy-done.25, bf16[960,512]{1,0:T(8,128)(2,1)S(1)} %copy-done.97, bf16[960,512]{1,0:T(8,128)(2,1)S(1)} %copy-done.96, bf16[2,512,1280]{2,1,0:T(8,128)(2,1)} %get-tuple-element.368.refs_2_, ...), custom_call_target="tpu_custom_call" | custom-call | flops 40000000000 | bytes 1000000 | tf_op jit(solution)/shard_map/outer_up/pallas_call | solution.py:843
  382.8 5.5 collective-permute-done.50
  390.8 4.3 outer_o.1
  398.1 7.1 %collective-permute-done.53 = bf16[1,480,640]{2,1,0:T(8,128)(2,1)S(1)} collective-permute-done((bf16[1,480,640]{2,1,0:T(8,128)(2,1)S(1)}, bf16[1,480,640]{2,1,0:T(8,128)(2,1)S(1)}, u32[]{:S(2)}, u32[]{:S(2)}) %collective-permute-start.53) | collective-permute-done | bytes 614432 | tf_op jit(solution)/shard_map/ppermute | solution.py:953
  422.4 13.7 %attend_back.9 = (bf16[512,384]{1,0:T(8,128)(2,1)S(1)}, bf16[2,2,512,128]{3,2,1,0:T(8,128)(2,1)S(1)}, bf16[2,2,512,128]{3,2,1,0:T(8,128)(2,1)S(1)}) custom-call(s32[3]{0:T(128)S(1)} %copy-done.25, bf16[15,512,128]{2,1,0:T(8,128)(2,1)} %copy-done.84, bf16[6,512,128]{2,1,0:T(8,128)(2,1)S(1)} %copy-done.109, bf16[2048,128]{1,0:T(8,128)(2,1)S(1)} %copy-done.6, ...), custom_call_target="tpu_custom_call" | custom-call | flops 40000000000 | bytes 1000000 | tf_op jit(solution)/shard_map/attend_back/pallas_call | solution.py:272
  443.2 13.4 %attend_back.10 = (bf16[512,384]{1,0:T(8,128)(2,1)S(1)}, bf16[2,2,512,128]{3,2,1,0:T(8,128)(2,1)S(1)}, bf16[2,2,512,128]{3,2,1,0:T(8,128)(2,1)S(1)}) custom-call(s32[3]{0:T(128)S(1)} %copy-done.25, bf16[15,512,128]{2,1,0:T(8,128)(2,1)} %copy-done.84, bf16[6,512,128]{2,1,0:T(8,128)(2,1)S(1)} %copy-done.107, bf16[2048,128]{1,0:T(8,128)(2,1)S(1)} %copy-done.6, ...), custom_call_target="tpu_custom_call" | custom-call | flops 40000000000 | bytes 1000000 | tf_op jit(solution)/shard_map/attend_back/pallas_call | solution.py:272
  460.3 7.2 %attend_back.11 = (bf16[512,256]{1,0:T(8,128)(2,1)S(1)}, bf16[2,1,512,128]{3,2,1,0:T(8,128)(2,1)S(1)}, bf16[2,1,512,128]{3,2,1,0:T(8,128)(2,1)S(1)}) custom-call(s32[3]{0:T(128)S(1)} %copy-done.25, bf16[15,512,128]{2,1,0:T(8,128)(2,1)S(1)} %copy-done.86, bf16[3,512,128]{2,1,0:T(8,128)(2,1)S(1)} %copy-done.131, bf16[2048,128]{1,0:T(8,128)(2,1)S(1)} %copy-done.7, ...), custom_call_target="tpu_custom_call" | custom-call | flops 40000000000 | bytes 1000000 | tf_op jit(solution)/shard_map/attend_back/pallas_call | solution.py:272
  469.5 4.9 collective-permute-done.66
  476.2 6.9 %collective-permute-done.68.refs_8_ = bf16[2,512,128]{2,1,0:T(8,128)(2,1)S(1)} collective-permute-done((bf16[2,512,128]{2,1,0:T(8,128)(2,1)S(1)}, bf16[2,512,128]{2,1,0:T(8,128)(2,1)S(1)}, u32[]{:S(2)}, u32[]{:S(2)}) %collective-permute-start.68) | collective-permute-done | bytes 262176 | tf_op jit(solution)/shard_map/ppermute | solution.py:953
  489.2 9.3 %collective-permute-done.69 = bf16[2,240,640]{2,1,0:T(8,128)(2,1)S(1)} collective-permute-done((bf16[2,240,640]{2,1,0:T(8,128)(2,1)S(1)}, bf16[2,240,640]{2,1,0:T(8,128)(2,1)S(1)}, u32[]{:S(2)}, u32[]{:S(2)}) %collective-permute-start.69) | collective-permute-done | bytes 614432 | tf_op jit(solution)/shard_map/ppermute | solution.py:953
  505.7 5.7 project_back.3
  524.3 7.7 %outer_in.1 = (bf16[2,1,256,1664]{3,2,1,0:T(8,128)(2,1)S(1)}, bf16[2,1,256,1664]{3,2,1,0:T(8,128)(2,1)}) custom-call(s32[3]{0:T(128)S(1)} %copy-done.25, bf16[960,512]{1,0:T(8,128)(2,1)S(1)} %copy-done.105, bf16[960,512]{1,0:T(8,128)(2,1)S(1)} %copy-done.103, bf16[512,1664]{1,0:T(8,128)(2,1)} %copy-done.88, bf16[512,1664]{1,0:T(8,128)(2,1)} %copy-done.87, ...), custom_call_target="tpu_custom_call" | custom-call | flops 40000000000 | bytes 1000000 | tf_op jit(solution)/shard_map/outer_in/pallas_call | solution.py:908
  545.3 11.9 %collective-permute-done.80 = bf16[2,240,640]{2,1,0:T(8,128)(2,1)S(1)} collective-permute-done((bf16[2,240,640]{2,1,0:T(8,128)(2,1)}, bf16[2,240,640]{2,1,0:T(8,128)(2,1)S(1)}, u32[]{:S(2)}, u32[]{:S(2)}) %collective-permute-start.80) | collective-permute-done | bytes 614432 | tf_op jit(solution)/shard_map/ppermute | solution.py:953
  560.1 9.2 %collective-permute-done.81 = bf16[2,240,640]{2,1,0:T(8,128)(2,1)S(1)} collective-permute-done((bf16[2,240,640]{2,1,0:T(8,128)(2,1)S(1)}, bf16[2,240,640]{2,1,0:T(8,128)(2,1)S(1)}, u32[]{:S(2)}, u32[]{:S(2)}) %collective-permute-start.81) | collective-permute-done | bytes 614432 | tf_op jit(solution)/shard_map/ppermute | solution.py:953
  576.7 4.3 collective-permute-done.85
  581.0 6.5 collective-permute-done.84
  602.4 5.3 collective-permute-done.89
  618.7 5.4 collective-permute-done.91
  624.3 8.9 %collective-permute-done.95 = bf16[2,240,640]{2,1,0:T(8,128)(2,1)S(1)} collective-permute-done((bf16[2,240,640]{2,1,0:T(8,128)(2,1)S(1)}, bf16[2,240,640]{2,1,0:T(8,128)(2,1)S(1)}, u32[]{:S(2)}, u32[]{:S(2)}) %collective-permute-start.95) | collective-permute-done | bytes 614432 | tf_op jit(solution)/shard_map/ppermute | solution.py:953
  647.5 5.8 collective-permute-done.101
  668.1 5.5 collective-permute-done.107
  (688 shorter events, 249.1 us)
Async XLA Ops:
  5.6 30.7 %collective-permute-start = (bf16[240,1664]{1,0:T(8,128)(2,1)S(1)}, bf16[240,1664]{1,0:T(8,128)(2,1)S(1)}, u32[]{:S(2)}, u32[]{:S(2)}) collective-permute-start(bf16[240,1664]{1,0:T(8,128)(2,1)S(1)} %pack.1.own.refs_14_), channel_id=1, source_target_pairs={{0,2},{1,3},{2,0},{3,1},{4,6},{5,7},{6,4},{7,5},{8,10},{9,11},{10,... | collective-permute-start | bytes 2396168 | tf_op jit(solution)/shard_map/ppermute | solution.py:953
  8.7 27.7 %collective-permute-start.1 = (bf16[240,1664]{1,0:T(8,128)(2,1)S(1)}, bf16[240,1664]{1,0:T(8,128)(2,1)S(1)}, u32[]{:S(2)}, u32[]{:S(2)}) collective-permute-start(bf16[240,1664]{1,0:T(8,128)(2,1)S(1)} %pack.1.own.refs_14_), channel_id=1, source_target_pairs={{0,1},{1,0},{2,3},{3,2},{4,5},{5,4},{6,7},{7,6},{8,9},{9,8},{10,11... | collective-permute-start | bytes 2396168 | tf_op jit(solution)/shard_map/ppermute | solution.py:953
  8.7 27.7 %collective-permute-start.2 = (bf16[960,256]{1,0:T(8,128)(2,1)}, bf16[960,256]{1,0:T(8,128)(2,1)}, u32[]{:S(2)}, u32[]{:S(2)}) collective-permute-start(bf16[960,256]{1,0:T(8,128)(2,1)} %slice.432), channel_id=1, source_target_pairs={{0,3},{1,2},{2,1},{3,0},{4,7},{5,6},{6,5},{7,4},{8,11},{9,10},{10,... | collective-permute-start | bytes 1474568 | tf_op jit(solution)/shard_map/ppermute | solution.py:953
  36.4 14.0 %collective-permute-start.3 = (bf16[240,1664]{1,0:T(8,128)(2,1)S(1)}, bf16[240,1664]{1,0:T(8,128)(2,1)S(1)}, u32[]{:S(2)}, u32[]{:S(2)}) collective-permute-start(bf16[240,1664]{1,0:T(8,128)(2,1)S(1)} %collective-permute-done.far.refs_16_), channel_id=1, source_target_pairs={{0,1},{1,0},{2,3},{3,2},{4,5},{5,4},{6,7},{7,6},{8,9},{9,8},{10,11... | collective-permute-start | bytes 2396168 | tf_op jit(solution)/shard_map/ppermute | solution.py:953
  37.0 13.3 %collective-permute-start.4 = (bf16[240,960]{1,0:T(8,128)(2,1)S(1)}, bf16[240,960]{1,0:T(8,128)(2,1)}, u32[]{:S(2)}, u32[]{:S(2)}) collective-permute-start(bf16[240,960]{1,0:T(8,128)(2,1)S(1)} %copy-done.193), channel_id=1, source_target_pairs={{0,2},{1,3},{2,0},{3,1},{4,6},{5,7},{6,4},{7,5},{8,10},{9,11},{10,... | collective-permute-start | bytes 1382408 | tf_op jit(solution)/shard_map/ppermute | solution.py:953
  50.3 15.0 %collective-permute-start.5 = (bf16[240,1280]{1,0:T(8,128)(2,1)S(1)}, bf16[240,1280]{1,0:T(8,128)(2,1)S(1)}, u32[]{:S(2)}, u32[]{:S(2)}) collective-permute-start(bf16[240,1280]{1,0:T(8,128)(2,1)S(1)} %slice_select_fusion.2), channel_id=1, source_target_pairs={{0,2},{1,3},{2,0},{3,1},{4,6},{5,7},{6,4},{7,5},{8,10},{9,11},{10,... | collective-permute-start | bytes 1843208 | tf_op jit(solution)/shard_map/ppermute | solution.py:953
  71.4 14.8 %collective-permute-start.10 = (bf16[240,1280]{1,0:T(8,128)(2,1)}, bf16[240,1280]{1,0:T(8,128)(2,1)S(1)}, u32[]{:S(2)}, u32[]{:S(2)}) collective-permute-start(bf16[240,1280]{1,0:T(8,128)(2,1)} %copy-done.183), channel_id=1, source_target_pairs={{0,4},{4,0},{8,12},{12,8},{16,20},{20,16},{24,28},{28,24},{1,5},{5... | collective-permute-start | bytes 1843208 | tf_op jit(solution)/shard_map/ppermute | solution.py:953
  86.2 19.3 %collective-permute-start.14 = (bf16[240,1280]{1,0:T(8,128)(2,1)S(1)}, bf16[240,1280]{1,0:T(8,128)(2,1)S(1)}, u32[]{:S(2)}, u32[]{:S(2)}) collective-permute-start(bf16[240,1280]{1,0:T(8,128)(2,1)S(1)} %slice_select_fusion.1), channel_id=1, source_target_pairs={{0,2},{1,3},{2,0},{3,1},{4,6},{5,7},{6,4},{7,5},{8,10},{9,11},{10,... | collective-permute-start | bytes 1843208 | tf_op jit(solution)/shard_map/ppermute | solution.py:953
  87.9 17.5 %collective-permute-start.15 = (bf16[2,512,128]{2,1,0:T(8,128)(2,1)S(1)}, bf16[2,512,128]{2,1,0:T(8,128)(2,1)S(1)}, u32[]{:S(2)}, u32[]{:S(2)}) collective-permute-start(bf16[2,512,128]{2,1,0:T(8,128)(2,1)S(1)} %get-tuple-element.262.own), channel_id=1, source_target_pairs={{0,2},{1,3},{2,0},{3,1},{4,6},{5,7},{6,4},{7,5},{8,10},{9,11},{10,... | collective-permute-start | bytes 786440 | tf_op jit(solution)/shard_map/ppermute | solution.py:953
  88.2 17.2 %collective-permute-start.16 = (bf16[2,512,128]{2,1,0:T(8,128)(2,1)S(1)}, bf16[2,512,128]{2,1,0:T(8,128)(2,1)S(1)}, u32[]{:S(2)}, u32[]{:S(2)}) collective-permute-start(bf16[2,512,128]{2,1,0:T(8,128)(2,1)S(1)} %collective-permute-done.11.far), channel_id=1, source_target_pairs={{0,1},{1,0},{2,3},{3,2},{4,5},{5,4},{6,7},{7,6},{8,9},{9,8},{10,11... | collective-permute-start | bytes 786440 | tf_op jit(solution)/shard_map/ppermute | solution.py:953
  119.9 16.1 %collective-permute-start.20 = (bf16[480,640]{1,0:T(8,128)(2,1)}, bf16[480,640]{1,0:T(8,128)(2,1)}, u32[]{:S(2)}, u32[]{:S(2)}) collective-permute-start(bf16[480,640]{1,0:T(8,128)(2,1)} %collective-permute-done.18.refs_22_.refs_21_), channel_id=1, source_target_pairs={{0,4},{4,0},{8,12},{12,8},{16,20},{20,16},{24,28},{28,24},{1,5},{5... | collective-permute-start | bytes 1843208 | tf_op jit(solution)/shard_map/ppermute | solution.py:953
  121.4 14.6 %collective-permute-start.21 = (bf16[240,2560]{1,0:T(8,128)(2,1)S(1)}, bf16[240,2560]{1,0:T(8,128)(2,1)S(1)}, u32[]{:S(2)}, u32[]{:S(2)}) collective-permute-start(bf16[240,2560]{1,0:T(8,128)(2,1)S(1)} %copy-done.165), channel_id=1, source_target_pairs={{0,1},{1,0},{2,3},{3,2},{4,5},{5,4},{6,7},{7,6},{8,9},{9,8},{10,11... | collective-permute-start | bytes 3686408 | tf_op jit(solution)/shard_map/ppermute | solution.py:953
  121.4 14.6 %collective-permute-start.22 = (bf16[240,2560]{1,0:T(8,128)(2,1)S(1)}, bf16[240,2560]{1,0:T(8,128)(2,1)S(1)}, u32[]{:S(2)}, u32[]{:S(2)}) collective-permute-start(bf16[240,2560]{1,0:T(8,128)(2,1)S(1)} %copy-done.166), channel_id=1, source_target_pairs={{0,1},{1,0},{2,3},{3,2},{4,5},{5,4},{6,7},{7,6},{8,9},{9,8},{10,11... | collective-permute-start | bytes 3686408 | tf_op jit(solution)/shard_map/ppermute | solution.py:953
  121.9 14.1 %collective-permute-start.23 = (bf16[960,640]{1,0:T(8,128)(2,1)S(1)}, bf16[960,640]{1,0:T(8,128)(2,1)S(1)}, u32[]{:S(2)}, u32[]{:S(2)}) collective-permute-start(bf16[960,640]{1,0:T(8,128)(2,1)S(1)} %bitcast.239), channel_id=1, source_target_pairs={{0,1},{1,0},{2,3},{3,2},{4,5},{5,4},{6,7},{7,6},{8,9},{9,8},{10,11... | collective-permute-start | bytes 3686408 | tf_op jit(solution)/shard_map/ppermute | solution.py:953
  189.8 13.0 %collective-permute-start.40 = (bf16[960,256]{1,0:T(8,128)(2,1)S(1)}, bf16[960,256]{1,0:T(8,128)(2,1)S(1)}, u32[]{:S(2)}, u32[]{:S(2)}) collective-permute-start(bf16[960,256]{1,0:T(8,128)(2,1)S(1)} %slice.435), channel_id=1, source_target_pairs={{0,3},{1,2},{2,1},{3,0},{4,7},{5,6},{6,5},{7,4},{8,11},{9,10},{10,... | collective-permute-start | bytes 1474568 | tf_op jit(solution)/shard_map/ppermute | solution.py:953
  253.9 16.4 %collective-permute-start.41 = (bf16[960,256]{1,0:T(8,128)(2,1)S(1)}, bf16[960,256]{1,0:T(8,128)(2,1)S(1)}, u32[]{:S(2)}, u32[]{:S(2)}) collective-permute-start(bf16[960,256]{1,0:T(8,128)(2,1)S(1)} %get-tuple-element.320), channel_id=1, source_target_pairs={{0,3},{1,2},{2,1},{3,0},{4,7},{5,6},{6,5},{7,4},{8,11},{9,10},{10,... | collective-permute-start | bytes 1474568 | tf_op jit(solution)/shard_map/ppermute | solution.py:953
  270.3 14.1 %collective-permute-start.42 = (bf16[2,2,512,128]{3,2,1,0:T(8,128)(2,1)S(1)}, bf16[2,2,512,128]{3,2,1,0:T(8,128)(2,1)S(1)}, u32[]{:S(2)}, u32[]{:S(2)}) collective-permute-start(bf16[2,2,512,128]{3,2,1,0:T(8,128)(2,1)S(1)} %get-tuple-element.327), channel_id=1, source_target_pairs={{0,1},{1,0},{2,3},{3,2},{4,5},{5,4},{6,7},{7,6},{8,9},{9,8},{10,11... | collective-permute-start | bytes 1572872 | tf_op jit(solution)/shard_map/ppermute | solution.py:953
  333.6 21.1 %collective-permute-start.48 = (bf16[2,1,960,640]{3,2,1,0:T(8,128)(2,1)S(1)}, bf16[2,1,960,640]{3,2,1,0:T(8,128)(2,1)}, u32[]{:S(2)}, u32[]{:S(2)}) collective-permute-start(bf16[2,1,960,640]{3,2,1,0:T(8,128)(2,1)S(1)} %copy-done.179), channel_id=1, source_target_pairs={{0,1},{1,0},{2,3},{3,2},{4,5},{5,4},{6,7},{7,6},{8,9},{9,8},{10,11... | collective-permute-start | bytes 7372808 | tf_op jit(solution)/shard_map/ppermute | solution.py:953
  356.5 16.3 %collective-permute-start.49 = (bf16[1,480,640]{2,1,0:T(8,128)(2,1)S(1)}, bf16[1,480,640]{2,1,0:T(8,128)(2,1)S(1)}, u32[]{:S(2)}, u32[]{:S(2)}) collective-permute-start(bf16[1,480,640]{2,1,0:T(8,128)(2,1)S(1)} %get-tuple-element.365), channel_id=1, source_target_pairs={{0,2},{1,3},{2,0},{3,1},{4,6},{5,7},{6,4},{7,5},{8,10},{9,11},{10,... | collective-permute-start | bytes 1843208 | tf_op jit(solution)/shard_map/ppermute | solution.py:953
  372.8 15.5 %collective-permute-start.50 = (bf16[1,480,640]{2,1,0:T(8,128)(2,1)S(1)}, bf16[1,480,640]{2,1,0:T(8,128)(2,1)S(1)}, u32[]{:S(2)}, u32[]{:S(2)}) collective-permute-start(bf16[1,480,640]{2,1,0:T(8,128)(2,1)S(1)} %get-tuple-element.371), channel_id=1, source_target_pairs={{0,2},{1,3},{2,0},{3,1},{4,6},{5,7},{6,4},{7,5},{8,10},{9,11},{10,... | collective-permute-start | bytes 1843208 | tf_op jit(solution)/shard_map/ppermute | solution.py:953
  373.3 15.4 %collective-permute-start.51 = (bf16[2,4,240,640]{3,2,1,0:T(8,128)(2,1)}, bf16[2,4,240,640]{3,2,1,0:T(8,128)(2,1)}, u32[]{:S(2)}, u32[]{:S(2)}) collective-permute-start(bf16[2,4,240,640]{3,2,1,0:T(8,128)(2,1)} %get-tuple-element.373), channel_id=1, source_target_pairs={{0,1},{1,0},{2,3},{3,2},{4,5},{5,4},{6,7},{7,6},{8,9},{9,8},{10,11... | collective-permute-start | bytes 7372808 | tf_op jit(solution)/shard_map/ppermute | solution.py:953
  388.8 18.5 %collective-permute-start.52 = (bf16[2,4,240,640]{3,2,1,0:T(8,128)(2,1)}, bf16[2,4,240,640]{3,2,1,0:T(8,128)(2,1)}, u32[]{:S(2)}, u32[]{:S(2)}) collective-permute-start(bf16[2,4,240,640]{3,2,1,0:T(8,128)(2,1)} %get-tuple-element.374), channel_id=1, source_target_pairs={{0,1},{1,0},{2,3},{3,2},{4,5},{5,4},{6,7},{7,6},{8,9},{9,8},{10,11... | collective-permute-start | bytes 7372808 | tf_op jit(solution)/shard_map/ppermute | solution.py:953
  388.9 16.3 %collective-permute-start.53 = (bf16[1,480,640]{2,1,0:T(8,128)(2,1)S(1)}, bf16[1,480,640]{2,1,0:T(8,128)(2,1)S(1)}, u32[]{:S(2)}, u32[]{:S(2)}) collective-permute-start(bf16[1,480,640]{2,1,0:T(8,128)(2,1)S(1)} %fusion.6), channel_id=1, source_target_pairs={{0,4},{4,0},{8,12},{12,8},{16,20},{20,16},{24,28},{28,24},{1,5},{5... | collective-permute-start | bytes 1843208 | tf_op jit(solution)/shard_map/ppermute | solution.py:953
  407.3 28.9 %collective-permute-start.57 = (bf16[1,120,640]{2,1,0:T(8,128)(2,1)}, bf16[1,120,640]{2,1,0:T(8,128)(2,1)}, u32[]{:S(2)}, u32[]{:S(2)}) collective-permute-start(bf16[1,120,640]{2,1,0:T(8,128)(2,1)} %get-tuple-element.390), channel_id=1, source_target_pairs={{0,24},{4,28},{8,16},{12,20},{16,8},{20,12},{24,0},{28,4},{1,25},{... | collective-permute-start | bytes 460808 | tf_op jit(solution)/shard_map/ppermute | solution.py:953
  410.0 26.2 %collective-permute-start.56 = (bf16[1,120,640]{2,1,0:T(8,128)(2,1)}, bf16[1,120,640]{2,1,0:T(8,128)(2,1)}, u32[]{:S(2)}, u32[]{:S(2)}) collective-permute-start(bf16[1,120,640]{2,1,0:T(8,128)(2,1)} %get-tuple-element.389), channel_id=1, source_target_pairs={{0,16},{4,20},{8,24},{12,28},{16,0},{20,4},{24,8},{28,12},{1,17},{... | collective-permute-start | bytes 460808 | tf_op jit(solution)/shard_map/ppermute | solution.py:953
  410.0 26.2 %collective-permute-start.55 = (bf16[1,120,640]{2,1,0:T(8,128)(2,1)}, bf16[1,120,640]{2,1,0:T(8,128)(2,1)}, u32[]{:S(2)}, u32[]{:S(2)}) collective-permute-start(bf16[1,120,640]{2,1,0:T(8,128)(2,1)} %get-tuple-element.388), channel_id=1, source_target_pairs={{0,8},{4,12},{8,0},{12,4},{16,24},{20,28},{24,16},{28,20},{1,9},{5... | collective-permute-start | bytes 460808 | tf_op jit(solution)/shard_map/ppermute | solution.py:953
  411.7 25.9 %collective-permute-start.54 = (bf16[2,240,640]{2,1,0:T(8,128)(2,1)}, bf16[2,240,640]{2,1,0:T(8,128)(2,1)}, u32[]{:S(2)}, u32[]{:S(2)}) collective-permute-start(bf16[2,240,640]{2,1,0:T(8,128)(2,1)} %get-tuple-element.383), channel_id=1, source_target_pairs={{0,2},{1,3},{2,0},{3,1},{4,6},{5,7},{6,4},{7,5},{8,10},{9,11},{10,... | collective-permute-start | bytes 1843208 | tf_op jit(solution)/shard_map/ppermute | solution.py:953
  414.4 23.1 %collective-permute-start.58 = (bf16[2,1,256,960]{2,3,1,0:T(8,128)(2,1)}, bf16[2,1,256,960]{2,3,1,0:T(8,128)(2,1)S(1)}, u32[]{:S(2)}, u32[]{:S(2)}) collective-permute-start(bf16[2,1,256,960]{2,3,1,0:T(8,128)(2,1)} %copy.65), channel_id=1, source_target_pairs={{0,1},{1,0},{2,3},{3,2},{4,5},{5,4},{6,7},{7,6},{8,9},{9,8},{10,11... | collective-permute-start | bytes 2949128 | tf_op jit(solution)/shard_map/ppermute | solution.py:953
  437.6 19.3 %collective-permute-start.60 = (bf16[2,2,512,128]{3,2,1,0:T(8,128)(2,1)S(1)}, bf16[2,2,512,128]{3,2,1,0:T(8,128)(2,1)S(1)}, u32[]{:S(2)}, u32[]{:S(2)}) collective-permute-start(bf16[2,2,512,128]{3,2,1,0:T(8,128)(2,1)S(1)} %get-tuple-element.395), channel_id=1, source_target_pairs={{0,1},{1,0},{2,3},{3,2},{4,5},{5,4},{6,7},{7,6},{8,9},{9,8},{10,11... | collective-permute-start | bytes 1572872 | tf_op jit(solution)/shard_map/ppermute | solution.py:953
  438.2 18.4 %collective-permute-start.63 = (bf16[1,120,640]{2,1,0:T(8,128)(2,1)S(1)}, bf16[1,120,640]{2,1,0:T(8,128)(2,1)S(1)}, u32[]{:S(2)}, u32[]{:S(2)}) collective-permute-start(bf16[1,120,640]{2,1,0:T(8,128)(2,1)S(1)} %fusion.23), channel_id=1, source_target_pairs={{0,8},{4,12},{8,0},{12,4},{16,24},{20,28},{24,16},{28,20},{1,9},{5... | collective-permute-start | bytes 460808 | tf_op jit(solution)/shard_map/ppermute | solution.py:953
  438.5 18.1 %collective-permute-start.61 = (bf16[1,120,640]{2,1,0:T(8,128)(2,1)S(1)}, bf16[1,120,640]{2,1,0:T(8,128)(2,1)S(1)}, u32[]{:S(2)}, u32[]{:S(2)}) collective-permute-start(bf16[1,120,640]{2,1,0:T(8,128)(2,1)S(1)} %fusion.23), channel_id=1, source_target_pairs={{0,24},{4,28},{8,16},{12,20},{16,8},{20,12},{24,0},{28,4},{1,25},{... | collective-permute-start | bytes 460808 | tf_op jit(solution)/shard_map/ppermute | solution.py:953
  441.3 15.3 %collective-permute-start.62 = (bf16[1,120,640]{2,1,0:T(8,128)(2,1)S(1)}, bf16[1,120,640]{2,1,0:T(8,128)(2,1)S(1)}, u32[]{:S(2)}, u32[]{:S(2)}) collective-permute-start(bf16[1,120,640]{2,1,0:T(8,128)(2,1)S(1)} %fusion.23), channel_id=1, source_target_pairs={{0,16},{4,20},{8,24},{12,28},{16,0},{20,4},{24,8},{28,12},{1,17},{... | collective-permute-start | bytes 460808 | tf_op jit(solution)/shard_map/ppermute | solution.py:953
  441.6 16.1 %collective-permute-start.59 = (bf16[2,240,640]{2,1,0:T(8,128)(2,1)}, bf16[2,240,640]{2,1,0:T(8,128)(2,1)S(1)}, u32[]{:S(2)}, u32[]{:S(2)}) collective-permute-start(bf16[2,240,640]{2,1,0:T(8,128)(2,1)} %get-tuple-element.393), channel_id=1, source_target_pairs={{0,2},{1,3},{2,0},{3,1},{4,6},{5,7},{6,4},{7,5},{8,10},{9,11},{10,... | collective-permute-start | bytes 1843208 | tf_op jit(solution)/shard_map/ppermute | solution.py:953
  458.5 15.9 %collective-permute-start.66 = (bf16[1,480,640]{2,1,0:T(8,128)(2,1)S(1)}, bf16[1,480,640]{2,1,0:T(8,128)(2,1)S(1)}, u32[]{:S(2)}, u32[]{:S(2)}) collective-permute-start(bf16[1,480,640]{2,1,0:T(8,128)(2,1)S(1)} %pad_maximum_fusion.1), channel_id=1, source_target_pairs={{0,4},{4,0},{8,12},{12,8},{16,20},{20,16},{24,28},{28,24},{1,5},{5... | collective-permute-start | bytes 1843208 | tf_op jit(solution)/shard_map/ppermute | solution.py:953
  483.1 15.4 %collective-permute-start.69 = (bf16[2,240,640]{2,1,0:T(8,128)(2,1)S(1)}, bf16[2,240,640]{2,1,0:T(8,128)(2,1)S(1)}, u32[]{:S(2)}, u32[]{:S(2)}) collective-permute-start(bf16[2,240,640]{2,1,0:T(8,128)(2,1)S(1)} %select_convert_fusion.1), channel_id=1, source_target_pairs={{0,4},{4,0},{8,12},{12,8},{16,20},{20,16},{24,28},{28,24},{1,5},{5... | collective-permute-start | bytes 1843208 | tf_op jit(solution)/shard_map/ppermute | solution.py:953
  499.7 14.0 %collective-permute-start.73 = (bf16[1,120,640]{2,1,0:T(8,128)(2,1)}, bf16[1,120,640]{2,1,0:T(8,128)(2,1)}, u32[]{:S(2)}, u32[]{:S(2)}) collective-permute-start(bf16[1,120,640]{2,1,0:T(8,128)(2,1)} %get-tuple-element.425), channel_id=1, source_target_pairs={{0,24},{4,28},{8,16},{12,20},{16,8},{20,12},{24,0},{28,4},{1,25},{... | collective-permute-start | bytes 460808 | tf_op jit(solution)/shard_map/ppermute | solution.py:953
  502.4 13.0 %collective-permute-start.72 = (bf16[1,120,640]{2,1,0:T(8,128)(2,1)}, bf16[1,120,640]{2,1,0:T(8,128)(2,1)}, u32[]{:S(2)}, u32[]{:S(2)}) collective-permute-start(bf16[1,120,640]{2,1,0:T(8,128)(2,1)} %get-tuple-element.424), channel_id=1, source_target_pairs={{0,16},{4,20},{8,24},{12,28},{16,0},{20,4},{24,8},{28,12},{1,17},{... | collective-permute-start | bytes 460808 | tf_op jit(solution)/shard_map/ppermute | solution.py:953
  502.4 13.0 %collective-permute-start.71 = (bf16[1,120,640]{2,1,0:T(8,128)(2,1)}, bf16[1,120,640]{2,1,0:T(8,128)(2,1)}, u32[]{:S(2)}, u32[]{:S(2)}) collective-permute-start(bf16[1,120,640]{2,1,0:T(8,128)(2,1)} %get-tuple-element.423), channel_id=1, source_target_pairs={{0,8},{4,12},{8,0},{12,4},{16,24},{20,28},{24,16},{28,20},{1,9},{5... | collective-permute-start | bytes 460808 | tf_op jit(solution)/shard_map/ppermute | solution.py:953
  504.1 14.0 %collective-permute-start.74 = (bf16[2,240,640]{2,1,0:T(8,128)(2,1)}, bf16[2,240,640]{2,1,0:T(8,128)(2,1)}, u32[]{:S(2)}, u32[]{:S(2)}) collective-permute-start(bf16[2,240,640]{2,1,0:T(8,128)(2,1)} %get-tuple-element.426), channel_id=1, source_target_pairs={{0,2},{1,3},{2,0},{3,1},{4,6},{5,7},{6,4},{7,5},{8,10},{9,11},{10,... | collective-permute-start | bytes 1843208 | tf_op jit(solution)/shard_map/ppermute | solution.py:953
  518.1 13.9 %collective-permute-start.77 = (bf16[1,120,640]{2,1,0:T(8,128)(2,1)S(1)}, bf16[1,120,640]{2,1,0:T(8,128)(2,1)S(1)}, u32[]{:S(2)}, u32[]{:S(2)}) collective-permute-start(bf16[1,120,640]{2,1,0:T(8,128)(2,1)S(1)} %fusion.20), channel_id=1, source_target_pairs={{0,8},{4,12},{8,0},{12,4},{16,24},{20,28},{24,16},{28,20},{1,9},{5... | collective-permute-start | bytes 460808 | tf_op jit(solution)/shard_map/ppermute | solution.py:953
  518.7 13.3 %collective-permute-start.75 = (bf16[1,120,640]{2,1,0:T(8,128)(2,1)S(1)}, bf16[1,120,640]{2,1,0:T(8,128)(2,1)S(1)}, u32[]{:S(2)}, u32[]{:S(2)}) collective-permute-start(bf16[1,120,640]{2,1,0:T(8,128)(2,1)S(1)} %fusion.20), channel_id=1, source_target_pairs={{0,24},{4,28},{8,16},{12,20},{16,8},{20,12},{24,0},{28,4},{1,25},{... | collective-permute-start | bytes 460808 | tf_op jit(solution)/shard_map/ppermute | solution.py:953
  537.4 20.1 %collective-permute-start.79 = (bf16[2,1,256,1664]{3,2,1,0:T(8,128)(2,1)}, bf16[2,1,256,1664]{3,2,1,0:T(8,128)(2,1)}, u32[]{:S(2)}, u32[]{:S(2)}) collective-permute-start(bf16[2,1,256,1664]{3,2,1,0:T(8,128)(2,1)} %get-tuple-element.439), channel_id=1, source_target_pairs={{0,1},{1,0},{2,3},{3,2},{4,5},{5,4},{6,7},{7,6},{8,9},{9,8},{10,11... | collective-permute-start | bytes 5111816 | tf_op jit(solution)/shard_map/ppermute | solution.py:953
  539.9 17.3 %collective-permute-start.80 = (bf16[2,240,640]{2,1,0:T(8,128)(2,1)}, bf16[2,240,640]{2,1,0:T(8,128)(2,1)S(1)}, u32[]{:S(2)}, u32[]{:S(2)}) collective-permute-start(bf16[2,240,640]{2,1,0:T(8,128)(2,1)} %select_convert_fusion), channel_id=1, source_target_pairs={{0,4},{4,0},{8,12},{12,8},{16,20},{20,16},{24,28},{28,24},{1,5},{5... | collective-permute-start | bytes 1843208 | tf_op jit(solution)/shard_map/ppermute | solution.py:953
  544.5 24.9 %collective-permute-start.81 = (bf16[2,240,640]{2,1,0:T(8,128)(2,1)S(1)}, bf16[2,240,640]{2,1,0:T(8,128)(2,1)S(1)}, u32[]{:S(2)}, u32[]{:S(2)}) collective-permute-start(bf16[2,240,640]{2,1,0:T(8,128)(2,1)S(1)} %copy-done.173), channel_id=1, source_target_pairs={{0,4},{4,0},{8,12},{12,8},{16,20},{20,16},{24,28},{28,24},{1,5},{5... | collective-permute-start | bytes 1843208 | tf_op jit(solution)/shard_map/ppermute | solution.py:953
  569.3 19.9 %collective-permute-start.82 = (bf16[1,256,1664]{2,1,0:T(8,128)(2,1)S(1)}, bf16[1,256,1664]{2,1,0:T(8,128)(2,1)S(1)}, u32[]{:S(2)}, u32[]{:S(2)}) collective-permute-start(bf16[1,256,1664]{2,1,0:T(8,128)(2,1)S(1)} %fusion.3), channel_id=1, source_target_pairs={{0,2},{1,3},{2,0},{3,1},{4,6},{5,7},{6,4},{7,5},{8,10},{9,11},{10,... | collective-permute-start | bytes 2555912 | tf_op jit(solution)/shard_map/ppermute | solution.py:953
  590.7 17.2 %collective-permute-start.87 = (bf16[1,128,1664]{2,1,0:T(8,128)(2,1)S(1)}, bf16[1,128,1664]{2,1,0:T(8,128)(2,1)S(1)}, u32[]{:S(2)}, u32[]{:S(2)}) collective-permute-start(bf16[1,128,1664]{2,1,0:T(8,128)(2,1)S(1)} %fusion.14), channel_id=1, source_target_pairs={{0,4},{4,0},{8,12},{12,8},{16,20},{20,16},{24,28},{28,24},{1,5},{5... | collective-permute-start | bytes 1277960 | tf_op jit(solution)/shard_map/ppermute | solution.py:953
  615.8 17.4 %collective-permute-start.95 = (bf16[2,240,640]{2,1,0:T(8,128)(2,1)S(1)}, bf16[2,240,640]{2,1,0:T(8,128)(2,1)S(1)}, u32[]{:S(2)}, u32[]{:S(2)}) collective-permute-start(bf16[2,240,640]{2,1,0:T(8,128)(2,1)S(1)} %maximum_maximum_fusion.1), channel_id=1, source_target_pairs={{0,4},{4,0},{8,12},{12,8},{16,20},{20,16},{24,28},{28,24},{1,5},{5... | collective-permute-start | bytes 1843208 | tf_op jit(solution)/shard_map/ppermute | solution.py:953
  633.1 20.3 %collective-permute-start.96 = (bf16[960,256]{1,0:T(8,128)(2,1)S(1)}, bf16[960,256]{1,0:T(8,128)(2,1)S(1)}, u32[]{:S(2)}, u32[]{:S(2)}) collective-permute-start(bf16[960,256]{1,0:T(8,128)(2,1)S(1)} %get-tuple-element.456), channel_id=1, source_target_pairs={{0,3},{1,2},{2,1},{3,0},{4,7},{5,6},{6,5},{7,4},{8,11},{9,10},{10,... | collective-permute-start | bytes 1474568 | tf_op jit(solution)/shard_map/ppermute | solution.py:953
  (256 other events, 2933.3 us)

commit v3 on v2

--- a/solution.py
+++ b/solution.py
@@ -182,7 +182,7 @@
             jax.ShapeDtypeStruct((tokens, width), bf16),
             jax.ShapeDtypeStruct((GROUP * heads_here, tokens, LANES), bf16),
         ],
-        compiler_params=params(48),
+        compiler_params=params(26),
         cost_estimate=cost(4e10, 1e6),
         name="attend",
     )(f, q, q_marks, key_marks, *pieces)
@@ -304,7 +304,7 @@
             jax.ShapeDtypeStruct((2, heads_here, tokens, LANES), bf16),
             jax.ShapeDtypeStruct((2, heads_here, tokens, LANES), bf16),
         ],
-        compiler_params=params(48),
+        compiler_params=params(22),
         cost_estimate=cost(4e10, 1e6),
         name="attend_back",
     )(f, q, marks, key_marks, *pieces, grad, attended, cos, sin)
@@ -332,55 +332,33 @@
     ]
 
 
-def tile_copies(info, bit, t, pieces, target, sems):
-    own, near, far_mine, far_other, last_mine, last_other = pieces
+def side_copies(info, bit, pieces, target, sems):
     f = info[0]
-    rows, width = own.shape[0], target.shape[2]
-    chip = (f >> 1) ^ t
-
-    def copy(source, m):
+    rows = pieces[0].shape[0]
+    copies = []
+    for k, (m, which) in enumerate(((0, None), (1, None), (2, 0), (2, 1), (3, 0), (3, 1))):
         at = pl.ds(pl.multiple_of((f ^ m) * rows, 16), rows)
-        return lambda: pltpu.make_async_copy(source, target.at[t, at, :], sems.at[t, m])
-
-    columns = pl.ds(pl.multiple_of(chip * width, width), width)
-    mine = chip == info[bit]
-    return [
-        (None, copy(own.at[:, columns], 0)),
-        (None, copy(near.at[:, columns], 1)),
-        (mine, copy(far_mine, 2)),
-        (~mine, copy(far_other, 2)),
-        (mine, copy(last_mine, 3)),
-        (~mine, copy(last_other, 3)),
-    ]
-
-
-def start_tile(copies):
-    for condition, copy in copies:
-        if condition is None:
-            copy().start()
+        if which is None:
+            place = target.at[at, :]
         else:
-            pl.when(condition)(lambda copy=copy: copy().start())
-
-
-def wait_tile(copies):
-    for k in (0, 1, 2, 4):
-        copies[k][1]().wait()
-
-
-def down_copies(info, bit, t, pieces, target, sems):
+            width = pieces[k].shape[1]
+            place = target.at[at, pl.ds(pl.multiple_of((info[bit] ^ which) * width, width), width)]
+        copies.append(pltpu.make_async_copy(pieces[k], place, sems.at[k]))
+    return copies
+
+
+def down_copies(info, bit, pieces, target, sems):
     f = info[0]
     width = pieces[0].shape[1]
     copies = []
-    for m in (2 * t, 2 * t + 1):
-        columns = pl.ds(pl.multiple_of(((f ^ m) & 1) * width, width), width)
-        if t == 0:
-            copies.append(pltpu.make_async_copy(pieces[m], target.at[t, :, columns], sems.at[m, 0]))
-            continue
-        for k in (0, 1):
-            source = pieces[2 + 2 * (m - 2) + k]
-            rows = source.shape[0]
-            at = pl.ds(pl.multiple_of((info[bit] ^ k) * rows, 16), rows)
-            copies.append(pltpu.make_async_copy(source, target.at[t, at, columns], sems.at[m, k]))
+    for k, (m, which) in enumerate(((0, None), (1, None), (2, 0), (2, 1), (3, 0), (3, 1))):
+        at = pl.ds(pl.multiple_of((f ^ m) * width, width), width)
+        if which is None:
+            place = target.at[:, at]
+        else:
+            rows = pieces[k].shape[0]
+            place = target.at[pl.ds(pl.multiple_of((info[bit] ^ which) * rows, 16), rows), at]
+        copies.append(pltpu.make_async_copy(pieces[k], place, sems.at[k]))
     return copies
 
 
@@ -435,26 +413,29 @@
     )(turned, came)
 
 
-def part_kernel(rows, first, second):
+def part_kernel(f_ref, rows, first, second):
     half = rows.shape[0] // 2
     first[...] = rows[:half, :].T
     second[...] = rows[half:, :].T
 
 
-def part(rows):
+def part(f, rows):
     tokens, width = rows.shape
     half = tokens // 2
-    spec = pl.BlockSpec((width, half), lambda i: (0, 0))
+    spec = pl.BlockSpec((width, half), lambda i, f: (0, 0))
     return pl.pallas_call(
         part_kernel,
-        grid=(1,),
-        in_specs=[pl.BlockSpec((tokens, width), lambda i: (0, 0))],
-        out_specs=[spec, spec],
+        grid_spec=pltpu.PrefetchScalarGridSpec(
+            num_scalar_prefetch=1,
+            grid=(1,),
+            in_specs=[pl.BlockSpec((tokens, width), lambda i, f: (0, 0))],
+            out_specs=[spec, spec],
+        ),
         out_shape=[jax.ShapeDtypeStruct((width, half), bf16)] * 2,
         compiler_params=params(16),
-        cost_estimate=cost(4e10, 1e6),
+        cost_estimate=cost(4e9, 1e6),
         name="part",
-    )(rows)
+    )(f, rows)
 
 
 def pack_kernel(key_t, value_t, query, out):
@@ -531,7 +512,7 @@
         ),
         out_shape=[like((width, tokens), bf16), like((HEADS, tokens, LANES), bf16)]
         + [like((heads_here, tokens, LANES), bf16) for _, heads_here in GROUPS],
-        compiler_params=params(40),
+        compiler_params=params(20),
         cost_estimate=cost(4e10, 1e6),
         name="project",
     )(f, hidden, gain, cos, sin, *pieces)
@@ -551,69 +532,50 @@
     attended, gain = refs[:PARTS], refs[PARTS]
     o, gate, up, down, refs = split_pieces(refs[PARTS + 1 :])
     outs, result = refs[:6], refs[6]
-    w_o, w_gate, w_up, w_down, n16, acc, *refs = refs[7:]
+    w_o, w_gate, w_up, w_down, n16, *refs = refs[7:]
     after, attended_t, normed_t, gate_out, up_out, hidden_out = refs[:6]
     o_sem, gate_sem, up_sem, down_sem, out_sem = refs[6:]
-    f = f_ref[0]
-    tiles, depth, wide = w_gate.shape[0], 4 * o[0].shape[0], w_gate.shape[2]
-
-    def leave(k, tile=0):
-        source, target = refs[k], outs[k]
-        if len(source.shape) == 3:
-            source, target = source.at[tile], target.at[tile]
-        return pltpu.make_async_copy(source, target, out_sem.at[k, tile])
-
-    bring = [
-        lambda: start_tile(tile_copies(f_ref, 2, 0, up, w_up, up_sem)),
-        lambda: start(down_copies(f_ref, 1, 0, down, w_down, down_sem)),
-        lambda: start_tile(tile_copies(f_ref, 1, 1, gate, w_gate, gate_sem)),
-        lambda: start_tile(tile_copies(f_ref, 2, 1, up, w_up, up_sem)),
-        lambda: start(down_copies(f_ref, 1, 1, down, w_down, down_sem)),
-    ]
-    start(row_copies(f, o, w_o, o_sem))
-    start_tile(tile_copies(f_ref, 1, 0, gate, w_gate, gate_sem))
+    depth, wide = 4 * o[0].shape[0], w_gate.shape[1]
+    o_copies = row_copies(f_ref[0], o, w_o, o_sem)
+    gate_copies = side_copies(f_ref, 1, gate, w_gate, gate_sem)
+    up_copies = side_copies(f_ref, 2, up, w_up, up_sem)
+    d_copies = down_copies(f_ref, 1, down, w_down, down_sem)
+    half = wide // 2
+
+    def leave(k, part=None):
+        if part is None:
+            return pltpu.make_async_copy(refs[k], outs[k], out_sem.at[k, 0])
+        columns = slice(part * half, (part + 1) * half)
+        return pltpu.make_async_copy(refs[k].at[:, columns], outs[k].at[:, columns], out_sem.at[k, part])
+
+    leaving = [leave(k) for k in range(3)] + [leave(k, part) for part in (0, 1) for k in (3, 4, 5)]
+    for copies in (o_copies, gate_copies, up_copies, d_copies):
+        start(copies)
     att = jnp.concatenate([attended[i][...] for i in ORDER], axis=1)
     attended_t[...] = att.T
-    leave(1).start()
     w_o[depth:, :] = jnp.zeros((w_o.shape[0] - depth, w_o.shape[1]), bf16)
-    wait(row_copies(f, o, w_o, o_sem))
-    bring.pop(0)()
+    wait(o_copies)
     value = h[...].astype(f32) + nn(att, w_o[...])
     after[...] = value
     normed = (value * inverse_of(value) * gain[...]).astype(bf16)
     n16[...] = normed
     normed_t[...] = normed.T
-    for t in range(tiles):
-        wait_tile(tile_copies(f_ref, 1, t, gate, w_gate, gate_sem))
-        if t == 0:
-            bring.pop(0)()
-        wait_tile(tile_copies(f_ref, 2, t, up, w_up, up_sem))
-        for at in range(0, wide, CHUNK):
-            columns = slice(at, at + CHUNK)
-            gate_act = nn(n16[...], w_gate[t, :, columns])
-            up_act = nn(n16[...], w_up[t, :, columns])
-            hidden = gate_act * jax.nn.sigmoid(gate_act) * up_act
-            gate_out[t, :, columns] = gate_act.astype(bf16)
-            up_out[t, :, columns] = up_act.astype(bf16)
-            hidden_out[t, :, columns] = hidden.astype(bf16)
-            if bring and at < 2 * CHUNK:
-                bring.pop(0)()
-        if t == 0:
-            leave(0).start()
-            leave(2).start()
-        for k in (3, 4, 5):
-            leave(k, t).start()
-        wait(down_copies(f_ref, 1, t, down, w_down, down_sem))
-        if bring:
-            bring.pop(0)()
-        part = nt(hidden_out[t], w_down[t])
-        acc[...] = part if t == 0 else acc[...] + part
-    result[...] = (after[...] + acc[...]).astype(result.dtype)
-    for k in (0, 1, 2):
-        leave(k).wait()
-    for t in range(tiles):
-        for k in (3, 4, 5):
-            leave(k, t).wait()
+    wait(gate_copies)
+    wait(up_copies)
+    for at in range(0, wide, CHUNK):
+        columns = slice(at, at + CHUNK)
+        gate_act = nn(n16[...], w_gate[:, columns])
+        up_act = nn(n16[...], w_up[:, columns])
+        hidden = gate_act * jax.nn.sigmoid(gate_act) * up_act
+        gate_out[:, columns] = gate_act.astype(bf16)
+        up_out[:, columns] = up_act.astype(bf16)
+        hidden_out[:, columns] = hidden.astype(bf16)
+        if at + CHUNK == half:
+            start(leaving[:6])
+    start(leaving[6:])
+    wait(d_copies)
+    result[...] = (after[...] + nt(hidden_out[...], w_down[...])).astype(result.dtype)
+    wait(leaving)
 
 
 def weight_scratch(o, gate):
@@ -621,24 +583,24 @@
     columns = gate.shape[1]
     return [
         pltpu.VMEM((4 * rows + HEAD, width), bf16),
-        pltpu.VMEM((2, 4 * rows, columns // 2), bf16),
-        pltpu.VMEM((2, 4 * rows, columns // 2), bf16),
-        pltpu.VMEM((2, width, columns // 2), bf16),
+        pltpu.VMEM((4 * rows, columns), bf16),
+        pltpu.VMEM((4 * rows, columns), bf16),
+        pltpu.VMEM((width, columns), bf16),
     ]
 
 
 def weight_sems():
     dma = pltpu.SemaphoreType.DMA
-    return [dma((4,)), dma((2, 4)), dma((2, 4)), dma((4, 2))]
+    return [dma((4,)), dma((6,)), dma((6,)), dma((6,))]
 
 
 def feed(f, hidden, attended, gain, o, gate, up, down, result_type):
     tokens, width = hidden.shape
-    wide = gate[0].shape[1] // 2
+    wide = gate[0].shape[1]
     lanes = (HEADS + 1) * HEAD
     full = lambda *shape: pl.BlockSpec(shape, lambda i, f: (0,) * len(shape))
     like = jax.ShapeDtypeStruct
-    kept = [((tokens, width), f32), ((lanes, tokens), bf16), ((width, tokens), bf16)] + [((2, tokens, wide), bf16)] * 3
+    kept = [((tokens, width), f32), ((lanes, tokens), bf16), ((width, tokens), bf16)] + [((tokens, wide), bf16)] * 3
     return pl.pallas_call(
         feed_kernel,
         grid_spec=pltpu.PrefetchScalarGridSpec(
@@ -647,13 +609,13 @@
             in_specs=[full(tokens, width)] + [full(*a.shape) for a in attended] + [full(1, width)] + [ANY] * 22,
             out_specs=[ANY] * 6 + [full(tokens, width)],
             scratch_shapes=weight_scratch(o[0], gate[0])
-            + [pltpu.VMEM((tokens, width), bf16), pltpu.VMEM((tokens, width), f32)]
+            + [pltpu.VMEM((tokens, width), bf16)]
             + [pltpu.VMEM(*k) for k in kept]
             + weight_sems()
             + [pltpu.SemaphoreType.DMA((6, 2))],
         ),
         out_shape=[like(*k) for k in kept] + [like((tokens, width), result_type)],
-        compiler_params=params(56),
+        compiler_params=params(48),
         cost_estimate=cost(4e10, 1e6),
         name="feed",
     )(f, hidden, *attended, gain, *o, *gate, *up, *down)
@@ -664,59 +626,46 @@
     o, gate, up, down, refs = split_pieces(refs[3:])
     outs, grad_after, branch_out = refs[:2], refs[2], refs[3]
     grad_attended, gain_grad = refs[4 : 4 + PARTS], refs[4 + PARTS]
-    w_o, w_gate, w_up, w_down, g16, acc, *refs = refs[5 + PARTS :]
+    w_o, w_gate, w_up, w_down, g16, *refs = refs[5 + PARTS :]
     after, gate_act, up_act, grad_gate, grad_up, o_sem, gate_sem, up_sem, down_sem, in_sem, out_sem = refs
-    f = f_ref[0]
-    tiles, depth, wide = w_gate.shape[0], 4 * o[0].shape[0], w_gate.shape[2]
-
-    def arrive(k, tile=0):
-        source, target = held[k], refs[k]
-        if k:
-            source, target = source.at[tile], target.at[tile]
-        return pltpu.make_async_copy(source, target, in_sem.at[k, tile])
-
-    def leave(k, tile):
-        return pltpu.make_async_copy(refs[3 + k].at[tile], outs[k].at[tile], out_sem.at[k, tile])
-
-    def bring_first(t):
-        start(down_copies(f_ref, 1, t, down, w_down, down_sem))
-        arrive(1, t).start()
-        arrive(2, t).start()
-
-    bring_first(0)
+    depth, wide = 4 * o[0].shape[0], w_gate.shape[1]
+    half = wide // 2
+    o_copies = row_copies(f_ref[0], o, w_o, o_sem)
+    gate_copies = side_copies(f_ref, 1, gate, w_gate, gate_sem)
+    up_copies = side_copies(f_ref, 2, up, w_up, up_sem)
+    d_copies = down_copies(f_ref, 1, down, w_down, down_sem)
+
+    def act_copies(part):
+        columns = slice(part * half, (part + 1) * half)
+        return [
+            pltpu.make_async_copy(held[k].at[:, columns], refs[k].at[:, columns], in_sem.at[k, part]) for k in (1, 2)
+        ]
+
+    after_copy = pltpu.make_async_copy(held[0], after, in_sem.at[0, 0])
+    leave = [pltpu.make_async_copy(refs[3 + k], outs[k], out_sem.at[k]) for k in (0, 1)]
+    first, second = act_copies(0), act_copies(1)
+    for copies in (d_copies, first, second, gate_copies, up_copies, [after_copy], o_copies):
+        start(copies)
     g16[...] = g[...].astype(bf16)
     w_o[depth:, :] = jnp.zeros((w_o.shape[0] - depth, w_o.shape[1]), bf16)
-    for t in range(tiles):
-        wait(down_copies(f_ref, 1, t, down, w_down, down_sem))
-        arrive(1, t).wait()
-        arrive(2, t).wait()
-        start_tile(tile_copies(f_ref, 1, t, gate, w_gate, gate_sem))
-        for at in range(0, wide, CHUNK):
+    wait(d_copies)
+    for part, copies in enumerate((first, second)):
+        wait(copies)
+        for at in range(part * half, (part + 1) * half, CHUNK):
             columns = slice(at, at + CHUNK)
-            grad_hidden = nn(g16[...], w_down[t, :, columns])
-            value = gate_act[t, :, columns].astype(f32)
+            grad_hidden = nn(g16[...], w_down[:, columns])
+            value = gate_act[:, columns].astype(f32)
             logistic = jax.nn.sigmoid(value)
             steep = logistic * (1.0 + value * (1.0 - logistic))
-            grad_gate[t, :, columns] = (grad_hidden * up_act[t, :, columns].astype(f32) * steep).astype(bf16)
-            grad_up[t, :, columns] = (grad_hidden * (value * logistic)).astype(bf16)
-            if at == CHUNK:
-                start_tile(tile_copies(f_ref, 2, t, up, w_up, up_sem))
-        leave(0, t).start()
-        leave(1, t).start()
-        wait_tile(tile_copies(f_ref, 1, t, gate, w_gate, gate_sem))
-        part = nt(grad_gate[t], w_gate[t])
-        acc[...] = part if t == 0 else acc[...] + part
-        wait_tile(tile_copies(f_ref, 2, t, up, w_up, up_sem))
-        if t + 1 < tiles:
-            bring_first(t + 1)
-        else:
-            arrive(0).start()
-            start(row_copies(f, o, w_o, o_sem))
-        part = nt(grad_up[t], w_up[t])
-        acc[...] += part
-    arrive(0).wait()
-    wait(row_copies(f, o, w_o, o_sem))
-    back, gain_part = norm_back(acc[...], after[...], gain[...])
+            grad_gate[:, columns] = (grad_hidden * up_act[:, columns].astype(f32) * steep).astype(bf16)
+            grad_up[:, columns] = (grad_hidden * (value * logistic)).astype(bf16)
+    wait(gate_copies)
+    wait(up_copies)
+    start(leave)
+    grad_normed = nt(grad_gate[...], w_gate[...]) + nt(grad_up[...], w_up[...])
+    wait([after_copy])
+    wait(o_copies)
+    back, gain_part = norm_back(grad_normed, after[...], gain[...])
     back = back + g[...].astype(f32)
     gain_grad[...] = gain_part
     grad_after[...] = back
@@ -728,18 +677,15 @@
         lanes = grad_attended[i].shape[1]
         grad_attended[i][...] = whole[:, at : at + lanes]
         at += lanes
-    for t in range(tiles):
-        leave(0, t).wait()
-        leave(1, t).wait()
+    wait(leave)
 
 
 def feed_back(f, g, after, gain, gate_act, up_act, o, gate, up, down):
     tokens, width = after.shape
-    wide = gate[0].shape[1] // 2
+    wide = gate[0].shape[1]
     full = lambda *shape: pl.BlockSpec(shape, lambda i, f: (0,) * len(shape))
     like = jax.ShapeDtypeStruct
     lanes = [pair_lanes(heads_here) for _, heads_here in GROUPS]
-    tile = (2, tokens, wide)
     dma = pltpu.SemaphoreType.DMA
     return pl.pallas_call(
         feed_back_kernel,
@@ -752,15 +698,15 @@
             + [full(1, width)],
             scratch_shapes=weight_scratch(o[0], gate[0])
             + [pltpu.VMEM((tokens, width), bf16), pltpu.VMEM((tokens, width), f32)]
-            + [pltpu.VMEM((tokens, width), f32)]
-            + [pltpu.VMEM(tile, bf16)] * 4
+            + [pltpu.VMEM((tokens, wide), bf16)] * 4
             + weight_sems()
-            + [dma((3, 2)), dma((2, 2))],
+            + [dma((3, 2)), dma((2,))],
         ),
-        out_shape=[like(tile, bf16), like(tile, bf16), like((tokens, width), f32), like((tokens, width), bf16)]
+        out_shape=[like((tokens, wide), bf16)] * 2
+        + [like((tokens, width), f32), like((tokens, width), bf16)]
         + [like((tokens, n), bf16) for n in lanes]
         + [like((1, width), f32)],
-        compiler_params=params(56),
+        compiler_params=params(52),
         cost_estimate=cost(4e10, 1e6),
         name="feed_back",
     )(f, g, gain, after, gate_act, up_act, *o, *gate, *up, *down)
@@ -816,106 +762,109 @@
             like((width, tokens), bf16),
             like((1, width), f32),
         ],
-        compiler_params=params(40),
+        compiler_params=params(20),
         cost_estimate=cost(4e10, 1e6),
         name="project_back",
     )(f, *arrays, *pieces)
 
 
-def outer_tiles_kernel(f_ref, *refs, rows):
-    left_first, left_second, right_first, right_second, keep, send, acc = refs
-    left = jnp.concatenate([left_first[...], left_second[...]], axis=1)
-    acc[...] = nn(left, jnp.concatenate([right_first[0], right_second[0]], axis=0))
+def joined(left_first, left_second, right_first, right_second):
+    left = jnp.concatenate([left_first, left_second], axis=1)
+    return nn(left, jnp.concatenate([right_first, right_second], axis=0))
+
+
+def outer_tiles_kernel(f_ref, left_first, left_second, right_first, right_second, *refs, rows):
+    outs, acc = refs[:4], refs[4]
+    acc[...] = joined(left_first[...], left_second[...], right_first[...], right_second[...])
     half = acc.shape[1] // 2
     for m in range(4):
-        out = send if m % 2 else keep
         from_row = pl.multiple_of((f_ref[0] ^ m) * rows, 16)
         for c in (0, 1):
-            out[m // 2, c] = acc[pl.ds(from_row, rows), c * half : (c + 1) * half].astype(bf16)
+            outs[m][c] = acc[pl.ds(from_row, rows), c * half : (c + 1) * half].astype(bf16)
 
 
 def outer_tiles(f, lefts, rights, rows, name):
     width, tokens = lefts[0].shape
-    wide = rights[0].shape[2]
+    wide = rights[0].shape[1] // 2
     left = pl.BlockSpec((width, tokens), lambda i, f: (0, 0))
-    right = pl.BlockSpec((1, tokens, wide), lambda i, f: (i, 0, 0))
-    out = pl.BlockSpec((2, 2, rows, wide // 2), lambda i, f: (0, (f[0] >> 1) ^ i, 0, 0))
+    right = pl.BlockSpec((tokens, wide), lambda i, f: (0, i))
+    out = pl.BlockSpec((2, rows, wide // 2), lambda i, f: (i, 0, 0))
     return pl.pallas_call(
         functools.partial(outer_tiles_kernel, rows=rows),
         grid_spec=pltpu.PrefetchScalarGridSpec(
             num_scalar_prefetch=1,
             grid=(2,),
             in_specs=[left, left, right, right],
-            out_specs=[out, out],
+            out_specs=[out] * 4,
             scratch_shapes=[pltpu.VMEM((width, wide), f32)],
         ),
-        out_shape=[jax.ShapeDtypeStruct((2, 4, rows, wide // 2), bf16)] * 2,
-        compiler_params=params(48),
+        out_shape=[jax.ShapeDtypeStruct((4, rows, wide // 2), bf16)] * 4,
+        compiler_params=params(28),
         cost_estimate=cost(4e10, 1e6),
         name=name,
     )(f, *lefts, *rights)
 
 
-def outer_down_kernel(f_ref, left_first, left_second, right_first, right_second, keep, send):
-    left = jnp.concatenate([left_first[...], left_second[...]], axis=1)
-    value = nn(left, jnp.concatenate([right_first[0], right_second[0]], axis=0))
+def outer_down_kernel(f_ref, left_first, left_second, right_first, right_second, own, near):
+    value = joined(left_first[...], left_second[...], right_first[...], right_second[...])
     half = value.shape[1] // 2
-    own = (f_ref[0] & 1) == 0
+    first = (f_ref[0] & 1) == 0
     lower, upper = value[:, :half], value[:, half:]
-    keep[0, 0] = jnp.where(own, lower, upper).astype(bf16)
-    send[0, 0] = jnp.where(own, upper, lower).astype(bf16)
-
-
-def outer_down(f, lefts, rights, name):
+    own[0] = jnp.where(first, lower, upper).astype(bf16)
+    near[0] = jnp.where(first, upper, lower).astype(bf16)
+
+
+def outer_down(f, lefts, rights, chip, name):
     width, tokens = lefts[0].shape
-    wide = rights[0].shape[2]
+    wide = rights[0].shape[1] // 2
     left = pl.BlockSpec((width, tokens), lambda i, f: (0, 0))
-    right = pl.BlockSpec((1, tokens, wide), lambda i, f: (i, 0, 0))
-    out = pl.BlockSpec((1, 1, width, wide // 2), lambda i, f: (i, 0, 0, 0))
+    right = pl.BlockSpec((tokens, wide), lambda i, f: (0, (f[0] >> 1) ^ chip))
+    out = pl.BlockSpec((1, width, wide // 2), lambda i, f: (0, 0, 0))
     return pl.pallas_call(
         outer_down_kernel,
         grid_spec=pltpu.PrefetchScalarGridSpec(
             num_scalar_prefetch=1,
-            grid=(2,),
+            grid=(1,),
             in_specs=[left, left, right, right],
             out_specs=[out, out],
         ),
-        out_shape=[jax.ShapeDtypeStruct((2, 1, width, wide // 2), bf16)] * 2,
-        compiler_params=params(48),
+        out_shape=[jax.ShapeDtypeStruct((1, width, wide // 2), bf16)] * 2,
+        compiler_params=params(28),
         cost_estimate=cost(4e10, 1e6),
         name=name,
     )(f, *lefts, *rights)
 
 
-def outer_kernel(f_ref, left_first, left_second, right_first, right_second, extra, keep, send, acc, *, rows):
-    left = jnp.concatenate([left_first[...], left_second[...]], axis=1)
-    acc[...] = nn(left, jnp.concatenate([right_first[...], right_second[...]], axis=0))
-    spare = keep.shape[2] - rows
+def outer_kernel(f_ref, left_first, left_second, right_first, right_second, extra, *refs, rows):
+    outs, acc = refs[:4], refs[4]
+    acc[...] = joined(left_first[...], left_second[...], right_first[...], right_second[...])
+    columns = acc.shape[1]
     for m in range(4):
-        out = send if m % 2 else keep
         device = f_ref[0] ^ m
-        out[m // 2, 0, :rows] = acc[pl.ds(pl.multiple_of(device * rows, 16), rows), :].astype(bf16)
-        out[m // 2, 0, rows:] = jnp.zeros((spare, acc.shape[1]), bf16)
-        out[m // 2, 0, rows:, : extra.shape[2]] = extra[device]
+        out = outs[m]
+        if columns < out.shape[2]:
+            out[0, :, columns:] = jnp.zeros((out.shape[1], out.shape[2] - columns), bf16)
+        out[0, :rows, :columns] = acc[pl.ds(pl.multiple_of(device * rows, 16), rows), :].astype(bf16)
+        out[0, rows:, :columns] = jnp.zeros((out.shape[1] - rows, columns), bf16)
+        out[0, rows:, : extra.shape[2]] = extra[device]
 
 
 def outer(f, lefts, rights, extra, rows, name):
     width, tokens = lefts[0].shape
-    columns = rights[0].shape[1]
-    padded = rows + extra.shape[1]
+    height, columns = 4 * rows, rights[0].shape[1]
+    shape = (1, rows + extra.shape[1], -(-columns // LANES) * LANES)
     full = lambda *shape: pl.BlockSpec(shape, lambda i, f: (0,) * len(shape))
-    height = width if width % (4 * rows) == 0 else width
     return pl.pallas_call(
         functools.partial(outer_kernel, rows=rows),
         grid_spec=pltpu.PrefetchScalarGridSpec(
             num_scalar_prefetch=1,
             grid=(1,),
-            in_specs=[full(width, tokens)] * 2 + [full(tokens, columns)] * 2 + [full(*extra.shape)],
-            out_specs=[full(2, 1, padded, columns)] * 2,
+            in_specs=[full(height, tokens)] * 2 + [full(tokens, columns)] * 2 + [full(*extra.shape)],
+            out_specs=[full(*shape)] * 4,
             scratch_shapes=[pltpu.VMEM((height, columns), f32)],
         ),
-        out_shape=[jax.ShapeDtypeStruct((2, 1, padded, columns), bf16)] * 2,
-        compiler_params=params(48),
+        out_shape=[jax.ShapeDtypeStruct(shape, bf16)] * 4,
+        compiler_params=params(28),
         cost_estimate=cost(4e10, 1e6),
         name=name,
     )(f, *lefts, *rights, extra)
@@ -958,14 +907,7 @@
 
 
 def levels_of(size):
-    bits = size.bit_length() - 1
-    levels = [(0, 2)] if bits else []
-    at = 1
-    while at < bits:
-        step = min(2, bits - at)
-        levels.append((at, 1 << step))
-        at += step
-    return levels
+    return [(bit, 2) for bit in range(size.bit_length() - 1)]
 
 
 def cut(array, count):
@@ -992,15 +934,18 @@
     return parts[0]
 
 
-def reduction(keep, send, halves):
-    shape = keep.shape[1:]
-    (near,) = yield [(send, "fsdp", 1)]
-    far = [add(k, n).astype(bf16) for k, n in zip(cut(keep[1], halves), cut(near[1], halves))]
-    came = []
-    for piece in far:
-        came += yield [(piece, "fsdp", 2)]
-    came = glue(came, shape) if halves > 1 else came[0]
-    part = add(keep[0], near[0]) + came.astype(f32)
+def reduction(own, near, far, last, halves):
+    shape = own.shape
+    if last is None:
+        beside, first = yield [(near, "fsdp", 1), (far, "fsdp", 2)]
+        crossed = [first]
+    else:
+        came, beside = yield [(last, "fsdp", 1), (near, "fsdp", 1)]
+        crossed = []
+        for ours, theirs in zip(cut(far, halves), cut(came, halves)):
+            crossed += yield [(add(ours, theirs).astype(bf16), "fsdp", 2)]
+    crossed = glue(crossed, shape) if halves > 1 else crossed[0]
+    part = add(own, beside) + crossed.astype(f32)
     index = lax.axis_index("dp")
     shapes = []
     for bit, count in levels_of(lax.axis_size("dp")):
@@ -1021,8 +966,8 @@
 
 
 class Unit:
-    def __init__(self, keep, send, halves=1):
-        self.steps = reduction(keep, send, halves)
+    def __init__(self, own, near, far, last, halves=1):
+        self.steps = reduction(own, near, far, last, halves)
         self.asks = next(self.steps)
         self.total = None
 
@@ -1101,8 +1046,8 @@
 
     w_own = pack(w_key, w_value, w_query)
     (w_far, w_near, other_tokens), _ = clock.phase([(w_own, *y), (w_own, *core), (tokens_t[:, half:], "fsdp", 3)])
-    (w_last, w_o_far), (h0, _) = clock.phase(
-        [(w_far, *core), (w_output, *y)], lambda turn: join(tokens_t, other_tokens), extra=(key_marks, q_marks, cos, sin)
+    (w_last, gate_far), (h0, _) = clock.phase(
+        [(w_far, *core), across("gate")], lambda turn: join(tokens_t, other_tokens), extra=(key_marks, q_marks, cos, sin)
     )
     w_in = (w_own, w_near, w_far, w_last)
 
@@ -1137,38 +1082,42 @@
         came.append(got)
         return (normed_t, q, gathered, attended, marks), came
 
-    def feed_phase(hidden, weights, run, result_type):
+    def feed_phase(hidden, weights, run, result_type, moves=()):
         normed_t, q, gathered, attended, marks = run
-        _, (after, attended_t, normed_ffn_t, gate_act, up_act, hidden_act, result) = clock.phase(
-            (), lambda turn: feed(turn, hidden, attended, gain_f, *weights, result_type)
+        got, (after, attended_t, normed_ffn_t, gate_act, up_act, hidden_act, result) = clock.phase(
+            moves, lambda turn: feed(turn, hidden, attended, gain_f, *weights, result_type)
         )
-        return result, (
+        return result, got, (
             hidden, normed_t, q, gathered, attended, marks, after, attended_t, normed_ffn_t, gate_act, up_act, hidden_act,
         )
 
     none = lambda came: []
     run, came = attend_phases(
         h0,
-        [across("gate")],
+        [across("up"), (gate_far, *side[0])],
         (
-            lambda came: [(w_o_far, *core)],
-            lambda came: [(came[0][0], *side[0])],
-            lambda came: [across("up")],
-            lambda came: [across("down"), (came[3][0], *side[1])],
-            lambda came: [(came[4][0], *side[0])] + [(shards[n], *core) for n in shards] + [(w_output, *core)],
+            lambda came: [(w_output, *core), (w_gate, *core)],
+            lambda came: [across("down"), (came[0][0], *side[1])],
+            lambda came: [(w_output, *y), (came[2][0], *side[0]), (w_up, *core)],
+            lambda came: [(gate_far, *core), (came[0][1], *core), (came[0][0], *core), (came[2][1], *core)],
+            lambda came: [(came[2][0], *core), (came[3][1], *core), (down_t, *core), (came[3][0], *core)],
         ),
     )
-    fars = {"gate": (came[0][0], came[2][0]), "up": (came[3][0], came[4][1]), "down": (came[4][0], came[5][0])}
-    nears = dict(zip(shards, came[5][1:4]))
-    lasts, _ = clock.phase([(x, *core) for n in shards for x in fars[n]])
-    lasts = {n: tuple(lasts[2 * i : 2 * i + 2]) for i, n in enumerate(shards)}
-    o = (w_output, came[5][4], w_o_far, came[1][0])
-    weights = (o,) + tuple((shards[n], nears[n], *fars[n], *lasts[n]) for n in ("gate", "up", "down"))
-    h1, first = feed_phase(h0, weights, run, f32)
-
-    run, came = attend_phases(h1, [], (none, none, none, lambda came: [(cotangent_t[:, half:], "fsdp", 3)], none))
-    other_cotangent = came[4][0]
-    h2, second = feed_phase(h1, weights, run, bf16)
+    up_far, gate_other = came[0]
+    down_far, up_other = came[2]
+    o_near, gate_near = came[1]
+    o_far, down_other, up_near = came[3]
+    gate_last, gate_other_last, up_last, up_other_last = came[4]
+    down_last, down_other_last, down_near, o_last = came[5]
+    weights = (
+        (w_output, o_near, o_far, o_last),
+        (w_gate, gate_near, gate_far, gate_other, gate_last, gate_other_last),
+        (w_up, up_near, up_far, up_other, up_last, up_other_last),
+        (down_t, down_near, down_far, down_other, down_last, down_other_last),
+    )
+    h1, (other_cotangent,), first = feed_phase(h0, weights, run, f32, [(cotangent_t[:, half:], "fsdp", 3)])
+    run, _ = attend_phases(h1, [], (none,) * 5)
+    h2, _, second = feed_phase(h1, weights, run, bf16)
     _, (cot, cot_turned) = clock.phase((), lambda turn: join(cotangent_t, other_cotangent))
 
     def feed_back_work(g, stored):
@@ -1220,62 +1169,64 @@
         )
 
     _, fed2 = clock.phase((), feed_back_work(cot, second))
-    out_first, out_second = part(h2)
+    out_first, out_second = part(f, h2)
     parts, extra = back_phases(
         fed2[4 : 4 + PARTS], second, lambda k: ([(out_second, "fsdp", 3)] if k == 0 else [], ())
     )
     output = jnp.concatenate([out_first, extra[0]], axis=1).T
     _, (grads2, middle, middle_turned, gain_a2) = clock.phase((), project_back_work(parts, second, fed2[2], f32))
 
-    _, down_pair = clock.phase(
-        (), lambda turn: outer_down(turn, (middle_turned, cot_turned), (first[11], second[11]), "outer_down")
-    )
-    down = Unit(*down_pair, 2)
+    def down_work(chip, name):
+        return lambda turn: outer_down(turn, (middle_turned, cot_turned), (first[11], second[11]), chip, name)
+
+    _, far_pair = clock.phase((), down_work(1, "outer_down_far"))
+    (far_beside,), own_pair = clock.phase([(far_pair[1], *core)], down_work(0, "outer_down_own"))
+    down = Unit(*own_pair, add(far_pair[0], far_beside).astype(bf16), None)
     _, fed1 = clock.phase((), feed_back_work(middle, first), (down,))
 
     def outer_work(i, name):
         return lambda turn: outer_tiles(turn, (first[8], second[8]), (fed1[i], fed2[i]), shard_rows, name)
 
     nothing = jnp.zeros((4, 16, LANES), bf16)
-    _, gate_pair = clock.phase((), outer_work(0, "outer_gate"), (down,))
-    gate = Unit(*gate_pair, 2)
-    _, up_pair = clock.phase((), outer_work(1, "outer_up"), (down, gate))
-    up = Unit(*up_pair, 2)
-    _, o_pair = clock.phase(
+    _, gate_parts = clock.phase((), outer_work(0, "outer_gate"))
+    gate = Unit(*gate_parts, 2)
+    _, (up_parts, o_parts) = clock.phase(
         (),
-        lambda turn: outer(turn, (first[7], second[7]), (fed1[3], fed2[3]), nothing, shard_rows, "outer_o"),
-        (down, up),
+        lambda turn: (
+            outer_work(1, "outer_up")(turn),
+            outer(turn, (first[7], second[7]), (fed1[3], fed2[3]), nothing, shard_rows, "outer_o"),
+        ),
+        (down, gate),
     )
-    out = Unit(*o_pair)
-    plan = ((gate, down, out), (gate, down), (down,), (), (gate,))
+    up, out = Unit(*up_parts, 2), Unit(*o_parts)
+    plan = ((gate, up, down, out), (gate, down), (up, gate, down), (gate,), ())
     parts, _ = back_phases(fed1[4 : 4 + PARTS], first, lambda k: ([], plan[k]))
     _, (grads1, grad_tokens, _, gain_a1) = clock.phase(
-        (), project_back_work(parts, first, fed1[2], bf16), (up, gate)
+        (), project_back_work(parts, first, fed1[2], bf16), (up, gate, down)
     )
     gains = jnp.concatenate([gain_a1 + gain_a2, fed1[4 + PARTS] + fed2[4 + PARTS]], axis=0)
     gains = gains.reshape(2, 4, width // 4).transpose(1, 0, 2).astype(bf16)
     gains = jnp.pad(gains, ((0, 0), (0, 14), (0, 256 - width // 4)))
-    _, in_pair = clock.phase(
+    _, in_parts = clock.phase(
         (),
         lambda turn: outer(turn, (first[1], second[1]), (grads1, grads2), gains, shard_rows, "outer_in"),
-        (up, gate),
+        (out, up, gate),
     )
-    into = Unit(*in_pair)
-    back_half, back_send = part(grad_tokens)
-    clock.phase((), None, (into, gate, up))
-    clock.phase((), None, (into, up))
-    clock.phase((), None, (out, into, up))
-    clock.phase((), None, (out, into, up))
-    (other_tokens,), _ = clock.phase([(back_send, "fsdp", 3)], None, (out, into))
+    into = Unit(*in_parts)
+    clock.phase((), None, (into, up, out))
+    _, (back_half, back_send) = clock.phase((), lambda turn: part(turn, grad_tokens), (into, up, gate, down, out))
+    clock.phase((), None, (into, up, out))
+    clock.phase((), None, (into, up, gate, out))
+    (other_tokens,), _ = clock.phase([(back_send, "fsdp", 3)], None, (into, up, out))
     grad_tokens = jnp.concatenate([back_half, other_tokens], axis=1).T
-    units = (down, gate, up, out, into)
+    units = (into, up, out, gate, down)
     while any(unit.asks for unit in units):
         clock.phase((), None, [unit for unit in units if unit.asks])
 
     grad_down = down.total[0].T.astype(f32)
     wide = lambda unit: jnp.concatenate([unit.total[i] for i in range(4)], axis=1).astype(f32)
     grad_gate, grad_up = wide(gate), wide(up)
-    grad_o = out.total[0, :shard_rows].astype(f32)
+    grad_o = out.total[0, :shard_rows, :width].astype(f32)
     total = into.total[0]
     grad_key, grad_value, grad_query = unpack(total, shard_rows)
     gains = total[shard_rows : shard_rows + 2, : width // 4].astype(f32)

time: 680 us -> 588 us (0.86)
  local copies, waits for them, and re-layouts: 56 us -> 24.5 us
  starting transfers between devices: 96.1 us -> 76.1 us
  Pallas kernels: 251 us -> 233 us
  waiting for transfers between devices: 227 us -> 211 us
  other arithmetic: 41.4 us -> 30.5 us
    unnamed x394 -> x334, local copies, waits for them, and re-layouts: 49.4 us -> 22.5 us
    ppermute x108 -> x102, starting transfers between devices: 96.1 us -> 76.1 us  [flip(): return lax.ppermute(array, axis, [(i, i ^ bit) for i in range(size)])]
    ppermute x108 -> x102, waiting for transfers between devices: 227 us -> 211 us  [flip(): return lax.ppermute(array, axis, [(i, i ^ bit) for i in range(size)])]
  transfers between devices with their start and end apart: 108 -> 102, of which waited for: 55 -> 45; matrix products, arithmetic and copies ran while one was open for 6% -> 5% of each run, Pallas kernels for 24% -> 28%
where the time goes in v3:
time: 588 us; the launch traced here: 579 us
  Pallas kernels  233 us (40%)
  waiting for transfers between devices  211 us (36%)
  starting transfers between devices  76.1 us (13%)
  other arithmetic  30.5 us (5%)
  local copies, waits for them, and re-layouts  24.5 us (4%)
    ppermute x102, waiting for transfers between devices, flip(): return lax.ppermute(array, axis, [(i, i ^ bit) for i in range(size)])  211 us
    ppermute x102, starting transfers between devices, flip(): return lax.ppermute(array, axis, [(i, i ^ bit) for i in range(size)])  76.1 us
    pallas_call x6, Pallas kernels, attend_back(): pl.pallas_call(attend_back_kernel, grid_spec=pltpu.PrefetchScalarGridSpec...  62.4 us
    pallas_call x2, Pallas kernels, feed_back(): pl.pallas_call(feed_back_kernel, grid_spec=pltpu.PrefetchScalarGridSpec(n...  44.4 us
    pallas_call x6, Pallas kernels, attend(): pl.pallas_call(attend_kernel, grid_spec=pltpu.PrefetchScalarGridSpec(num_...  37.3 us
    pallas_call x2, Pallas kernels, feed(): pl.pallas_call(feed_kernel, grid_spec=pltpu.PrefetchScalarGridSpec(num_sc...  35.3 us
    unnamed x334, local copies, waits for them, and re-layouts  22.5 us
    pallas_call x2, Pallas kernels, outer_tiles(): pl.pallas_call(functools.partial(outer_tiles_kernel, rows=rows), grid_spe...  14.1 us
  transfers between devices with their start and end apart: 102, of which 45 were waited for; matrix products, arithmetic and copies ran while one was open for 5% of the time, Pallas kernels for 28%

profile of v3, /device:TPU:0, one launch (start us, length us, event | category | flops | bytes accessed | tf_op | source)
XLA Modules:
  0.0 578.7 jit_solution(7467306378320017251)
XLA Ops:
  11.2 24.3 %collective-permute-done.2.second = bf16[960,256]{1,0:T(8,128)(2,1)S(1)} collective-permute-done((bf16[960,256]{1,0:T(8,128)(2,1)S(1)}, bf16[960,256]{1,0:T(8,128)(2,1)S(1)}, u32[]{:S(2)}, u32[]{:S(2)}) %collective-permute-start.2) | collective-permute-done | bytes 491552 | tf_op jit(solution)/shard_map/ppermute | solution.py:902
  38.8 13.1 %collective-permute-done.3.refs_10_.refs_9_ = bf16[240,1280]{1,0:T(8,128)(2,1)S(1)} collective-permute-done((bf16[240,1280]{1,0:T(8,128)(2,1)S(1)}, bf16[240,1280]{1,0:T(8,128)(2,1)S(1)}, u32[]{:S(2)}, u32[]{:S(2)}) %collective-permute-start.3) | collective-permute-done | bytes 614432 | tf_op jit(solution)/shard_map/ppermute | solution.py:902
  55.2 4.3 project.2
  60.5 7.3 %collective-permute-done.5.refs_16_.refs_15_ = bf16[240,1280]{1,0:T(8,128)(2,1)S(1)} collective-permute-done((bf16[240,1280]{1,0:T(8,128)(2,1)S(1)}, bf16[240,1280]{1,0:T(8,128)(2,1)S(1)}, u32[]{:S(2)}, u32[]{:S(2)}) %collective-permute-start.5) | collective-permute-done | bytes 614432 | tf_op jit(solution)/shard_map/ppermute | solution.py:902
  70.5 5.2 collective-permute-done.7.far
  81.2 15.7 %collective-permute-done.13.far = bf16[2,512,128]{2,1,0:T(8,128)(2,1)S(1)} collective-permute-done((bf16[2,512,128]{2,1,0:T(8,128)(2,1)S(1)}, bf16[2,512,128]{2,1,0:T(8,128)(2,1)S(1)}, u32[]{:S(2)}, u32[]{:S(2)}) %collective-permute-start.13) | collective-permute-done | bytes 262176 | tf_op jit(solution)/shard_map/ppermute | solution.py:902
  105.2 10.5 %collective-permute-done.19.far = bf16[2,512,128]{2,1,0:T(8,128)(2,1)S(1)} collective-permute-done((bf16[2,512,128]{2,1,0:T(8,128)(2,1)S(1)}, bf16[2,512,128]{2,1,0:T(8,128)(2,1)S(1)}, u32[]{:S(2)}, u32[]{:S(2)}) %collective-permute-start.19) | collective-permute-done | bytes 262176 | tf_op jit(solution)/shard_map/ppermute | solution.py:902
  116.9 7.5 %attend.7 = (bf16[512,384]{1,0:T(8,128)(2,1)S(1)}, bf16[6,512,128]{2,1,0:T(8,128)(2,1)S(1)}) custom-call(s32[3]{0:T(128)S(1)} %pad_add_fusion.1.f_ref, bf16[15,512,128]{2,1,0:T(8,128)(2,1)S(1)} %get-tuple-element.275.q, bf16[512,128]{1,0:T(8,128)(2,1)S(1)} %select_convert_fusion.13.q_marks, bf16[2048,128]{1,0:T(8,128)(2,1)S(1)} %fusion.2.key_marks, ...), custom_call_target="tpu_custom_call" | custom-call | flops 40000000000 | bytes 1000000 | tf_op jit(solution)/shard_map/attend/pallas_call | solution.py:154
  126.5 7.1 %attend.8 = (bf16[512,384]{1,0:T(8,128)(2,1)S(1)}, bf16[6,512,128]{2,1,0:T(8,128)(2,1)S(1)}) custom-call(s32[3]{0:T(128)S(1)} %pad_add_fusion.1.f_ref, bf16[15,512,128]{2,1,0:T(8,128)(2,1)S(1)} %get-tuple-element.275.q, bf16[512,128]{1,0:T(8,128)(2,1)S(1)} %select_convert_fusion.13.q_marks, bf16[2048,128]{1,0:T(8,128)(2,1)S(1)} %fusion.2.key_marks, ...), custom_call_target="tpu_custom_call" | custom-call | flops 40000000000 | bytes 1000000 | tf_op jit(solution)/shard_map/attend/pallas_call | solution.py:154
  136.2 17.6 %feed.2 = (f32[512,960]{1,0:T(8,128)}, bf16[1024,512]{1,0:T(8,128)(2,1)}, bf16[960,512]{1,0:T(8,128)(2,1)}, bf16[512,2560]{1,0:T(8,128)(2,1)}, bf16[512,2560]{1,...) custom-call(s32[3]{0:T(128)S(1)} %pad_add_fusion.1.f_ref, bf16[512,960]{1,0:T(8,128)(2,1)} %copy-done.104, ...), custom_call_target="tpu_custom_call" | custom-call | flops 40000000000 | bytes 1000000 | tf_op jit(solution)/shard_map/feed/pallas_call | solution.py:604
  155.5 4.4 project.3
  160.9 4.9 collective-permute-done.32.far
  168.0 5.4 collective-permute-done.35.far
  174.6 4.1 attend.9
  180.0 7.1 %attend.10 = (bf16[512,384]{1,0:T(8,128)(2,1)S(1)}, bf16[6,512,128]{2,1,0:T(8,128)(2,1)S(1)}) custom-call(s32[3]{0:T(128)S(1)} %pad_add_fusion.1.f_ref, bf16[15,512,128]{2,1,0:T(8,128)(2,1)S(1)} %get-tuple-element.308.q, bf16[512,128]{1,0:T(8,128)(2,1)S(1)} %select_convert_fusion.13.q_marks, bf16[2048,128]{1,0:T(8,128)(2,1)S(1)} %fusion.2.key_marks, ...), custom_call_target="tpu_custom_call" | custom-call | flops 40000000000 | bytes 1000000 | tf_op jit(solution)/shard_map/attend/pallas_call | solution.py:154
  187.2 7.3 %attend.11 = (bf16[512,384]{1,0:T(8,128)(2,1)S(1)}, bf16[6,512,128]{2,1,0:T(8,128)(2,1)S(1)}) custom-call(s32[3]{0:T(128)S(1)} %pad_add_fusion.1.f_ref, bf16[15,512,128]{2,1,0:T(8,128)(2,1)S(1)} %get-tuple-element.308.q, bf16[512,128]{1,0:T(8,128)(2,1)S(1)} %select_convert_fusion.13.q_marks, bf16[2048,128]{1,0:T(8,128)(2,1)S(1)} %fusion.2.key_marks, ...), custom_call_target="tpu_custom_call" | custom-call | flops 40000000000 | bytes 1000000 | tf_op jit(solution)/shard_map/attend/pallas_call | solution.py:154
  194.7 17.7 %feed.3 = (f32[512,960]{1,0:T(8,128)}, bf16[1024,512]{1,0:T(8,128)(2,1)}, bf16[960,512]{1,0:T(8,128)(2,1)}, bf16[512,2560]{1,0:T(8,128)(2,1)}, bf16[512,2560]{1,...) custom-call(s32[3]{0:T(128)S(1)} %pad_add_fusion.1.f_ref, ...), custom_call_target="tpu_custom_call" | custom-call | flops 40000000000 | bytes 1000000 | tf_op jit(solution)/shard_map/feed/pallas_call | solution.py:604
  214.5 22.2 %feed_back.2 = (bf16[512,2560]{1,0:T(8,128)(2,1)}, bf16[512,2560]{1,0:T(8,128)(2,1)}, f32[512,960]{1,0:T(8,128)}, bf16[512,960]{1,0:T(8,128)(2,1)}, bf16[512,256...) custom-call(s32[3]{0:T(128)S(1)} %pad_add_fusion.1.f_ref, ...), custom_call_target="tpu_custom_call" | custom-call | flops 40000000000 | bytes 1000000 | tf_op jit(solution)/shard_map/feed_back/pallas_call | solution.py:690
  238.4 12.4 %attend_back.6 = (bf16[512,384]{1,0:T(8,128)(2,1)S(1)}, bf16[2,2,512,128]{3,2,1,0:T(8,128)(2,1)S(1)}, bf16[2,2,512,128]{3,2,1,0:T(8,128)(2,1)S(1)}) custom-call(s32[3]{0:T(128)S(1)} %pad_add_fusion.1.f_ref, bf16[15,512,128]{2,1,0:T(8,128)(2,1)S(1)} %copy-done.93, bf16[6,512,128]{2,1,0:T(8,128)(2,1)S(1)} %copy-done.120, ...), custom_call_target="tpu_custom_call" | custom-call | flops 40000000000 | bytes 1000000 | tf_op jit(solution)/shard_map/attend_back/pallas_call | solution.py:272
  250.9 12.6 %attend_back.7 = (bf16[512,384]{1,0:T(8,128)(2,1)S(1)}, bf16[2,2,512,128]{3,2,1,0:T(8,128)(2,1)S(1)}, bf16[2,2,512,128]{3,2,1,0:T(8,128)(2,1)S(1)}) custom-call(s32[3]{0:T(128)S(1)} %pad_add_fusion.1.f_ref, bf16[15,512,128]{2,1,0:T(8,128)(2,1)S(1)} %copy-done.93, bf16[6,512,128]{2,1,0:T(8,128)(2,1)S(1)} %get-tuple-element.334.marks, ...), custom_call_target="tpu_custom_call" | custom-call | flops 40000000000 | bytes 1000000 | tf_op jit(solution)/shard_map/attend_back/pallas_call | solution.py:272
  264.9 6.6 %attend_back.8 = (bf16[512,256]{1,0:T(8,128)(2,1)S(1)}, bf16[2,1,512,128]{3,2,1,0:T(8,128)(2,1)S(1)}, bf16[2,1,512,128]{3,2,1,0:T(8,128)(2,1)}) custom-call(s32[3]{0:T(128)S(1)} %pad_add_fusion.1.f_ref, bf16[15,512,128]{2,1,0:T(8,128)(2,1)S(1)} %copy-done.93, bf16[3,512,128]{2,1,0:T(8,128)(2,1)S(1)} %copy-done.136, bf16[2048,128]{1,0:T(8,128)(2,1)S(1)} %fusion.2.key_marks, ...), custom_call_target="tpu_custom_call" | custom-call | flops 40000000000 | bytes 1000000 | tf_op jit(solution)/shard_map/attend_back/pallas_call | solution.py:272
  276.3 5.8 %collective-permute-done.46.refs_8_ = bf16[2,512,128]{2,1,0:T(8,128)(2,1)} collective-permute-done((bf16[2,512,128]{2,1,0:T(8,128)(2,1)}, bf16[2,512,128]{2,1,0:T(8,128)(2,1)}, u32[]{:S(2)}, u32[]{:S(2)}) %collective-permute-start.46) | collective-permute-done | bytes 262176 | tf_op jit(solution)/shard_map/ppermute | solution.py:902
  292.3 6.1 %project_back.2 = (bf16[512,1664]{1,0:T(8,128)(2,1)S(1)}, f32[512,960]{1,0:T(8,128)S(1)}, bf16[960,512]{1,0:T(8,128)(2,1)S(1)}, f32[1,960]{1,0:T(1,128)S(1)}) custom-call(s32[3]{0:T(128)S(1)} %pad_add_fusion.1.f_ref, bf16[512,256]{1,0:T(8,128)(2,1)S(1)} %copy-done.142, bf16[512,384]{1,0:T(8,128)(2,1)S(1)} %copy-done.130, bf16[512,384]{1,0:T(8,128)(2,1)S(1)} %copy-done.132, ...), custom_call_target="tpu_custom_call" | custom-call | flops 40000000000 | bytes 1000000 | tf_op jit(solution)/shard_map/project_back/pallas_call | solution.py:750
  308.6 22.2 %feed_back.3 = (bf16[512,2560]{1,0:T(8,128)(2,1)}, bf16[512,2560]{1,0:T(8,128)(2,1)}, f32[512,960]{1,0:T(8,128)}, bf16[512,960]{1,0:T(8,128)(2,1)}, bf16[512,256...) custom-call(s32[3]{0:T(128)S(1)} %pad_add_fusion.1.f_ref, ...), custom_call_target="tpu_custom_call" | custom-call | flops 40000000000 | bytes 1000000 | tf_op jit(solution)/shard_map/feed_back/pallas_call | solution.py:690
  331.4 4.8 collective-permute-done.50
  339.4 6.9 %outer_gate.1 = (bf16[4,240,640]{2,1,0:T(8,128)(2,1)S(1)}, bf16[4,240,640]{2,1,0:T(8,128)(2,1)S(1)}, bf16[4,240,640]{2,1,0:T(8,128)(2,1)S(1)}, bf16[4,240,640]{2,1,0:T(8,128)(2,1)S(1)}) custom-call(s32[3]{0:T(128)S(1)} %pad_add_fusion.1.f_ref, bf16[960,512]{1,0:T(8,128)(2,1)S(1)} %copy-done.108, bf16[960,512]{1,0:T(8,128)(2,1)S(1)} %copy-done.107, ...), custom_call_target="tpu_custom_call" | custom-call | flops 40000000000 | bytes 1000000 | tf_op jit(solution)/shard_map/outer_gate/pallas_call | solution.py:792
  347.2 7.3 %outer_up.1 = (bf16[4,240,640]{2,1,0:T(8,128)(2,1)S(1)}, bf16[4,240,640]{2,1,0:T(8,128)(2,1)S(1)}, bf16[4,240,640]{2,1,0:T(8,128)(2,1)S(1)}, bf16[4,240,640]{2,1,0:T(8,128)(2,1)S(1)}) custom-call(s32[3]{0:T(128)S(1)} %pad_add_fusion.1.f_ref, bf16[960,512]{1,0:T(8,128)(2,1)S(1)} %copy-done.108, bf16[960,512]{1,0:T(8,128)(2,1)S(1)} %copy-done.107, ...), custom_call_target="tpu_custom_call" | custom-call | flops 40000000000 | bytes 1000000 | tf_op jit(solution)/shard_map/outer_up/pallas_call | solution.py:792
  357.5 5.2 collective-permute-done.52
  367.2 12.3 %attend_back.9 = (bf16[512,384]{1,0:T(8,128)(2,1)S(1)}, bf16[2,2,512,128]{3,2,1,0:T(8,128)(2,1)S(1)}, bf16[2,2,512,128]{3,2,1,0:T(8,128)(2,1)S(1)}) custom-call(s32[3]{0:T(128)S(1)} %pad_add_fusion.1.f_ref, bf16[15,512,128]{2,1,0:T(8,128)(2,1)S(1)} %copy-done.95, bf16[6,512,128]{2,1,0:T(8,128)(2,1)S(1)} %copy-done.118, bf16[2048,128]{1,0:T(8,128)(2,1)S(1)} %copy-done.1, ...), custom_call_target="tpu_custom_call" | custom-call | flops 40000000000 | bytes 1000000 | tf_op jit(solution)/shard_map/attend_back/pallas_call | solution.py:272
  385.9 12.5 %attend_back.10 = (bf16[512,384]{1,0:T(8,128)(2,1)S(1)}, bf16[2,2,512,128]{3,2,1,0:T(8,128)(2,1)S(1)}, bf16[2,2,512,128]{3,2,1,0:T(8,128)(2,1)S(1)}) custom-call(s32[3]{0:T(128)S(1)} %pad_add_fusion.1.f_ref, bf16[15,512,128]{2,1,0:T(8,128)(2,1)S(1)} %copy-done.95, bf16[6,512,128]{2,1,0:T(8,128)(2,1)S(1)} %copy-done.116, bf16[2048,128]{1,0:T(8,128)(2,1)S(1)} %copy-done.1, ...), custom_call_target="tpu_custom_call" | custom-call | flops 40000000000 | bytes 1000000 | tf_op jit(solution)/shard_map/attend_back/pallas_call | solution.py:272
  403.9 6.1 %attend_back.11 = (bf16[512,256]{1,0:T(8,128)(2,1)S(1)}, bf16[2,1,512,128]{3,2,1,0:T(8,128)(2,1)S(1)}, bf16[2,1,512,128]{3,2,1,0:T(8,128)(2,1)S(1)}) custom-call(s32[3]{0:T(128)S(1)} %pad_add_fusion.1.f_ref, bf16[15,512,128]{2,1,0:T(8,128)(2,1)S(1)} %copy-done.95, bf16[3,512,128]{2,1,0:T(8,128)(2,1)S(1)} %copy-done.134, bf16[2048,128]{1,0:T(8,128)(2,1)S(1)} %copy-done.1, ...), custom_call_target="tpu_custom_call" | custom-call | flops 40000000000 | bytes 1000000 | tf_op jit(solution)/shard_map/attend_back/pallas_call | solution.py:272
  410.2 6.6 %collective-permute-done.64 = bf16[2,240,640]{2,1,0:T(8,128)(2,1)S(1)} collective-permute-done((bf16[2,240,640]{2,1,0:T(8,128)(2,1)S(1)}, bf16[2,240,640]{2,1,0:T(8,128)(2,1)S(1)}, u32[]{:S(2)}, u32[]{:S(2)}) %collective-permute-start.64) | collective-permute-done | bytes 614432 | tf_op jit(solution)/shard_map/ppermute | solution.py:902
  417.0 5.6 collective-permute-done.63
  424.6 7.1 %collective-permute-done.70.refs_8_ = bf16[2,512,128]{2,1,0:T(8,128)(2,1)S(1)} collective-permute-done((bf16[2,512,128]{2,1,0:T(8,128)(2,1)S(1)}, bf16[2,512,128]{2,1,0:T(8,128)(2,1)S(1)}, u32[]{:S(2)}, u32[]{:S(2)}) %collective-permute-start.70) | collective-permute-done | bytes 262176 | tf_op jit(solution)/shard_map/ppermute | solution.py:902
  440.6 5.9 %project_back.3 = (bf16[512,1664]{1,0:T(8,128)(2,1)S(1)}, bf16[512,960]{1,0:T(8,128)(2,1)S(1)}, bf16[960,512]{1,0:T(8,128)(2,1)}, f32[1,960]{1,0:T(1,128)S(1)}) custom-call(s32[3]{0:T(128)S(1)} %pad_add_fusion.1.f_ref, bf16[512,256]{1,0:T(8,128)(2,1)S(1)} %get-tuple-element.425.refs_0_, bf16[512,384]{1,0:T(8,128)(2,1)S(1)} %get-tuple-element.405.refs_1_, ...), custom_call_target="tpu_custom_call" | custom-call | flops 40000000000 | bytes 1000000 | tf_op jit(solution)/shard_map/project_back/pallas_call | solution.py:750
  458.2 4.6 outer_in.1
  462.8 5.2 collective-permute-done.76
  471.2 4.3 collective-permute-done.80
  475.6 4.8 collective-permute-done.79
  486.0 6.2 %collective-permute-done.84 = bf16[1,64,1024]{2,1,0:T(8,128)(2,1)S(1)} collective-permute-done((bf16[1,64,1024]{2,1,0:T(8,128)(2,1)S(1)}, bf16[1,64,1024]{2,1,0:T(8,128)(2,1)S(1)}, u32[]{:S(2)}, u32[]{:S(2)}) %collective-permute-start.84) | collective-permute-done | bytes 131104 | tf_op jit(solution)/shard_map/ppermute | solution.py:902
  492.3 4.6 collective-permute-done.85
  497.1 4.3 collective-permute-done.82
  505.6 4.8 collective-permute-done.89
  519.7 5.6 collective-permute-done.90
  525.4 4.6 collective-permute-done.91
  545.9 4.6 collective-permute-done.97
  560.6 5.3 collective-permute-done.100
  571.0 5.2 collective-permute-done.101
  (631 shorter events, 179.6 us)
Async XLA Ops:
  4.9 30.6 %collective-permute-start = (bf16[240,1664]{1,0:T(8,128)(2,1)S(1)}, bf16[240,1664]{1,0:T(8,128)(2,1)S(1)}, u32[]{:S(2)}, u32[]{:S(2)}) collective-permute-start(bf16[240,1664]{1,0:T(8,128)(2,1)S(1)} %pack.1.own.refs_14_), channel_id=1, source_target_pairs={{0,2},{1,3},{2,0},{3,1},{4,6},{5,7},{6,4},{7,5},{8,10},{9,11},{10,... | collective-permute-start | bytes 2396168 | tf_op jit(solution)/shard_map/ppermute | solution.py:902
  7.9 27.6 %collective-permute-start.1 = (bf16[240,1664]{1,0:T(8,128)(2,1)S(1)}, bf16[240,1664]{1,0:T(8,128)(2,1)S(1)}, u32[]{:S(2)}, u32[]{:S(2)}) collective-permute-start(bf16[240,1664]{1,0:T(8,128)(2,1)S(1)} %pack.1.own.refs_14_), channel_id=1, source_target_pairs={{0,1},{1,0},{2,3},{3,2},{4,5},{5,4},{6,7},{7,6},{8,9},{9,8},{10,11... | collective-permute-start | bytes 2396168 | tf_op jit(solution)/shard_map/ppermute | solution.py:902
  7.9 27.6 %collective-permute-start.2 = (bf16[960,256]{1,0:T(8,128)(2,1)S(1)}, bf16[960,256]{1,0:T(8,128)(2,1)S(1)}, u32[]{:S(2)}, u32[]{:S(2)}) collective-permute-start(bf16[960,256]{1,0:T(8,128)(2,1)S(1)} %slice.345), channel_id=1, source_target_pairs={{0,3},{1,2},{2,1},{3,0},{4,7},{5,6},{6,5},{7,4},{8,11},{9,10},{10,... | collective-permute-start | bytes 1474568 | tf_op jit(solution)/shard_map/ppermute | solution.py:902
  35.5 16.4 %collective-permute-start.3 = (bf16[240,1280]{1,0:T(8,128)(2,1)S(1)}, bf16[240,1280]{1,0:T(8,128)(2,1)S(1)}, u32[]{:S(2)}, u32[]{:S(2)}) collective-permute-start(bf16[240,1280]{1,0:T(8,128)(2,1)S(1)} %slice_select_fusion.1), channel_id=1, source_target_pairs={{0,2},{1,3},{2,0},{3,1},{4,6},{5,7},{6,4},{7,5},{8,10},{9,11},{10,... | collective-permute-start | bytes 1843208 | tf_op jit(solution)/shard_map/ppermute | solution.py:902
  36.9 15.0 %collective-permute-start.4 = (bf16[240,1664]{1,0:T(8,128)(2,1)S(1)}, bf16[240,1664]{1,0:T(8,128)(2,1)S(1)}, u32[]{:S(2)}, u32[]{:S(2)}) collective-permute-start(bf16[240,1664]{1,0:T(8,128)(2,1)S(1)} %collective-permute-done.far.refs_16_), channel_id=1, source_target_pairs={{0,1},{1,0},{2,3},{3,2},{4,5},{5,4},{6,7},{7,6},{8,9},{9,8},{10,11... | collective-permute-start | bytes 2396168 | tf_op jit(solution)/shard_map/ppermute | solution.py:902
  51.9 15.9 %collective-permute-start.5 = (bf16[240,1280]{1,0:T(8,128)(2,1)S(1)}, bf16[240,1280]{1,0:T(8,128)(2,1)S(1)}, u32[]{:S(2)}, u32[]{:S(2)}) collective-permute-start(bf16[240,1280]{1,0:T(8,128)(2,1)S(1)} %slice_select_fusion.2), channel_id=1, source_target_pairs={{0,2},{1,3},{2,0},{3,1},{4,6},{5,7},{6,4},{7,5},{8,10},{9,11},{10,... | collective-permute-start | bytes 1843208 | tf_op jit(solution)/shard_map/ppermute | solution.py:902
  53.7 15.6 %collective-permute-start.6 = (bf16[240,1280]{1,0:T(8,128)(2,1)S(1)}, bf16[240,1280]{1,0:T(8,128)(2,1)S(1)}, u32[]{:S(2)}, u32[]{:S(2)}) collective-permute-start(bf16[240,1280]{1,0:T(8,128)(2,1)S(1)} %collective-permute-done.3.refs_10_.refs_9_), channel_id=1, source_target_pairs={{0,4},{4,0},{8,12},{12,8},{16,20},{20,16},{24,28},{28,24},{1,5},{5... | collective-permute-start | bytes 1843208 | tf_op jit(solution)/shard_map/ppermute | solution.py:902
  75.8 21.1 %collective-permute-start.12 = (bf16[480,640]{1,0:T(8,128)(2,1)S(1)}, bf16[480,640]{1,0:T(8,128)(2,1)S(1)}, u32[]{:S(2)}, u32[]{:S(2)}) collective-permute-start(bf16[480,640]{1,0:T(8,128)(2,1)S(1)} %slice_select_fusion), channel_id=1, source_target_pairs={{0,2},{1,3},{2,0},{3,1},{4,6},{5,7},{6,4},{7,5},{8,10},{9,11},{10,... | collective-permute-start | bytes 1843208 | tf_op jit(solution)/shard_map/ppermute | solution.py:902
  76.2 20.7 %collective-permute-start.16 = (bf16[240,1280]{1,0:T(8,128)(2,1)S(1)}, bf16[240,1280]{1,0:T(8,128)(2,1)S(1)}, u32[]{:S(2)}, u32[]{:S(2)}) collective-permute-start(bf16[240,1280]{1,0:T(8,128)(2,1)S(1)} %collective-permute-done.5.refs_16_.refs_15_), channel_id=1, source_target_pairs={{0,8},{4,12},{8,0},{12,4},{16,24},{20,28},{24,16},{28,20},{1,9},{5... | collective-permute-start | bytes 1843208 | tf_op jit(solution)/shard_map/ppermute | solution.py:902
  77.8 19.1 %collective-permute-start.13 = (bf16[2,512,128]{2,1,0:T(8,128)(2,1)S(1)}, bf16[2,512,128]{2,1,0:T(8,128)(2,1)S(1)}, u32[]{:S(2)}, u32[]{:S(2)}) collective-permute-start(bf16[2,512,128]{2,1,0:T(8,128)(2,1)S(1)} %get-tuple-element.265.own), channel_id=1, source_target_pairs={{0,2},{1,3},{2,0},{3,1},{4,6},{5,7},{6,4},{7,5},{8,10},{9,11},{10,... | collective-permute-start | bytes 786440 | tf_op jit(solution)/shard_map/ppermute | solution.py:902
  79.4 17.4 %collective-permute-start.15 = (bf16[2,512,128]{2,1,0:T(8,128)(2,1)S(1)}, bf16[2,512,128]{2,1,0:T(8,128)(2,1)S(1)}, u32[]{:S(2)}, u32[]{:S(2)}) collective-permute-start(bf16[2,512,128]{2,1,0:T(8,128)(2,1)S(1)} %get-tuple-element.271.own), channel_id=1, source_target_pairs={{0,1},{1,0},{2,3},{3,2},{4,5},{5,4},{6,7},{7,6},{8,9},{9,8},{10,11... | collective-permute-start | bytes 786440 | tf_op jit(solution)/shard_map/ppermute | solution.py:902
  96.9 18.8 %collective-permute-start.17 = (bf16[480,640]{1,0:T(8,128)(2,1)S(1)}, bf16[480,640]{1,0:T(8,128)(2,1)S(1)}, u32[]{:S(2)}, u32[]{:S(2)}) collective-permute-start(bf16[480,640]{1,0:T(8,128)(2,1)S(1)} %collective-permute-done.12.refs_22_.refs_21_), channel_id=1, source_target_pairs={{0,4},{4,0},{8,12},{12,8},{16,20},{20,16},{24,28},{28,24},{1,5},{5... | collective-permute-start | bytes 1843208 | tf_op jit(solution)/shard_map/ppermute | solution.py:902
  98.5 17.2 %collective-permute-start.18 = (bf16[240,960]{1,0:T(8,128)(2,1)S(1)}, bf16[240,960]{1,0:T(8,128)(2,1)S(1)}, u32[]{:S(2)}, u32[]{:S(2)}) collective-permute-start(bf16[240,960]{1,0:T(8,128)(2,1)S(1)} %copy-done.31), channel_id=1, source_target_pairs={{0,2},{1,3},{2,0},{3,1},{4,6},{5,7},{6,4},{7,5},{8,10},{9,11},{10,... | collective-permute-start | bytes 1382408 | tf_op jit(solution)/shard_map/ppermute | solution.py:902
  98.8 16.9 %collective-permute-start.19 = (bf16[2,512,128]{2,1,0:T(8,128)(2,1)S(1)}, bf16[2,512,128]{2,1,0:T(8,128)(2,1)S(1)}, u32[]{:S(2)}, u32[]{:S(2)}) collective-permute-start(bf16[2,512,128]{2,1,0:T(8,128)(2,1)S(1)} %get-tuple-element.271.own), channel_id=1, source_target_pairs={{0,2},{1,3},{2,0},{3,1},{4,6},{5,7},{6,4},{7,5},{8,10},{9,11},{10,... | collective-permute-start | bytes 786440 | tf_op jit(solution)/shard_map/ppermute | solution.py:902
  100.5 15.2 %collective-permute-start.20 = (bf16[2,512,128]{2,1,0:T(8,128)(2,1)S(1)}, bf16[2,512,128]{2,1,0:T(8,128)(2,1)S(1)}, u32[]{:S(2)}, u32[]{:S(2)}) collective-permute-start(bf16[2,512,128]{2,1,0:T(8,128)(2,1)S(1)} %collective-permute-done.13.far), channel_id=1, source_target_pairs={{0,1},{1,0},{2,3},{3,2},{4,5},{5,4},{6,7},{7,6},{8,9},{9,8},{10,11... | collective-permute-start | bytes 786440 | tf_op jit(solution)/shard_map/ppermute | solution.py:902
  100.5 15.2 %collective-permute-start.21 = (bf16[240,2560]{1,0:T(8,128)(2,1)S(1)}, bf16[240,2560]{1,0:T(8,128)(2,1)S(1)}, u32[]{:S(2)}, u32[]{:S(2)}) collective-permute-start(bf16[240,2560]{1,0:T(8,128)(2,1)S(1)} %copy-done.145), channel_id=1, source_target_pairs={{0,1},{1,0},{2,3},{3,2},{4,5},{5,4},{6,7},{7,6},{8,9},{9,8},{10,11... | collective-permute-start | bytes 3686408 | tf_op jit(solution)/shard_map/ppermute | solution.py:902
  134.6 19.2 %collective-permute-start.31 = (bf16[960,256]{1,0:T(8,128)(2,1)S(1)}, bf16[960,256]{1,0:T(8,128)(2,1)S(1)}, u32[]{:S(2)}, u32[]{:S(2)}) collective-permute-start(bf16[960,256]{1,0:T(8,128)(2,1)S(1)} %slice.344), channel_id=1, source_target_pairs={{0,3},{1,2},{2,1},{3,0},{4,7},{5,6},{6,5},{7,4},{8,11},{9,10},{10,... | collective-permute-start | bytes 1474568 | tf_op jit(solution)/shard_map/ppermute | solution.py:902
  236.7 14.1 %collective-permute-start.41 = (bf16[960,256]{1,0:T(8,128)(2,1)S(1)}, bf16[960,256]{1,0:T(8,128)(2,1)S(1)}, u32[]{:S(2)}, u32[]{:S(2)}) collective-permute-start(bf16[960,256]{1,0:T(8,128)(2,1)S(1)} %get-tuple-element.325), channel_id=1, source_target_pairs={{0,3},{1,2},{2,1},{3,0},{4,7},{5,6},{6,5},{7,4},{8,11},{9,10},{10,... | collective-permute-start | bytes 1474568 | tf_op jit(solution)/shard_map/ppermute | solution.py:902
  250.8 12.8 %collective-permute-start.42 = (bf16[2,2,512,128]{3,2,1,0:T(8,128)(2,1)S(1)}, bf16[2,2,512,128]{3,2,1,0:T(8,128)(2,1)S(1)}, u32[]{:S(2)}, u32[]{:S(2)}) collective-permute-start(bf16[2,2,512,128]{3,2,1,0:T(8,128)(2,1)S(1)} %get-tuple-element.332), channel_id=1, source_target_pairs={{0,1},{1,0},{2,3},{3,2},{4,5},{5,4},{6,7},{7,6},{8,9},{9,8},{10,11... | collective-permute-start | bytes 1572872 | tf_op jit(solution)/shard_map/ppermute | solution.py:902
  306.8 29.5 %collective-permute-start.50 = (bf16[1,960,640]{2,1,0:T(8,128)(2,1)S(1)}, bf16[1,960,640]{2,1,0:T(8,128)(2,1)S(1)}, u32[]{:S(2)}, u32[]{:S(2)}) collective-permute-start(bf16[1,960,640]{2,1,0:T(8,128)(2,1)S(1)} %add_convert_fusion), channel_id=1, source_target_pairs={{0,2},{1,3},{2,0},{3,1},{4,6},{5,7},{6,4},{7,5},{8,10},{9,11},{10,... | collective-permute-start | bytes 3686408 | tf_op jit(solution)/shard_map/ppermute | solution.py:902
  308.4 27.8 %collective-permute-start.49 = (bf16[1,960,640]{2,1,0:T(8,128)(2,1)S(1)}, bf16[1,960,640]{2,1,0:T(8,128)(2,1)S(1)}, u32[]{:S(2)}, u32[]{:S(2)}) collective-permute-start(bf16[1,960,640]{2,1,0:T(8,128)(2,1)S(1)} %get-tuple-element.364), channel_id=1, source_target_pairs={{0,1},{1,0},{2,3},{3,2},{4,5},{5,4},{6,7},{7,6},{8,9},{9,8},{10,11... | collective-permute-start | bytes 3686408 | tf_op jit(solution)/shard_map/ppermute | solution.py:902
  346.3 16.6 %collective-permute-start.51 = (bf16[4,240,640]{2,1,0:T(8,128)(2,1)S(1)}, bf16[4,240,640]{2,1,0:T(8,128)(2,1)S(1)}, u32[]{:S(2)}, u32[]{:S(2)}) collective-permute-start(bf16[4,240,640]{2,1,0:T(8,128)(2,1)S(1)} %get-tuple-element.384), channel_id=1, source_target_pairs={{0,1},{1,0},{2,3},{3,2},{4,5},{5,4},{6,7},{7,6},{8,9},{9,8},{10,11... | collective-permute-start | bytes 3686408 | tf_op jit(solution)/shard_map/ppermute | solution.py:902
  346.4 16.3 %collective-permute-start.52 = (bf16[1,480,640]{2,1,0:T(8,128)(2,1)S(1)}, bf16[1,480,640]{2,1,0:T(8,128)(2,1)S(1)}, u32[]{:S(2)}, u32[]{:S(2)}) collective-permute-start(bf16[1,480,640]{2,1,0:T(8,128)(2,1)S(1)} %fusion.3), channel_id=1, source_target_pairs={{0,4},{4,0},{8,12},{12,8},{16,20},{20,16},{24,28},{28,24},{1,5},{5... | collective-permute-start | bytes 1843208 | tf_op jit(solution)/shard_map/ppermute | solution.py:902
  347.0 16.3 %collective-permute-start.53 = (bf16[4,240,640]{2,1,0:T(8,128)(2,1)S(1)}, bf16[4,240,640]{2,1,0:T(8,128)(2,1)S(1)}, u32[]{:S(2)}, u32[]{:S(2)}) collective-permute-start(bf16[4,240,640]{2,1,0:T(8,128)(2,1)S(1)} %get-tuple-element.392), channel_id=1, source_target_pairs={{0,1},{1,0},{2,3},{3,2},{4,5},{5,4},{6,7},{7,6},{8,9},{9,8},{10,11... | collective-permute-start | bytes 3686408 | tf_op jit(solution)/shard_map/ppermute | solution.py:902
  363.3 16.5 %collective-permute-start.54 = (bf16[1,256,1024]{2,1,0:T(8,128)(2,1)S(1)}, bf16[1,256,1024]{2,1,0:T(8,128)(2,1)S(1)}, u32[]{:S(2)}, u32[]{:S(2)}) collective-permute-start(bf16[1,256,1024]{2,1,0:T(8,128)(2,1)S(1)} %get-tuple-element.394), channel_id=1, source_target_pairs={{0,1},{1,0},{2,3},{3,2},{4,5},{5,4},{6,7},{7,6},{8,9},{9,8},{10,11... | collective-permute-start | bytes 1572872 | tf_op jit(solution)/shard_map/ppermute | solution.py:902
  363.4 18.1 %collective-permute-start.55 = (bf16[4,240,640]{2,1,0:T(8,128)(2,1)S(1)}, bf16[4,240,640]{2,1,0:T(8,128)(2,1)S(1)}, u32[]{:S(2)}, u32[]{:S(2)}) collective-permute-start(bf16[4,240,640]{2,1,0:T(8,128)(2,1)S(1)} %get-tuple-element.395), channel_id=1, source_target_pairs={{0,1},{1,0},{2,3},{3,2},{4,5},{5,4},{6,7},{7,6},{8,9},{9,8},{10,11... | collective-permute-start | bytes 3686408 | tf_op jit(solution)/shard_map/ppermute | solution.py:902
  363.9 17.6 %collective-permute-start.58 = (bf16[4,240,640]{2,1,0:T(8,128)(2,1)S(1)}, bf16[4,240,640]{2,1,0:T(8,128)(2,1)S(1)}, u32[]{:S(2)}, u32[]{:S(2)}) collective-permute-start(bf16[4,240,640]{2,1,0:T(8,128)(2,1)S(1)} %get-tuple-element.403), channel_id=1, source_target_pairs={{0,1},{1,0},{2,3},{3,2},{4,5},{5,4},{6,7},{7,6},{8,9},{9,8},{10,11... | collective-permute-start | bytes 3686408 | tf_op jit(solution)/shard_map/ppermute | solution.py:902
  364.0 15.5 %collective-permute-start.56 = (bf16[1,240,640]{2,1,0:T(8,128)(2,1)S(1)}, bf16[1,240,640]{2,1,0:T(8,128)(2,1)S(1)}, u32[]{:S(2)}, u32[]{:S(2)}) collective-permute-start(bf16[1,240,640]{2,1,0:T(8,128)(2,1)S(1)} %fusion.7), channel_id=1, source_target_pairs={{0,8},{4,12},{8,0},{12,4},{16,24},{20,28},{24,16},{28,20},{1,9},{5... | collective-permute-start | bytes 921608 | tf_op jit(solution)/shard_map/ppermute | solution.py:902
  365.6 15.9 %collective-permute-start.57 = (bf16[2,240,640]{2,1,0:T(8,128)(2,1)S(1)}, bf16[2,240,640]{2,1,0:T(8,128)(2,1)S(1)}, u32[]{:S(2)}, u32[]{:S(2)}) collective-permute-start(bf16[2,240,640]{2,1,0:T(8,128)(2,1)S(1)} %get-tuple-element.402), channel_id=1, source_target_pairs={{0,2},{1,3},{2,0},{3,1},{4,6},{5,7},{6,4},{7,5},{8,10},{9,11},{10,... | collective-permute-start | bytes 1843208 | tf_op jit(solution)/shard_map/ppermute | solution.py:902
  381.5 18.0 %collective-permute-start.60 = (bf16[2,2,512,128]{3,2,1,0:T(8,128)(2,1)S(1)}, bf16[2,2,512,128]{3,2,1,0:T(8,128)(2,1)S(1)}, u32[]{:S(2)}, u32[]{:S(2)}) collective-permute-start(bf16[2,2,512,128]{3,2,1,0:T(8,128)(2,1)S(1)} %get-tuple-element.406), channel_id=1, source_target_pairs={{0,1},{1,0},{2,3},{3,2},{4,5},{5,4},{6,7},{7,6},{8,9},{9,8},{10,11... | collective-permute-start | bytes 1572872 | tf_op jit(solution)/shard_map/ppermute | solution.py:902
  381.7 18.0 %collective-permute-start.61 = (bf16[2,240,640]{2,1,0:T(8,128)(2,1)S(1)}, bf16[2,240,640]{2,1,0:T(8,128)(2,1)S(1)}, u32[]{:S(2)}, u32[]{:S(2)}) collective-permute-start(bf16[2,240,640]{2,1,0:T(8,128)(2,1)S(1)} %get-tuple-element.412), channel_id=1, source_target_pairs={{0,2},{1,3},{2,0},{3,1},{4,6},{5,7},{6,4},{7,5},{8,10},{9,11},{10,... | collective-permute-start | bytes 1843208 | tf_op jit(solution)/shard_map/ppermute | solution.py:902
  383.2 16.3 %collective-permute-start.62 = (bf16[1,120,640]{2,1,0:T(8,128)(2,1)S(1)}, bf16[1,120,640]{2,1,0:T(8,128)(2,1)S(1)}, u32[]{:S(2)}, u32[]{:S(2)}) collective-permute-start(bf16[1,120,640]{2,1,0:T(8,128)(2,1)S(1)} %fusion.23), channel_id=1, source_target_pairs={{0,16},{4,20},{8,24},{12,28},{16,0},{20,4},{24,8},{28,12},{1,17},{... | collective-permute-start | bytes 460808 | tf_op jit(solution)/shard_map/ppermute | solution.py:902
  400.5 16.3 %collective-permute-start.64 = (bf16[2,240,640]{2,1,0:T(8,128)(2,1)S(1)}, bf16[2,240,640]{2,1,0:T(8,128)(2,1)S(1)}, u32[]{:S(2)}, u32[]{:S(2)}) collective-permute-start(bf16[2,240,640]{2,1,0:T(8,128)(2,1)S(1)} %select_convert_fusion.1), channel_id=1, source_target_pairs={{0,4},{4,0},{8,12},{12,8},{16,20},{20,16},{24,28},{28,24},{1,5},{5... | collective-permute-start | bytes 1843208 | tf_op jit(solution)/shard_map/ppermute | solution.py:902
  401.1 15.9 %collective-permute-start.66 = (bf16[2,512,128]{2,1,0:T(8,128)(2,1)S(1)}, bf16[2,512,128]{2,1,0:T(8,128)(2,1)S(1)}, u32[]{:S(2)}, u32[]{:S(2)}) collective-permute-start(bf16[2,512,128]{2,1,0:T(8,128)(2,1)S(1)} %get-tuple-element.423), channel_id=1, source_target_pairs={{0,2},{1,3},{2,0},{3,1},{4,6},{5,7},{6,4},{7,5},{8,10},{9,11},{10,... | collective-permute-start | bytes 786440 | tf_op jit(solution)/shard_map/ppermute | solution.py:902
  401.6 21.0 %collective-permute-start.63 = (bf16[2,240,640]{2,1,0:T(8,128)(2,1)S(1)}, bf16[2,240,640]{2,1,0:T(8,128)(2,1)S(1)}, u32[]{:S(2)}, u32[]{:S(2)}) collective-permute-start(bf16[2,240,640]{2,1,0:T(8,128)(2,1)S(1)} %get-tuple-element.415), channel_id=1, source_target_pairs={{0,2},{1,3},{2,0},{3,1},{4,6},{5,7},{6,4},{7,5},{8,10},{9,11},{10,... | collective-permute-start | bytes 1843208 | tf_op jit(solution)/shard_map/ppermute | solution.py:902
  403.1 13.9 %collective-permute-start.67 = (bf16[1,120,640]{2,1,0:T(8,128)(2,1)S(1)}, bf16[1,120,640]{2,1,0:T(8,128)(2,1)S(1)}, u32[]{:S(2)}, u32[]{:S(2)}) collective-permute-start(bf16[1,120,640]{2,1,0:T(8,128)(2,1)S(1)} %fusion.10), channel_id=1, source_target_pairs={{0,16},{4,20},{8,24},{12,28},{16,0},{20,4},{24,8},{28,12},{1,17},{... | collective-permute-start | bytes 460808 | tf_op jit(solution)/shard_map/ppermute | solution.py:902
  437.6 14.9 %collective-permute-start.72 = (bf16[2,240,640]{2,1,0:T(8,128)(2,1)}, bf16[2,240,640]{2,1,0:T(8,128)(2,1)}, u32[]{:S(2)}, u32[]{:S(2)}) collective-permute-start(bf16[2,240,640]{2,1,0:T(8,128)(2,1)} %get-tuple-element.431), channel_id=1, source_target_pairs={{0,2},{1,3},{2,0},{3,1},{4,6},{5,7},{6,4},{7,5},{8,10},{9,11},{10,... | collective-permute-start | bytes 1843208 | tf_op jit(solution)/shard_map/ppermute | solution.py:902
  454.4 14.4 %collective-permute-start.75 = (bf16[2,240,640]{2,1,0:T(8,128)(2,1)S(1)}, bf16[2,240,640]{2,1,0:T(8,128)(2,1)S(1)}, u32[]{:S(2)}, u32[]{:S(2)}) collective-permute-start(bf16[2,240,640]{2,1,0:T(8,128)(2,1)S(1)} %select_convert_fusion), channel_id=1, source_target_pairs={{0,4},{4,0},{8,12},{12,8},{16,20},{20,16},{24,28},{28,24},{1,5},{5... | collective-permute-start | bytes 1843208 | tf_op jit(solution)/shard_map/ppermute | solution.py:902
  455.9 12.1 %collective-permute-start.76 = (bf16[1,256,1024]{2,1,0:T(8,128)(2,1)S(1)}, bf16[1,256,1024]{2,1,0:T(8,128)(2,1)S(1)}, u32[]{:S(2)}, u32[]{:S(2)}) collective-permute-start(bf16[1,256,1024]{2,1,0:T(8,128)(2,1)S(1)} %copy-done.153), channel_id=1, source_target_pairs={{0,2},{1,3},{2,0},{3,1},{4,6},{5,7},{6,4},{7,5},{8,10},{9,11},{10,... | collective-permute-start | bytes 1572872 | tf_op jit(solution)/shard_map/ppermute | solution.py:902
  456.5 12.5 %collective-permute-start.77 = (bf16[1,120,640]{2,1,0:T(8,128)(2,1)S(1)}, bf16[1,120,640]{2,1,0:T(8,128)(2,1)S(1)}, u32[]{:S(2)}, u32[]{:S(2)}) collective-permute-start(bf16[1,120,640]{2,1,0:T(8,128)(2,1)S(1)} %fusion.9), channel_id=1, source_target_pairs={{0,16},{4,20},{8,24},{12,28},{16,0},{20,4},{24,8},{28,12},{1,17},{... | collective-permute-start | bytes 460808 | tf_op jit(solution)/shard_map/ppermute | solution.py:902
  480.8 20.6 %collective-permute-start.82 = (bf16[1,256,1664]{2,1,0:T(8,128)(2,1)S(1)}, bf16[1,256,1664]{2,1,0:T(8,128)(2,1)S(1)}, u32[]{:S(2)}, u32[]{:S(2)}) collective-permute-start(bf16[1,256,1664]{2,1,0:T(8,128)(2,1)S(1)} %add_convert_fusion.1), channel_id=1, source_target_pairs={{0,2},{1,3},{2,0},{3,1},{4,6},{5,7},{6,4},{7,5},{8,10},{9,11},{10,... | collective-permute-start | bytes 2555912 | tf_op jit(solution)/shard_map/ppermute | solution.py:902
  480.8 11.4 %collective-permute-start.83 = (bf16[1,120,640]{2,1,0:T(8,128)(2,1)S(1)}, bf16[1,120,640]{2,1,0:T(8,128)(2,1)S(1)}, u32[]{:S(2)}, u32[]{:S(2)}) collective-permute-start(bf16[1,120,640]{2,1,0:T(8,128)(2,1)S(1)} %fusion.25), channel_id=1, source_target_pairs={{0,16},{4,20},{8,24},{12,28},{16,0},{20,4},{24,8},{28,12},{1,17},{... | collective-permute-start | bytes 460808 | tf_op jit(solution)/shard_map/ppermute | solution.py:902
  483.3 13.6 %collective-permute-start.85 = (bf16[1,240,640]{2,1,0:T(8,128)(2,1)S(1)}, bf16[1,240,640]{2,1,0:T(8,128)(2,1)S(1)}, u32[]{:S(2)}, u32[]{:S(2)}) collective-permute-start(bf16[1,240,640]{2,1,0:T(8,128)(2,1)S(1)} %pad_maximum_fusion.6), channel_id=1, source_target_pairs={{0,8},{4,12},{8,0},{12,4},{16,24},{20,28},{24,16},{28,20},{1,9},{5... | collective-permute-start | bytes 921608 | tf_op jit(solution)/shard_map/ppermute | solution.py:902
  484.5 17.2 %collective-permute-start.86 = (bf16[1,480,640]{2,1,0:T(8,128)(2,1)S(1)}, bf16[1,480,640]{2,1,0:T(8,128)(2,1)S(1)}, u32[]{:S(2)}, u32[]{:S(2)}) collective-permute-start(bf16[1,480,640]{2,1,0:T(8,128)(2,1)S(1)} %pad_maximum_fusion), channel_id=1, source_target_pairs={{0,4},{4,0},{8,12},{12,8},{16,20},{20,16},{24,28},{28,24},{1,5},{5... | collective-permute-start | bytes 1843208 | tf_op jit(solution)/shard_map/ppermute | solution.py:902
  517.8 12.3 %collective-permute-start.91 = (bf16[1,240,640]{2,1,0:T(8,128)(2,1)S(1)}, bf16[1,240,640]{2,1,0:T(8,128)(2,1)S(1)}, u32[]{:S(2)}, u32[]{:S(2)}) collective-permute-start(bf16[1,240,640]{2,1,0:T(8,128)(2,1)S(1)} %pad_maximum_fusion.7), channel_id=1, source_target_pairs={{0,8},{4,12},{8,0},{12,4},{16,24},{20,28},{24,16},{28,20},{1,9},{5... | collective-permute-start | bytes 921608 | tf_op jit(solution)/shard_map/ppermute | solution.py:902
  519.1 13.4 %collective-permute-start.93 = (bf16[2,240,640]{2,1,0:T(8,128)(2,1)S(1)}, bf16[2,240,640]{2,1,0:T(8,128)(2,1)S(1)}, u32[]{:S(2)}, u32[]{:S(2)}) collective-permute-start(bf16[2,240,640]{2,1,0:T(8,128)(2,1)S(1)} %pad_maximum_fusion.1), channel_id=1, source_target_pairs={{0,4},{4,0},{8,12},{12,8},{16,20},{20,16},{24,28},{28,24},{1,5},{5... | collective-permute-start | bytes 1843208 | tf_op jit(solution)/shard_map/ppermute | solution.py:902
  532.5 12.4 %collective-permute-start.94 = (bf16[960,256]{1,0:T(8,128)(2,1)S(1)}, bf16[960,256]{1,0:T(8,128)(2,1)S(1)}, u32[]{:S(2)}, u32[]{:S(2)}) collective-permute-start(bf16[960,256]{1,0:T(8,128)(2,1)S(1)} %get-tuple-element.470), channel_id=1, source_target_pairs={{0,3},{1,2},{2,1},{3,0},{4,7},{5,6},{6,5},{7,4},{8,11},{9,10},{10,... | collective-permute-start | bytes 1474568 | tf_op jit(solution)/shard_map/ppermute | solution.py:902
  535.5 15.0 %collective-permute-start.97 = (bf16[2,240,640]{2,1,0:T(8,128)(2,1)S(1)}, bf16[2,240,640]{2,1,0:T(8,128)(2,1)S(1)}, u32[]{:S(2)}, u32[]{:S(2)}) collective-permute-start(bf16[2,240,640]{2,1,0:T(8,128)(2,1)S(1)} %pad_maximum_fusion.2), channel_id=1, source_target_pairs={{0,4},{4,0},{8,12},{12,8},{16,20},{20,16},{24,28},{28,24},{1,5},{5... | collective-permute-start | bytes 1843208 | tf_op jit(solution)/shard_map/ppermute | solution.py:902
  (221 other events, 3157.3 us)

commit v4 on v3

--- a/solution.py
+++ b/solution.py
@@ -712,6 +712,102 @@
     )(f, g, gain, after, gate_act, up_act, *o, *gate, *up, *down)
 
 
+def feed_turn_kernel(f_ref, h, g, *refs):
+    attended, gain = refs[:PARTS], refs[PARTS]
+    o, gate, up, down, refs = split_pieces(refs[PARTS + 1 :])
+    outs, result, grad_after, branch_out = refs[:5], refs[5], refs[6], refs[7]
+    grad_attended, gain_grad = refs[8 : 8 + PARTS], refs[8 + PARTS]
+    w_o, w_gate, w_up, w_down, n16, after, gate_out, up_out, *refs = refs[9 + PARTS :]
+    attended_t, normed_t, hidden_out, grad_gate, grad_up = refs[:5]
+    o_sem, gate_sem, up_sem, down_sem, out_sem = refs[5:]
+    depth, wide = 4 * o[0].shape[0], w_gate.shape[1]
+    o_copies = row_copies(f_ref[0], o, w_o, o_sem)
+    gate_copies = side_copies(f_ref, 1, gate, w_gate, gate_sem)
+    up_copies = side_copies(f_ref, 2, up, w_up, up_sem)
+    d_copies = down_copies(f_ref, 1, down, w_down, down_sem)
+    leaving = [pltpu.make_async_copy(refs[k], outs[k], out_sem.at[k]) for k in range(5)]
+    for copies in (o_copies, gate_copies, up_copies, d_copies):
+        start(copies)
+    att = jnp.concatenate([attended[i][...] for i in ORDER], axis=1)
+    attended_t[...] = att.T
+    w_o[depth:, :] = jnp.zeros((w_o.shape[0] - depth, w_o.shape[1]), bf16)
+    wait(o_copies)
+    value = h[...].astype(f32) + nn(att, w_o[...])
+    after[...] = value
+    normed = (value * inverse_of(value) * gain[...]).astype(bf16)
+    n16[...] = normed
+    normed_t[...] = normed.T
+    wait(gate_copies)
+    wait(up_copies)
+    for at in range(0, wide, CHUNK):
+        columns = slice(at, at + CHUNK)
+        gate_act = nn(n16[...], w_gate[:, columns])
+        up_act = nn(n16[...], w_up[:, columns])
+        gate_out[:, columns] = gate_act.astype(bf16)
+        up_out[:, columns] = up_act.astype(bf16)
+        hidden_out[:, columns] = (gate_act * jax.nn.sigmoid(gate_act) * up_act).astype(bf16)
+    start(leaving[:3])
+    wait(d_copies)
+    result[...] = (after[...] + nt(hidden_out[...], w_down[...])).astype(result.dtype)
+    for at in range(0, wide, CHUNK):
+        columns = slice(at, at + CHUNK)
+        grad_hidden = nn(g[...], w_down[:, columns])
+        value = gate_out[:, columns].astype(f32)
+        logistic = jax.nn.sigmoid(value)
+        steep = logistic * (1.0 + value * (1.0 - logistic))
+        grad_gate[:, columns] = (grad_hidden * up_out[:, columns].astype(f32) * steep).astype(bf16)
+        grad_up[:, columns] = (grad_hidden * (value * logistic)).astype(bf16)
+    start(leaving[3:])
+    grad_normed = nt(grad_gate[...], w_gate[...]) + nt(grad_up[...], w_up[...])
+    back, gain_part = norm_back(grad_normed, after[...], gain[...])
+    back = back + g[...].astype(f32)
+    gain_grad[...] = gain_part
+    grad_after[...] = back
+    branch = back.astype(bf16)
+    branch_out[...] = branch
+    whole = nt(branch, w_o[...]).astype(bf16)
+    at = 0
+    for i in ORDER:
+        lanes = grad_attended[i].shape[1]
+        grad_attended[i][...] = whole[:, at : at + lanes]
+        at += lanes
+    wait(leaving)
+
+
+def feed_turn(f, hidden, g, attended, gain, o, gate, up, down):
+    tokens, width = hidden.shape
+    wide = gate[0].shape[1]
+    full = lambda *shape: pl.BlockSpec(shape, lambda i, f: (0,) * len(shape))
+    like = jax.ShapeDtypeStruct
+    lanes = [pair_lanes(heads_here) for _, heads_here in GROUPS]
+    kept = [(((HEADS + 1) * HEAD, tokens), bf16), ((width, tokens), bf16)] + [((tokens, wide), bf16)] * 3
+    return pl.pallas_call(
+        feed_turn_kernel,
+        grid_spec=pltpu.PrefetchScalarGridSpec(
+            num_scalar_prefetch=1,
+            grid=(1,),
+            in_specs=[full(tokens, width)] * 2 + [full(*a.shape) for a in attended] + [full(1, width)] + [ANY] * 22,
+            out_specs=[ANY] * 5
+            + [full(tokens, width)] * 3
+            + [full(tokens, n) for n in lanes]
+            + [full(1, width)],
+            scratch_shapes=weight_scratch(o[0], gate[0])
+            + [pltpu.VMEM((tokens, width), bf16), pltpu.VMEM((tokens, width), f32)]
+            + [pltpu.VMEM((tokens, wide), bf16)] * 2
+            + [pltpu.VMEM(*k) for k in kept]
+            + weight_sems()
+            + [pltpu.SemaphoreType.DMA((5,))],
+        ),
+        out_shape=[like(*k) for k in kept]
+        + [like((tokens, width), bf16), like((tokens, width), f32), like((tokens, width), bf16)]
+        + [like((tokens, n), bf16) for n in lanes]
+        + [like((1, width), f32)],
+        compiler_params=params(60),
+        cost_estimate=cost(4e10, 1e6),
+        name="feed_turn",
+    )(f, hidden, g, *attended, gain, *o, *gate, *up, *down)
+
+
 def project_back_kernel(f_ref, *refs):
     grad_q, kept, came = refs[:PARTS], refs[PARTS : 2 * PARTS], refs[2 * PARTS : 3 * PARTS]
     cos_ref, sin_ref, h, gain, grad_after, own, near, far, last = refs[3 * PARTS : 3 * PARTS + 9]
@@ -1117,8 +1213,11 @@
     )
     h1, (other_cotangent,), first = feed_phase(h0, weights, run, f32, [(cotangent_t[:, half:], "fsdp", 3)])
     run, _ = attend_phases(h1, [], (none,) * 5)
-    h2, _, second = feed_phase(h1, weights, run, bf16)
-    _, (cot, cot_turned) = clock.phase((), lambda turn: join(cotangent_t, other_cotangent))
+    cot, cot_turned = join(cotangent_t, other_cotangent)
+    _, turn_out = clock.phase((), lambda turn: feed_turn(turn, h1, cot, run[3], gain_f, *weights))
+    attended_t, normed_ffn_t, hidden_act, grad_gate, grad_up, h2, *rest = turn_out
+    second = (h1, run[0], run[1], run[2], run[3], run[4], None, attended_t, normed_ffn_t, None, None, hidden_act)
+    fed2 = (grad_gate, grad_up, *rest)
 
     def feed_back_work(g, stored):
         return lambda turn: feed_back(turn, g, stored[6], gain_f, stored[9], stored[10], *weights)
@@ -1168,7 +1267,6 @@
             turn, *parts, cos, sin, stored[0], gain_a, grad_after, w_in, result_type
         )
 
-    _, fed2 = clock.phase((), feed_back_work(cot, second))
     out_first, out_second = part(f, h2)
     parts, extra = back_phases(
         fed2[4 : 4 + PARTS], second, lambda k: ([(out_second, "fsdp", 3)] if k == 0 else [], ())

time: 588 us -> 574 us (0.976)
  Pallas kernels: 233 us -> 223 us
  local copies, waits for them, and re-layouts: 24.5 us -> 31.4 us
    pallas_call x0 -> x1, Pallas kernels: none -> 31.9 us  [feed_turn(): pl.pallas_call(feed_turn_kernel, grid_spec=pltpu.PrefetchScalarGridSpec(n...]
    pallas_call x2 -> x1, Pallas kernels: 44.4 us -> 22.3 us  [feed_back(): pl.pallas_call(feed_back_kernel, grid_spec=pltpu.PrefetchScalarGridSpec(n...]
    pallas_call x2 -> x1, Pallas kernels: 35.3 us -> 17.7 us  [feed(): pl.pallas_call(feed_kernel, grid_spec=pltpu.PrefetchScalarGridSpec(num_sc...]
    unnamed x334 -> x356, local copies, waits for them, and re-layouts: 22.5 us -> 28.6 us
  transfers between devices with their start and end apart: 102 -> 102, of which waited for: 45 -> 47; matrix products, arithmetic and copies ran while one was open for 5% -> 4% of each run, Pallas kernels for 28% -> 29%
where the time goes in v4:
time: 574 us; the launch traced here: 570 us
  Pallas kernels  223 us (39%)
  waiting for transfers between devices  208 us (36%)
  starting transfers between devices  75.1 us (13%)
  local copies, waits for them, and re-layouts  31.4 us (5%)
  other arithmetic  28.4 us (5%)
    ppermute x102, waiting for transfers between devices, flip(): return lax.ppermute(array, axis, [(i, i ^ bit) for i in range(size)])  208 us
    ppermute x102, starting transfers between devices, flip(): return lax.ppermute(array, axis, [(i, i ^ bit) for i in range(size)])  75.1 us
    pallas_call x6, Pallas kernels, attend_back(): pl.pallas_call(attend_back_kernel, grid_spec=pltpu.PrefetchScalarGridSpec...  61.9 us
    pallas_call x6, Pallas kernels, attend(): pl.pallas_call(attend_kernel, grid_spec=pltpu.PrefetchScalarGridSpec(num_...  37.1 us
    pallas_call x1, Pallas kernels, feed_turn(): pl.pallas_call(feed_turn_kernel, grid_spec=pltpu.PrefetchScalarGridSpec(n...  31.9 us
    unnamed x356, local copies, waits for them, and re-layouts  28.6 us
    pallas_call x1, Pallas kernels, feed_back(): pl.pallas_call(feed_back_kernel, grid_spec=pltpu.PrefetchScalarGridSpec(n...  22.3 us
    pallas_call x1, Pallas kernels, feed(): pl.pallas_call(feed_kernel, grid_spec=pltpu.PrefetchScalarGridSpec(num_sc...  17.7 us
  transfers between devices with their start and end apart: 102, of which 47 were waited for; matrix products, arithmetic and copies ran while one was open for 4% of the time, Pallas kernels for 29%

profile of v4, /device:TPU:0, one launch (start us, length us, event | category | flops | bytes accessed | tf_op | source)
XLA Modules:
  0.0 569.6 jit_solution(9293652082782872189)
XLA Ops:
  11.9 24.4 %collective-permute-done.2.second = bf16[960,256]{1,0:T(8,128)(2,1)S(1)} collective-permute-done((bf16[960,256]{1,0:T(8,128)(2,1)}, bf16[960,256]{1,0:T(8,128)(2,1)S(1)}, u32[]{:S(2)}, u32[]{:S(2)}) %collective-permute-start.2) | collective-permute-done | bytes 491552 | tf_op jit(solution)/shard_map/ppermute | solution.py:998
  39.9 12.8 %collective-permute-done.3.refs_10_.refs_9_ = bf16[240,1280]{1,0:T(8,128)(2,1)S(1)} collective-permute-done((bf16[240,1280]{1,0:T(8,128)(2,1)S(1)}, bf16[240,1280]{1,0:T(8,128)(2,1)S(1)}, u32[]{:S(2)}, u32[]{:S(2)}) %collective-permute-start.3) | collective-permute-done | bytes 614432 | tf_op jit(solution)/shard_map/ppermute | solution.py:998
  56.0 4.5 project.2
  61.5 6.3 %collective-permute-done.5.refs_16_.refs_15_ = bf16[240,1280]{1,0:T(8,128)(2,1)S(1)} collective-permute-done((bf16[240,1280]{1,0:T(8,128)(2,1)S(1)}, bf16[240,1280]{1,0:T(8,128)(2,1)S(1)}, u32[]{:S(2)}, u32[]{:S(2)}) %collective-permute-start.5) | collective-permute-done | bytes 614432 | tf_op jit(solution)/shard_map/ppermute | solution.py:998
  70.4 5.2 collective-permute-done.7.far
  81.1 15.7 %collective-permute-done.13.far = bf16[2,512,128]{2,1,0:T(8,128)(2,1)S(1)} collective-permute-done((bf16[2,512,128]{2,1,0:T(8,128)(2,1)S(1)}, bf16[2,512,128]{2,1,0:T(8,128)(2,1)S(1)}, u32[]{:S(2)}, u32[]{:S(2)}) %collective-permute-start.13) | collective-permute-done | bytes 262176 | tf_op jit(solution)/shard_map/ppermute | solution.py:998
  100.6 4.1 attend.6
  104.8 12.7 %collective-permute-done.19.far = bf16[2,512,128]{2,1,0:T(8,128)(2,1)S(1)} collective-permute-done((bf16[2,512,128]{2,1,0:T(8,128)(2,1)S(1)}, bf16[2,512,128]{2,1,0:T(8,128)(2,1)S(1)}, u32[]{:S(2)}, u32[]{:S(2)}) %collective-permute-start.19) | collective-permute-done | bytes 262176 | tf_op jit(solution)/shard_map/ppermute | solution.py:998
  119.0 7.3 %attend.7 = (bf16[512,384]{1,0:T(8,128)(2,1)S(1)}, bf16[6,512,128]{2,1,0:T(8,128)(2,1)S(1)}) custom-call(s32[3]{0:T(128)S(1)} %pad_add_fusion.1.f_ref, bf16[15,512,128]{2,1,0:T(8,128)(2,1)S(1)} %get-tuple-element.271.q, bf16[512,128]{1,0:T(8,128)(2,1)S(1)} %select_convert_fusion.13.q_marks, bf16[2048,128]{1,0:T(8,128)(2,1)S(1)} %fusion.2.key_marks, ...), custom_call_target="tpu_custom_call" | custom-call | flops 40000000000 | bytes 1000000 | tf_op jit(solution)/shard_map/attend/pallas_call | solution.py:154
  128.5 7.1 %attend.8 = (bf16[512,384]{1,0:T(8,128)(2,1)S(1)}, bf16[6,512,128]{2,1,0:T(8,128)(2,1)S(1)}) custom-call(s32[3]{0:T(128)S(1)} %pad_add_fusion.1.f_ref, bf16[15,512,128]{2,1,0:T(8,128)(2,1)S(1)} %get-tuple-element.271.q, bf16[512,128]{1,0:T(8,128)(2,1)S(1)} %select_convert_fusion.13.q_marks, bf16[2048,128]{1,0:T(8,128)(2,1)S(1)} %fusion.2.key_marks, ...), custom_call_target="tpu_custom_call" | custom-call | flops 40000000000 | bytes 1000000 | tf_op jit(solution)/shard_map/attend/pallas_call | solution.py:154
  138.5 17.7 %feed.1 = (f32[512,960]{1,0:T(8,128)}, bf16[1024,512]{1,0:T(8,128)(2,1)}, bf16[960,512]{1,0:T(8,128)(2,1)}, bf16[512,2560]{1,0:T(8,128)(2,1)}, bf16[512,2560]{1,...) custom-call(s32[3]{0:T(128)S(1)} %pad_add_fusion.1.f_ref, bf16[512,960]{1,0:T(8,128)(2,1)} %copy-done.110, ...), custom_call_target="tpu_custom_call" | custom-call | flops 40000000000 | bytes 1000000 | tf_op jit(solution)/shard_map/feed/pallas_call | solution.py:604
  157.9 4.4 project.3
  163.3 5.0 collective-permute-done.32.far
  170.6 5.2 collective-permute-done.35.far
  176.4 4.1 attend.9
  182.5 7.1 %attend.10 = (bf16[512,384]{1,0:T(8,128)(2,1)S(1)}, bf16[6,512,128]{2,1,0:T(8,128)(2,1)S(1)}) custom-call(s32[3]{0:T(128)S(1)} %pad_add_fusion.1.f_ref, bf16[15,512,128]{2,1,0:T(8,128)(2,1)S(1)} %get-tuple-element.304.q, bf16[512,128]{1,0:T(8,128)(2,1)S(1)} %select_convert_fusion.13.q_marks, bf16[2048,128]{1,0:T(8,128)(2,1)S(1)} %fusion.2.key_marks, ...), custom_call_target="tpu_custom_call" | custom-call | flops 40000000000 | bytes 1000000 | tf_op jit(solution)/shard_map/attend/pallas_call | solution.py:154
  191.2 7.3 %attend.11 = (bf16[512,384]{1,0:T(8,128)(2,1)S(1)}, bf16[6,512,128]{2,1,0:T(8,128)(2,1)S(1)}) custom-call(s32[3]{0:T(128)S(1)} %pad_add_fusion.1.f_ref, bf16[15,512,128]{2,1,0:T(8,128)(2,1)S(1)} %get-tuple-element.304.q, bf16[512,128]{1,0:T(8,128)(2,1)S(1)} %select_convert_fusion.13.q_marks, bf16[2048,128]{1,0:T(8,128)(2,1)S(1)} %fusion.2.key_marks, ...), custom_call_target="tpu_custom_call" | custom-call | flops 40000000000 | bytes 1000000 | tf_op jit(solution)/shard_map/attend/pallas_call | solution.py:154
  200.2 31.9 %feed_turn.1 = (bf16[1024,512]{1,0:T(8,128)(2,1)}, bf16[960,512]{1,0:T(8,128)(2,1)}, bf16[512,2560]{1,0:T(8,128)(2,1)}, bf16[512,2560]{1,0:T(8,128)(2,1)}, bf16[...) custom-call(s32[3]{0:T(128)} %copy-done.13, ...), custom_call_target="tpu_custom_call" | custom-call | flops 40000000000 | bytes 1000000 | tf_op jit(solution)/shard_map/feed_turn/pallas_call | solution.py:784
  235.6 12.2 %attend_back.6 = (bf16[512,384]{1,0:T(8,128)(2,1)S(1)}, bf16[2,2,512,128]{3,2,1,0:T(8,128)(2,1)S(1)}, bf16[2,2,512,128]{3,2,1,0:T(8,128)(2,1)S(1)}) custom-call(s32[3]{0:T(128)S(1)} %copy-done.14, bf16[15,512,128]{2,1,0:T(8,128)(2,1)S(1)} %copy-done.99, bf16[6,512,128]{2,1,0:T(8,128)(2,1)S(1)} %copy-done.128, bf16[2048,128]{1,0:T(8,128)(2,1)S(1)} %fusion.2.key_marks, ...), custom_call_target="tpu_custom_call" | custom-call | flops 40000000000 | bytes 1000000 | tf_op jit(solution)/shard_map/attend_back/pallas_call | solution.py:272
  249.1 12.6 %attend_back.7 = (bf16[512,384]{1,0:T(8,128)(2,1)S(1)}, bf16[2,2,512,128]{3,2,1,0:T(8,128)(2,1)S(1)}, bf16[2,2,512,128]{3,2,1,0:T(8,128)(2,1)S(1)}) custom-call(s32[3]{0:T(128)S(1)} %copy-done.14, bf16[15,512,128]{2,1,0:T(8,128)(2,1)S(1)} %copy-done.99, bf16[6,512,128]{2,1,0:T(8,128)(2,1)S(1)} %copy-done.126, bf16[2048,128]{1,0:T(8,128)(2,1)S(1)} %fusion.2.key_marks, ...), custom_call_target="tpu_custom_call" | custom-call | flops 40000000000 | bytes 1000000 | tf_op jit(solution)/shard_map/attend_back/pallas_call | solution.py:272
  263.2 6.0 %attend_back.8 = (bf16[512,256]{1,0:T(8,128)(2,1)S(1)}, bf16[2,1,512,128]{3,2,1,0:T(8,128)(2,1)S(1)}, bf16[2,1,512,128]{3,2,1,0:T(8,128)(2,1)S(1)}) custom-call(s32[3]{0:T(128)S(1)} %copy-done.14, bf16[15,512,128]{2,1,0:T(8,128)(2,1)S(1)} %copy-done.99, bf16[3,512,128]{2,1,0:T(8,128)(2,1)S(1)} %copy-done.146, bf16[2048,128]{1,0:T(8,128)(2,1)S(1)} %fusion.2.key_marks, ...), custom_call_target="tpu_custom_call" | custom-call | flops 40000000000 | bytes 1000000 | tf_op jit(solution)/shard_map/attend_back/pallas_call | solution.py:272
  273.7 6.1 %collective-permute-done.46.refs_8_ = bf16[2,512,128]{2,1,0:T(8,128)(2,1)S(1)} collective-permute-done((bf16[2,512,128]{2,1,0:T(8,128)(2,1)}, bf16[2,512,128]{2,1,0:T(8,128)(2,1)S(1)}, u32[]{:S(2)}, u32[]{:S(2)}) %collective-permute-start.46) | collective-permute-done | bytes 262176 | tf_op jit(solution)/shard_map/ppermute | solution.py:998
  290.0 4.9 project_back.2
  296.3 3.3 outer_down_far.1
  299.7 3.3 outer_down_own.1
  304.7 22.3 %feed_back.1 = (bf16[512,2560]{1,0:T(8,128)(2,1)}, bf16[512,2560]{1,0:T(8,128)(2,1)}, f32[512,960]{1,0:T(8,128)}, bf16[512,960]{1,0:T(8,128)(2,1)}, bf16[512,256...) custom-call(s32[3]{0:T(128)S(1)} %copy-done.14, ...), custom_call_target="tpu_custom_call" | custom-call | flops 40000000000 | bytes 1000000 | tf_op jit(solution)/shard_map/feed_back/pallas_call | solution.py:690
  327.6 5.3 collective-permute-done.50
  336.0 6.9 %outer_gate.1 = (bf16[4,240,640]{2,1,0:T(8,128)(2,1)S(1)}, bf16[4,240,640]{2,1,0:T(8,128)(2,1)S(1)}, bf16[4,240,640]{2,1,0:T(8,128)(2,1)S(1)}, bf16[4,240,640]{2,1,0:T(8,128)(2,1)S(1)}) custom-call(s32[3]{0:T(128)S(1)} %copy-done.14, bf16[960,512]{1,0:T(8,128)(2,1)S(1)} %copy-done.114, bf16[960,512]{1,0:T(8,128)(2,1)S(1)} %copy-done.113, ...), custom_call_target="tpu_custom_call" | custom-call | flops 40000000000 | bytes 1000000 | tf_op jit(solution)/shard_map/outer_gate/pallas_call | solution.py:888
  344.0 7.0 %outer_up.1 = (bf16[4,240,640]{2,1,0:T(8,128)(2,1)S(1)}, bf16[4,240,640]{2,1,0:T(8,128)(2,1)S(1)}, bf16[4,240,640]{2,1,0:T(8,128)(2,1)S(1)}, bf16[4,240,640]{2,1,0:T(8,128)(2,1)S(1)}) custom-call(s32[3]{0:T(128)S(1)} %copy-done.14, bf16[960,512]{1,0:T(8,128)(2,1)S(1)} %copy-done.114, bf16[960,512]{1,0:T(8,128)(2,1)S(1)} %copy-done.113, ...), custom_call_target="tpu_custom_call" | custom-call | flops 40000000000 | bytes 1000000 | tf_op jit(solution)/shard_map/outer_up/pallas_call | solution.py:888
  354.1 3.9 collective-permute-done.52
  361.7 12.3 %attend_back.9 = (bf16[512,384]{1,0:T(8,128)(2,1)S(1)}, bf16[2,2,512,128]{3,2,1,0:T(8,128)(2,1)S(1)}, bf16[2,2,512,128]{3,2,1,0:T(8,128)(2,1)S(1)}) custom-call(s32[3]{0:T(128)S(1)} %copy-done.14, bf16[15,512,128]{2,1,0:T(8,128)(2,1)S(1)} %copy-done.101, bf16[6,512,128]{2,1,0:T(8,128)(2,1)S(1)} %copy-done.124, bf16[2048,128]{1,0:T(8,128)(2,1)S(1)} %copy-done.1, ...), custom_call_target="tpu_custom_call" | custom-call | flops 40000000000 | bytes 1000000 | tf_op jit(solution)/shard_map/attend_back/pallas_call | solution.py:272
  380.1 12.7 %attend_back.10 = (bf16[512,384]{1,0:T(8,128)(2,1)S(1)}, bf16[2,2,512,128]{3,2,1,0:T(8,128)(2,1)S(1)}, bf16[2,2,512,128]{3,2,1,0:T(8,128)(2,1)S(1)}) custom-call(s32[3]{0:T(128)S(1)} %copy-done.14, bf16[15,512,128]{2,1,0:T(8,128)(2,1)S(1)} %copy-done.101, bf16[6,512,128]{2,1,0:T(8,128)(2,1)S(1)} %copy-done.122, bf16[2048,128]{1,0:T(8,128)(2,1)S(1)} %copy-done.1, ...), custom_call_target="tpu_custom_call" | custom-call | flops 40000000000 | bytes 1000000 | tf_op jit(solution)/shard_map/attend_back/pallas_call | solution.py:272
  398.3 6.1 %attend_back.11 = (bf16[512,256]{1,0:T(8,128)(2,1)S(1)}, bf16[2,1,512,128]{3,2,1,0:T(8,128)(2,1)S(1)}, bf16[2,1,512,128]{3,2,1,0:T(8,128)(2,1)S(1)}) custom-call(s32[3]{0:T(128)S(1)} %copy-done.14, bf16[15,512,128]{2,1,0:T(8,128)(2,1)S(1)} %copy-done.101, bf16[3,512,128]{2,1,0:T(8,128)(2,1)S(1)} %copy-done.144, bf16[2048,128]{1,0:T(8,128)(2,1)S(1)} %copy-done.1, ...), custom_call_target="tpu_custom_call" | custom-call | flops 40000000000 | bytes 1000000 | tf_op jit(solution)/shard_map/attend_back/pallas_call | solution.py:272
  404.6 6.6 %collective-permute-done.64 = bf16[2,240,640]{2,1,0:T(8,128)(2,1)S(1)} collective-permute-done((bf16[2,240,640]{2,1,0:T(8,128)(2,1)S(1)}, bf16[2,240,640]{2,1,0:T(8,128)(2,1)S(1)}, u32[]{:S(2)}, u32[]{:S(2)}) %collective-permute-start.64) | collective-permute-done | bytes 614432 | tf_op jit(solution)/shard_map/ppermute | solution.py:998
  411.5 6.3 %collective-permute-done.66.refs_7_ = bf16[2,512,128]{2,1,0:T(8,128)(2,1)S(1)} collective-permute-done((bf16[2,512,128]{2,1,0:T(8,128)(2,1)S(1)}, bf16[2,512,128]{2,1,0:T(8,128)(2,1)S(1)}, u32[]{:S(2)}, u32[]{:S(2)}) %collective-permute-start.66) | collective-permute-done | bytes 262176 | tf_op jit(solution)/shard_map/ppermute | solution.py:998
  420.4 6.4 %collective-permute-done.70.refs_8_ = bf16[2,512,128]{2,1,0:T(8,128)(2,1)S(1)} collective-permute-done((bf16[2,512,128]{2,1,0:T(8,128)(2,1)S(1)}, bf16[2,512,128]{2,1,0:T(8,128)(2,1)S(1)}, u32[]{:S(2)}, u32[]{:S(2)}) %collective-permute-start.70) | collective-permute-done | bytes 262176 | tf_op jit(solution)/shard_map/ppermute | solution.py:998
  435.0 5.9 %project_back.3 = (bf16[512,1664]{1,0:T(8,128)(2,1)S(1)}, bf16[512,960]{1,0:T(8,128)(2,1)S(1)}, bf16[960,512]{1,0:T(8,128)(2,1)}, f32[1,960]{1,0:T(1,128)S(1)}) custom-call(s32[3]{0:T(128)S(1)} %copy-done.14, bf16[512,256]{1,0:T(8,128)(2,1)S(1)} %get-tuple-element.417.refs_0_, bf16[512,384]{1,0:T(8,128)(2,1)S(1)} %get-tuple-element.397.refs_1_, ...), custom_call_target="tpu_custom_call" | custom-call | flops 40000000000 | bytes 1000000 | tf_op jit(solution)/shard_map/project_back/pallas_call | solution.py:846
  455.0 4.6 outer_in.1
  461.5 3.1 collective-permute-done.75
  467.2 4.1 collective-permute-done.80
  483.1 4.7 collective-permute-done.85
  488.0 7.4 %collective-permute-done.82 = bf16[1,256,1664]{2,1,0:T(8,128)(2,1)S(1)} collective-permute-done((bf16[1,256,1664]{2,1,0:T(8,128)(2,1)S(1)}, bf16[1,256,1664]{2,1,0:T(8,128)(2,1)S(1)}, u32[]{:S(2)}, u32[]{:S(2)}) %collective-permute-start.82) | collective-permute-done | bytes 852000 | tf_op jit(solution)/shard_map/ppermute | solution.py:998
  513.5 5.4 collective-permute-done.90
  519.2 6.5 %collective-permute-done.93 = bf16[2,240,640]{2,1,0:T(8,128)(2,1)S(1)} collective-permute-done((bf16[2,240,640]{2,1,0:T(8,128)(2,1)S(1)}, bf16[2,240,640]{2,1,0:T(8,128)(2,1)S(1)}, u32[]{:S(2)}, u32[]{:S(2)}) %collective-permute-start.93) | collective-permute-done | bytes 614432 | tf_op jit(solution)/shard_map/ppermute | solution.py:998
  533.7 9.4 %collective-permute-done.94 = bf16[960,256]{1,0:T(8,128)(2,1)S(1)} collective-permute-done((bf16[960,256]{1,0:T(8,128)(2,1)S(1)}, bf16[960,256]{1,0:T(8,128)(2,1)S(1)}, u32[]{:S(2)}, u32[]{:S(2)}) %collective-permute-start.94) | collective-permute-done | bytes 491552 | tf_op jit(solution)/shard_map/ppermute | solution.py:998
  545.4 6.4 %collective-permute-done.98 = bf16[1,32,1664]{2,1,0:T(8,128)(2,1)S(1)} collective-permute-done((bf16[1,32,1664]{2,1,0:T(8,128)(2,1)S(1)}, bf16[1,32,1664]{2,1,0:T(8,128)(2,1)S(1)}, u32[]{:S(2)}, u32[]{:S(2)}) %collective-permute-start.98) | collective-permute-done | bytes 106528 | tf_op jit(solution)/shard_map/ppermute | solution.py:998
  554.1 4.0 collective-permute-done.100
  561.8 5.5 collective-permute-done.101
  (652 shorter events, 172.2 us)
Async XLA Ops:
  5.6 30.7 %collective-permute-start = (bf16[240,1664]{1,0:T(8,128)(2,1)S(1)}, bf16[240,1664]{1,0:T(8,128)(2,1)S(1)}, u32[]{:S(2)}, u32[]{:S(2)}) collective-permute-start(bf16[240,1664]{1,0:T(8,128)(2,1)S(1)} %pack.1.own.refs_14_), channel_id=1, source_target_pairs={{0,2},{1,3},{2,0},{3,1},{4,6},{5,7},{6,4},{7,5},{8,10},{9,11},{10,... | collective-permute-start | bytes 2396168 | tf_op jit(solution)/shard_map/ppermute | solution.py:998
  8.6 27.7 %collective-permute-start.1 = (bf16[240,1664]{1,0:T(8,128)(2,1)S(1)}, bf16[240,1664]{1,0:T(8,128)(2,1)S(1)}, u32[]{:S(2)}, u32[]{:S(2)}) collective-permute-start(bf16[240,1664]{1,0:T(8,128)(2,1)S(1)} %pack.1.own.refs_14_), channel_id=1, source_target_pairs={{0,1},{1,0},{2,3},{3,2},{4,5},{5,4},{6,7},{7,6},{8,9},{9,8},{10,11... | collective-permute-start | bytes 2396168 | tf_op jit(solution)/shard_map/ppermute | solution.py:998
  8.7 27.7 %collective-permute-start.2 = (bf16[960,256]{1,0:T(8,128)(2,1)}, bf16[960,256]{1,0:T(8,128)(2,1)S(1)}, u32[]{:S(2)}, u32[]{:S(2)}) collective-permute-start(bf16[960,256]{1,0:T(8,128)(2,1)} %slice.345), channel_id=1, source_target_pairs={{0,3},{1,2},{2,1},{3,0},{4,7},{5,6},{6,5},{7,4},{8,11},{9,10},{10,... | collective-permute-start | bytes 1474568 | tf_op jit(solution)/shard_map/ppermute | solution.py:998
  36.4 16.4 %collective-permute-start.4 = (bf16[240,1664]{1,0:T(8,128)(2,1)S(1)}, bf16[240,1664]{1,0:T(8,128)(2,1)S(1)}, u32[]{:S(2)}, u32[]{:S(2)}) collective-permute-start(bf16[240,1664]{1,0:T(8,128)(2,1)S(1)} %collective-permute-done.far.refs_16_), channel_id=1, source_target_pairs={{0,1},{1,0},{2,3},{3,2},{4,5},{5,4},{6,7},{7,6},{8,9},{9,8},{10,11... | collective-permute-start | bytes 2396168 | tf_op jit(solution)/shard_map/ppermute | solution.py:998
  36.9 15.8 %collective-permute-start.3 = (bf16[240,1280]{1,0:T(8,128)(2,1)S(1)}, bf16[240,1280]{1,0:T(8,128)(2,1)S(1)}, u32[]{:S(2)}, u32[]{:S(2)}) collective-permute-start(bf16[240,1280]{1,0:T(8,128)(2,1)S(1)} %slice_select_fusion.1), channel_id=1, source_target_pairs={{0,2},{1,3},{2,0},{3,1},{4,6},{5,7},{6,4},{7,5},{8,10},{9,11},{10,... | collective-permute-start | bytes 1843208 | tf_op jit(solution)/shard_map/ppermute | solution.py:998
  52.7 15.1 %collective-permute-start.5 = (bf16[240,1280]{1,0:T(8,128)(2,1)S(1)}, bf16[240,1280]{1,0:T(8,128)(2,1)S(1)}, u32[]{:S(2)}, u32[]{:S(2)}) collective-permute-start(bf16[240,1280]{1,0:T(8,128)(2,1)S(1)} %slice_select_fusion.2), channel_id=1, source_target_pairs={{0,2},{1,3},{2,0},{3,1},{4,6},{5,7},{6,4},{7,5},{8,10},{9,11},{10,... | collective-permute-start | bytes 1843208 | tf_op jit(solution)/shard_map/ppermute | solution.py:998
  54.5 14.7 %collective-permute-start.6 = (bf16[240,1280]{1,0:T(8,128)(2,1)S(1)}, bf16[240,1280]{1,0:T(8,128)(2,1)S(1)}, u32[]{:S(2)}, u32[]{:S(2)}) collective-permute-start(bf16[240,1280]{1,0:T(8,128)(2,1)S(1)} %collective-permute-done.3.refs_10_.refs_9_), channel_id=1, source_target_pairs={{0,4},{4,0},{8,12},{12,8},{16,20},{20,16},{24,28},{28,24},{1,5},{5... | collective-permute-start | bytes 1843208 | tf_op jit(solution)/shard_map/ppermute | solution.py:998
  75.7 21.1 %collective-permute-start.12 = (bf16[480,640]{1,0:T(8,128)(2,1)S(1)}, bf16[480,640]{1,0:T(8,128)(2,1)S(1)}, u32[]{:S(2)}, u32[]{:S(2)}) collective-permute-start(bf16[480,640]{1,0:T(8,128)(2,1)S(1)} %slice_select_fusion), channel_id=1, source_target_pairs={{0,2},{1,3},{2,0},{3,1},{4,6},{5,7},{6,4},{7,5},{8,10},{9,11},{10,... | collective-permute-start | bytes 1843208 | tf_op jit(solution)/shard_map/ppermute | solution.py:998
  76.2 20.7 %collective-permute-start.16 = (bf16[240,1280]{1,0:T(8,128)(2,1)S(1)}, bf16[240,1280]{1,0:T(8,128)(2,1)S(1)}, u32[]{:S(2)}, u32[]{:S(2)}) collective-permute-start(bf16[240,1280]{1,0:T(8,128)(2,1)S(1)} %collective-permute-done.5.refs_16_.refs_15_), channel_id=1, source_target_pairs={{0,8},{4,12},{8,0},{12,4},{16,24},{20,28},{24,16},{28,20},{1,9},{5... | collective-permute-start | bytes 1843208 | tf_op jit(solution)/shard_map/ppermute | solution.py:998
  77.9 18.9 %collective-permute-start.13 = (bf16[2,512,128]{2,1,0:T(8,128)(2,1)S(1)}, bf16[2,512,128]{2,1,0:T(8,128)(2,1)S(1)}, u32[]{:S(2)}, u32[]{:S(2)}) collective-permute-start(bf16[2,512,128]{2,1,0:T(8,128)(2,1)S(1)} %get-tuple-element.261.own), channel_id=1, source_target_pairs={{0,2},{1,3},{2,0},{3,1},{4,6},{5,7},{6,4},{7,5},{8,10},{9,11},{10,... | collective-permute-start | bytes 786440 | tf_op jit(solution)/shard_map/ppermute | solution.py:998
  79.4 17.4 %collective-permute-start.15 = (bf16[2,512,128]{2,1,0:T(8,128)(2,1)S(1)}, bf16[2,512,128]{2,1,0:T(8,128)(2,1)S(1)}, u32[]{:S(2)}, u32[]{:S(2)}) collective-permute-start(bf16[2,512,128]{2,1,0:T(8,128)(2,1)S(1)} %get-tuple-element.267.own), channel_id=1, source_target_pairs={{0,1},{1,0},{2,3},{3,2},{4,5},{5,4},{6,7},{7,6},{8,9},{9,8},{10,11... | collective-permute-start | bytes 786440 | tf_op jit(solution)/shard_map/ppermute | solution.py:998
  96.9 20.6 %collective-permute-start.21 = (bf16[240,2560]{1,0:T(8,128)(2,1)S(1)}, bf16[240,2560]{1,0:T(8,128)(2,1)S(1)}, u32[]{:S(2)}, u32[]{:S(2)}) collective-permute-start(bf16[240,2560]{1,0:T(8,128)(2,1)S(1)} %copy-done.155), channel_id=1, source_target_pairs={{0,1},{1,0},{2,3},{3,2},{4,5},{5,4},{6,7},{7,6},{8,9},{9,8},{10,11... | collective-permute-start | bytes 3686408 | tf_op jit(solution)/shard_map/ppermute | solution.py:998
  97.0 20.5 %collective-permute-start.17 = (bf16[480,640]{1,0:T(8,128)(2,1)S(1)}, bf16[480,640]{1,0:T(8,128)(2,1)S(1)}, u32[]{:S(2)}, u32[]{:S(2)}) collective-permute-start(bf16[480,640]{1,0:T(8,128)(2,1)S(1)} %collective-permute-done.12.refs_22_.refs_21_), channel_id=1, source_target_pairs={{0,4},{4,0},{8,12},{12,8},{16,20},{20,16},{24,28},{28,24},{1,5},{5... | collective-permute-start | bytes 1843208 | tf_op jit(solution)/shard_map/ppermute | solution.py:998
  98.5 18.9 %collective-permute-start.18 = (bf16[240,960]{1,0:T(8,128)(2,1)S(1)}, bf16[240,960]{1,0:T(8,128)(2,1)S(1)}, u32[]{:S(2)}, u32[]{:S(2)}) collective-permute-start(bf16[240,960]{1,0:T(8,128)(2,1)S(1)} %copy-done.31), channel_id=1, source_target_pairs={{0,2},{1,3},{2,0},{3,1},{4,6},{5,7},{6,4},{7,5},{8,10},{9,11},{10,... | collective-permute-start | bytes 1382408 | tf_op jit(solution)/shard_map/ppermute | solution.py:998
  99.0 18.4 %collective-permute-start.19 = (bf16[2,512,128]{2,1,0:T(8,128)(2,1)S(1)}, bf16[2,512,128]{2,1,0:T(8,128)(2,1)S(1)}, u32[]{:S(2)}, u32[]{:S(2)}) collective-permute-start(bf16[2,512,128]{2,1,0:T(8,128)(2,1)S(1)} %get-tuple-element.267.own), channel_id=1, source_target_pairs={{0,2},{1,3},{2,0},{3,1},{4,6},{5,7},{6,4},{7,5},{8,10},{9,11},{10,... | collective-permute-start | bytes 786440 | tf_op jit(solution)/shard_map/ppermute | solution.py:998
  100.6 16.9 %collective-permute-start.20 = (bf16[2,512,128]{2,1,0:T(8,128)(2,1)S(1)}, bf16[2,512,128]{2,1,0:T(8,128)(2,1)S(1)}, u32[]{:S(2)}, u32[]{:S(2)}) collective-permute-start(bf16[2,512,128]{2,1,0:T(8,128)(2,1)S(1)} %collective-permute-done.13.far), channel_id=1, source_target_pairs={{0,1},{1,0},{2,3},{3,2},{4,5},{5,4},{6,7},{7,6},{8,9},{9,8},{10,11... | collective-permute-start | bytes 786440 | tf_op jit(solution)/shard_map/ppermute | solution.py:998
  136.7 19.6 %collective-permute-start.31 = (bf16[960,256]{1,0:T(8,128)(2,1)S(1)}, bf16[960,256]{1,0:T(8,128)(2,1)S(1)}, u32[]{:S(2)}, u32[]{:S(2)}) collective-permute-start(bf16[960,256]{1,0:T(8,128)(2,1)S(1)} %slice.344), channel_id=1, source_target_pairs={{0,3},{1,2},{2,1},{3,0},{4,7},{5,6},{6,5},{7,4},{8,11},{9,10},{10,... | collective-permute-start | bytes 1474568 | tf_op jit(solution)/shard_map/ppermute | solution.py:998
  234.3 14.3 %collective-permute-start.41 = (bf16[960,256]{1,0:T(8,128)(2,1)S(1)}, bf16[960,256]{1,0:T(8,128)(2,1)S(1)}, u32[]{:S(2)}, u32[]{:S(2)}) collective-permute-start(bf16[960,256]{1,0:T(8,128)(2,1)S(1)} %get-tuple-element.317), channel_id=1, source_target_pairs={{0,3},{1,2},{2,1},{3,0},{4,7},{5,6},{6,5},{7,4},{8,11},{9,10},{10,... | collective-permute-start | bytes 1474568 | tf_op jit(solution)/shard_map/ppermute | solution.py:998
  248.6 13.2 %collective-permute-start.42 = (bf16[2,2,512,128]{3,2,1,0:T(8,128)(2,1)S(1)}, bf16[2,2,512,128]{3,2,1,0:T(8,128)(2,1)S(1)}, u32[]{:S(2)}, u32[]{:S(2)}) collective-permute-start(bf16[2,2,512,128]{3,2,1,0:T(8,128)(2,1)S(1)} %get-tuple-element.324), channel_id=1, source_target_pairs={{0,1},{1,0},{2,3},{3,2},{4,5},{5,4},{6,7},{7,6},{8,9},{9,8},{10,11... | collective-permute-start | bytes 1572872 | tf_op jit(solution)/shard_map/ppermute | solution.py:998
  303.3 24.3 %collective-permute-start.49 = (bf16[1,960,640]{2,1,0:T(8,128)(2,1)S(1)}, bf16[1,960,640]{2,1,0:T(8,128)(2,1)S(1)}, u32[]{:S(2)}, u32[]{:S(2)}) collective-permute-start(bf16[1,960,640]{2,1,0:T(8,128)(2,1)S(1)} %get-tuple-element.356), channel_id=1, source_target_pairs={{0,1},{1,0},{2,3},{3,2},{4,5},{5,4},{6,7},{7,6},{8,9},{9,8},{10,11... | collective-permute-start | bytes 3686408 | tf_op jit(solution)/shard_map/ppermute | solution.py:998
  303.9 29.0 %collective-permute-start.50 = (bf16[1,960,640]{2,1,0:T(8,128)(2,1)S(1)}, bf16[1,960,640]{2,1,0:T(8,128)(2,1)S(1)}, u32[]{:S(2)}, u32[]{:S(2)}) collective-permute-start(bf16[1,960,640]{2,1,0:T(8,128)(2,1)S(1)} %add_convert_fusion), channel_id=1, source_target_pairs={{0,2},{1,3},{2,0},{3,1},{4,6},{5,7},{6,4},{7,5},{8,10},{9,11},{10,... | collective-permute-start | bytes 3686408 | tf_op jit(solution)/shard_map/ppermute | solution.py:998
  342.9 15.1 %collective-permute-start.52 = (bf16[1,480,640]{2,1,0:T(8,128)(2,1)S(1)}, bf16[1,480,640]{2,1,0:T(8,128)(2,1)S(1)}, u32[]{:S(2)}, u32[]{:S(2)}) collective-permute-start(bf16[1,480,640]{2,1,0:T(8,128)(2,1)S(1)} %fusion.3), channel_id=1, source_target_pairs={{0,4},{4,0},{8,12},{12,8},{16,20},{20,16},{24,28},{28,24},{1,5},{5... | collective-permute-start | bytes 1843208 | tf_op jit(solution)/shard_map/ppermute | solution.py:998
  343.5 14.7 %collective-permute-start.51 = (bf16[4,240,640]{2,1,0:T(8,128)(2,1)S(1)}, bf16[4,240,640]{2,1,0:T(8,128)(2,1)S(1)}, u32[]{:S(2)}, u32[]{:S(2)}) collective-permute-start(bf16[4,240,640]{2,1,0:T(8,128)(2,1)S(1)} %get-tuple-element.376), channel_id=1, source_target_pairs={{0,1},{1,0},{2,3},{3,2},{4,5},{5,4},{6,7},{7,6},{8,9},{9,8},{10,11... | collective-permute-start | bytes 3686408 | tf_op jit(solution)/shard_map/ppermute | solution.py:998
  343.5 15.1 %collective-permute-start.53 = (bf16[4,240,640]{2,1,0:T(8,128)(2,1)S(1)}, bf16[4,240,640]{2,1,0:T(8,128)(2,1)S(1)}, u32[]{:S(2)}, u32[]{:S(2)}) collective-permute-start(bf16[4,240,640]{2,1,0:T(8,128)(2,1)S(1)} %get-tuple-element.384), channel_id=1, source_target_pairs={{0,1},{1,0},{2,3},{3,2},{4,5},{5,4},{6,7},{7,6},{8,9},{9,8},{10,11... | collective-permute-start | bytes 3686408 | tf_op jit(solution)/shard_map/ppermute | solution.py:998
  358.6 15.4 %collective-permute-start.56 = (bf16[1,240,640]{2,1,0:T(8,128)(2,1)S(1)}, bf16[1,240,640]{2,1,0:T(8,128)(2,1)S(1)}, u32[]{:S(2)}, u32[]{:S(2)}) collective-permute-start(bf16[1,240,640]{2,1,0:T(8,128)(2,1)S(1)} %fusion.7), channel_id=1, source_target_pairs={{0,8},{4,12},{8,0},{12,4},{16,24},{20,28},{24,16},{28,20},{1,9},{5... | collective-permute-start | bytes 921608 | tf_op jit(solution)/shard_map/ppermute | solution.py:998
  360.3 16.3 %collective-permute-start.55 = (bf16[4,240,640]{2,1,0:T(8,128)(2,1)S(1)}, bf16[4,240,640]{2,1,0:T(8,128)(2,1)S(1)}, u32[]{:S(2)}, u32[]{:S(2)}) collective-permute-start(bf16[4,240,640]{2,1,0:T(8,128)(2,1)S(1)} %get-tuple-element.387), channel_id=1, source_target_pairs={{0,1},{1,0},{2,3},{3,2},{4,5},{5,4},{6,7},{7,6},{8,9},{9,8},{10,11... | collective-permute-start | bytes 3686408 | tf_op jit(solution)/shard_map/ppermute | solution.py:998
  360.3 16.3 %collective-permute-start.58 = (bf16[4,240,640]{2,1,0:T(8,128)(2,1)S(1)}, bf16[4,240,640]{2,1,0:T(8,128)(2,1)S(1)}, u32[]{:S(2)}, u32[]{:S(2)}) collective-permute-start(bf16[4,240,640]{2,1,0:T(8,128)(2,1)S(1)} %get-tuple-element.395), channel_id=1, source_target_pairs={{0,1},{1,0},{2,3},{3,2},{4,5},{5,4},{6,7},{7,6},{8,9},{9,8},{10,11... | collective-permute-start | bytes 3686408 | tf_op jit(solution)/shard_map/ppermute | solution.py:998
  360.8 15.8 %collective-permute-start.57 = (bf16[2,240,640]{2,1,0:T(8,128)(2,1)S(1)}, bf16[2,240,640]{2,1,0:T(8,128)(2,1)S(1)}, u32[]{:S(2)}, u32[]{:S(2)}) collective-permute-start(bf16[2,240,640]{2,1,0:T(8,128)(2,1)S(1)} %get-tuple-element.394), channel_id=1, source_target_pairs={{0,2},{1,3},{2,0},{3,1},{4,6},{5,7},{6,4},{7,5},{8,10},{9,11},{10,... | collective-permute-start | bytes 1843208 | tf_op jit(solution)/shard_map/ppermute | solution.py:998
  361.6 13.2 %collective-permute-start.54 = (bf16[1,256,1024]{2,1,0:T(8,128)(2,1)S(1)}, bf16[1,256,1024]{2,1,0:T(8,128)(2,1)S(1)}, u32[]{:S(2)}, u32[]{:S(2)}) collective-permute-start(bf16[1,256,1024]{2,1,0:T(8,128)(2,1)S(1)} %get-tuple-element.386), channel_id=1, source_target_pairs={{0,1},{1,0},{2,3},{3,2},{4,5},{5,4},{6,7},{7,6},{8,9},{9,8},{10,11... | collective-permute-start | bytes 1572872 | tf_op jit(solution)/shard_map/ppermute | solution.py:998
  376.5 17.4 %collective-permute-start.62 = (bf16[1,120,640]{2,1,0:T(8,128)(2,1)S(1)}, bf16[1,120,640]{2,1,0:T(8,128)(2,1)S(1)}, u32[]{:S(2)}, u32[]{:S(2)}) collective-permute-start(bf16[1,120,640]{2,1,0:T(8,128)(2,1)S(1)} %fusion.23), channel_id=1, source_target_pairs={{0,16},{4,20},{8,24},{12,28},{16,0},{20,4},{24,8},{28,12},{1,17},{... | collective-permute-start | bytes 460808 | tf_op jit(solution)/shard_map/ppermute | solution.py:998
  379.2 15.4 %collective-permute-start.61 = (bf16[2,240,640]{2,1,0:T(8,128)(2,1)S(1)}, bf16[2,240,640]{2,1,0:T(8,128)(2,1)S(1)}, u32[]{:S(2)}, u32[]{:S(2)}) collective-permute-start(bf16[2,240,640]{2,1,0:T(8,128)(2,1)S(1)} %get-tuple-element.404), channel_id=1, source_target_pairs={{0,2},{1,3},{2,0},{3,1},{4,6},{5,7},{6,4},{7,5},{8,10},{9,11},{10,... | collective-permute-start | bytes 1843208 | tf_op jit(solution)/shard_map/ppermute | solution.py:998
  380.0 14.0 %collective-permute-start.60 = (bf16[2,2,512,128]{3,2,1,0:T(8,128)(2,1)S(1)}, bf16[2,2,512,128]{3,2,1,0:T(8,128)(2,1)S(1)}, u32[]{:S(2)}, u32[]{:S(2)}) collective-permute-start(bf16[2,2,512,128]{3,2,1,0:T(8,128)(2,1)S(1)} %get-tuple-element.398), channel_id=1, source_target_pairs={{0,1},{1,0},{2,3},{3,2},{4,5},{5,4},{6,7},{7,6},{8,9},{9,8},{10,11... | collective-permute-start | bytes 1572872 | tf_op jit(solution)/shard_map/ppermute | solution.py:998
  395.3 15.9 %collective-permute-start.64 = (bf16[2,240,640]{2,1,0:T(8,128)(2,1)S(1)}, bf16[2,240,640]{2,1,0:T(8,128)(2,1)S(1)}, u32[]{:S(2)}, u32[]{:S(2)}) collective-permute-start(bf16[2,240,640]{2,1,0:T(8,128)(2,1)S(1)} %select_convert_fusion.1), channel_id=1, source_target_pairs={{0,4},{4,0},{8,12},{12,8},{16,20},{20,16},{24,28},{28,24},{1,5},{5... | collective-permute-start | bytes 1843208 | tf_op jit(solution)/shard_map/ppermute | solution.py:998
  395.9 21.9 %collective-permute-start.63 = (bf16[2,240,640]{2,1,0:T(8,128)(2,1)S(1)}, bf16[2,240,640]{2,1,0:T(8,128)(2,1)S(1)}, u32[]{:S(2)}, u32[]{:S(2)}) collective-permute-start(bf16[2,240,640]{2,1,0:T(8,128)(2,1)S(1)} %get-tuple-element.407), channel_id=1, source_target_pairs={{0,2},{1,3},{2,0},{3,1},{4,6},{5,7},{6,4},{7,5},{8,10},{9,11},{10,... | collective-permute-start | bytes 1843208 | tf_op jit(solution)/shard_map/ppermute | solution.py:998
  397.1 20.7 %collective-permute-start.66 = (bf16[2,512,128]{2,1,0:T(8,128)(2,1)S(1)}, bf16[2,512,128]{2,1,0:T(8,128)(2,1)S(1)}, u32[]{:S(2)}, u32[]{:S(2)}) collective-permute-start(bf16[2,512,128]{2,1,0:T(8,128)(2,1)S(1)} %get-tuple-element.415), channel_id=1, source_target_pairs={{0,2},{1,3},{2,0},{3,1},{4,6},{5,7},{6,4},{7,5},{8,10},{9,11},{10,... | collective-permute-start | bytes 786440 | tf_op jit(solution)/shard_map/ppermute | solution.py:998
  397.9 13.6 %collective-permute-start.67 = (bf16[1,120,640]{2,1,0:T(8,128)(2,1)S(1)}, bf16[1,120,640]{2,1,0:T(8,128)(2,1)S(1)}, u32[]{:S(2)}, u32[]{:S(2)}) collective-permute-start(bf16[1,120,640]{2,1,0:T(8,128)(2,1)S(1)} %fusion.10), channel_id=1, source_target_pairs={{0,16},{4,20},{8,24},{12,28},{16,0},{20,4},{24,8},{28,12},{1,17},{... | collective-permute-start | bytes 460808 | tf_op jit(solution)/shard_map/ppermute | solution.py:998
  432.7 10.5 %collective-permute-start.73 = (bf16[1,120,640]{2,1,0:T(8,128)(2,1)}, bf16[1,120,640]{2,1,0:T(8,128)(2,1)}, u32[]{:S(2)}, u32[]{:S(2)}) collective-permute-start(bf16[1,120,640]{2,1,0:T(8,128)(2,1)} %fusion.24), channel_id=1, source_target_pairs={{0,16},{4,20},{8,24},{12,28},{16,0},{20,4},{24,8},{28,12},{1,17},{... | collective-permute-start | bytes 460808 | tf_op jit(solution)/shard_map/ppermute | solution.py:998
  433.1 14.6 %collective-permute-start.72 = (bf16[2,240,640]{2,1,0:T(8,128)(2,1)}, bf16[2,240,640]{2,1,0:T(8,128)(2,1)}, u32[]{:S(2)}, u32[]{:S(2)}) collective-permute-start(bf16[2,240,640]{2,1,0:T(8,128)(2,1)} %get-tuple-element.423), channel_id=1, source_target_pairs={{0,2},{1,3},{2,0},{3,1},{4,6},{5,7},{6,4},{7,5},{8,10},{9,11},{10,... | collective-permute-start | bytes 1843208 | tf_op jit(solution)/shard_map/ppermute | solution.py:998
  434.3 11.0 %collective-permute-start.74 = (bf16[1,240,640]{2,1,0:T(8,128)(2,1)}, bf16[1,240,640]{2,1,0:T(8,128)(2,1)}, u32[]{:S(2)}, u32[]{:S(2)}) collective-permute-start(bf16[1,240,640]{2,1,0:T(8,128)(2,1)} %pad_maximum_fusion.5), channel_id=1, source_target_pairs={{0,8},{4,12},{8,0},{12,4},{16,24},{20,28},{24,16},{28,20},{1,9},{5... | collective-permute-start | bytes 921608 | tf_op jit(solution)/shard_map/ppermute | solution.py:998
  449.6 11.5 %collective-permute-start.76 = (bf16[1,256,1024]{2,1,0:T(8,128)(2,1)S(1)}, bf16[1,256,1024]{2,1,0:T(8,128)(2,1)S(1)}, u32[]{:S(2)}, u32[]{:S(2)}) collective-permute-start(bf16[1,256,1024]{2,1,0:T(8,128)(2,1)S(1)} %copy-done.163), channel_id=1, source_target_pairs={{0,2},{1,3},{2,0},{3,1},{4,6},{5,7},{6,4},{7,5},{8,10},{9,11},{10,... | collective-permute-start | bytes 1572872 | tf_op jit(solution)/shard_map/ppermute | solution.py:998
  450.9 13.7 %collective-permute-start.75 = (bf16[2,240,640]{2,1,0:T(8,128)(2,1)S(1)}, bf16[2,240,640]{2,1,0:T(8,128)(2,1)S(1)}, u32[]{:S(2)}, u32[]{:S(2)}) collective-permute-start(bf16[2,240,640]{2,1,0:T(8,128)(2,1)S(1)} %select_convert_fusion), channel_id=1, source_target_pairs={{0,4},{4,0},{8,12},{12,8},{16,20},{20,16},{24,28},{28,24},{1,5},{5... | collective-permute-start | bytes 1843208 | tf_op jit(solution)/shard_map/ppermute | solution.py:998
  452.5 12.4 %collective-permute-start.77 = (bf16[1,120,640]{2,1,0:T(8,128)(2,1)S(1)}, bf16[1,120,640]{2,1,0:T(8,128)(2,1)S(1)}, u32[]{:S(2)}, u32[]{:S(2)}) collective-permute-start(bf16[1,120,640]{2,1,0:T(8,128)(2,1)S(1)} %fusion.9), channel_id=1, source_target_pairs={{0,16},{4,20},{8,24},{12,28},{16,0},{20,4},{24,8},{28,12},{1,17},{... | collective-permute-start | bytes 460808 | tf_op jit(solution)/shard_map/ppermute | solution.py:998
  473.9 22.1 %collective-permute-start.86 = (bf16[1,480,640]{2,1,0:T(8,128)(2,1)S(1)}, bf16[1,480,640]{2,1,0:T(8,128)(2,1)S(1)}, u32[]{:S(2)}, u32[]{:S(2)}) collective-permute-start(bf16[1,480,640]{2,1,0:T(8,128)(2,1)S(1)} %pad_maximum_fusion), channel_id=1, source_target_pairs={{0,4},{4,0},{8,12},{12,8},{16,20},{20,16},{24,28},{28,24},{1,5},{5... | collective-permute-start | bytes 1843208 | tf_op jit(solution)/shard_map/ppermute | solution.py:998
  477.1 18.4 %collective-permute-start.82 = (bf16[1,256,1664]{2,1,0:T(8,128)(2,1)S(1)}, bf16[1,256,1664]{2,1,0:T(8,128)(2,1)S(1)}, u32[]{:S(2)}, u32[]{:S(2)}) collective-permute-start(bf16[1,256,1664]{2,1,0:T(8,128)(2,1)S(1)} %add_convert_fusion.1), channel_id=1, source_target_pairs={{0,2},{1,3},{2,0},{3,1},{4,6},{5,7},{6,4},{7,5},{8,10},{9,11},{10,... | collective-permute-start | bytes 2555912 | tf_op jit(solution)/shard_map/ppermute | solution.py:998
  477.9 10.0 %collective-permute-start.85 = (bf16[1,240,640]{2,1,0:T(8,128)(2,1)S(1)}, bf16[1,240,640]{2,1,0:T(8,128)(2,1)S(1)}, u32[]{:S(2)}, u32[]{:S(2)}) collective-permute-start(bf16[1,240,640]{2,1,0:T(8,128)(2,1)S(1)} %pad_maximum_fusion.6), channel_id=1, source_target_pairs={{0,8},{4,12},{8,0},{12,4},{16,24},{20,28},{24,16},{28,20},{1,9},{5... | collective-permute-start | bytes 921608 | tf_op jit(solution)/shard_map/ppermute | solution.py:998
  511.6 14.1 %collective-permute-start.93 = (bf16[2,240,640]{2,1,0:T(8,128)(2,1)S(1)}, bf16[2,240,640]{2,1,0:T(8,128)(2,1)S(1)}, u32[]{:S(2)}, u32[]{:S(2)}) collective-permute-start(bf16[2,240,640]{2,1,0:T(8,128)(2,1)S(1)} %pad_maximum_fusion.1), channel_id=1, source_target_pairs={{0,4},{4,0},{8,12},{12,8},{16,20},{20,16},{24,28},{28,24},{1,5},{5... | collective-permute-start | bytes 1843208 | tf_op jit(solution)/shard_map/ppermute | solution.py:998
  525.7 18.5 %collective-permute-start.97 = (bf16[2,240,640]{2,1,0:T(8,128)(2,1)S(1)}, bf16[2,240,640]{2,1,0:T(8,128)(2,1)S(1)}, u32[]{:S(2)}, u32[]{:S(2)}) collective-permute-start(bf16[2,240,640]{2,1,0:T(8,128)(2,1)S(1)} %pad_maximum_fusion.2), channel_id=1, source_target_pairs={{0,4},{4,0},{8,12},{12,8},{16,20},{20,16},{24,28},{28,24},{1,5},{5... | collective-permute-start | bytes 1843208 | tf_op jit(solution)/shard_map/ppermute | solution.py:998
  530.3 12.9 %collective-permute-start.94 = (bf16[960,256]{1,0:T(8,128)(2,1)S(1)}, bf16[960,256]{1,0:T(8,128)(2,1)S(1)}, u32[]{:S(2)}, u32[]{:S(2)}) collective-permute-start(bf16[960,256]{1,0:T(8,128)(2,1)S(1)} %get-tuple-element.462), channel_id=1, source_target_pairs={{0,3},{1,2},{2,1},{3,0},{4,7},{5,6},{6,5},{7,4},{8,11},{9,10},{10,... | collective-permute-start | bytes 1474568 | tf_op jit(solution)/shard_map/ppermute | solution.py:998
  (232 other events, 3142.5 us)

commit v5 on v4

--- a/solution.py
+++ b/solution.py
@@ -182,7 +182,7 @@
             jax.ShapeDtypeStruct((tokens, width), bf16),
             jax.ShapeDtypeStruct((GROUP * heads_here, tokens, LANES), bf16),
         ],
-        compiler_params=params(26),
+        compiler_params=params(20),
         cost_estimate=cost(4e10, 1e6),
         name="attend",
     )(f, q, q_marks, key_marks, *pieces)
@@ -304,7 +304,7 @@
             jax.ShapeDtypeStruct((2, heads_here, tokens, LANES), bf16),
             jax.ShapeDtypeStruct((2, heads_here, tokens, LANES), bf16),
         ],
-        compiler_params=params(22),
+        compiler_params=params(20),
         cost_estimate=cost(4e10, 1e6),
         name="attend_back",
     )(f, q, marks, key_marks, *pieces, grad, attended, cos, sin)
@@ -615,7 +615,7 @@
             + [pltpu.SemaphoreType.DMA((6, 2))],
         ),
         out_shape=[like(*k) for k in kept] + [like((tokens, width), result_type)],
-        compiler_params=params(48),
+        compiler_params=params(42),
         cost_estimate=cost(4e10, 1e6),
         name="feed",
     )(f, hidden, *attended, gain, *o, *gate, *up, *down)
@@ -706,7 +706,7 @@
         + [like((tokens, width), f32), like((tokens, width), bf16)]
         + [like((tokens, n), bf16) for n in lanes]
         + [like((1, width), f32)],
-        compiler_params=params(52),
+        compiler_params=params(46),
         cost_estimate=cost(4e10, 1e6),
         name="feed_back",
     )(f, g, gain, after, gate_act, up_act, *o, *gate, *up, *down)
@@ -802,7 +802,7 @@
         + [like((tokens, width), bf16), like((tokens, width), f32), like((tokens, width), bf16)]
         + [like((tokens, n), bf16) for n in lanes]
         + [like((1, width), f32)],
-        compiler_params=params(60),
+        compiler_params=params(54),
         cost_estimate=cost(4e10, 1e6),
         name="feed_turn",
     )(f, hidden, g, *attended, gain, *o, *gate, *up, *down)

time: 574 us -> 574 us (level)
    unnamed x356 -> x352, local copies, waits for them, and re-layouts: 28.6 us -> 30 us
  transfers between devices with their start and end apart: 102 -> 102, of which waited for: 47 -> 46; matrix products, arithmetic and copies ran while one was open for 4% -> 4% of each run, Pallas kernels for 29% -> 28%
where the time goes in v5:
time: 574 us; the launch traced here: 569 us
  Pallas kernels  222 us (39%)
  waiting for transfers between devices  209 us (36%)
  starting transfers between devices  74.4 us (13%)
  local copies, waits for them, and re-layouts  32 us (6%)
  other arithmetic  27.6 us (5%)
    ppermute x102, waiting for transfers between devices, flip(): return lax.ppermute(array, axis, [(i, i ^ bit) for i in range(size)])  209 us
    ppermute x102, starting transfers between devices, flip(): return lax.ppermute(array, axis, [(i, i ^ bit) for i in range(size)])  74.4 us
    pallas_call x6, Pallas kernels, attend_back(): pl.pallas_call(attend_back_kernel, grid_spec=pltpu.PrefetchScalarGridSpec...  62.7 us
    pallas_call x6, Pallas kernels, attend(): pl.pallas_call(attend_kernel, grid_spec=pltpu.PrefetchScalarGridSpec(num_...  37.4 us
    pallas_call x1, Pallas kernels, feed_turn(): pl.pallas_call(feed_turn_kernel, grid_spec=pltpu.PrefetchScalarGridSpec(n...  31.7 us
    unnamed x352, local copies, waits for them, and re-layouts  30 us
    pallas_call x1, Pallas kernels, feed_back(): pl.pallas_call(feed_back_kernel, grid_spec=pltpu.PrefetchScalarGridSpec(n...  19.8 us
    pallas_call x1, Pallas kernels, feed(): pl.pallas_call(feed_kernel, grid_spec=pltpu.PrefetchScalarGridSpec(num_sc...  16.6 us
  transfers between devices with their start and end apart: 102, of which 46 were waited for; matrix products, arithmetic and copies ran while one was open for 4% of the time, Pallas kernels for 28%

profile of v5, /device:TPU:0, one launch (start us, length us, event | category | flops | bytes accessed | tf_op | source)
XLA Modules:
  0.0 569.2 jit_solution(12645682961408171804)
XLA Ops:
  11.2 24.3 %collective-permute-done.2.second = bf16[960,256]{1,0:T(8,128)(2,1)S(1)} collective-permute-done((bf16[960,256]{1,0:T(8,128)(2,1)S(1)}, bf16[960,256]{1,0:T(8,128)(2,1)S(1)}, u32[]{:S(2)}, u32[]{:S(2)}) %collective-permute-start.2) | collective-permute-done | bytes 491552 | tf_op jit(solution)/shard_map/ppermute | solution.py:998
  39.1 12.8 %collective-permute-done.3.refs_10_.refs_9_ = bf16[240,1280]{1,0:T(8,128)(2,1)S(1)} collective-permute-done((bf16[240,1280]{1,0:T(8,128)(2,1)S(1)}, bf16[240,1280]{1,0:T(8,128)(2,1)S(1)}, u32[]{:S(2)}, u32[]{:S(2)}) %collective-permute-start.3) | collective-permute-done | bytes 614432 | tf_op jit(solution)/shard_map/ppermute | solution.py:998
  55.3 4.5 project.2
  60.8 6.3 %collective-permute-done.5.refs_16_.refs_15_ = bf16[240,1280]{1,0:T(8,128)(2,1)S(1)} collective-permute-done((bf16[240,1280]{1,0:T(8,128)(2,1)S(1)}, bf16[240,1280]{1,0:T(8,128)(2,1)S(1)}, u32[]{:S(2)}, u32[]{:S(2)}) %collective-permute-start.5) | collective-permute-done | bytes 614432 | tf_op jit(solution)/shard_map/ppermute | solution.py:998
  69.7 5.2 collective-permute-done.7.far
  80.4 15.7 %collective-permute-done.13.far = bf16[2,512,128]{2,1,0:T(8,128)(2,1)S(1)} collective-permute-done((bf16[2,512,128]{2,1,0:T(8,128)(2,1)S(1)}, bf16[2,512,128]{2,1,0:T(8,128)(2,1)S(1)}, u32[]{:S(2)}, u32[]{:S(2)}) %collective-permute-start.13) | collective-permute-done | bytes 262176 | tf_op jit(solution)/shard_map/ppermute | solution.py:998
  99.8 4.1 attend.6
  104.7 12.0 %collective-permute-done.19.far = bf16[2,512,128]{2,1,0:T(8,128)(2,1)S(1)} collective-permute-done((bf16[2,512,128]{2,1,0:T(8,128)(2,1)S(1)}, bf16[2,512,128]{2,1,0:T(8,128)(2,1)S(1)}, u32[]{:S(2)}, u32[]{:S(2)}) %collective-permute-start.19) | collective-permute-done | bytes 262176 | tf_op jit(solution)/shard_map/ppermute | solution.py:998
  119.3 7.5 %attend.7 = (bf16[512,384]{1,0:T(8,128)(2,1)S(1)}, bf16[6,512,128]{2,1,0:T(8,128)(2,1)S(1)}) custom-call(s32[3]{0:T(128)S(1)} %pad_add_fusion.1.f_ref, bf16[15,512,128]{2,1,0:T(8,128)(2,1)S(1)} %get-tuple-element.271.q, bf16[512,128]{1,0:T(8,128)(2,1)S(1)} %select_convert_fusion.13.q_marks, bf16[2048,128]{1,0:T(8,128)(2,1)S(1)} %fusion.2.key_marks, ...), custom_call_target="tpu_custom_call" | custom-call | flops 40000000000 | bytes 1000000 | tf_op jit(solution)/shard_map/attend/pallas_call | solution.py:154
  128.0 7.1 %attend.8 = (bf16[512,384]{1,0:T(8,128)(2,1)S(1)}, bf16[6,512,128]{2,1,0:T(8,128)(2,1)S(1)}) custom-call(s32[3]{0:T(128)S(1)} %pad_add_fusion.1.f_ref, bf16[15,512,128]{2,1,0:T(8,128)(2,1)S(1)} %get-tuple-element.271.q, bf16[512,128]{1,0:T(8,128)(2,1)S(1)} %select_convert_fusion.13.q_marks, bf16[2048,128]{1,0:T(8,128)(2,1)S(1)} %fusion.2.key_marks, ...), custom_call_target="tpu_custom_call" | custom-call | flops 40000000000 | bytes 1000000 | tf_op jit(solution)/shard_map/attend/pallas_call | solution.py:154
  137.8 16.6 %feed.1 = (f32[512,960]{1,0:T(8,128)}, bf16[1024,512]{1,0:T(8,128)(2,1)S(1)}, bf16[960,512]{1,0:T(8,128)(2,1)S(1)}, bf16[512,2560]{1,0:T(8,128)(2,1)}, bf16[512,...) custom-call(s32[3]{0:T(128)S(1)} %pad_add_fusion.1.f_ref, bf16[512,960]{1,0:T(8,128)(2,1)} %copy-done.115, ...), custom_call_target="tpu_custom_call" | custom-call | flops 40000000000 | bytes 1000000 | tf_op jit(solution)/shard_map/feed/pallas_call | solution.py:604
  156.8 4.2 project.3
  161.8 5.2 collective-permute-done.32.far
  169.5 5.5 collective-permute-done.35.far
  175.3 4.1 attend.9
  182.0 7.1 %attend.10 = (bf16[512,384]{1,0:T(8,128)(2,1)S(1)}, bf16[6,512,128]{2,1,0:T(8,128)(2,1)S(1)}) custom-call(s32[3]{0:T(128)S(1)} %pad_add_fusion.1.f_ref, bf16[15,512,128]{2,1,0:T(8,128)(2,1)S(1)} %get-tuple-element.304.q, bf16[512,128]{1,0:T(8,128)(2,1)S(1)} %select_convert_fusion.13.q_marks, bf16[2048,128]{1,0:T(8,128)(2,1)S(1)} %fusion.2.key_marks, ...), custom_call_target="tpu_custom_call" | custom-call | flops 40000000000 | bytes 1000000 | tf_op jit(solution)/shard_map/attend/pallas_call | solution.py:154
  189.8 7.5 %attend.11 = (bf16[512,384]{1,0:T(8,128)(2,1)S(1)}, bf16[6,512,128]{2,1,0:T(8,128)(2,1)S(1)}) custom-call(s32[3]{0:T(128)S(1)} %pad_add_fusion.1.f_ref, bf16[15,512,128]{2,1,0:T(8,128)(2,1)S(1)} %get-tuple-element.304.q, bf16[512,128]{1,0:T(8,128)(2,1)S(1)} %select_convert_fusion.13.q_marks, bf16[2048,128]{1,0:T(8,128)(2,1)S(1)} %fusion.2.key_marks, ...), custom_call_target="tpu_custom_call" | custom-call | flops 40000000000 | bytes 1000000 | tf_op jit(solution)/shard_map/attend/pallas_call | solution.py:154
  198.1 31.7 %feed_turn.1 = (bf16[1024,512]{1,0:T(8,128)(2,1)}, bf16[960,512]{1,0:T(8,128)(2,1)}, bf16[512,2560]{1,0:T(8,128)(2,1)}, bf16[512,2560]{1,0:T(8,128)(2,1)}, bf16[...) custom-call(s32[3]{0:T(128)} %copy-done.13, ...), custom_call_target="tpu_custom_call" | custom-call | flops 40000000000 | bytes 1000000 | tf_op jit(solution)/shard_map/feed_turn/pallas_call | solution.py:784
  232.8 12.3 %attend_back.6 = (bf16[512,384]{1,0:T(8,128)(2,1)S(1)}, bf16[2,2,512,128]{3,2,1,0:T(8,128)(2,1)S(1)}, bf16[2,2,512,128]{3,2,1,0:T(8,128)(2,1)S(1)}) custom-call(s32[3]{0:T(128)S(1)} %copy-done.14, bf16[15,512,128]{2,1,0:T(8,128)(2,1)S(1)} %get-tuple-element.304.q, bf16[6,512,128]{2,1,0:T(8,128)(2,1)S(1)} %get-tuple-element.319.marks, ...), custom_call_target="tpu_custom_call" | custom-call | flops 40000000000 | bytes 1000000 | tf_op jit(solution)/shard_map/attend_back/pallas_call | solution.py:272
  245.7 12.8 %attend_back.7 = (bf16[512,384]{1,0:T(8,128)(2,1)S(1)}, bf16[2,2,512,128]{3,2,1,0:T(8,128)(2,1)S(1)}, bf16[2,2,512,128]{3,2,1,0:T(8,128)(2,1)S(1)}) custom-call(s32[3]{0:T(128)S(1)} %copy-done.14, bf16[15,512,128]{2,1,0:T(8,128)(2,1)S(1)} %get-tuple-element.304.q, bf16[6,512,128]{2,1,0:T(8,128)(2,1)S(1)} %get-tuple-element.326.marks, ...), custom_call_target="tpu_custom_call" | custom-call | flops 40000000000 | bytes 1000000 | tf_op jit(solution)/shard_map/attend_back/pallas_call | solution.py:272
  260.7 6.7 %attend_back.8 = (bf16[512,256]{1,0:T(8,128)(2,1)S(1)}, bf16[2,1,512,128]{3,2,1,0:T(8,128)(2,1)S(1)}, bf16[2,1,512,128]{3,2,1,0:T(8,128)(2,1)}) custom-call(s32[3]{0:T(128)S(1)} %copy-done.14, bf16[15,512,128]{2,1,0:T(8,128)(2,1)S(1)} %get-tuple-element.304.q, bf16[3,512,128]{2,1,0:T(8,128)(2,1)S(1)} %copy-done.149, bf16[2048,128]{1,0:T(8,128)(2,1)S(1)} %fusion.2.key_marks, ...), custom_call_target="tpu_custom_call" | custom-call | flops 40000000000 | bytes 1000000 | tf_op jit(solution)/shard_map/attend_back/pallas_call | solution.py:272
  270.1 7.2 %collective-permute-done.46.refs_8_ = bf16[2,512,128]{2,1,0:T(8,128)(2,1)} collective-permute-done((bf16[2,512,128]{2,1,0:T(8,128)(2,1)}, bf16[2,512,128]{2,1,0:T(8,128)(2,1)}, u32[]{:S(2)}, u32[]{:S(2)}) %collective-permute-start.46) | collective-permute-done | bytes 262176 | tf_op jit(solution)/shard_map/ppermute | solution.py:998
  287.5 6.4 %project_back.2 = (bf16[512,1664]{1,0:T(8,128)(2,1)S(1)}, f32[512,960]{1,0:T(8,128)S(1)}, bf16[960,512]{1,0:T(8,128)(2,1)S(1)}, f32[1,960]{1,0:T(1,128)S(1)}) custom-call(s32[3]{0:T(128)S(1)} %copy-done.14, bf16[512,256]{1,0:T(8,128)(2,1)S(1)} %copy-done.156, bf16[512,384]{1,0:T(8,128)(2,1)S(1)} %copy-done.143, bf16[512,384]{1,0:T(8,128)(2,1)S(1)} %copy-done.145, ...), custom_call_target="tpu_custom_call" | custom-call | flops 40000000000 | bytes 1000000 | tf_op jit(solution)/shard_map/project_back/pallas_call | solution.py:846
  296.4 3.3 outer_down_far.1
  299.8 3.3 outer_down_own.1
  305.1 19.8 %feed_back.1 = (bf16[512,2560]{1,0:T(8,128)(2,1)}, bf16[512,2560]{1,0:T(8,128)(2,1)}, f32[512,960]{1,0:T(8,128)}, bf16[512,960]{1,0:T(8,128)(2,1)}, bf16[512,256...) custom-call(s32[3]{0:T(128)S(1)} %copy-done.14, ...), custom_call_target="tpu_custom_call" | custom-call | flops 40000000000 | bytes 1000000 | tf_op jit(solution)/shard_map/feed_back/pallas_call | solution.py:690
  325.5 7.5 %collective-permute-done.50 = bf16[1,960,640]{2,1,0:T(8,128)(2,1)S(1)} collective-permute-done((bf16[1,960,640]{2,1,0:T(8,128)(2,1)S(1)}, bf16[1,960,640]{2,1,0:T(8,128)(2,1)S(1)}, u32[]{:S(2)}, u32[]{:S(2)}) %collective-permute-start.50) | collective-permute-done | bytes 1228832 | tf_op jit(solution)/shard_map/ppermute | solution.py:998
  336.2 6.9 %outer_gate.1 = (bf16[4,240,640]{2,1,0:T(8,128)(2,1)S(1)}, bf16[4,240,640]{2,1,0:T(8,128)(2,1)S(1)}, bf16[4,240,640]{2,1,0:T(8,128)(2,1)S(1)}, bf16[4,240,640]{2,1,0:T(8,128)(2,1)S(1)}) custom-call(s32[3]{0:T(128)S(1)} %copy-done.14, bf16[960,512]{1,0:T(8,128)(2,1)S(1)} %copy-done.121, bf16[960,512]{1,0:T(8,128)(2,1)S(1)} %copy-done.119, ...), custom_call_target="tpu_custom_call" | custom-call | flops 40000000000 | bytes 1000000 | tf_op jit(solution)/shard_map/outer_gate/pallas_call | solution.py:888
  344.2 7.3 %outer_up.1 = (bf16[4,240,640]{2,1,0:T(8,128)(2,1)S(1)}, bf16[4,240,640]{2,1,0:T(8,128)(2,1)S(1)}, bf16[4,240,640]{2,1,0:T(8,128)(2,1)S(1)}, bf16[4,240,640]{2,1,0:T(8,128)(2,1)S(1)}) custom-call(s32[3]{0:T(128)S(1)} %copy-done.14, bf16[960,512]{1,0:T(8,128)(2,1)S(1)} %copy-done.121, bf16[960,512]{1,0:T(8,128)(2,1)S(1)} %copy-done.119, ...), custom_call_target="tpu_custom_call" | custom-call | flops 40000000000 | bytes 1000000 | tf_op jit(solution)/shard_map/outer_up/pallas_call | solution.py:888
  354.5 3.6 collective-permute-done.52
  361.6 12.3 %attend_back.9 = (bf16[512,384]{1,0:T(8,128)(2,1)S(1)}, bf16[2,2,512,128]{3,2,1,0:T(8,128)(2,1)S(1)}, bf16[2,2,512,128]{3,2,1,0:T(8,128)(2,1)S(1)}) custom-call(s32[3]{0:T(128)S(1)} %copy-done.14, bf16[15,512,128]{2,1,0:T(8,128)(2,1)S(1)} %copy-done.106, bf16[6,512,128]{2,1,0:T(8,128)(2,1)S(1)} %copy-done.131, bf16[2048,128]{1,0:T(8,128)(2,1)S(1)} %copy-done.1, ...), custom_call_target="tpu_custom_call" | custom-call | flops 40000000000 | bytes 1000000 | tf_op jit(solution)/shard_map/attend_back/pallas_call | solution.py:272
  380.2 12.5 %attend_back.10 = (bf16[512,384]{1,0:T(8,128)(2,1)S(1)}, bf16[2,2,512,128]{3,2,1,0:T(8,128)(2,1)S(1)}, bf16[2,2,512,128]{3,2,1,0:T(8,128)(2,1)S(1)}) custom-call(s32[3]{0:T(128)S(1)} %copy-done.14, bf16[15,512,128]{2,1,0:T(8,128)(2,1)S(1)} %copy-done.106, bf16[6,512,128]{2,1,0:T(8,128)(2,1)S(1)} %copy-done.129, bf16[2048,128]{1,0:T(8,128)(2,1)S(1)} %copy-done.1, ...), custom_call_target="tpu_custom_call" | custom-call | flops 40000000000 | bytes 1000000 | tf_op jit(solution)/shard_map/attend_back/pallas_call | solution.py:272
  398.3 6.1 %attend_back.11 = (bf16[512,256]{1,0:T(8,128)(2,1)S(1)}, bf16[2,1,512,128]{3,2,1,0:T(8,128)(2,1)S(1)}, bf16[2,1,512,128]{3,2,1,0:T(8,128)(2,1)S(1)}) custom-call(s32[3]{0:T(128)S(1)} %copy-done.14, bf16[15,512,128]{2,1,0:T(8,128)(2,1)S(1)} %copy-done.106, bf16[3,512,128]{2,1,0:T(8,128)(2,1)S(1)} %copy-done.147, bf16[2048,128]{1,0:T(8,128)(2,1)S(1)} %copy-done.1, ...), custom_call_target="tpu_custom_call" | custom-call | flops 40000000000 | bytes 1000000 | tf_op jit(solution)/shard_map/attend_back/pallas_call | solution.py:272
  404.6 6.6 %collective-permute-done.64 = bf16[2,240,640]{2,1,0:T(8,128)(2,1)S(1)} collective-permute-done((bf16[2,240,640]{2,1,0:T(8,128)(2,1)S(1)}, bf16[2,240,640]{2,1,0:T(8,128)(2,1)S(1)}, u32[]{:S(2)}, u32[]{:S(2)}) %collective-permute-start.64) | collective-permute-done | bytes 614432 | tf_op jit(solution)/shard_map/ppermute | solution.py:998
  411.4 6.3 %collective-permute-done.66.refs_7_ = bf16[2,512,128]{2,1,0:T(8,128)(2,1)S(1)} collective-permute-done((bf16[2,512,128]{2,1,0:T(8,128)(2,1)S(1)}, bf16[2,512,128]{2,1,0:T(8,128)(2,1)S(1)}, u32[]{:S(2)}, u32[]{:S(2)}) %collective-permute-start.66) | collective-permute-done | bytes 262176 | tf_op jit(solution)/shard_map/ppermute | solution.py:998
  420.6 6.2 %collective-permute-done.70.refs_8_ = bf16[2,512,128]{2,1,0:T(8,128)(2,1)S(1)} collective-permute-done((bf16[2,512,128]{2,1,0:T(8,128)(2,1)S(1)}, bf16[2,512,128]{2,1,0:T(8,128)(2,1)S(1)}, u32[]{:S(2)}, u32[]{:S(2)}) %collective-permute-start.70) | collective-permute-done | bytes 262176 | tf_op jit(solution)/shard_map/ppermute | solution.py:998
  435.2 5.9 %project_back.3 = (bf16[512,1664]{1,0:T(8,128)(2,1)S(1)}, bf16[512,960]{1,0:T(8,128)(2,1)S(1)}, bf16[960,512]{1,0:T(8,128)(2,1)}, f32[1,960]{1,0:T(1,128)S(1)}) custom-call(s32[3]{0:T(128)S(1)} %copy-done.14, bf16[512,256]{1,0:T(8,128)(2,1)S(1)} %get-tuple-element.417.refs_0_, bf16[512,384]{1,0:T(8,128)(2,1)S(1)} %get-tuple-element.397.refs_1_, ...), custom_call_target="tpu_custom_call" | custom-call | flops 40000000000 | bytes 1000000 | tf_op jit(solution)/shard_map/project_back/pallas_call | solution.py:846
  455.2 4.6 outer_in.1
  461.7 3.1 collective-permute-done.75
  467.4 4.2 collective-permute-done.80
  483.2 4.6 collective-permute-done.85
  488.1 7.6 %collective-permute-done.82 = bf16[1,256,1664]{2,1,0:T(8,128)(2,1)S(1)} collective-permute-done((bf16[1,256,1664]{2,1,0:T(8,128)(2,1)S(1)}, bf16[1,256,1664]{2,1,0:T(8,128)(2,1)S(1)}, u32[]{:S(2)}, u32[]{:S(2)}) %collective-permute-start.82) | collective-permute-done | bytes 852000 | tf_op jit(solution)/shard_map/ppermute | solution.py:998
  513.7 5.4 collective-permute-done.90
  519.4 6.4 %collective-permute-done.93 = bf16[2,240,640]{2,1,0:T(8,128)(2,1)S(1)} collective-permute-done((bf16[2,240,640]{2,1,0:T(8,128)(2,1)S(1)}, bf16[2,240,640]{2,1,0:T(8,128)(2,1)S(1)}, u32[]{:S(2)}, u32[]{:S(2)}) %collective-permute-start.93) | collective-permute-done | bytes 614432 | tf_op jit(solution)/shard_map/ppermute | solution.py:998
  533.9 9.2 %collective-permute-done.94 = bf16[960,256]{1,0:T(8,128)(2,1)S(1)} collective-permute-done((bf16[960,256]{1,0:T(8,128)(2,1)S(1)}, bf16[960,256]{1,0:T(8,128)(2,1)S(1)}, u32[]{:S(2)}, u32[]{:S(2)}) %collective-permute-start.94) | collective-permute-done | bytes 491552 | tf_op jit(solution)/shard_map/ppermute | solution.py:998
  545.4 6.2 %collective-permute-done.98 = bf16[1,32,1664]{2,1,0:T(8,128)(2,1)S(1)} collective-permute-done((bf16[1,32,1664]{2,1,0:T(8,128)(2,1)S(1)}, bf16[1,32,1664]{2,1,0:T(8,128)(2,1)S(1)}, u32[]{:S(2)}, u32[]{:S(2)}) %collective-permute-start.98) | collective-permute-done | bytes 106528 | tf_op jit(solution)/shard_map/ppermute | solution.py:998
  553.9 4.0 collective-permute-done.100
  561.5 5.3 collective-permute-done.101
  (648 shorter events, 170.6 us)
Async XLA Ops:
  4.9 30.6 %collective-permute-start = (bf16[240,1664]{1,0:T(8,128)(2,1)S(1)}, bf16[240,1664]{1,0:T(8,128)(2,1)S(1)}, u32[]{:S(2)}, u32[]{:S(2)}) collective-permute-start(bf16[240,1664]{1,0:T(8,128)(2,1)S(1)} %pack.1.own.refs_14_), channel_id=1, source_target_pairs={{0,2},{1,3},{2,0},{3,1},{4,6},{5,7},{6,4},{7,5},{8,10},{9,11},{10,... | collective-permute-start | bytes 2396168 | tf_op jit(solution)/shard_map/ppermute | solution.py:998
  7.9 27.6 %collective-permute-start.1 = (bf16[240,1664]{1,0:T(8,128)(2,1)S(1)}, bf16[240,1664]{1,0:T(8,128)(2,1)S(1)}, u32[]{:S(2)}, u32[]{:S(2)}) collective-permute-start(bf16[240,1664]{1,0:T(8,128)(2,1)S(1)} %pack.1.own.refs_14_), channel_id=1, source_target_pairs={{0,1},{1,0},{2,3},{3,2},{4,5},{5,4},{6,7},{7,6},{8,9},{9,8},{10,11... | collective-permute-start | bytes 2396168 | tf_op jit(solution)/shard_map/ppermute | solution.py:998
  7.9 27.6 %collective-permute-start.2 = (bf16[960,256]{1,0:T(8,128)(2,1)S(1)}, bf16[960,256]{1,0:T(8,128)(2,1)S(1)}, u32[]{:S(2)}, u32[]{:S(2)}) collective-permute-start(bf16[960,256]{1,0:T(8,128)(2,1)S(1)} %slice.345), channel_id=1, source_target_pairs={{0,3},{1,2},{2,1},{3,0},{4,7},{5,6},{6,5},{7,4},{8,11},{9,10},{10,... | collective-permute-start | bytes 1474568 | tf_op jit(solution)/shard_map/ppermute | solution.py:998
  35.5 16.5 %collective-permute-start.4 = (bf16[240,1664]{1,0:T(8,128)(2,1)S(1)}, bf16[240,1664]{1,0:T(8,128)(2,1)S(1)}, u32[]{:S(2)}, u32[]{:S(2)}) collective-permute-start(bf16[240,1664]{1,0:T(8,128)(2,1)S(1)} %collective-permute-done.far.refs_16_), channel_id=1, source_target_pairs={{0,1},{1,0},{2,3},{3,2},{4,5},{5,4},{6,7},{7,6},{8,9},{9,8},{10,11... | collective-permute-start | bytes 2396168 | tf_op jit(solution)/shard_map/ppermute | solution.py:998
  36.1 15.8 %collective-permute-start.3 = (bf16[240,1280]{1,0:T(8,128)(2,1)S(1)}, bf16[240,1280]{1,0:T(8,128)(2,1)S(1)}, u32[]{:S(2)}, u32[]{:S(2)}) collective-permute-start(bf16[240,1280]{1,0:T(8,128)(2,1)S(1)} %slice_select_fusion.1), channel_id=1, source_target_pairs={{0,2},{1,3},{2,0},{3,1},{4,6},{5,7},{6,4},{7,5},{8,10},{9,11},{10,... | collective-permute-start | bytes 1843208 | tf_op jit(solution)/shard_map/ppermute | solution.py:998
  52.0 15.1 %collective-permute-start.5 = (bf16[240,1280]{1,0:T(8,128)(2,1)S(1)}, bf16[240,1280]{1,0:T(8,128)(2,1)S(1)}, u32[]{:S(2)}, u32[]{:S(2)}) collective-permute-start(bf16[240,1280]{1,0:T(8,128)(2,1)S(1)} %slice_select_fusion.2), channel_id=1, source_target_pairs={{0,2},{1,3},{2,0},{3,1},{4,6},{5,7},{6,4},{7,5},{8,10},{9,11},{10,... | collective-permute-start | bytes 1843208 | tf_op jit(solution)/shard_map/ppermute | solution.py:998
  53.8 14.7 %collective-permute-start.6 = (bf16[240,1280]{1,0:T(8,128)(2,1)S(1)}, bf16[240,1280]{1,0:T(8,128)(2,1)S(1)}, u32[]{:S(2)}, u32[]{:S(2)}) collective-permute-start(bf16[240,1280]{1,0:T(8,128)(2,1)S(1)} %collective-permute-done.3.refs_10_.refs_9_), channel_id=1, source_target_pairs={{0,4},{4,0},{8,12},{12,8},{16,20},{20,16},{24,28},{28,24},{1,5},{5... | collective-permute-start | bytes 1843208 | tf_op jit(solution)/shard_map/ppermute | solution.py:998
  75.0 21.1 %collective-permute-start.12 = (bf16[480,640]{1,0:T(8,128)(2,1)S(1)}, bf16[480,640]{1,0:T(8,128)(2,1)S(1)}, u32[]{:S(2)}, u32[]{:S(2)}) collective-permute-start(bf16[480,640]{1,0:T(8,128)(2,1)S(1)} %slice_select_fusion), channel_id=1, source_target_pairs={{0,2},{1,3},{2,0},{3,1},{4,6},{5,7},{6,4},{7,5},{8,10},{9,11},{10,... | collective-permute-start | bytes 1843208 | tf_op jit(solution)/shard_map/ppermute | solution.py:998
  75.4 20.7 %collective-permute-start.16 = (bf16[240,1280]{1,0:T(8,128)(2,1)S(1)}, bf16[240,1280]{1,0:T(8,128)(2,1)S(1)}, u32[]{:S(2)}, u32[]{:S(2)}) collective-permute-start(bf16[240,1280]{1,0:T(8,128)(2,1)S(1)} %collective-permute-done.5.refs_16_.refs_15_), channel_id=1, source_target_pairs={{0,8},{4,12},{8,0},{12,4},{16,24},{20,28},{24,16},{28,20},{1,9},{5... | collective-permute-start | bytes 1843208 | tf_op jit(solution)/shard_map/ppermute | solution.py:998
  77.1 18.9 %collective-permute-start.13 = (bf16[2,512,128]{2,1,0:T(8,128)(2,1)S(1)}, bf16[2,512,128]{2,1,0:T(8,128)(2,1)S(1)}, u32[]{:S(2)}, u32[]{:S(2)}) collective-permute-start(bf16[2,512,128]{2,1,0:T(8,128)(2,1)S(1)} %get-tuple-element.261.own), channel_id=1, source_target_pairs={{0,2},{1,3},{2,0},{3,1},{4,6},{5,7},{6,4},{7,5},{8,10},{9,11},{10,... | collective-permute-start | bytes 786440 | tf_op jit(solution)/shard_map/ppermute | solution.py:998
  78.7 17.4 %collective-permute-start.15 = (bf16[2,512,128]{2,1,0:T(8,128)(2,1)S(1)}, bf16[2,512,128]{2,1,0:T(8,128)(2,1)S(1)}, u32[]{:S(2)}, u32[]{:S(2)}) collective-permute-start(bf16[2,512,128]{2,1,0:T(8,128)(2,1)S(1)} %get-tuple-element.267.own), channel_id=1, source_target_pairs={{0,1},{1,0},{2,3},{3,2},{4,5},{5,4},{6,7},{7,6},{8,9},{9,8},{10,11... | collective-permute-start | bytes 786440 | tf_op jit(solution)/shard_map/ppermute | solution.py:998
  96.1 20.6 %collective-permute-start.21 = (bf16[240,2560]{1,0:T(8,128)(2,1)S(1)}, bf16[240,2560]{1,0:T(8,128)(2,1)S(1)}, u32[]{:S(2)}, u32[]{:S(2)}) collective-permute-start(bf16[240,2560]{1,0:T(8,128)(2,1)S(1)} %copy-done.160), channel_id=1, source_target_pairs={{0,1},{1,0},{2,3},{3,2},{4,5},{5,4},{6,7},{7,6},{8,9},{9,8},{10,11... | collective-permute-start | bytes 3686408 | tf_op jit(solution)/shard_map/ppermute | solution.py:998
  96.2 20.5 %collective-permute-start.17 = (bf16[480,640]{1,0:T(8,128)(2,1)S(1)}, bf16[480,640]{1,0:T(8,128)(2,1)S(1)}, u32[]{:S(2)}, u32[]{:S(2)}) collective-permute-start(bf16[480,640]{1,0:T(8,128)(2,1)S(1)} %collective-permute-done.12.refs_22_.refs_21_), channel_id=1, source_target_pairs={{0,4},{4,0},{8,12},{12,8},{16,20},{20,16},{24,28},{28,24},{1,5},{5... | collective-permute-start | bytes 1843208 | tf_op jit(solution)/shard_map/ppermute | solution.py:998
  97.8 18.9 %collective-permute-start.18 = (bf16[240,960]{1,0:T(8,128)(2,1)S(1)}, bf16[240,960]{1,0:T(8,128)(2,1)S(1)}, u32[]{:S(2)}, u32[]{:S(2)}) collective-permute-start(bf16[240,960]{1,0:T(8,128)(2,1)S(1)} %copy-done.45), channel_id=1, source_target_pairs={{0,2},{1,3},{2,0},{3,1},{4,6},{5,7},{6,4},{7,5},{8,10},{9,11},{10,... | collective-permute-start | bytes 1382408 | tf_op jit(solution)/shard_map/ppermute | solution.py:998
  98.3 18.4 %collective-permute-start.19 = (bf16[2,512,128]{2,1,0:T(8,128)(2,1)S(1)}, bf16[2,512,128]{2,1,0:T(8,128)(2,1)S(1)}, u32[]{:S(2)}, u32[]{:S(2)}) collective-permute-start(bf16[2,512,128]{2,1,0:T(8,128)(2,1)S(1)} %get-tuple-element.267.own), channel_id=1, source_target_pairs={{0,2},{1,3},{2,0},{3,1},{4,6},{5,7},{6,4},{7,5},{8,10},{9,11},{10,... | collective-permute-start | bytes 786440 | tf_op jit(solution)/shard_map/ppermute | solution.py:998
  99.8 16.9 %collective-permute-start.20 = (bf16[2,512,128]{2,1,0:T(8,128)(2,1)S(1)}, bf16[2,512,128]{2,1,0:T(8,128)(2,1)S(1)}, u32[]{:S(2)}, u32[]{:S(2)}) collective-permute-start(bf16[2,512,128]{2,1,0:T(8,128)(2,1)S(1)} %collective-permute-done.13.far), channel_id=1, source_target_pairs={{0,1},{1,0},{2,3},{3,2},{4,5},{5,4},{6,7},{7,6},{8,9},{9,8},{10,11... | collective-permute-start | bytes 786440 | tf_op jit(solution)/shard_map/ppermute | solution.py:998
  116.7 10.1 %collective-permute-start.23 = (bf16[240,1280]{1,0:T(8,128)(2,1)S(1)}, bf16[240,1280]{1,0:T(8,128)(2,1)S(1)}, u32[]{:S(2)}, u32[]{:S(2)}) collective-permute-start(bf16[240,1280]{1,0:T(8,128)(2,1)S(1)} %collective-permute-done.3.refs_10_.refs_9_), channel_id=1, source_target_pairs={{0,1},{1,0},{2,3},{3,2},{4,5},{5,4},{6,7},{7,6},{8,9},{9,8},{10,11... | collective-permute-start | bytes 1843208 | tf_op jit(solution)/shard_map/ppermute | solution.py:998
  136.1 18.4 %collective-permute-start.31 = (bf16[960,256]{1,0:T(8,128)(2,1)S(1)}, bf16[960,256]{1,0:T(8,128)(2,1)S(1)}, u32[]{:S(2)}, u32[]{:S(2)}) collective-permute-start(bf16[960,256]{1,0:T(8,128)(2,1)S(1)} %slice.344), channel_id=1, source_target_pairs={{0,3},{1,2},{2,1},{3,0},{4,7},{5,6},{6,5},{7,4},{8,11},{9,10},{10,... | collective-permute-start | bytes 1474568 | tf_op jit(solution)/shard_map/ppermute | solution.py:998
  231.9 13.2 %collective-permute-start.41 = (bf16[960,256]{1,0:T(8,128)(2,1)S(1)}, bf16[960,256]{1,0:T(8,128)(2,1)S(1)}, u32[]{:S(2)}, u32[]{:S(2)}) collective-permute-start(bf16[960,256]{1,0:T(8,128)(2,1)S(1)} %get-tuple-element.317), channel_id=1, source_target_pairs={{0,3},{1,2},{2,1},{3,0},{4,7},{5,6},{6,5},{7,4},{8,11},{9,10},{10,... | collective-permute-start | bytes 1474568 | tf_op jit(solution)/shard_map/ppermute | solution.py:998
  245.1 13.5 %collective-permute-start.42 = (bf16[2,2,512,128]{3,2,1,0:T(8,128)(2,1)S(1)}, bf16[2,2,512,128]{3,2,1,0:T(8,128)(2,1)S(1)}, u32[]{:S(2)}, u32[]{:S(2)}) collective-permute-start(bf16[2,2,512,128]{3,2,1,0:T(8,128)(2,1)S(1)} %get-tuple-element.324), channel_id=1, source_target_pairs={{0,1},{1,0},{2,3},{3,2},{4,5},{5,4},{6,7},{7,6},{8,9},{9,8},{10,11... | collective-permute-start | bytes 1572872 | tf_op jit(solution)/shard_map/ppermute | solution.py:998
  303.5 22.0 %collective-permute-start.49 = (bf16[1,960,640]{2,1,0:T(8,128)(2,1)S(1)}, bf16[1,960,640]{2,1,0:T(8,128)(2,1)S(1)}, u32[]{:S(2)}, u32[]{:S(2)}) collective-permute-start(bf16[1,960,640]{2,1,0:T(8,128)(2,1)S(1)} %get-tuple-element.356), channel_id=1, source_target_pairs={{0,1},{1,0},{2,3},{3,2},{4,5},{5,4},{6,7},{7,6},{8,9},{9,8},{10,11... | collective-permute-start | bytes 3686408 | tf_op jit(solution)/shard_map/ppermute | solution.py:998
  304.1 29.0 %collective-permute-start.50 = (bf16[1,960,640]{2,1,0:T(8,128)(2,1)S(1)}, bf16[1,960,640]{2,1,0:T(8,128)(2,1)S(1)}, u32[]{:S(2)}, u32[]{:S(2)}) collective-permute-start(bf16[1,960,640]{2,1,0:T(8,128)(2,1)S(1)} %add_convert_fusion), channel_id=1, source_target_pairs={{0,2},{1,3},{2,0},{3,1},{4,6},{5,7},{6,4},{7,5},{8,10},{9,11},{10,... | collective-permute-start | bytes 3686408 | tf_op jit(solution)/shard_map/ppermute | solution.py:998
  343.1 15.1 %collective-permute-start.52 = (bf16[1,480,640]{2,1,0:T(8,128)(2,1)S(1)}, bf16[1,480,640]{2,1,0:T(8,128)(2,1)S(1)}, u32[]{:S(2)}, u32[]{:S(2)}) collective-permute-start(bf16[1,480,640]{2,1,0:T(8,128)(2,1)S(1)} %fusion.3), channel_id=1, source_target_pairs={{0,4},{4,0},{8,12},{12,8},{16,20},{20,16},{24,28},{28,24},{1,5},{5... | collective-permute-start | bytes 1843208 | tf_op jit(solution)/shard_map/ppermute | solution.py:998
  343.7 14.7 %collective-permute-start.51 = (bf16[4,240,640]{2,1,0:T(8,128)(2,1)S(1)}, bf16[4,240,640]{2,1,0:T(8,128)(2,1)S(1)}, u32[]{:S(2)}, u32[]{:S(2)}) collective-permute-start(bf16[4,240,640]{2,1,0:T(8,128)(2,1)S(1)} %get-tuple-element.376), channel_id=1, source_target_pairs={{0,1},{1,0},{2,3},{3,2},{4,5},{5,4},{6,7},{7,6},{8,9},{9,8},{10,11... | collective-permute-start | bytes 3686408 | tf_op jit(solution)/shard_map/ppermute | solution.py:998
  343.7 15.1 %collective-permute-start.53 = (bf16[4,240,640]{2,1,0:T(8,128)(2,1)S(1)}, bf16[4,240,640]{2,1,0:T(8,128)(2,1)S(1)}, u32[]{:S(2)}, u32[]{:S(2)}) collective-permute-start(bf16[4,240,640]{2,1,0:T(8,128)(2,1)S(1)} %get-tuple-element.384), channel_id=1, source_target_pairs={{0,1},{1,0},{2,3},{3,2},{4,5},{5,4},{6,7},{7,6},{8,9},{9,8},{10,11... | collective-permute-start | bytes 3686408 | tf_op jit(solution)/shard_map/ppermute | solution.py:998
  358.8 15.1 %collective-permute-start.56 = (bf16[1,240,640]{2,1,0:T(8,128)(2,1)S(1)}, bf16[1,240,640]{2,1,0:T(8,128)(2,1)S(1)}, u32[]{:S(2)}, u32[]{:S(2)}) collective-permute-start(bf16[1,240,640]{2,1,0:T(8,128)(2,1)S(1)} %fusion.7), channel_id=1, source_target_pairs={{0,8},{4,12},{8,0},{12,4},{16,24},{20,28},{24,16},{28,20},{1,9},{5... | collective-permute-start | bytes 921608 | tf_op jit(solution)/shard_map/ppermute | solution.py:998
  360.4 16.3 %collective-permute-start.55 = (bf16[4,240,640]{2,1,0:T(8,128)(2,1)S(1)}, bf16[4,240,640]{2,1,0:T(8,128)(2,1)S(1)}, u32[]{:S(2)}, u32[]{:S(2)}) collective-permute-start(bf16[4,240,640]{2,1,0:T(8,128)(2,1)S(1)} %get-tuple-element.387), channel_id=1, source_target_pairs={{0,1},{1,0},{2,3},{3,2},{4,5},{5,4},{6,7},{7,6},{8,9},{9,8},{10,11... | collective-permute-start | bytes 3686408 | tf_op jit(solution)/shard_map/ppermute | solution.py:998
  360.4 16.3 %collective-permute-start.58 = (bf16[4,240,640]{2,1,0:T(8,128)(2,1)S(1)}, bf16[4,240,640]{2,1,0:T(8,128)(2,1)S(1)}, u32[]{:S(2)}, u32[]{:S(2)}) collective-permute-start(bf16[4,240,640]{2,1,0:T(8,128)(2,1)S(1)} %get-tuple-element.395), channel_id=1, source_target_pairs={{0,1},{1,0},{2,3},{3,2},{4,5},{5,4},{6,7},{7,6},{8,9},{9,8},{10,11... | collective-permute-start | bytes 3686408 | tf_op jit(solution)/shard_map/ppermute | solution.py:998
  360.9 15.8 %collective-permute-start.57 = (bf16[2,240,640]{2,1,0:T(8,128)(2,1)S(1)}, bf16[2,240,640]{2,1,0:T(8,128)(2,1)S(1)}, u32[]{:S(2)}, u32[]{:S(2)}) collective-permute-start(bf16[2,240,640]{2,1,0:T(8,128)(2,1)S(1)} %get-tuple-element.394), channel_id=1, source_target_pairs={{0,2},{1,3},{2,0},{3,1},{4,6},{5,7},{6,4},{7,5},{8,10},{9,11},{10,... | collective-permute-start | bytes 1843208 | tf_op jit(solution)/shard_map/ppermute | solution.py:998
  361.5 13.2 %collective-permute-start.54 = (bf16[1,256,1024]{2,1,0:T(8,128)(2,1)S(1)}, bf16[1,256,1024]{2,1,0:T(8,128)(2,1)S(1)}, u32[]{:S(2)}, u32[]{:S(2)}) collective-permute-start(bf16[1,256,1024]{2,1,0:T(8,128)(2,1)S(1)} %get-tuple-element.386), channel_id=1, source_target_pairs={{0,1},{1,0},{2,3},{3,2},{4,5},{5,4},{6,7},{7,6},{8,9},{9,8},{10,11... | collective-permute-start | bytes 1572872 | tf_op jit(solution)/shard_map/ppermute | solution.py:998
  376.7 17.3 %collective-permute-start.62 = (bf16[1,120,640]{2,1,0:T(8,128)(2,1)S(1)}, bf16[1,120,640]{2,1,0:T(8,128)(2,1)S(1)}, u32[]{:S(2)}, u32[]{:S(2)}) collective-permute-start(bf16[1,120,640]{2,1,0:T(8,128)(2,1)S(1)} %fusion.23), channel_id=1, source_target_pairs={{0,16},{4,20},{8,24},{12,28},{16,0},{20,4},{24,8},{28,12},{1,17},{... | collective-permute-start | bytes 460808 | tf_op jit(solution)/shard_map/ppermute | solution.py:998
  379.4 15.2 %collective-permute-start.61 = (bf16[2,240,640]{2,1,0:T(8,128)(2,1)S(1)}, bf16[2,240,640]{2,1,0:T(8,128)(2,1)S(1)}, u32[]{:S(2)}, u32[]{:S(2)}) collective-permute-start(bf16[2,240,640]{2,1,0:T(8,128)(2,1)S(1)} %get-tuple-element.404), channel_id=1, source_target_pairs={{0,2},{1,3},{2,0},{3,1},{4,6},{5,7},{6,4},{7,5},{8,10},{9,11},{10,... | collective-permute-start | bytes 1843208 | tf_op jit(solution)/shard_map/ppermute | solution.py:998
  380.2 13.9 %collective-permute-start.60 = (bf16[2,2,512,128]{3,2,1,0:T(8,128)(2,1)S(1)}, bf16[2,2,512,128]{3,2,1,0:T(8,128)(2,1)S(1)}, u32[]{:S(2)}, u32[]{:S(2)}) collective-permute-start(bf16[2,2,512,128]{3,2,1,0:T(8,128)(2,1)S(1)} %get-tuple-element.398), channel_id=1, source_target_pairs={{0,1},{1,0},{2,3},{3,2},{4,5},{5,4},{6,7},{7,6},{8,9},{9,8},{10,11... | collective-permute-start | bytes 1572872 | tf_op jit(solution)/shard_map/ppermute | solution.py:998
  395.3 15.9 %collective-permute-start.64 = (bf16[2,240,640]{2,1,0:T(8,128)(2,1)S(1)}, bf16[2,240,640]{2,1,0:T(8,128)(2,1)S(1)}, u32[]{:S(2)}, u32[]{:S(2)}) collective-permute-start(bf16[2,240,640]{2,1,0:T(8,128)(2,1)S(1)} %select_convert_fusion.1), channel_id=1, source_target_pairs={{0,4},{4,0},{8,12},{12,8},{16,20},{20,16},{24,28},{28,24},{1,5},{5... | collective-permute-start | bytes 1843208 | tf_op jit(solution)/shard_map/ppermute | solution.py:998
  395.9 21.9 %collective-permute-start.63 = (bf16[2,240,640]{2,1,0:T(8,128)(2,1)S(1)}, bf16[2,240,640]{2,1,0:T(8,128)(2,1)S(1)}, u32[]{:S(2)}, u32[]{:S(2)}) collective-permute-start(bf16[2,240,640]{2,1,0:T(8,128)(2,1)S(1)} %get-tuple-element.407), channel_id=1, source_target_pairs={{0,2},{1,3},{2,0},{3,1},{4,6},{5,7},{6,4},{7,5},{8,10},{9,11},{10,... | collective-permute-start | bytes 1843208 | tf_op jit(solution)/shard_map/ppermute | solution.py:998
  397.3 20.5 %collective-permute-start.66 = (bf16[2,512,128]{2,1,0:T(8,128)(2,1)S(1)}, bf16[2,512,128]{2,1,0:T(8,128)(2,1)S(1)}, u32[]{:S(2)}, u32[]{:S(2)}) collective-permute-start(bf16[2,512,128]{2,1,0:T(8,128)(2,1)S(1)} %get-tuple-element.415), channel_id=1, source_target_pairs={{0,2},{1,3},{2,0},{3,1},{4,6},{5,7},{6,4},{7,5},{8,10},{9,11},{10,... | collective-permute-start | bytes 786440 | tf_op jit(solution)/shard_map/ppermute | solution.py:998
  397.9 13.5 %collective-permute-start.67 = (bf16[1,120,640]{2,1,0:T(8,128)(2,1)S(1)}, bf16[1,120,640]{2,1,0:T(8,128)(2,1)S(1)}, u32[]{:S(2)}, u32[]{:S(2)}) collective-permute-start(bf16[1,120,640]{2,1,0:T(8,128)(2,1)S(1)} %fusion.10), channel_id=1, source_target_pairs={{0,16},{4,20},{8,24},{12,28},{16,0},{20,4},{24,8},{28,12},{1,17},{... | collective-permute-start | bytes 460808 | tf_op jit(solution)/shard_map/ppermute | solution.py:998
  432.8 10.7 %collective-permute-start.73 = (bf16[1,120,640]{2,1,0:T(8,128)(2,1)}, bf16[1,120,640]{2,1,0:T(8,128)(2,1)}, u32[]{:S(2)}, u32[]{:S(2)}) collective-permute-start(bf16[1,120,640]{2,1,0:T(8,128)(2,1)} %fusion.24), channel_id=1, source_target_pairs={{0,16},{4,20},{8,24},{12,28},{16,0},{20,4},{24,8},{28,12},{1,17},{... | collective-permute-start | bytes 460808 | tf_op jit(solution)/shard_map/ppermute | solution.py:998
  433.1 14.6 %collective-permute-start.72 = (bf16[2,240,640]{2,1,0:T(8,128)(2,1)}, bf16[2,240,640]{2,1,0:T(8,128)(2,1)}, u32[]{:S(2)}, u32[]{:S(2)}) collective-permute-start(bf16[2,240,640]{2,1,0:T(8,128)(2,1)} %get-tuple-element.423), channel_id=1, source_target_pairs={{0,2},{1,3},{2,0},{3,1},{4,6},{5,7},{6,4},{7,5},{8,10},{9,11},{10,... | collective-permute-start | bytes 1843208 | tf_op jit(solution)/shard_map/ppermute | solution.py:998
  434.6 11.0 %collective-permute-start.74 = (bf16[1,240,640]{2,1,0:T(8,128)(2,1)}, bf16[1,240,640]{2,1,0:T(8,128)(2,1)}, u32[]{:S(2)}, u32[]{:S(2)}) collective-permute-start(bf16[1,240,640]{2,1,0:T(8,128)(2,1)} %pad_maximum_fusion.5), channel_id=1, source_target_pairs={{0,8},{4,12},{8,0},{12,4},{16,24},{20,28},{24,16},{28,20},{1,9},{5... | collective-permute-start | bytes 921608 | tf_op jit(solution)/shard_map/ppermute | solution.py:998
  449.7 11.7 %collective-permute-start.76 = (bf16[1,256,1024]{2,1,0:T(8,128)(2,1)S(1)}, bf16[1,256,1024]{2,1,0:T(8,128)(2,1)S(1)}, u32[]{:S(2)}, u32[]{:S(2)}) collective-permute-start(bf16[1,256,1024]{2,1,0:T(8,128)(2,1)S(1)} %copy-done.168), channel_id=1, source_target_pairs={{0,2},{1,3},{2,0},{3,1},{4,6},{5,7},{6,4},{7,5},{8,10},{9,11},{10,... | collective-permute-start | bytes 1572872 | tf_op jit(solution)/shard_map/ppermute | solution.py:998
  451.2 13.7 %collective-permute-start.75 = (bf16[2,240,640]{2,1,0:T(8,128)(2,1)S(1)}, bf16[2,240,640]{2,1,0:T(8,128)(2,1)S(1)}, u32[]{:S(2)}, u32[]{:S(2)}) collective-permute-start(bf16[2,240,640]{2,1,0:T(8,128)(2,1)S(1)} %select_convert_fusion), channel_id=1, source_target_pairs={{0,4},{4,0},{8,12},{12,8},{16,20},{20,16},{24,28},{28,24},{1,5},{5... | collective-permute-start | bytes 1843208 | tf_op jit(solution)/shard_map/ppermute | solution.py:998
  452.6 12.5 %collective-permute-start.77 = (bf16[1,120,640]{2,1,0:T(8,128)(2,1)S(1)}, bf16[1,120,640]{2,1,0:T(8,128)(2,1)S(1)}, u32[]{:S(2)}, u32[]{:S(2)}) collective-permute-start(bf16[1,120,640]{2,1,0:T(8,128)(2,1)S(1)} %fusion.9), channel_id=1, source_target_pairs={{0,16},{4,20},{8,24},{12,28},{16,0},{20,4},{24,8},{28,12},{1,17},{... | collective-permute-start | bytes 460808 | tf_op jit(solution)/shard_map/ppermute | solution.py:998
  474.1 22.1 %collective-permute-start.86 = (bf16[1,480,640]{2,1,0:T(8,128)(2,1)S(1)}, bf16[1,480,640]{2,1,0:T(8,128)(2,1)S(1)}, u32[]{:S(2)}, u32[]{:S(2)}) collective-permute-start(bf16[1,480,640]{2,1,0:T(8,128)(2,1)S(1)} %pad_maximum_fusion), channel_id=1, source_target_pairs={{0,4},{4,0},{8,12},{12,8},{16,20},{20,16},{24,28},{28,24},{1,5},{5... | collective-permute-start | bytes 1843208 | tf_op jit(solution)/shard_map/ppermute | solution.py:998
  477.3 18.4 %collective-permute-start.82 = (bf16[1,256,1664]{2,1,0:T(8,128)(2,1)S(1)}, bf16[1,256,1664]{2,1,0:T(8,128)(2,1)S(1)}, u32[]{:S(2)}, u32[]{:S(2)}) collective-permute-start(bf16[1,256,1664]{2,1,0:T(8,128)(2,1)S(1)} %add_convert_fusion.1), channel_id=1, source_target_pairs={{0,2},{1,3},{2,0},{3,1},{4,6},{5,7},{6,4},{7,5},{8,10},{9,11},{10,... | collective-permute-start | bytes 2555912 | tf_op jit(solution)/shard_map/ppermute | solution.py:998
  511.8 14.0 %collective-permute-start.93 = (bf16[2,240,640]{2,1,0:T(8,128)(2,1)S(1)}, bf16[2,240,640]{2,1,0:T(8,128)(2,1)S(1)}, u32[]{:S(2)}, u32[]{:S(2)}) collective-permute-start(bf16[2,240,640]{2,1,0:T(8,128)(2,1)S(1)} %pad_maximum_fusion.1), channel_id=1, source_target_pairs={{0,4},{4,0},{8,12},{12,8},{16,20},{20,16},{24,28},{28,24},{1,5},{5... | collective-permute-start | bytes 1843208 | tf_op jit(solution)/shard_map/ppermute | solution.py:998
  525.9 18.3 %collective-permute-start.97 = (bf16[2,240,640]{2,1,0:T(8,128)(2,1)S(1)}, bf16[2,240,640]{2,1,0:T(8,128)(2,1)S(1)}, u32[]{:S(2)}, u32[]{:S(2)}) collective-permute-start(bf16[2,240,640]{2,1,0:T(8,128)(2,1)S(1)} %pad_maximum_fusion.2), channel_id=1, source_target_pairs={{0,4},{4,0},{8,12},{12,8},{16,20},{20,16},{24,28},{28,24},{1,5},{5... | collective-permute-start | bytes 1843208 | tf_op jit(solution)/shard_map/ppermute | solution.py:998
  530.5 12.7 %collective-permute-start.94 = (bf16[960,256]{1,0:T(8,128)(2,1)S(1)}, bf16[960,256]{1,0:T(8,128)(2,1)S(1)}, u32[]{:S(2)}, u32[]{:S(2)}) collective-permute-start(bf16[960,256]{1,0:T(8,128)(2,1)S(1)} %get-tuple-element.462), channel_id=1, source_target_pairs={{0,3},{1,2},{2,1},{3,0},{4,7},{5,6},{6,5},{7,4},{8,11},{9,10},{10,... | collective-permute-start | bytes 1474568 | tf_op jit(solution)/shard_map/ppermute | solution.py:998
  (230 other events, 3141.6 us)
